TPU v7x, 32 devices: a whole 2x2x4 slice. The times are simulated.
32 devices in a mesh: groups: 2 (over y), nodes: 4 (over z), feat: 4 (over x, core).
Axes of the slice: x: 2, y: 2, z: 4, core: 2. Of those that a mesh axis runs over, the one named last changes fastest.
Arguments:
- latent: bfloat16 [128, 512], P(('groups', 'nodes'), 'feat'), parts along dimension 0, may hold values from -6 to 6
- edge_state: bfloat16 [2048, 512], P(('groups', 'nodes'), 'feat'), parts along dimension 0, may hold values from -6 to 6
- send_rows: int32 [8, 4, 8], P('groups'), parts along dimension 0, may hold values from 0 to 15, as said below
- sender_slot: int32 [2048], P(('groups', 'nodes')), parts along dimension 0, may hold values from 0 to 47, as said below
- receiver_row: int32 [2048], P(('groups', 'nodes')), parts along dimension 0, may hold values from 0 to 15
- edge_in_weight: bfloat16 [512, 1536], P('feat'), may hold values from -0.15625 to 0.15625
- edge_out_weight: bfloat16 [512, 512], P('feat'), may hold values from -0.25 to 0.25
- edge_gain: bfloat16 [512], P('feat'), may hold values from 0.5 to 1.5
- node_in_weight: bfloat16 [512, 1024], P('feat'), may hold values from -0.1875 to 0.1875
- node_out_weight: bfloat16 [512, 512], P('feat'), may hold values from -0.25 to 0.25
- node_gain: bfloat16 [512], P('feat'), may hold values from 0.5 to 1.5
- edge_cot: bfloat16 [2048, 512], P(('groups', 'nodes'), 'feat'), parts along dimension 0, may hold values from -6 to 6
- node_cot: bfloat16 [128, 512], P(('groups', 'nodes'), 'feat'), parts along dimension 0, may hold values from -6 to 6
Outputs:
- edge_next: bfloat16 [2048, 512], P(('groups', 'nodes'), 'feat'), parts along dimension 0
- node_next: bfloat16 [128, 512], P(('groups', 'nodes'), 'feat'), parts along dimension 0
- edge_grad: bfloat16 [2048, 512], P(('groups', 'nodes'), 'feat'), parts along dimension 0
- node_grad: bfloat16 [128, 512], P(('groups', 'nodes'), 'feat'), parts along dimension 0
There are 2 independent parts, one for each index of `groups`. A program takes and returns all parts, laid end to end along the dimension named above; an argument that names none is the same for every part. Nothing has to cross between parts.
Inputs may be any that keep to these rules, and one draw needn't show every extreme that they name: The 8 rows send_rows[s, d, 0:8] of one pair are distinct rows of block s. `sender_slot`: for an edge of block b, an entry at or above 16 is 16 + s * 8 + k with s != b; the entries of block b that refer to pair (s, b) use its first slots only; blocks next to b along the curve fill all 8 slots.
All inputs are finite; a program needn't handle non-finite values.
Results may differ from a plain program's by a relative error of at most 0.015.
Values may be sent and summed in bfloat16 or wider, within the bound.
No kernel may reach another device: no remote copies, remote signals or barrier semaphores. Data moves between devices by JAX's collectives and lax.ppermute only.
A program may use at most 64 MiB of HBM per device.

v0:
```python
import jax
import jax.numpy as jnp
from jax import lax
from jax.sharding import PartitionSpec as P

D = 512


epsilon = 1e-05


def one_hot(indices, classes, out_type):
    return (indices[:, None] == jnp.arange(classes, dtype=jnp.int32)[None, :]).astype(out_type)


def swish_slope(pre_act):
    sigma = jax.nn.sigmoid(pre_act)
    return sigma * (1.0 + pre_act * (1.0 - sigma))


def contract_rows(grads, weight):
    return lax.dot_general(
        grads, weight, (((1,), (1,)), ((), ())), preferred_element_type=jnp.float32
    )


def exact_dot(left, right):
    return jnp.dot(left, right, preferred_element_type=jnp.float32, precision=lax.Precision.HIGHEST)


def global_sender(sender_slot, send_rows, my_index, node_dev, slot_count):
    remote_slot = jnp.maximum(sender_slot - node_dev, 0)
    source_dev = remote_slot // slot_count
    source_k = remote_slot % slot_count
    far_rows = send_rows[source_dev, my_index, source_k]
    return jnp.where(
        sender_slot < node_dev, my_index * node_dev + sender_slot, source_dev * node_dev + far_rows
    )


def fold_inputs(values, weight_cols, start_sum):
    return start_sum + contract_rows(
        lax.all_gather(values, "feat", axis=1, tiled=True), weight_cols
    )


def normalize(partial_value):
    col_slice = lax.psum_scatter(
        partial_value.astype(jnp.bfloat16), "feat", scatter_dimension=1, tiled=True
    ).astype(jnp.float32)
    row_total, row_squares = lax.psum(
        (jnp.sum(col_slice, axis=1), jnp.sum(col_slice * col_slice, axis=1)), "feat"
    )
    row_mean = (row_total / D)[:, None]
    row_square = (row_squares / D)[:, None]
    inverse = lax.rsqrt(row_square - row_mean * row_mean + epsilon)
    return ((col_slice - row_mean) * inverse, inverse)


def norm_back(grad_normed, normed, inverse):
    row_total, row_cross = lax.psum(
        (jnp.sum(grad_normed, axis=1), jnp.sum(grad_normed * normed, axis=1)), "feat"
    )
    return inverse * (grad_normed - row_total[:, None] / D - normed * row_cross[:, None] / D)


def back_hidden(grad_cols, out_weight, pre_act):
    hidden_sum = contract_rows(lax.all_gather(grad_cols, "feat", axis=1, tiled=True), out_weight)
    return (hidden_sum * swish_slope(pre_act)).astype(jnp.bfloat16)


def shards(
    latent,
    edge_state,
    send_rows,
    sender_slot,
    receiver_row,
    edge_in_weight,
    edge_out_weight,
    edge_gain,
    node_in_weight,
    node_out_weight,
    node_gain,
    edge_cot,
    node_cot,
):
    node_dev = latent.shape[0]
    slot_count = send_rows.shape[2]
    my_index = lax.axis_index("nodes")
    sender_weight = edge_in_weight[:, D : 2 * D]
    full_rows = lax.all_gather(latent, "feat", axis=1, tiled=True)
    source_table = lax.all_gather(full_rows, "nodes", axis=0, tiled=True)
    source_index = global_sender(sender_slot, send_rows, my_index, node_dev, slot_count)
    pick_rows = one_hot(source_index, source_table.shape[0], jnp.bfloat16)
    sender_rows = jnp.dot(pick_rows, source_table, preferred_element_type=jnp.float32).astype(
        jnp.bfloat16
    )
    start_sum = contract_rows(sender_rows, sender_weight)
    take_receiver = one_hot(receiver_row, node_dev, jnp.bfloat16)
    receiver_rows = jnp.dot(take_receiver, full_rows, preferred_element_type=jnp.float32).astype(
        jnp.bfloat16
    )
    start_sum = start_sum + contract_rows(receiver_rows, edge_in_weight[:, 2 * D :])
    edge_pre = fold_inputs(edge_state, edge_in_weight[:, :D], start_sum)
    edge_act = jax.nn.silu(edge_pre).astype(jnp.bfloat16)
    edge_normed, edge_inverse = normalize(
        jnp.dot(edge_act, edge_out_weight, preferred_element_type=jnp.float32)
    )
    edge_next = (
        edge_state.astype(jnp.float32) + edge_normed * edge_gain.astype(jnp.float32)
    ).astype(jnp.bfloat16)
    aggregate = jnp.dot(take_receiver.T, edge_next, preferred_element_type=jnp.float32).astype(
        jnp.bfloat16
    )
    node_start = contract_rows(full_rows, node_in_weight[:, :D])
    node_pre = fold_inputs(aggregate, node_in_weight[:, D:], node_start)
    node_act = jax.nn.silu(node_pre).astype(jnp.bfloat16)
    node_normed, node_inverse = normalize(
        jnp.dot(node_act, node_out_weight, preferred_element_type=jnp.float32)
    )
    node_next = (latent.astype(jnp.float32) + node_normed * node_gain.astype(jnp.float32)).astype(
        jnp.bfloat16
    )
    node_grad_in = node_cot.astype(jnp.float32)
    node_dy = norm_back(
        node_grad_in * node_gain.astype(jnp.float32), node_normed, node_inverse
    ).astype(jnp.bfloat16)
    node_dpre = back_hidden(node_dy, node_out_weight, node_pre)
    node_dx = jnp.dot(node_dpre, node_in_weight, preferred_element_type=jnp.float32)
    agg_grad = lax.psum_scatter(
        node_dx[:, D:].astype(jnp.bfloat16), "feat", scatter_dimension=1, tiled=True
    ).astype(jnp.float32)
    edge_total = edge_cot.astype(jnp.float32) + jnp.take(agg_grad, receiver_row, axis=0)
    edge_dy = norm_back(
        edge_total * edge_gain.astype(jnp.float32), edge_normed, edge_inverse
    ).astype(jnp.bfloat16)
    edge_dpre = back_hidden(edge_dy, edge_out_weight, edge_pre)
    receiver_float = take_receiver.astype(jnp.float32)
    edge_dx = jnp.dot(edge_dpre, edge_in_weight, preferred_element_type=jnp.float32)
    edge_de = edge_dx[:, :D]
    node_part = node_dx[:, :D] + exact_dot(receiver_float.T, edge_dx[:, 2 * D :])
    table_grad = exact_dot(pick_rows.astype(jnp.float32).T, edge_dx[:, D : 2 * D])
    node_part = node_part + lax.psum_scatter(
        table_grad.astype(jnp.bfloat16), "nodes", scatter_dimension=0, tiled=True
    ).astype(jnp.float32)
    edge_share, node_share = (
        lax.psum_scatter(
            edge_de.astype(jnp.bfloat16), "feat", scatter_dimension=1, tiled=True
        ).astype(jnp.float32),
        lax.psum_scatter(
            node_part.astype(jnp.bfloat16), "feat", scatter_dimension=1, tiled=True
        ).astype(jnp.float32),
    )
    edge_grad = (edge_total + edge_share).astype(jnp.bfloat16)
    node_grad = (node_grad_in + node_share).astype(jnp.bfloat16)
    return (edge_next, node_next, edge_grad, node_grad)


def solution(mesh):
    placed = (
        P(("groups", "nodes"), "feat"),
        P(("groups", "nodes"), "feat"),
        P("groups", None, None),
        P(("groups", "nodes")),
        P(("groups", "nodes")),
        P("feat", None),
        P("feat", None),
        P("feat"),
        P("feat", None),
        P("feat", None),
        P("feat"),
        P(("groups", "nodes"), "feat"),
        P(("groups", "nodes"), "feat"),
    )
    return jax.shard_map(
        shards,
        mesh=mesh,
        in_specs=placed,
        out_specs=(
            P(("groups", "nodes"), "feat"),
            P(("groups", "nodes"), "feat"),
            P(("groups", "nodes"), "feat"),
            P(("groups", "nodes"), "feat"),
        ),
        check_vma=False,
    )
```

profile of v0, /device:TPU:0, one launch (start us, length us, event | category | flops | bytes accessed | tf_op | source)
XLA Modules:
  0.0 220.8 jit_solution(10074045152309841268)
XLA Ops:
  7.3 6.5 %all_gather.18 = bf16[16,512]{1,0:T(8,128)(2,1)S(1)} all-gather(bf16[16,128]{1,0:T(8,128)(2,1)} %param.13), channel_id=1, replica_groups=mesh['groups'=2,'nodes'=4,'feat'=4] {'feat'}, dimensions={1}, use_global_device_ids=true | all-gather | bytes 20480 | tf_op jit(solution)/shard_map/all_gather | solution.py:91
  13.7 13.8 %all_gather.19 = bf16[64,512]{1,0:T(8,128)(2,1)S(1)} all-gather(bf16[16,512]{1,0:T(8,128)(2,1)S(1)} %all_gather.18), channel_id=1, replica_groups=mesh['groups'=2,'nodes'=4,'feat'=4] {'nodes'}, dimensions={0}, use_global_device_ids=true | all-gather | bytes 81920 | tf_op jit(solution)/shard_map/all_gather | solution.py:92
  27.6 6.0 %all_gather.20 = bf16[256,512]{1,0:T(8,128)(2,1)S(1)} all-gather(bf16[256,128]{1,0:T(8,128)(2,1)} %param.14), channel_id=1, replica_groups=mesh['groups'=2,'nodes'=4,'feat'=4] {'feat'}, dimensions={1}, use_global_device_ids=true | all-gather | bytes 327680 | tf_op jit(solution)/shard_map/all_gather | solution.py:43
  34.3 2.6 %gather_fusion = s32[256]{0:T(256)S(1)} fusion(s32[4,4,8]{2,1,0:T(4,128)} %param.15, s32[256]{0:T(256)S(1)} %fusion.66), kind=kCustom, calls=%fused_computation | custom fusion | bytes 5120 | tf_op jit(solution)/shard_map/gather | solution.py:35
  38.3 0.8 copy.17
  39.4 21.1 %reduce-scatter.19.cloned.1.call-done = bf16[128,256]{1,0:T(8,128)(2,1)} async-done(((bf16[512,256]{1,0:T(8,128)(2,1)}), bf16[128,256]{1,0:T(8,128)(2,1)}) %reduce-scatter.19.cloned.1.call-update) | async-done | bytes 65552
  60.4 0.9 copy.18
  61.5 5.8 %all-reduce.3 = (f32[256]{0:T(256)S(1)}, f32[256]{0:T(256)S(1)}) all-reduce(f32[256]{0:T(256)S(1)} %get-tuple-element.7, f32[256]{0:T(256)S(1)} %get-tuple-element.6), channel_id=1, replica_groups=mesh['groups'=2,'nodes'=4,'feat'=4] {'feat'}, use_global_device_ids=true, to_apply=%region_4.5 | all-reduce | flops 512 | bytes 4096 | tf_op jit(solution)/shard_map/psum | solution.py:51
  67.7 5.2 %all_gather.21 = bf16[16,512]{1,0:T(8,128)(2,1)S(1)} all-gather(bf16[16,128]{1,0:T(8,128)(2,1)S(1)} %convolution_convert_fusion.5), channel_id=1, replica_groups=mesh['groups'=2,'nodes'=4,'feat'=4] {'feat'}, dimensions={1}, use_global_device_ids=true | all-gather | bytes 20480 | tf_op jit(solution)/shard_map/all_gather | solution.py:43
  74.0 20.7 %reduce-scatter.21.cloned.1.call-done = bf16[128,16]{1,0:T(8,128)(2,1)} async-done(((bf16[512,16]{1,0:T(8,128)(2,1)}), bf16[128,16]{1,0:T(8,128)(2,1)}) %reduce-scatter.21.cloned.1.call-update) | async-done | bytes 4112
  95.7 5.8 %all-reduce.2 = (f32[16]{0:T(128)S(1)}, f32[16]{0:T(128)S(1)}) all-reduce(f32[16]{0:T(128)S(1)} %get-tuple-element.11, f32[16]{0:T(128)S(1)} %get-tuple-element.10), channel_id=1, replica_groups=mesh['groups'=2,'nodes'=4,'feat'=4] {'feat'}, use_global_device_ids=true, to_apply=%region_9.10 | all-reduce | flops 32 | bytes 256 | tf_op jit(solution)/shard_map/psum | solution.py:51
  101.6 5.7 %all-reduce.1 = (f32[16]{0:T(128)S(1)}, f32[16]{0:T(128)S(1)}) all-reduce(f32[16]{0:T(128)S(1)} %get-tuple-element.9, f32[16]{0:T(128)S(1)} %get-tuple-element.8), channel_id=1, replica_groups=mesh['groups'=2,'nodes'=4,'feat'=4] {'feat'}, use_global_device_ids=true, to_apply=%region_13.14 | all-reduce | flops 32 | bytes 256 | tf_op jit(solution)/shard_map/psum | solution.py:61
  108.0 5.2 %all_gather.22 = bf16[16,512]{1,0:T(8,128)(2,1)S(1)} all-gather(bf16[16,128]{1,0:T(8,128)(2,1)S(1)} %get-tuple-element.20), channel_id=1, replica_groups=mesh['groups'=2,'nodes'=4,'feat'=4] {'feat'}, dimensions={1}, use_global_device_ids=true | all-gather | bytes 20480 | tf_op jit(solution)/shard_map/all_gather | solution.py:68
  114.3 20.5 %reduce-scatter.23.cloned.1.call-done = bf16[128,16]{1,0:T(8,128)(2,1)} async-done(((bf16[512,16]{1,0:T(8,128)(2,1)}), bf16[128,16]{1,0:T(8,128)(2,1)}) %reduce-scatter.23.cloned.1.call-update) | async-done | bytes 4112
  134.8 0.8 copy.22
  136.7 5.8 %all-reduce = (f32[256]{0:T(256)S(1)}, f32[256]{0:T(256)S(1)}) all-reduce(f32[256]{0:T(256)S(1)} %get-tuple-element.5, f32[256]{0:T(256)S(1)} %get-tuple-element.4), channel_id=1, replica_groups=mesh['groups'=2,'nodes'=4,'feat'=4] {'feat'}, use_global_device_ids=true, to_apply=%region_18.19 | all-reduce | flops 512 | bytes 4096 | tf_op jit(solution)/shard_map/psum | solution.py:61
  142.7 5.8 %all_gather.23 = bf16[256,512]{1,0:T(8,128)(2,1)S(1)} all-gather(bf16[256,128]{1,0:T(8,128)(2,1)S(1)} %fusion.21), channel_id=1, replica_groups=mesh['groups'=2,'nodes'=4,'feat'=4] {'feat'}, dimensions={1}, use_global_device_ids=true | all-gather | bytes 327680 | tf_op jit(solution)/shard_map/all_gather | solution.py:68
  149.2 1.0 convolution_convert_fusion.3
  150.2 19.5 %reduce-scatter.17.cloned.1.call-done = bf16[16,512]{1,0:T(8,128)(2,1)} async-done(((bf16[64,512]{1,0:T(8,128)(2,1)}), bf16[16,512]{1,0:T(8,128)(2,1)}) %reduce-scatter.17.cloned.1.call-update) | async-done | bytes 16400 | tf_op jit(solution)/shard_map/reduce_scatter | solution.py:143
  169.7 1.0 fusion.6
  171.7 0.8 copy.23
  172.5 17.2 %reduce-scatter.27.cloned.1.call-done = bf16[128,16]{1,0:T(8,128)(2,1)} async-done(((bf16[512,16]{1,0:T(8,128)(2,1)}), bf16[128,16]{1,0:T(8,128)(2,1)}) %reduce-scatter.27.cloned.1.call-update) | async-done | bytes 4112
  191.2 21.1 %reduce-scatter.25.cloned.1.call-done = bf16[128,256]{1,0:T(8,128)(2,1)} async-done(((bf16[512,256]{1,0:T(8,128)(2,1)}), bf16[128,256]{1,0:T(8,128)(2,1)}) %reduce-scatter.25.cloned.1.call-update) | async-done | bytes 65552
  212.3 0.9 copy.24
  (77 shorter events, 12.0 us)
Async XLA Ops:
  7.2 30.8 %copy-start = (bf16[128,512]{1,0:T(8,128)(2,1)S(1)}, bf16[128,512]{1,0:T(8,128)(2,1)}, u32[]{:S(2)}) copy-start(bf16[128,512]{1,0:T(8,128)(2,1)} %param.19) | copy-start | bytes 393220
  7.2 29.7 %copy-start.10 = (s32[256]{0:T(256)S(1)}, s32[256]{0:T(256)}, u32[]{:S(2)}) copy-start(s32[256]{0:T(256)} %param.16) | copy-start | bytes 3076
  7.2 29.7 %copy-start.1 = (bf16[128,1536]{1,0:T(8,128)(2,1)S(1)}, bf16[128,1536]{1,0:T(8,128)(2,1)}, u32[]{:S(2)}) copy-start(bf16[128,1536]{1,0:T(8,128)(2,1)} %param.18) | copy-start | bytes 1179652
  7.2 30.1 %copy-start.9 = (s32[256]{0:T(256)S(1)}, s32[256]{0:T(256)}, u32[]{:S(2)}) copy-start(s32[256]{0:T(256)} %param.17) | copy-start | bytes 3076
  7.2 53.2 %reduce-scatter.19.cloned.1.call-start = ((), (), s32[]{:S(2)}) async-start(), calls=%async_computation.7 | async-start | bytes 327680
  36.9 2.3 %copy-start.11 = (bf16[128]{0:T(256)(128)(2,1)S(1)}, bf16[128]{0:T(256)(128)(2,1)}, u32[]{:S(2)}) copy-start(bf16[128]{0:T(256)(128)(2,1)} %param.20) | copy-start | bytes 772
  36.9 2.3 %copy-start.2 = (bf16[128,1024]{1,0:T(8,128)(2,1)S(1)}, bf16[128,1024]{1,0:T(8,128)(2,1)}, u32[]{:S(2)}) copy-start(bf16[128,1024]{1,0:T(8,128)(2,1)} %param.21) | copy-start | bytes 786436
  36.9 30.4 %copy-start.5 = (bf16[256,128]{1,0:T(8,128)(2,1)S(1)}, bf16[256,128]{1,0:T(8,128)(2,1)}, u32[]{:S(2)}) copy-start(bf16[256,128]{1,0:T(8,128)(2,1)} %param.14) | copy-start | bytes 196612
  37.8 35.3 %copy-start.4 = (bf16[128,512]{1,0:T(8,128)(2,1)S(1)}, bf16[128,512]{1,0:T(8,128)(2,1)}, u32[]{:S(2)}) copy-start(bf16[128,512]{1,0:T(8,128)(2,1)} %param.22) | copy-start | bytes 393220
  37.8 36.2 %copy-start.12 = (bf16[128]{0:T(256)(128)(2,1)S(1)}, bf16[128]{0:T(256)(128)(2,1)}, u32[]{:S(2)}) copy-start(bf16[128]{0:T(256)(128)(2,1)} %param.23) | copy-start | bytes 772
  38.0 63.4 %copy-start.7 = (bf16[16,128]{1,0:T(8,128)(2,1)S(1)}, bf16[16,128]{1,0:T(8,128)(2,1)}, u32[]{:S(2)}) copy-start(bf16[16,128]{1,0:T(8,128)(2,1)} %param.25) | copy-start | bytes 12292
  38.0 69.3 %copy-start.8 = (bf16[16,128]{1,0:T(8,128)(2,1)S(1)}, bf16[16,128]{1,0:T(8,128)(2,1)}, u32[]{:S(2)}) copy-start(bf16[16,128]{1,0:T(8,128)(2,1)} %param.13) | copy-start | bytes 12292
  39.1 55.6 %reduce-scatter.21.cloned.1.call-start = ((), (), s32[]{:S(2)}) async-start(), calls=%async_computation.8 | async-start | bytes 163840
  61.4 75.0 %copy-start.3 = (bf16[256,128]{1,0:T(8,128)(2,1)S(1)}, bf16[256,128]{1,0:T(8,128)(2,1)}, u32[]{:S(2)}) copy-start(bf16[256,128]{1,0:T(8,128)(2,1)} %param.24) | copy-start | bytes 196612
  67.5 69.2 %copy-start.6 = (bf16[256,128]{1,0:T(8,128)(2,1)}, bf16[256,128]{1,0:T(8,128)(2,1)S(1)}, u32[]{:S(2)}) copy-start(bf16[256,128]{1,0:T(8,128)(2,1)S(1)} %fusion.16) | copy-start | bytes 196612
  73.9 60.9 %reduce-scatter.23.cloned.1.call-start = ((), (), s32[]{:S(2)}) async-start(), calls=%async_computation.9 | async-start | bytes 163840
  114.3 55.5 %reduce-scatter.17.cloned.1.call-start = ((), (), s32[]{:S(2)}) async-start(), calls=%async_computation.6 | async-start | bytes 81920 | tf_op jit(solution)/shard_map/reduce_scatter | solution.py:143
  150.2 39.6 %reduce-scatter.27.cloned.1.call-start = ((), (), s32[]{:S(2)}) async-start(), calls=%async_computation.11 | async-start | bytes 163840
  171.6 40.7 %reduce-scatter.25.cloned.1.call-start = ((), (), s32[]{:S(2)}) async-start(), calls=%async_computation.10 | async-start | bytes 327680
Sparse Core Ops, SparseCore 0:
  39.3 21.1 reduce-scatter.18
  74.1 20.6 reduce-scatter.20
  114.4 20.3 reduce-scatter.22
  150.3 19.3 reduce-scatter.16
  172.0 17.7 reduce-scatter.26
  192.2 20.0 reduce-scatter.24
where the time goes:
time: 221 us
  waiting for transfers between devices  120 us (54%)
  blocking collectives  65.4 us (30%)
  between operations  14.4 us (7%)
  local copies, waits for them, and re-layouts  11.8 us (5%)
  matrix products  4.91 us (2%)
  other arithmetic  3.94 us (2%)
    unnamed x11, waiting for transfers between devices  101 us
    reduce_scatter x1, waiting for transfers between devices, shards(): lax.psum_scatter(table_grad.astype(jnp.bfloat16), 'nodes', scatter_dimens...  19.5 us
    all_gather x1, blocking collectives, shards(): source_table = lax.all_gather(full_rows, 'nodes', axis=0, tiled=True)  13.8 us
    psum x2, blocking collectives, normalize(): lax.psum((jnp.sum(col_slice, axis=1), jnp.sum(col_slice * col_slice, axis...  11.5 us
    psum x2, blocking collectives, norm_back(): lax.psum((jnp.sum(grad_normed, axis=1), jnp.sum(grad_normed * normed, axi...  11.4 us
    all_gather x2, blocking collectives, fold_inputs(): lax.all_gather(values, 'feat', axis=1, tiled=True)  11.2 us
    all_gather x2, blocking collectives, back_hidden(): lax.all_gather(grad_cols, 'feat', axis=1, tiled=True)  11 us
    unnamed x36, local copies, waits for them, and re-layouts  8.36 us
  transfers between devices with their start and end apart: 6, of which 6 were waited for; matrix products, arithmetic and copies ran while one was open for 1% of the time, Pallas kernels for 0%

commit v1 on v0

v1 whole, which is shorter than its diff:
```python
import jax
import jax.numpy as jnp
from jax import lax
from jax.sharding import PartitionSpec as P

epsilon = 1e-05
f32 = jnp.float32
bf16 = jnp.bfloat16


def one_hot(indices, classes):
    return (indices[:, None] == jnp.arange(classes, dtype=jnp.int32)[None, :]).astype(bf16)


def dot(left, right):
    return jnp.dot(left, right, preferred_element_type=f32)


def dot_rows(left, right):
    return lax.dot_general(left, right, (((1,), (1,)), ((), ())), preferred_element_type=f32)


def dot_cols(left, right):
    return lax.dot_general(left, right, (((0,), (0,)), ((), ())), preferred_element_type=f32)


def split(values):
    high = values.astype(bf16)
    return high, (values - high.astype(f32)).astype(bf16)


def swish_slope(pre_act):
    sigma = jax.nn.sigmoid(pre_act)
    return sigma * (1.0 + pre_act * (1.0 - sigma))


def normalize(values):
    mean = jnp.mean(values, axis=1, keepdims=True)
    square = jnp.mean(values * values, axis=1, keepdims=True)
    inverse = lax.rsqrt(square - mean * mean + epsilon)
    return (values - mean) * inverse, inverse


def norm_back(grad, normed, inverse):
    total = jnp.mean(grad, axis=1, keepdims=True)
    cross = jnp.mean(grad * normed, axis=1, keepdims=True)
    return inverse * (grad - total - normed * cross)


def side_by_side(blocks):
    count, rows, width = blocks.shape
    return blocks.transpose(1, 0, 2).reshape(rows, count * width)


def shards(
    latent,
    edge_state,
    send_rows,
    sender_slot,
    receiver_row,
    edge_in_weight,
    edge_out_weight,
    edge_gain,
    node_in_weight,
    node_out_weight,
    node_gain,
    edge_cot,
    node_cot,
):
    node_dev, width = latent.shape
    edge_dev = edge_state.shape[0]
    blocks = send_rows.shape[0]
    slots = send_rows.shape[2]
    feats = lax.axis_size("feat")
    features = width * feats
    block = lax.axis_index("nodes")
    feat = lax.axis_index("feat")

    def ring_gather(values):
        held = [values]
        for step in range(1, feats):
            held.append(
                lax.ppermute(
                    values, "feat", [(i, (i + step) % feats) for i in range(feats)]
                )
            )
        rising = jnp.stack(held[::-1] + held[::-1])
        return lax.dynamic_slice_in_dim(rising, feats - 1 - feat, feats, axis=0)

    def gather(values):
        return lax.all_gather(values, "feat", axis=0)

    gains = lax.all_gather(jnp.stack([edge_gain, node_gain]), "feat", axis=1, tiled=True).astype(f32)
    cots = side_by_side(ring_gather(jnp.concatenate([edge_cot, node_cot])))
    edge_cot_full, node_cot_full = cots[:edge_dev].astype(f32), cots[edge_dev:].astype(f32)
    out_full = ring_gather(edge_out_weight).reshape(-1, features)

    table = lax.all_gather(latent, ("nodes", "feat"), axis=0)
    table = table.reshape(blocks, feats, node_dev, width).transpose(0, 2, 1, 3)
    table = table.reshape(blocks * node_dev, features)
    state = side_by_side(gather(edge_state))
    own = lax.dynamic_slice_in_dim(table, block * node_dev, node_dev, axis=0)

    lent = lax.dynamic_index_in_dim(send_rows, block, axis=1, keepdims=False)
    lent = lent + node_dev * jnp.arange(blocks, dtype=jnp.int32)[:, None]
    rows_of = jnp.concatenate(
        [block * node_dev + jnp.arange(node_dev, dtype=jnp.int32), lent.reshape(-1)]
    )
    pick = dot(
        one_hot(sender_slot, node_dev + blocks * slots), one_hot(rows_of, blocks * node_dev)
    ).astype(bf16)
    take = one_hot(receiver_row, node_dev)

    sender_rows = dot(pick, table).astype(bf16)
    receiver_rows = dot(take, own).astype(bf16)
    edge_pre = dot_rows(jnp.concatenate([state, sender_rows, receiver_rows], axis=1), edge_in_weight)
    edge_act = jax.nn.silu(edge_pre).astype(bf16)

    act_full = side_by_side(gather(edge_act))
    edge_normed, edge_inverse = normalize(dot(act_full, out_full))
    edge_next_full = (state.astype(f32) + edge_normed * gains[0]).astype(bf16)
    edge_next = lax.dynamic_slice_in_dim(edge_next_full, feat * width, width, axis=1)
    aggregate = dot_cols(take, edge_next_full).astype(bf16)
    node_pre = dot_rows(jnp.concatenate([own, aggregate], axis=1), node_in_weight)
    node_act = jax.nn.silu(node_pre).astype(bf16)

    node_out = jnp.sum(gather(dot(node_act, node_out_weight).astype(bf16)).astype(f32), axis=0)
    node_normed, node_inverse = normalize(node_out)
    node_next_full = (own.astype(f32) + node_normed * gains[1]).astype(bf16)
    node_next = lax.dynamic_slice_in_dim(node_next_full, feat * width, width, axis=1)
    node_dy = norm_back(node_cot_full * gains[1], node_normed, node_inverse).astype(bf16)
    node_dpre = (dot_rows(node_dy, node_out_weight) * swish_slope(node_pre)).astype(bf16)
    node_dx = dot(node_dpre, node_in_weight)

    agg_grad = jnp.sum(gather(node_dx[:, features:].astype(bf16)).astype(f32), axis=0)
    high, low = split(agg_grad)
    edge_total = edge_cot_full + dot(take, high) + dot(take, low)
    edge_dy = norm_back(edge_total * gains[0], edge_normed, edge_inverse).astype(bf16)
    edge_dpre = (dot_rows(edge_dy, edge_out_weight) * swish_slope(edge_pre)).astype(bf16)

    edge_de = dot(edge_dpre, edge_in_weight[:, :features]).astype(bf16)
    edge_de = edge_de.reshape(edge_dev, feats, width).transpose(1, 0, 2)
    edge_share = jnp.sum(lax.all_to_all(edge_de, "feat", 0, 0).astype(f32), axis=0)
    own_total = lax.dynamic_slice_in_dim(edge_total, feat * width, width, axis=1)
    edge_grad = (own_total + edge_share).astype(bf16)

    sent_high, sent_low = split(dot_cols(pick, edge_dpre))
    sender_weight = edge_in_weight[:, features : 2 * features]
    sent = dot(sent_high, sender_weight) + dot(sent_low, sender_weight)
    got_high, got_low = split(dot_cols(take, edge_dpre))
    receiver_weight = edge_in_weight[:, 2 * features :]
    home = dot(got_high, receiver_weight) + dot(got_low, receiver_weight) + node_dx[:, :features]
    sent = sent.reshape(blocks, node_dev, features)
    is_home = (jnp.arange(blocks) == block)[:, None, None]
    sent = (sent + jnp.where(is_home, home[None], 0.0)).astype(bf16)
    sent = sent.reshape(blocks, node_dev, feats, width).transpose(0, 2, 1, 3)
    sent = sent.reshape(blocks * feats, node_dev, width)
    node_share = jnp.sum(lax.all_to_all(sent, ("nodes", "feat"), 0, 0).astype(f32), axis=0)
    node_grad = (node_cot.astype(f32) + node_share).astype(bf16)
    return (edge_next, node_next, edge_grad, node_grad)


def solution(mesh):
    rows = P(("groups", "nodes"), "feat")
    flat = P(("groups", "nodes"))
    matrix = P("feat", None)
    vector = P("feat")
    return jax.shard_map(
        shards,
        mesh=mesh,
        in_specs=(
            rows,
            rows,
            P("groups", None, None),
            flat,
            flat,
            matrix,
            matrix,
            vector,
            matrix,
            matrix,
            vector,
            rows,
            rows,
        ),
        out_specs=(rows, rows, rows, rows),
        check_vma=False,
    )
```

time: 221 us -> 92 us (0.42)
  waiting for transfers between devices: 120 us -> 14 us
  blocking collectives: 65.4 us -> 48.6 us
  between operations: 14.4 us -> 1.03 us
  starting transfers between devices: 0.25 us -> 13.5 us
  local copies, waits for them, and re-layouts: 11.8 us -> 5.58 us
    unnamed x11 -> x0, waiting for transfers between devices: 101 us -> none
    psum x4 -> x0, blocking collectives: 22.9 us -> none  [the longest x2 11.5 us: normalize(): lax.psum((jnp.sum(col_slice, axis=1), jnp.sum(col_slice * col_slice, axis...]
    reduce_scatter x1 -> x0, waiting for transfers between devices: 19.5 us -> none  [shards(): lax.psum_scatter(table_grad.astype(jnp.bfloat16), 'nodes', scatter_dimens...]
    all_to_all x0 -> x2, waiting for transfers between devices: none -> 10.6 us  [the longest x1 5.37 us: shards(): lax.all_to_all(edge_de, 'feat', 0, 0).astype(f32)]
    all_to_all x0 -> x2, starting transfers between devices: none -> 6.91 us  [the longest x1 3.5 us: shards(): lax.all_to_all(sent, ('nodes', 'feat'), 0, 0).astype(f32)]
    ppermute x0 -> x6, starting transfers between devices: none -> 6.55 us  [ring_gather(): lax.ppermute(values, 'feat', [(i, (i + step) % feats) for i in range(feat...]
    unnamed x36 -> x33, local copies, waits for them, and re-layouts: 8.36 us -> 2.08 us
    all_gather x6, blocking collectives: 42.4 us -> 48.6 us  [the longest x4 22.4 us: gather(): return lax.all_gather(values, 'feat', axis=0)]
  transfers between devices with their start and end apart: 6 -> 8, of which waited for: 6 -> 3; matrix products, arithmetic and copies ran while one was open for 1% -> 8% of each run, Pallas kernels for 0% -> 0%
where the time goes in v1:
time: 92 us; the launch traced here: 91.5 us
  blocking collectives  48.6 us (53%)
  waiting for transfers between devices  14 us (15%)
  starting transfers between devices  13.5 us (15%)
  local copies, waits for them, and re-layouts  5.58 us (6%)
  matrix products  5.37 us (6%)
  other arithmetic  3.47 us (4%)
  between operations  1.03 us (1%)
    all_gather x4, blocking collectives, gather(): return lax.all_gather(values, 'feat', axis=0)  22.4 us
    all_gather x1, blocking collectives, shards(): table = lax.all_gather(latent, ('nodes', 'feat'), axis=0)  21.2 us
    ppermute x6, starting transfers between devices, ring_gather(): lax.ppermute(values, 'feat', [(i, (i + step) % feats) for i in range(feat...  6.55 us
    all_to_all x1, waiting for transfers between devices, shards(): lax.all_to_all(edge_de, 'feat', 0, 0).astype(f32)  5.37 us
    all_to_all x1, waiting for transfers between devices, shards(): lax.all_to_all(sent, ('nodes', 'feat'), 0, 0).astype(f32)  5.26 us
    all_gather x1, blocking collectives, shards(): lax.all_gather(jnp.stack([edge_gain, node_gain]), 'feat', axis=1, tiled=T...  5.04 us
    dot_general x13, matrix products, dot(): return jnp.dot(left, right, preferred_element_type=f32)  3.83 us
    all_to_all x1, starting transfers between devices, shards(): lax.all_to_all(sent, ('nodes', 'feat'), 0, 0).astype(f32)  3.5 us
  transfers between devices with their start and end apart: 8, of which 3 were waited for; matrix products, arithmetic and copies ran while one was open for 8% of the time, Pallas kernels for 0%

profile of v1, /device:TPU:0, one launch (start us, length us, event | category | flops | bytes accessed | tf_op | source)
XLA Modules:
  0.0 91.5 jit_solution(1396278043240236479)
XLA Ops:
  0.6 2.4 %collective-permute-start = (bf16[128,512]{1,0:T(8,128)(2,1)}, bf16[128,512]{1,0:T(8,128)(2,1)S(1)}, u32[]{:S(2)}, u32[]{:S(2)}) collective-permute-start(bf16[128,512]{1,0:T(8,128)(2,1)} %param.19), channel_id=1, source_target_pairs={{0,3},{1,0},{2,1},{3,2},{4,7},{5,4},{6,5},{7,6},{8,11},{9,8},{10,9... | collective-permute-start | bytes 393224 | tf_op jit(solution)/shard_map/ppermute | solution.py:83
  3.1 0.6 collective-permute-start.1
  3.9 0.8 constant_dynamic-update-slice_fusion.1
  4.7 0.7 constant_dynamic-update-slice_fusion
  5.4 1.6 %collective-permute-start.3 = (bf16[272,128]{1,0:T(8,128)(2,1)S(1)}, bf16[272,128]{1,0:T(8,128)(2,1)S(1)}, u32[]{:S(2)}, u32[]{:S(2)}) collective-permute-start(bf16[272,128]{1,0:T(8,128)(2,1)S(1)} %constant_dynamic-update-slice_fusion), channel_id=1, source_target_pairs={{0,3},{1,0},{2,1},{3,2},{4,7},{5,4},{6,5},{7,6},{8,11},{9,8},{10,9... | collective-permute-start | bytes 208904 | tf_op jit(solution)/shard_map/ppermute | solution.py:83
  7.0 1.4 %collective-permute-start.4 = (bf16[272,128]{1,0:T(8,128)(2,1)S(1)}, bf16[272,128]{1,0:T(8,128)(2,1)S(1)}, u32[]{:S(2)}, u32[]{:S(2)}) collective-permute-start(bf16[272,128]{1,0:T(8,128)(2,1)S(1)} %constant_dynamic-update-slice_fusion), channel_id=1, source_target_pairs={{0,2},{1,3},{2,0},{3,1},{4,6},{5,7},{6,4},{7,5},{8,10},{9,11},{10,... | collective-permute-start | bytes 208904 | tf_op jit(solution)/shard_map/ppermute | solution.py:83
  8.4 21.2 %all-gather.1 = bf16[256,128]{1,0:T(8,128)(2,1)S(1)} all-gather(bf16[16,128]{1,0:T(8,128)(2,1)} %param.13), channel_id=3, replica_groups=mesh['groups'=2,'nodes'=4,'feat'=4] {'nodes','feat'}, dimensions={0}, use_global_device_ids=true | all-gather | bytes 69632 | tf_op jit(solution)/shard_map/all_gather | solution.py:98
  29.7 0.7 dynamic-slice_reduce_fusion
  30.7 0.9 %convolution_convert_fusion.3 = bf16[256,64]{0,1:T(8,128)(2,1)S(1)} fusion(s32[256]{0:T(256)} %param.16, s32[48]{0:T(128)S(1)} %pad_add_fusion), kind=kOutput, calls=%fused_computation.10 | convolution fusion | flops 1604608 | bytes 33984 | tf_op jit(solution)/shard_map/dot_general | solution.py:16
  31.9 6.1 %all-gather = bf16[1024,128]{1,0:T(8,128)(2,1)S(1)} all-gather(bf16[256,128]{1,0:T(8,128)(2,1)} %param.14), channel_id=2, replica_groups=mesh['groups'=2,'nodes'=4,'feat'=4] {'feat'}, dimensions={0}, use_global_device_ids=true | all-gather | bytes 327680 | tf_op jit(solution)/shard_map/all_gather | solution.py:91
  38.3 5.0 %all_gather.39 = bf16[2,512]{1,0:T(2,128)(2,1)S(1)} all-gather(bf16[2,128]{1,0:T(2,128)(2,1)S(1)} %pad_maximum_fusion.1), channel_id=1, replica_groups=mesh['groups'=2,'nodes'=4,'feat'=4] {'feat'}, dimensions={1}, use_global_device_ids=true | all-gather | bytes 2560 | tf_op jit(solution)/shard_map/all_gather | solution.py:93
  44.1 5.8 %all-gather.2 = bf16[1024,128]{1,0:T(8,128)(2,1)S(1)} all-gather(bf16[256,128]{1,0:T(8,128)(2,1)S(1)} %get-tuple-element.20), channel_id=4, replica_groups=mesh['groups'=2,'nodes'=4,'feat'=4] {'feat'}, dimensions={0}, use_global_device_ids=true | all-gather | bytes 327680 | tf_op jit(solution)/shard_map/all_gather | solution.py:91
  50.3 3.4 %collective-permute-done.5 = bf16[272,128]{1,0:T(8,128)(2,1)S(1)} collective-permute-done((bf16[272,128]{1,0:T(8,128)(2,1)S(1)}, bf16[272,128]{1,0:T(8,128)(2,1)S(1)}, u32[]{:S(2)}, u32[]{:S(2)}) %collective-permute-start.5) | collective-permute-done | bytes 69664 | tf_op jit(solution)/shard_map/ppermute | solution.py:83
  53.9 0.7 copy-done.3
  56.1 5.2 %all-gather.3 = bf16[64,512]{1,0:T(8,128)(2,1)S(1)} all-gather(bf16[16,512]{1,0:T(8,128)(2,1)S(1)} %convolution_convert_fusion.4), channel_id=5, replica_groups=mesh['groups'=2,'nodes'=4,'feat'=4] {'feat'}, dimensions={0}, use_global_device_ids=true | all-gather | bytes 81920 | tf_op jit(solution)/shard_map/all_gather | solution.py:91
  62.4 5.2 %all-gather.4 = bf16[64,512]{1,0:T(8,128)(2,1)S(1)} all-gather(bf16[16,512]{1,0:T(8,128)(2,1)S(1)} %slice.83), channel_id=6, replica_groups=mesh['groups'=2,'nodes'=4,'feat'=4] {'feat'}, dimensions={0}, use_global_device_ids=true | all-gather | bytes 81920 | tf_op jit(solution)/shard_map/all_gather | solution.py:91
  70.4 0.6 pad_maximum_fusion
  71.0 3.5 %all-to-all-start.1 = ((bf16[16,16,128]{2,1,0:T(8,128)(2,1)}), bf16[16,16,128]{2,1,0:T(8,128)(2,1)S(1)}, u32[]{:S(2)}, u32[]{:S(2)}) async-start(bf16[16,16,128]{2,1,0:T(8,128)(2,1)} %bitcast.25), calls=%async_computation.1 | async-start | bytes 131072 | tf_op jit(solution)/shard_map/all_to_all | solution.py:158
  74.8 0.7 copy.51
  75.5 0.6 constant_dynamic-slice_fusion
  76.1 5.3 %all-to-all-done.1 = bf16[16,16,128]{2,1,0:T(8,128)(2,1)S(1)} async-done(((bf16[16,16,128]{2,1,0:T(8,128)(2,1)}), bf16[16,16,128]{2,1,0:T(8,128)(2,1)S(1)}, u32[]{:S(2)}, u32[]{:S(2)}) %all-to-all-start.1) | async-done | bytes 65568 | tf_op jit(solution)/shard_map/all_to_all | solution.py:158
  81.4 3.4 %all-to-all-start = ((bf16[4,256,128]{2,1,0:T(8,128)(2,1)}), bf16[4,256,128]{2,1,0:T(8,128)(2,1)S(1)}, u32[]{:S(2)}, u32[]{:S(2)}) async-start(bf16[4,256,128]{2,1,0:T(8,128)(2,1)} %bitcast.109), calls=%async_computation | async-start | bytes 524288 | tf_op jit(solution)/shard_map/all_to_all | solution.py:143
  85.5 5.4 %all-to-all-done = bf16[4,256,128]{2,1,0:T(8,128)(2,1)S(1)} async-done(((bf16[4,256,128]{2,1,0:T(8,128)(2,1)}), bf16[4,256,128]{2,1,0:T(8,128)(2,1)S(1)}, u32[]{:S(2)}, u32[]{:S(2)}) %all-to-all-start) | async-done | bytes 262176 | tf_op jit(solution)/shard_map/all_to_all | solution.py:143
  90.9 0.7 add_convert_fusion.2
  (94 shorter events, 8.4 us)
Async XLA Ops:
  0.6 54.9 %copy-start = (bf16[128,1024]{1,0:T(8,128)(2,1)S(1)}, bf16[128,1024]{1,0:T(8,128)(2,1)}, u32[]{:S(2)}) copy-start(bf16[128,1024]{1,0:T(8,128)(2,1)} %param.21) | copy-start | bytes 786436
  0.6 53.2 %collective-permute-start = (bf16[128,512]{1,0:T(8,128)(2,1)}, bf16[128,512]{1,0:T(8,128)(2,1)S(1)}, u32[]{:S(2)}, u32[]{:S(2)}) collective-permute-start(bf16[128,512]{1,0:T(8,128)(2,1)} %param.19), channel_id=1, source_target_pairs={{0,3},{1,0},{2,1},{3,2},{4,7},{5,4},{6,5},{7,6},{8,11},{9,8},{10,9... | collective-permute-start | bytes 393224 | tf_op jit(solution)/shard_map/ppermute | solution.py:83
  3.1 50.8 %collective-permute-start.1 = (bf16[128,512]{1,0:T(8,128)(2,1)}, bf16[128,512]{1,0:T(8,128)(2,1)S(1)}, u32[]{:S(2)}, u32[]{:S(2)}) collective-permute-start(bf16[128,512]{1,0:T(8,128)(2,1)} %param.19), channel_id=1, source_target_pairs={{0,2},{1,3},{2,0},{3,1},{4,6},{5,7},{6,4},{7,5},{8,10},{9,11},{10,... | collective-permute-start | bytes 393224 | tf_op jit(solution)/shard_map/ppermute | solution.py:83
  3.7 50.2 %collective-permute-start.2 = (bf16[128,512]{1,0:T(8,128)(2,1)}, bf16[128,512]{1,0:T(8,128)(2,1)S(1)}, u32[]{:S(2)}, u32[]{:S(2)}) collective-permute-start(bf16[128,512]{1,0:T(8,128)(2,1)} %param.19), channel_id=1, source_target_pairs={{0,1},{1,2},{2,3},{3,0},{4,5},{5,6},{6,7},{7,4},{8,9},{9,10},{10,1... | collective-permute-start | bytes 393224 | tf_op jit(solution)/shard_map/ppermute | solution.py:83
  5.4 44.5 %collective-permute-start.3 = (bf16[272,128]{1,0:T(8,128)(2,1)S(1)}, bf16[272,128]{1,0:T(8,128)(2,1)S(1)}, u32[]{:S(2)}, u32[]{:S(2)}) collective-permute-start(bf16[272,128]{1,0:T(8,128)(2,1)S(1)} %constant_dynamic-update-slice_fusion), channel_id=1, source_target_pairs={{0,3},{1,0},{2,1},{3,2},{4,7},{5,4},{6,5},{7,6},{8,11},{9,8},{10,9... | collective-permute-start | bytes 208904 | tf_op jit(solution)/shard_map/ppermute | solution.py:83
  7.0 43.3 %collective-permute-start.4 = (bf16[272,128]{1,0:T(8,128)(2,1)S(1)}, bf16[272,128]{1,0:T(8,128)(2,1)S(1)}, u32[]{:S(2)}, u32[]{:S(2)}) collective-permute-start(bf16[272,128]{1,0:T(8,128)(2,1)S(1)} %constant_dynamic-update-slice_fusion), channel_id=1, source_target_pairs={{0,2},{1,3},{2,0},{3,1},{4,6},{5,7},{6,4},{7,5},{8,10},{9,11},{10,... | collective-permute-start | bytes 208904 | tf_op jit(solution)/shard_map/ppermute | solution.py:83
  29.6 8.7 %copy-start.6 = (bf16[128]{0:T(256)(128)(2,1)S(1)}, bf16[128]{0:T(256)(128)(2,1)}, u32[]{:S(2)}) copy-start(bf16[128]{0:T(256)(128)(2,1)} %param.23) | copy-start | bytes 772
  29.6 8.7 %copy-start.7 = (bf16[128]{0:T(256)(128)(2,1)S(1)}, bf16[128]{0:T(256)(128)(2,1)}, u32[]{:S(2)}) copy-start(bf16[128]{0:T(256)(128)(2,1)} %param.20) | copy-start | bytes 772
  29.6 13.7 %copy-start.5 = (s32[256]{0:T(256)S(1)}, s32[256]{0:T(256)}, u32[]{:S(2)}) copy-start(s32[256]{0:T(256)} %param.17) | copy-start | bytes 3076
  31.7 12.0 %copy-start.1 = (bf16[128,1536]{1,0:T(8,128)(2,1)S(1)}, bf16[128,1536]{1,0:T(8,128)(2,1)}, u32[]{:S(2)}) copy-start(bf16[128,1536]{1,0:T(8,128)(2,1)} %param.18) | copy-start | bytes 1179652
  49.9 3.7 %collective-permute-start.5 = (bf16[272,128]{1,0:T(8,128)(2,1)S(1)}, bf16[272,128]{1,0:T(8,128)(2,1)S(1)}, u32[]{:S(2)}, u32[]{:S(2)}) collective-permute-start(bf16[272,128]{1,0:T(8,128)(2,1)S(1)} %constant_dynamic-update-slice_fusion), channel_id=1, source_target_pairs={{0,1},{1,2},{2,3},{3,0},{4,5},{5,6},{6,7},{7,4},{8,9},{9,10},{10,1... | collective-permute-start | bytes 208904 | tf_op jit(solution)/shard_map/ppermute | solution.py:83
  53.7 0.9 copy-start.3
  55.1 0.9 copy-start.2
  70.4 14.5 %copy-start.4 = (bf16[16,128]{1,0:T(8,128)(2,1)S(1)}, bf16[16,128]{1,0:T(8,128)(2,1)}, u32[]{:S(2)}) copy-start(bf16[16,128]{1,0:T(8,128)(2,1)} %param.25) | copy-start | bytes 12292
  71.0 10.4 %all-to-all-start.1 = ((bf16[16,16,128]{2,1,0:T(8,128)(2,1)}), bf16[16,16,128]{2,1,0:T(8,128)(2,1)S(1)}, u32[]{:S(2)}, u32[]{:S(2)}) async-start(bf16[16,16,128]{2,1,0:T(8,128)(2,1)} %bitcast.25), calls=%async_computation.1 | async-start | bytes 131072 | tf_op jit(solution)/shard_map/all_to_all | solution.py:158
  81.4 9.4 %all-to-all-start = ((bf16[4,256,128]{2,1,0:T(8,128)(2,1)}), bf16[4,256,128]{2,1,0:T(8,128)(2,1)S(1)}, u32[]{:S(2)}, u32[]{:S(2)}) async-start(bf16[4,256,128]{2,1,0:T(8,128)(2,1)} %bitcast.109), calls=%async_computation | async-start | bytes 524288 | tf_op jit(solution)/shard_map/all_to_all | solution.py:143

commit v2 on v1

v2 whole, which is shorter than its diff:
```python
import jax
import jax.numpy as jnp
from jax import lax
from jax.sharding import PartitionSpec as P

epsilon = 1e-05
f32 = jnp.float32
bf16 = jnp.bfloat16


def one_hot(indices, classes):
    return (indices[:, None] == jnp.arange(classes, dtype=jnp.int32)[None, :]).astype(bf16)


def dot(left, right):
    return jnp.dot(left, right, preferred_element_type=f32)


def dot_rows(left, right):
    return lax.dot_general(left, right, (((1,), (1,)), ((), ())), preferred_element_type=f32)


def dot_cols(left, right):
    return lax.dot_general(left, right, (((0,), (0,)), ((), ())), preferred_element_type=f32)


def split(values):
    high = values.astype(bf16)
    return high, (values - high.astype(f32)).astype(bf16)


def swish_slope(pre_act):
    sigma = jax.nn.sigmoid(pre_act)
    return sigma * (1.0 + pre_act * (1.0 - sigma))


def normalize(values):
    mean = jnp.mean(values, axis=1, keepdims=True)
    square = jnp.mean(values * values, axis=1, keepdims=True)
    inverse = lax.rsqrt(square - mean * mean + epsilon)
    return (values - mean) * inverse, inverse


def norm_back(grad, normed, inverse):
    total = jnp.mean(grad, axis=1, keepdims=True)
    cross = jnp.mean(grad * normed, axis=1, keepdims=True)
    return inverse * (grad - total - normed * cross)


def side_by_side(blocks):
    count, rows, width = blocks.shape
    return blocks.transpose(1, 0, 2).reshape(rows, count * width)


def shards(
    latent,
    edge_state,
    send_rows,
    sender_slot,
    receiver_row,
    edge_in_weight,
    edge_out_weight,
    edge_gain,
    node_in_weight,
    node_out_weight,
    node_gain,
    edge_cot,
    node_cot,
):
    node_dev, width = latent.shape
    edge_dev = edge_state.shape[0]
    blocks = send_rows.shape[0]
    slots = send_rows.shape[2]
    feats = lax.axis_size("feat")
    features = width * feats
    block = lax.axis_index("nodes")
    feat = lax.axis_index("feat")

    def shifted(values, axis, step):
        count = lax.axis_size(axis)
        return lax.ppermute(values, axis, [(i, (i + step) % count) for i in range(count)])

    def ring(values):
        return [values] + [shifted(values, "feat", step) for step in range(1, feats)]

    def rising(held):
        twice = jnp.stack(held[::-1] + held[::-1])
        return lax.dynamic_slice_in_dim(twice, feats - 1 - feat, feats, axis=0)

    def total_over_feat(partial):
        return sum(part.astype(f32) for part in ring(partial.astype(bf16)))

    state_weight = edge_in_weight[:, :features]
    sender_weight = edge_in_weight[:, features : 2 * features]
    receiver_weight = edge_in_weight[:, 2 * features :]

    first = side_by_side(rising(ring(jnp.concatenate([latent, edge_state]))))
    own, state = first[:node_dev], first[node_dev:]
    lent_rows = jnp.stack(split(dot_rows(own, sender_weight)))
    tables = [lent_rows] + [shifted(lent_rows, "nodes", step) for step in range(1, blocks)]

    held_out = ring(edge_out_weight)
    extra = jnp.concatenate([edge_cot, node_cot, edge_gain[None], node_gain[None]])
    extra = side_by_side(rising(ring(extra))).astype(f32)
    edge_cot_full = extra[:edge_dev]
    node_cot_full = extra[edge_dev : edge_dev + node_dev]
    edge_gains = extra[edge_dev + node_dev : edge_dev + node_dev + 1]
    node_gains = extra[edge_dev + node_dev + 1 :]

    lent = lax.dynamic_index_in_dim(send_rows, block, axis=1, keepdims=False)
    steps = (block - jnp.arange(blocks, dtype=jnp.int32)) % blocks
    rows_of = jnp.concatenate(
        [jnp.arange(node_dev, dtype=jnp.int32), (lent + node_dev * steps[:, None]).reshape(-1)]
    )
    pick = dot(
        one_hot(sender_slot, node_dev + blocks * slots), one_hot(rows_of, blocks * node_dev)
    ).astype(bf16)
    take = one_hot(receiver_row, node_dev)

    edge_pre = dot_rows(state, state_weight)
    high, low = split(dot_rows(own, receiver_weight))
    edge_pre = edge_pre + dot(take, high) + dot(take, low)
    lent_high = jnp.concatenate([part[0] for part in tables])
    lent_low = jnp.concatenate([part[1] for part in tables])
    edge_pre = edge_pre + dot(pick, lent_high) + dot(pick, lent_low)
    edge_act = jax.nn.silu(edge_pre).astype(bf16)

    edge_out = sum(dot(act, weight) for act, weight in zip(ring(edge_act), held_out))
    edge_normed, edge_inverse = normalize(edge_out)
    edge_next_full = (state.astype(f32) + edge_normed * edge_gains).astype(bf16)
    edge_next = lax.dynamic_slice_in_dim(edge_next_full, feat * width, width, axis=1)
    aggregate = dot_cols(take, edge_next_full).astype(bf16)
    node_pre = dot_rows(jnp.concatenate([own, aggregate], axis=1), node_in_weight)
    node_act = jax.nn.silu(node_pre).astype(bf16)

    node_normed, node_inverse = normalize(total_over_feat(dot(node_act, node_out_weight)))
    node_next_full = (own.astype(f32) + node_normed * node_gains).astype(bf16)
    node_next = lax.dynamic_slice_in_dim(node_next_full, feat * width, width, axis=1)
    node_dy = norm_back(node_cot_full * node_gains, node_normed, node_inverse).astype(bf16)
    node_dpre = (dot_rows(node_dy, node_out_weight) * swish_slope(node_pre)).astype(bf16)

    high, low = split(total_over_feat(dot(node_dpre, node_in_weight[:, features:])))
    edge_total = edge_cot_full + dot(take, high) + dot(take, low)
    edge_dy = norm_back(edge_total * edge_gains, edge_normed, edge_inverse).astype(bf16)
    edge_dpre = (dot_rows(edge_dy, edge_out_weight) * swish_slope(edge_pre)).astype(bf16)

    def scatter(partial):
        rows = partial.shape[0]
        partial = partial.astype(bf16).reshape(rows, feats, width).transpose(1, 0, 2)
        total = lax.dynamic_index_in_dim(partial, feat, axis=0, keepdims=False).astype(f32)
        for step in range(1, feats):
            sent = lax.dynamic_index_in_dim(partial, (feat + step) % feats, axis=0, keepdims=False)
            total = total + shifted(sent, "feat", step).astype(f32)
        return total

    parts = dot_cols(pick, edge_dpre).reshape(blocks, node_dev, -1)
    sent = parts[0]
    for step in range(1, blocks):
        got = shifted(jnp.stack(split(parts[step])), "nodes", blocks - step).astype(f32)
        sent = sent + got[0] + got[1]
    edge_share = scatter(dot(edge_dpre, state_weight))
    own_total = lax.dynamic_slice_in_dim(edge_total, feat * width, width, axis=1)
    edge_grad = (own_total + edge_share).astype(bf16)

    got_high, got_low = split(dot_cols(take, edge_dpre))
    home = dot(node_dpre, node_in_weight[:, :features])
    home = home + dot(got_high, receiver_weight) + dot(got_low, receiver_weight)
    sent_high, sent_low = split(sent)
    home = home + dot(sent_high, sender_weight) + dot(sent_low, sender_weight)
    node_grad = (node_cot.astype(f32) + scatter(home)).astype(bf16)
    return (edge_next, node_next, edge_grad, node_grad)


def solution(mesh):
    rows = P(("groups", "nodes"), "feat")
    flat = P(("groups", "nodes"))
    matrix = P("feat", None)
    vector = P("feat")
    return jax.shard_map(
        shards,
        mesh=mesh,
        in_specs=(
            rows,
            rows,
            P("groups", None, None),
            flat,
            flat,
            matrix,
            matrix,
            vector,
            matrix,
            matrix,
            vector,
            rows,
            rows,
        ),
        out_specs=(rows, rows, rows, rows),
        check_vma=False,
    )
```

time: 92 us -> 65.9 us (0.72)
  blocking collectives: 48.6 us -> 0 us
  starting transfers between devices: 13.5 us -> 31.9 us
  local copies, waits for them, and re-layouts: 5.58 us -> 7.64 us
  waiting for transfers between devices: 14 us -> 16 us
    all_gather x6 -> x0, blocking collectives: 48.6 us -> none  [the longest x4 22.4 us: gather(): return lax.all_gather(values, 'feat', axis=0)]
    ppermute x6 -> x30, starting transfers between devices: 6.55 us -> 31.9 us  [shifted(): lax.ppermute(values, axis, [(i, (i + step) % count) for i in range(count)])]
    ppermute x6 -> x30, waiting for transfers between devices: 3.37 us -> 16 us  [shifted(): lax.ppermute(values, axis, [(i, (i + step) % count) for i in range(count)])]
    all_to_all x2 -> x0, waiting for transfers between devices: 10.6 us -> none  [the longest x1 5.37 us: shards(): lax.all_to_all(edge_de, 'feat', 0, 0).astype(f32)]
    all_to_all x2 -> x0, starting transfers between devices: 6.91 us -> none  [the longest x1 3.5 us: shards(): lax.all_to_all(sent, ('nodes', 'feat'), 0, 0).astype(f32)]
    unnamed x33 -> x38, local copies, waits for them, and re-layouts: 2.08 us -> 4.5 us
    dot_general x13 -> x19, matrix products: 3.83 us -> 3.92 us  [dot(): return jnp.dot(left, right, preferred_element_type=f32)]
  transfers between devices with their start and end apart: 8 -> 30, of which waited for: 3 -> 16; matrix products, arithmetic and copies ran while one was open for 8% -> 10% of each run, Pallas kernels for 0% -> 0%
where the time goes in v2:
time: 65.9 us; the launch traced here: 65 us
  starting transfers between devices  31.9 us (48%)
  waiting for transfers between devices  16 us (24%)
  local copies, waits for them, and re-layouts  7.64 us (12%)
  matrix products  5.77 us (9%)
  other arithmetic  2.63 us (4%)
  between operations  1.09 us (2%)
    ppermute x30, starting transfers between devices, shifted(): lax.ppermute(values, axis, [(i, (i + step) % count) for i in range(count)])  31.9 us
    ppermute x30, waiting for transfers between devices, shifted(): lax.ppermute(values, axis, [(i, (i + step) % count) for i in range(count)])  16 us
    unnamed x38, local copies, waits for them, and re-layouts  4.5 us
    dot_general x19, matrix products, dot(): return jnp.dot(left, right, preferred_element_type=f32)  3.92 us
  transfers between devices with their start and end apart: 30, of which 16 were waited for; matrix products, arithmetic and copies ran while one was open for 10% of the time, Pallas kernels for 0%

profile of v2, /device:TPU:0, one launch (start us, length us, event | category | flops | bytes accessed | tf_op | source)
XLA Modules:
  0.0 65.0 jit_solution(5521673766093074427)
XLA Ops:
  2.3 2.4 %collective-permute-start = (bf16[272,128]{1,0:T(8,128)(2,1)S(1)}, bf16[272,128]{1,0:T(8,128)(2,1)S(1)}, u32[]{:S(2)}, u32[]{:S(2)}) collective-permute-start(bf16[272,128]{1,0:T(8,128)(2,1)S(1)} %constant_dynamic-update-slice_fusion), channel_id=1, source_target_pairs={{0,3},{1,0},{2,1},{3,2},{4,7},{5,4},{6,5},{7,6},{8,11},{9,8},{10,9... | collective-permute-start | bytes 208904 | tf_op jit(solution)/shard_map/ppermute | solution.py:81
  5.5 1.3 %collective-permute-start.7 = (bf16[128,512]{1,0:T(8,128)(2,1)S(1)}, bf16[128,512]{1,0:T(8,128)(2,1)S(1)}, u32[]{:S(2)}, u32[]{:S(2)}) collective-permute-start(bf16[128,512]{1,0:T(8,128)(2,1)S(1)} %copy-done.4), channel_id=1, source_target_pairs={{0,1},{1,2},{2,3},{3,0},{4,5},{5,6},{6,7},{7,4},{8,9},{9,10},{10,1... | collective-permute-start | bytes 393224 | tf_op jit(solution)/shard_map/ppermute | solution.py:81
  9.9 1.3 %collective-permute-start.9 = (bf16[128,512]{1,0:T(8,128)(2,1)S(1)}, bf16[128,512]{1,0:T(8,128)(2,1)S(1)}, u32[]{:S(2)}, u32[]{:S(2)}) collective-permute-start(bf16[128,512]{1,0:T(8,128)(2,1)S(1)} %copy-done.4), channel_id=1, source_target_pairs={{0,2},{1,3},{2,0},{3,1},{4,6},{5,7},{6,4},{7,5},{8,10},{9,11},{10,... | collective-permute-start | bytes 393224 | tf_op jit(solution)/shard_map/ppermute | solution.py:81
  14.8 1.1 %collective-permute-done.12 = bf16[274,128]{1,0:T(8,128)(2,1)S(1)} collective-permute-done((bf16[274,128]{1,0:T(8,128)(2,1)S(1)}, bf16[274,128]{1,0:T(8,128)(2,1)S(1)}, u32[]{:S(2)}, u32[]{:S(2)}) %collective-permute-start.12) | collective-permute-done | bytes 70176 | tf_op jit(solution)/shard_map/ppermute | solution.py:81
  16.8 0.9 %collective-permute-done.13 = bf16[274,128]{1,0:T(8,128)(2,1)S(1)} collective-permute-done((bf16[274,128]{1,0:T(8,128)(2,1)S(1)}, bf16[274,128]{1,0:T(8,128)(2,1)S(1)}, u32[]{:S(2)}, u32[]{:S(2)}) %collective-permute-start.13) | collective-permute-done | bytes 70176 | tf_op jit(solution)/shard_map/ppermute | solution.py:81
  17.8 1.6 %collective-permute-start.3 = (bf16[2,16,128]{2,1,0:T(8,128)(2,1)S(1)}, bf16[2,16,128]{2,1,0:T(8,128)(2,1)S(1)}, u32[]{:S(2)}, u32[]{:S(2)}) collective-permute-start(bf16[2,16,128]{2,1,0:T(8,128)(2,1)S(1)} %pad_maximum_fusion.1), channel_id=1, source_target_pairs={{0,4},{4,8},{8,12},{12,0},{1,5},{5,9},{9,13},{13,1},{2,6},{6,10},{... | collective-permute-start | bytes 24584 | tf_op jit(solution)/shard_map/ppermute | solution.py:81
  19.8 2.6 %collective-permute-start.4 = (bf16[2,16,128]{2,1,0:T(8,128)(2,1)S(1)}, bf16[2,16,128]{2,1,0:T(8,128)(2,1)S(1)}, u32[]{:S(2)}, u32[]{:S(2)}) collective-permute-start(bf16[2,16,128]{2,1,0:T(8,128)(2,1)S(1)} %pad_maximum_fusion.1), channel_id=1, source_target_pairs={{0,8},{4,12},{8,0},{12,4},{1,9},{5,13},{9,1},{13,5},{2,10},{6,14},... | collective-permute-start | bytes 24584 | tf_op jit(solution)/shard_map/ppermute | solution.py:81
  23.2 1.8 %collective-permute-start.5 = (bf16[2,16,128]{2,1,0:T(8,128)(2,1)S(1)}, bf16[2,16,128]{2,1,0:T(8,128)(2,1)S(1)}, u32[]{:S(2)}, u32[]{:S(2)}) collective-permute-start(bf16[2,16,128]{2,1,0:T(8,128)(2,1)S(1)} %pad_maximum_fusion.1), channel_id=1, source_target_pairs={{0,12},{4,0},{8,4},{12,8},{1,13},{5,1},{9,5},{13,9},{2,14},{6,2},{... | collective-permute-start | bytes 24584 | tf_op jit(solution)/shard_map/ppermute | solution.py:81
  25.0 1.8 %collective-permute-done.5 = bf16[2,16,128]{2,1,0:T(8,128)(2,1)S(1)} collective-permute-done((bf16[2,16,128]{2,1,0:T(8,128)(2,1)S(1)}, bf16[2,16,128]{2,1,0:T(8,128)(2,1)S(1)}, u32[]{:S(2)}, u32[]{:S(2)}) %collective-permute-start.5) | collective-permute-done | bytes 8224 | tf_op jit(solution)/shard_map/ppermute | solution.py:81
  27.6 1.8 %collective-permute-start.10 = (bf16[256,128]{1,0:T(8,128)(2,1)S(1)}, bf16[256,128]{1,0:T(8,128)(2,1)S(1)}, u32[]{:S(2)}, u32[]{:S(2)}) collective-permute-start(bf16[256,128]{1,0:T(8,128)(2,1)S(1)} %get-tuple-element.41), channel_id=1, source_target_pairs={{0,3},{1,0},{2,1},{3,2},{4,7},{5,4},{6,5},{7,6},{8,11},{9,8},{10,9... | collective-permute-start | bytes 196616 | tf_op jit(solution)/shard_map/ppermute | solution.py:81
  29.4 1.4 %collective-permute-start.8 = (bf16[256,128]{1,0:T(8,128)(2,1)S(1)}, bf16[256,128]{1,0:T(8,128)(2,1)S(1)}, u32[]{:S(2)}, u32[]{:S(2)}) collective-permute-start(bf16[256,128]{1,0:T(8,128)(2,1)S(1)} %get-tuple-element.41), channel_id=1, source_target_pairs={{0,2},{1,3},{2,0},{3,1},{4,6},{5,7},{6,4},{7,5},{8,10},{9,11},{10,... | collective-permute-start | bytes 196616 | tf_op jit(solution)/shard_map/ppermute | solution.py:81
  31.6 2.3 %collective-permute-done.8 = bf16[256,128]{1,0:T(8,128)(2,1)S(1)} collective-permute-done((bf16[256,128]{1,0:T(8,128)(2,1)S(1)}, bf16[256,128]{1,0:T(8,128)(2,1)S(1)}, u32[]{:S(2)}, u32[]{:S(2)}) %collective-permute-start.8) | collective-permute-done | bytes 65568 | tf_op jit(solution)/shard_map/ppermute | solution.py:81
  35.7 1.2 %collective-permute-start.16 = (bf16[16,512]{1,0:T(8,128)(2,1)S(1)}, bf16[16,512]{1,0:T(8,128)(2,1)S(1)}, u32[]{:S(2)}, u32[]{:S(2)}) collective-permute-start(bf16[16,512]{1,0:T(8,128)(2,1)S(1)} %convolution_convert_fusion.3), channel_id=1, source_target_pairs={{0,2},{1,3},{2,0},{3,1},{4,6},{5,7},{6,4},{7,5},{8,10},{9,11},{10,... | collective-permute-start | bytes 49160 | tf_op jit(solution)/shard_map/ppermute | solution.py:81
  36.9 1.4 %collective-permute-start.17 = (bf16[16,512]{1,0:T(8,128)(2,1)S(1)}, bf16[16,512]{1,0:T(8,128)(2,1)S(1)}, u32[]{:S(2)}, u32[]{:S(2)}) collective-permute-start(bf16[16,512]{1,0:T(8,128)(2,1)S(1)} %convolution_convert_fusion.3), channel_id=1, source_target_pairs={{0,3},{1,0},{2,1},{3,2},{4,7},{5,4},{6,5},{7,6},{8,11},{9,8},{10,9... | collective-permute-start | bytes 49160 | tf_op jit(solution)/shard_map/ppermute | solution.py:81
  40.4 1.0 %collective-permute-start.18 = (bf16[16,512]{1,0:T(8,128)(2,1)S(1)}, bf16[16,512]{1,0:T(8,128)(2,1)S(1)}, u32[]{:S(2)}, u32[]{:S(2)}) collective-permute-start(bf16[16,512]{1,0:T(8,128)(2,1)S(1)} %convolution_convert_fusion.2), channel_id=1, source_target_pairs={{0,1},{1,2},{2,3},{3,0},{4,5},{5,6},{6,7},{7,4},{8,9},{9,10},{10,1... | collective-permute-start | bytes 49160 | tf_op jit(solution)/shard_map/ppermute | solution.py:81
  41.4 1.1 %collective-permute-start.19 = (bf16[16,512]{1,0:T(8,128)(2,1)S(1)}, bf16[16,512]{1,0:T(8,128)(2,1)S(1)}, u32[]{:S(2)}, u32[]{:S(2)}) collective-permute-start(bf16[16,512]{1,0:T(8,128)(2,1)S(1)} %convolution_convert_fusion.2), channel_id=1, source_target_pairs={{0,2},{1,3},{2,0},{3,1},{4,6},{5,7},{6,4},{7,5},{8,10},{9,11},{10,... | collective-permute-start | bytes 49160 | tf_op jit(solution)/shard_map/ppermute | solution.py:81
  43.6 1.5 %collective-permute-done.19 = bf16[16,512]{1,0:T(8,128)(2,1)S(1)} collective-permute-done((bf16[16,512]{1,0:T(8,128)(2,1)S(1)}, bf16[16,512]{1,0:T(8,128)(2,1)S(1)}, u32[]{:S(2)}, u32[]{:S(2)}) %collective-permute-start.19) | collective-permute-done | bytes 16416 | tf_op jit(solution)/shard_map/ppermute | solution.py:81
  46.9 3.7 %collective-permute-start.24 = (bf16[2,16,128]{2,1,0:T(8,128)(2,1)S(1)}, bf16[2,16,128]{2,1,0:T(8,128)(2,1)S(1)}, u32[]{:S(2)}, u32[]{:S(2)}) collective-permute-start(bf16[2,16,128]{2,1,0:T(8,128)(2,1)S(1)} %pad_maximum_fusion.2), channel_id=1, source_target_pairs={{0,12},{4,0},{8,4},{12,8},{1,13},{5,1},{9,5},{13,9},{2,14},{6,2},{... | collective-permute-start | bytes 24584 | tf_op jit(solution)/shard_map/ppermute | solution.py:81
  51.9 3.3 %collective-permute-done.25 = bf16[2,16,128]{2,1,0:T(8,128)(2,1)S(1)} collective-permute-done((bf16[2,16,128]{2,1,0:T(8,128)(2,1)S(1)}, bf16[2,16,128]{2,1,0:T(8,128)(2,1)S(1)}, u32[]{:S(2)}, u32[]{:S(2)}) %collective-permute-start.25) | collective-permute-done | bytes 8224 | tf_op jit(solution)/shard_map/ppermute | solution.py:81
  56.5 1.2 %collective-permute-start.28 = (bf16[16,128]{1,0:T(8,128)(2,1)S(1)}, bf16[16,128]{1,0:T(8,128)(2,1)S(1)}, u32[]{:S(2)}, u32[]{:S(2)}) collective-permute-start(bf16[16,128]{1,0:T(8,128)(2,1)S(1)} %bitcast.192), channel_id=1, source_target_pairs={{0,2},{1,3},{2,0},{3,1},{4,6},{5,7},{6,4},{7,5},{8,10},{9,11},{10,... | collective-permute-start | bytes 12296 | tf_op jit(solution)/shard_map/ppermute | solution.py:81
  57.7 1.4 %collective-permute-start.29 = (bf16[16,128]{1,0:T(8,128)(2,1)S(1)}, bf16[16,128]{1,0:T(8,128)(2,1)S(1)}, u32[]{:S(2)}, u32[]{:S(2)}) collective-permute-start(bf16[16,128]{1,0:T(8,128)(2,1)S(1)} %bitcast.194), channel_id=1, source_target_pairs={{0,3},{1,0},{2,1},{3,2},{4,7},{5,4},{6,5},{7,6},{8,11},{9,8},{10,9... | collective-permute-start | bytes 12296 | tf_op jit(solution)/shard_map/ppermute | solution.py:81
  59.4 1.0 %collective-permute-start.22 = (bf16[256,128]{1,0:T(8,128)(2,1)S(1)}, bf16[256,128]{1,0:T(8,128)(2,1)S(1)}, u32[]{:S(2)}, u32[]{:S(2)}) collective-permute-start(bf16[256,128]{1,0:T(8,128)(2,1)S(1)} %bitcast.177), channel_id=1, source_target_pairs={{0,2},{1,3},{2,0},{3,1},{4,6},{5,7},{6,4},{7,5},{8,10},{9,11},{10,... | collective-permute-start | bytes 196616 | tf_op jit(solution)/shard_map/ppermute | solution.py:81
  60.6 1.5 %collective-permute-start.23 = (bf16[256,128]{1,0:T(8,128)(2,1)S(1)}, bf16[256,128]{1,0:T(8,128)(2,1)S(1)}, u32[]{:S(2)}, u32[]{:S(2)}) collective-permute-start(bf16[256,128]{1,0:T(8,128)(2,1)S(1)} %bitcast.178), channel_id=1, source_target_pairs={{0,3},{1,0},{2,1},{3,2},{4,7},{5,4},{6,5},{7,6},{8,11},{9,8},{10,9... | collective-permute-start | bytes 196616 | tf_op jit(solution)/shard_map/ppermute | solution.py:81
  62.9 1.4 %collective-permute-done.22 = bf16[256,128]{1,0:T(8,128)(2,1)S(1)} collective-permute-done((bf16[256,128]{1,0:T(8,128)(2,1)S(1)}, bf16[256,128]{1,0:T(8,128)(2,1)S(1)}, u32[]{:S(2)}, u32[]{:S(2)}) %collective-permute-start.22) | collective-permute-done | bytes 65568 | tf_op jit(solution)/shard_map/ppermute | solution.py:81
  (152 shorter events, 24.0 us)
Async XLA Ops:
  2.3 7.7 %collective-permute-start = (bf16[272,128]{1,0:T(8,128)(2,1)S(1)}, bf16[272,128]{1,0:T(8,128)(2,1)S(1)}, u32[]{:S(2)}, u32[]{:S(2)}) collective-permute-start(bf16[272,128]{1,0:T(8,128)(2,1)S(1)} %constant_dynamic-update-slice_fusion), channel_id=1, source_target_pairs={{0,3},{1,0},{2,1},{3,2},{4,7},{5,4},{6,5},{7,6},{8,11},{9,8},{10,9... | collective-permute-start | bytes 208904 | tf_op jit(solution)/shard_map/ppermute | solution.py:81
  4.7 6.6 %collective-permute-start.1 = (bf16[272,128]{1,0:T(8,128)(2,1)S(1)}, bf16[272,128]{1,0:T(8,128)(2,1)S(1)}, u32[]{:S(2)}, u32[]{:S(2)}) collective-permute-start(bf16[272,128]{1,0:T(8,128)(2,1)S(1)} %constant_dynamic-update-slice_fusion), channel_id=1, source_target_pairs={{0,2},{1,3},{2,0},{3,1},{4,6},{5,7},{6,4},{7,5},{8,10},{9,11},{10,... | collective-permute-start | bytes 208904 | tf_op jit(solution)/shard_map/ppermute | solution.py:81
  5.3 6.2 %collective-permute-start.2 = (bf16[272,128]{1,0:T(8,128)(2,1)S(1)}, bf16[272,128]{1,0:T(8,128)(2,1)S(1)}, u32[]{:S(2)}, u32[]{:S(2)}) collective-permute-start(bf16[272,128]{1,0:T(8,128)(2,1)S(1)} %constant_dynamic-update-slice_fusion), channel_id=1, source_target_pairs={{0,1},{1,2},{2,3},{3,0},{4,5},{5,6},{6,7},{7,4},{8,9},{9,10},{10,1... | collective-permute-start | bytes 208904 | tf_op jit(solution)/shard_map/ppermute | solution.py:81
  5.5 23.9 %collective-permute-start.7 = (bf16[128,512]{1,0:T(8,128)(2,1)S(1)}, bf16[128,512]{1,0:T(8,128)(2,1)S(1)}, u32[]{:S(2)}, u32[]{:S(2)}) collective-permute-start(bf16[128,512]{1,0:T(8,128)(2,1)S(1)} %copy-done.4), channel_id=1, source_target_pairs={{0,1},{1,2},{2,3},{3,0},{4,5},{5,6},{6,7},{7,4},{8,9},{9,10},{10,1... | collective-permute-start | bytes 393224 | tf_op jit(solution)/shard_map/ppermute | solution.py:81
  6.8 24.4 %collective-permute-start.11 = (bf16[128,512]{1,0:T(8,128)(2,1)S(1)}, bf16[128,512]{1,0:T(8,128)(2,1)S(1)}, u32[]{:S(2)}, u32[]{:S(2)}) collective-permute-start(bf16[128,512]{1,0:T(8,128)(2,1)S(1)} %copy-done.4), channel_id=1, source_target_pairs={{0,3},{1,0},{2,1},{3,2},{4,7},{5,4},{6,5},{7,6},{8,11},{9,8},{10,9... | collective-permute-start | bytes 393224 | tf_op jit(solution)/shard_map/ppermute | solution.py:81
  9.9 21.7 %collective-permute-start.9 = (bf16[128,512]{1,0:T(8,128)(2,1)S(1)}, bf16[128,512]{1,0:T(8,128)(2,1)S(1)}, u32[]{:S(2)}, u32[]{:S(2)}) collective-permute-start(bf16[128,512]{1,0:T(8,128)(2,1)S(1)} %copy-done.4), channel_id=1, source_target_pairs={{0,2},{1,3},{2,0},{3,1},{4,6},{5,7},{6,4},{7,5},{8,10},{9,11},{10,... | collective-permute-start | bytes 393224 | tf_op jit(solution)/shard_map/ppermute | solution.py:81
  11.2 4.7 %collective-permute-start.12 = (bf16[274,128]{1,0:T(8,128)(2,1)S(1)}, bf16[274,128]{1,0:T(8,128)(2,1)S(1)}, u32[]{:S(2)}, u32[]{:S(2)}) collective-permute-start(bf16[274,128]{1,0:T(8,128)(2,1)S(1)} %pad_maximum_fusion), channel_id=1, source_target_pairs={{0,3},{1,0},{2,1},{3,2},{4,7},{5,4},{6,5},{7,6},{8,11},{9,8},{10,9... | collective-permute-start | bytes 210440 | tf_op jit(solution)/shard_map/ppermute | solution.py:81
  11.5 6.3 %collective-permute-start.13 = (bf16[274,128]{1,0:T(8,128)(2,1)S(1)}, bf16[274,128]{1,0:T(8,128)(2,1)S(1)}, u32[]{:S(2)}, u32[]{:S(2)}) collective-permute-start(bf16[274,128]{1,0:T(8,128)(2,1)S(1)} %pad_maximum_fusion), channel_id=1, source_target_pairs={{0,2},{1,3},{2,0},{3,1},{4,6},{5,7},{6,4},{7,5},{8,10},{9,11},{10,... | collective-permute-start | bytes 210440 | tf_op jit(solution)/shard_map/ppermute | solution.py:81
  15.9 3.9 %collective-permute-start.14 = (bf16[274,128]{1,0:T(8,128)(2,1)S(1)}, bf16[274,128]{1,0:T(8,128)(2,1)S(1)}, u32[]{:S(2)}, u32[]{:S(2)}) collective-permute-start(bf16[274,128]{1,0:T(8,128)(2,1)S(1)} %pad_maximum_fusion), channel_id=1, source_target_pairs={{0,1},{1,2},{2,3},{3,0},{4,5},{5,6},{6,7},{7,4},{8,9},{9,10},{10,1... | collective-permute-start | bytes 210440 | tf_op jit(solution)/shard_map/ppermute | solution.py:81
  17.8 5.4 %collective-permute-start.3 = (bf16[2,16,128]{2,1,0:T(8,128)(2,1)S(1)}, bf16[2,16,128]{2,1,0:T(8,128)(2,1)S(1)}, u32[]{:S(2)}, u32[]{:S(2)}) collective-permute-start(bf16[2,16,128]{2,1,0:T(8,128)(2,1)S(1)} %pad_maximum_fusion.1), channel_id=1, source_target_pairs={{0,4},{4,8},{8,12},{12,0},{1,5},{5,9},{9,13},{13,1},{2,6},{6,10},{... | collective-permute-start | bytes 24584 | tf_op jit(solution)/shard_map/ppermute | solution.py:81
  19.8 5.2 %collective-permute-start.4 = (bf16[2,16,128]{2,1,0:T(8,128)(2,1)S(1)}, bf16[2,16,128]{2,1,0:T(8,128)(2,1)S(1)}, u32[]{:S(2)}, u32[]{:S(2)}) collective-permute-start(bf16[2,16,128]{2,1,0:T(8,128)(2,1)S(1)} %pad_maximum_fusion.1), channel_id=1, source_target_pairs={{0,8},{4,12},{8,0},{12,4},{1,9},{5,13},{9,1},{13,5},{2,10},{6,14},... | collective-permute-start | bytes 24584 | tf_op jit(solution)/shard_map/ppermute | solution.py:81
  27.3 3.7 %collective-permute-start.6 = (bf16[256,128]{1,0:T(8,128)(2,1)S(1)}, bf16[256,128]{1,0:T(8,128)(2,1)S(1)}, u32[]{:S(2)}, u32[]{:S(2)}) collective-permute-start(bf16[256,128]{1,0:T(8,128)(2,1)S(1)} %get-tuple-element.41), channel_id=1, source_target_pairs={{0,1},{1,2},{2,3},{3,0},{4,5},{5,6},{6,7},{7,4},{8,9},{9,10},{10,1... | collective-permute-start | bytes 196616 | tf_op jit(solution)/shard_map/ppermute | solution.py:81
  27.6 3.8 %collective-permute-start.10 = (bf16[256,128]{1,0:T(8,128)(2,1)S(1)}, bf16[256,128]{1,0:T(8,128)(2,1)S(1)}, u32[]{:S(2)}, u32[]{:S(2)}) collective-permute-start(bf16[256,128]{1,0:T(8,128)(2,1)S(1)} %get-tuple-element.41), channel_id=1, source_target_pairs={{0,3},{1,0},{2,1},{3,2},{4,7},{5,4},{6,5},{7,6},{8,11},{9,8},{10,9... | collective-permute-start | bytes 196616 | tf_op jit(solution)/shard_map/ppermute | solution.py:81
  29.4 4.5 %collective-permute-start.8 = (bf16[256,128]{1,0:T(8,128)(2,1)S(1)}, bf16[256,128]{1,0:T(8,128)(2,1)S(1)}, u32[]{:S(2)}, u32[]{:S(2)}) collective-permute-start(bf16[256,128]{1,0:T(8,128)(2,1)S(1)} %get-tuple-element.41), channel_id=1, source_target_pairs={{0,2},{1,3},{2,0},{3,1},{4,6},{5,7},{6,4},{7,5},{8,10},{9,11},{10,... | collective-permute-start | bytes 196616 | tf_op jit(solution)/shard_map/ppermute | solution.py:81
  35.7 3.8 %collective-permute-start.16 = (bf16[16,512]{1,0:T(8,128)(2,1)S(1)}, bf16[16,512]{1,0:T(8,128)(2,1)S(1)}, u32[]{:S(2)}, u32[]{:S(2)}) collective-permute-start(bf16[16,512]{1,0:T(8,128)(2,1)S(1)} %convolution_convert_fusion.3), channel_id=1, source_target_pairs={{0,2},{1,3},{2,0},{3,1},{4,6},{5,7},{6,4},{7,5},{8,10},{9,11},{10,... | collective-permute-start | bytes 49160 | tf_op jit(solution)/shard_map/ppermute | solution.py:81
  46.9 5.0 %collective-permute-start.24 = (bf16[2,16,128]{2,1,0:T(8,128)(2,1)S(1)}, bf16[2,16,128]{2,1,0:T(8,128)(2,1)S(1)}, u32[]{:S(2)}, u32[]{:S(2)}) collective-permute-start(bf16[2,16,128]{2,1,0:T(8,128)(2,1)S(1)} %pad_maximum_fusion.2), channel_id=1, source_target_pairs={{0,12},{4,0},{8,4},{12,8},{1,13},{5,1},{9,5},{13,9},{2,14},{6,2},{... | collective-permute-start | bytes 24584 | tf_op jit(solution)/shard_map/ppermute | solution.py:81
  50.5 4.6 %collective-permute-start.25 = (bf16[2,16,128]{2,1,0:T(8,128)(2,1)S(1)}, bf16[2,16,128]{2,1,0:T(8,128)(2,1)S(1)}, u32[]{:S(2)}, u32[]{:S(2)}) collective-permute-start(bf16[2,16,128]{2,1,0:T(8,128)(2,1)S(1)} %pad_maximum_fusion.3), channel_id=1, source_target_pairs={{0,8},{4,12},{8,0},{12,4},{1,9},{5,13},{9,1},{13,5},{2,10},{6,14},... | collective-permute-start | bytes 24584 | tf_op jit(solution)/shard_map/ppermute | solution.py:81
  50.6 5.5 %collective-permute-start.26 = (bf16[2,16,128]{2,1,0:T(8,128)(2,1)S(1)}, bf16[2,16,128]{2,1,0:T(8,128)(2,1)S(1)}, u32[]{:S(2)}, u32[]{:S(2)}) collective-permute-start(bf16[2,16,128]{2,1,0:T(8,128)(2,1)S(1)} %pad_maximum_fusion.4), channel_id=1, source_target_pairs={{0,4},{4,8},{8,12},{12,0},{1,5},{5,9},{9,13},{13,1},{2,6},{6,10},{... | collective-permute-start | bytes 24584 | tf_op jit(solution)/shard_map/ppermute | solution.py:81
  56.4 4.2 %collective-permute-start.27 = (bf16[16,128]{1,0:T(8,128)(2,1)S(1)}, bf16[16,128]{1,0:T(8,128)(2,1)S(1)}, u32[]{:S(2)}, u32[]{:S(2)}) collective-permute-start(bf16[16,128]{1,0:T(8,128)(2,1)S(1)} %bitcast.193), channel_id=1, source_target_pairs={{0,1},{1,2},{2,3},{3,0},{4,5},{5,6},{6,7},{7,4},{8,9},{9,10},{10,1... | collective-permute-start | bytes 12296 | tf_op jit(solution)/shard_map/ppermute | solution.py:81
  56.5 5.6 %collective-permute-start.28 = (bf16[16,128]{1,0:T(8,128)(2,1)S(1)}, bf16[16,128]{1,0:T(8,128)(2,1)S(1)}, u32[]{:S(2)}, u32[]{:S(2)}) collective-permute-start(bf16[16,128]{1,0:T(8,128)(2,1)S(1)} %bitcast.192), channel_id=1, source_target_pairs={{0,2},{1,3},{2,0},{3,1},{4,6},{5,7},{6,4},{7,5},{8,10},{9,11},{10,... | collective-permute-start | bytes 12296 | tf_op jit(solution)/shard_map/ppermute | solution.py:81
  57.7 4.4 %collective-permute-start.29 = (bf16[16,128]{1,0:T(8,128)(2,1)S(1)}, bf16[16,128]{1,0:T(8,128)(2,1)S(1)}, u32[]{:S(2)}, u32[]{:S(2)}) collective-permute-start(bf16[16,128]{1,0:T(8,128)(2,1)S(1)} %bitcast.194), channel_id=1, source_target_pairs={{0,3},{1,0},{2,1},{3,2},{4,7},{5,4},{6,5},{7,6},{8,11},{9,8},{10,9... | collective-permute-start | bytes 12296 | tf_op jit(solution)/shard_map/ppermute | solution.py:81
  59.2 3.7 %collective-permute-start.21 = (bf16[256,128]{1,0:T(8,128)(2,1)S(1)}, bf16[256,128]{1,0:T(8,128)(2,1)S(1)}, u32[]{:S(2)}, u32[]{:S(2)}) collective-permute-start(bf16[256,128]{1,0:T(8,128)(2,1)S(1)} %bitcast.176), channel_id=1, source_target_pairs={{0,1},{1,2},{2,3},{3,0},{4,5},{5,6},{6,7},{7,4},{8,9},{9,10},{10,1... | collective-permute-start | bytes 196616 | tf_op jit(solution)/shard_map/ppermute | solution.py:81
  59.4 5.0 %collective-permute-start.22 = (bf16[256,128]{1,0:T(8,128)(2,1)S(1)}, bf16[256,128]{1,0:T(8,128)(2,1)S(1)}, u32[]{:S(2)}, u32[]{:S(2)}) collective-permute-start(bf16[256,128]{1,0:T(8,128)(2,1)S(1)} %bitcast.177), channel_id=1, source_target_pairs={{0,2},{1,3},{2,0},{3,1},{4,6},{5,7},{6,4},{7,5},{8,10},{9,11},{10,... | collective-permute-start | bytes 196616 | tf_op jit(solution)/shard_map/ppermute | solution.py:81
  60.6 3.8 %collective-permute-start.23 = (bf16[256,128]{1,0:T(8,128)(2,1)S(1)}, bf16[256,128]{1,0:T(8,128)(2,1)S(1)}, u32[]{:S(2)}, u32[]{:S(2)}) collective-permute-start(bf16[256,128]{1,0:T(8,128)(2,1)S(1)} %bitcast.178), channel_id=1, source_target_pairs={{0,3},{1,0},{2,1},{3,2},{4,7},{5,4},{6,5},{7,6},{8,11},{9,8},{10,9... | collective-permute-start | bytes 196616 | tf_op jit(solution)/shard_map/ppermute | solution.py:81
  (16 other events, 65.3 us)

commit v3 on v1

v3 whole, which is shorter than its diff:
```python
import functools

import jax
import jax.numpy as jnp
from jax import lax
from jax.experimental import pallas as pl
from jax.experimental.pallas import tpu as pltpu
from jax.sharding import PartitionSpec as P

epsilon = 1e-05
f32 = jnp.float32
bf16 = jnp.bfloat16
cores = 2


def dot(left, right):
    return jnp.dot(left, right, preferred_element_type=f32)


def dot_rows(left, right):
    return lax.dot_general(left, right, (((1,), (1,)), ((), ())), preferred_element_type=f32)


def dot_cols(left, right):
    return lax.dot_general(left, right, (((0,), (0,)), ((), ())), preferred_element_type=f32)


def split(values):
    high = values.astype(bf16)
    return high, (values - high.astype(f32)).astype(bf16)


def sigmoid(values):
    return 1.0 / (1.0 + jnp.exp(-values))


def swish_slope(pre_act):
    sigma = sigmoid(pre_act)
    return sigma * (1.0 + pre_act * (1.0 - sigma))


def normalize(values):
    mean = jnp.mean(values, axis=1, keepdims=True)
    square = jnp.mean(values * values, axis=1, keepdims=True)
    inverse = lax.rsqrt(square - mean * mean + epsilon)
    return (values - mean) * inverse, inverse


def norm_back(grad, normed, inverse):
    total = jnp.mean(grad, axis=1, keepdims=True)
    cross = jnp.mean(grad * normed, axis=1, keepdims=True)
    return inverse * (grad - total - normed * cross)


def to_hidden(rows, mine, other):
    return jnp.concatenate([dot_rows(rows, mine), dot_rows(rows, other)], axis=1)


def from_hidden(hidden, mine, other):
    half = mine.shape[0]
    return dot(hidden[:, :half], mine) + dot(hidden[:, half:], other)


def place():
    feat = lax.axis_index("feat")
    return feat // cores, feat % cores


def pair(mine, other, core):
    return jnp.where(core == 0, jnp.concatenate([mine, other], 1), jnp.concatenate([other, mine], 1))


def lanes(group, width):
    return pl.ds(pl.multiple_of(group * width, width), width)


def put_groups(full_ref, parts):
    group, _ = place()
    width = parts[0].shape[1]
    for step, part in enumerate(parts):
        full_ref[:, lanes(group ^ step, width)] = part[...]


def stage(kernel, outs, operands, scalars=0, flops=1 << 24):
    specs = [pl.BlockSpec(memory_space=pltpu.VMEM)] * (len(operands) - scalars)
    specs += [pl.BlockSpec(memory_space=pltpu.SMEM)] * scalars
    moved = sum(o.size * o.dtype.itemsize for o in operands)
    return pl.pallas_call(
        kernel,
        out_shape=[jax.ShapeDtypeStruct(shape, kind) for shape, kind in outs],
        in_specs=specs,
        out_specs=[pl.BlockSpec(memory_space=pltpu.VMEM)] * len(outs),
        cost_estimate=pl.CostEstimate(flops=flops, bytes_accessed=moved, transcendentals=0),
    )(*operands)


def merge_inputs(latent, latent2, state, state2, edge_cot, node_cot, gain_e, gain_n, pack, extra):
    _, core = place()
    nodes = latent.shape[0]
    half = state.shape[0] // cores
    mine = pl.ds(pl.multiple_of(core * half, half), half)
    theirs = pl.ds(pl.multiple_of((1 - core) * half, half), half)
    pack[:nodes] = pair(latent[...], latent2[...], core)
    pack[nodes:] = pair(state[mine], state2[mine], core)
    extra[:half] = edge_cot[theirs]
    extra[half : half + nodes] = node_cot[...]
    extra[half + nodes :] = gains(gain_e, gain_n, nodes)


def gains(gain_e, gain_n, rows):
    shape = (rows, gain_e.shape[1])
    row = lax.broadcasted_iota(jnp.int32, shape, 0)
    e = jnp.broadcast_to(gain_e[...].astype(f32), shape)
    n = jnp.broadcast_to(gain_n[...].astype(f32), shape)
    return jnp.where(row == 0, e, n).astype(bf16)


def lend_rows(groups, *refs):
    packs, (mine, other, full, lent) = refs[:groups], refs[groups:]
    put_groups(full, packs)
    features = full.shape[1]
    nodes = lent.shape[0] // 2
    sender = slice(features, 2 * features)
    high, low = split(to_hidden(full[:nodes], mine[:, sender], other[:, sender]))
    lent[:nodes] = high
    lent[nodes:] = low


def start_edges(
    full, mine, other, extra2, edge_cot, node_cot, gain_e, gain_n, slot, receiver, send_rows, pre, pick, take, extra
):
    _, core = place()
    block = lax.axis_index("nodes")
    features = full.shape[1]
    nodes, half = take.shape
    blocks, _, slots = send_rows.shape

    own = pl.ds(pl.multiple_of(core * half, half), half)
    my_extra = jnp.concatenate(
        [edge_cot[own], node_cot[...], gains(gain_e, gain_n, nodes)], axis=0
    )
    extra[...] = pair(my_extra, extra2[...], core)

    slot_row = slot[pl.ds(core, 1)]
    sender = slot_row
    for source in range(blocks):
        for k in range(slots):
            row = (source ^ block) * nodes + send_rows[source, block, k]
            sender = jnp.where(slot_row == nodes + source * slots + k, row, sender)
    table = pick.shape[0]
    pick[...] = (lax.broadcasted_iota(jnp.int32, (table, half), 0) == sender).astype(f32).astype(bf16)
    here = receiver[pl.ds(core, 1)]
    take_rows = (lax.broadcasted_iota(jnp.int32, (nodes, half), 0) == here).astype(f32).astype(bf16)
    take[...] = take_rows

    last = slice(2 * features, 3 * features)
    high, low = split(to_hidden(full[:nodes], mine[:, last], other[:, last]))
    state = full[nodes:]
    pre[...] = (
        to_hidden(state, mine[:, :features], other[:, :features])
        + dot_cols(take_rows, high)
        + dot_cols(take_rows, low)
    )


def finish_edges(blocks, *refs):
    tables, (pre, pick, mine, other, edge_pre, part, sent) = refs[:blocks], refs[blocks:]
    nodes = tables[0].shape[0] // 2
    high = jnp.concatenate([t[:nodes] for t in tables], axis=0)
    low = jnp.concatenate([t[nodes:] for t in tables], axis=0)
    value = pre[...] + dot_cols(pick[...], high) + dot_cols(pick[...], low)
    edge_pre[...] = value
    out = from_hidden((value * sigmoid(value)).astype(bf16), mine[...], other[...])
    part[...] = out
    sent[...] = out.astype(bf16)


def total(refs):
    value = refs[0][...]
    for ref in refs[1:]:
        value = value + ref[...].astype(f32)
    return value


def update_edges(groups, *refs):
    parts, extras = refs[:groups], refs[groups : 2 * groups]
    full, take, normed, inverse, kept, lent, aggregate, extra, next_all = refs[2 * groups :]
    group, core = place()
    put_groups(extra, extras)
    nodes, half = take.shape
    width = kept.shape[1]
    normed_rows, inverse_rows = normalize(total(parts))
    normed[...] = normed_rows
    inverse[...] = inverse_rows
    gain = extra[half + nodes :].astype(f32)[0:1]
    rows = (full[nodes:].astype(f32) + normed_rows * gain).astype(bf16)
    aggregate[...] = dot(take[...], rows)
    next_all[...] = rows
    mine = next_all[:, lanes(group, width * cores)]
    kept[...] = jnp.where(core == 0, mine[:, :width], mine[:, width:])
    lent[...] = jnp.where(core == 0, mine[:, width:], mine[:, :width])


def start_nodes(aggregate, aggregate2, full, in_mine, in_other, out_mine, out_other, node_pre, part, sent):
    nodes = aggregate.shape[0]
    together = (aggregate[...] + aggregate2[...]).astype(bf16)
    rows = jnp.concatenate([full[:nodes], together], axis=1)
    pre = to_hidden(rows, in_mine[...], in_other[...])
    node_pre[...] = pre
    out = from_hidden((pre * sigmoid(pre)).astype(bf16), out_mine[...], out_other[...])
    part[...] = out
    sent[...] = out.astype(bf16)


def turn_nodes(groups, *refs):
    parts = refs[:groups]
    full, extra, node_pre, in_mine, in_other, out_mine, out_other, node_next, dpre, part, sent, next_all = refs[groups:]
    group, core = place()
    nodes, features = part.shape
    half = extra.shape[0] - 2 * nodes
    width = node_next.shape[1]
    gain = extra[half + nodes :].astype(f32)[1:2]
    normed, inverse = normalize(total(parts))
    next_all[...] = (full[:nodes].astype(f32) + normed * gain).astype(bf16)
    mine = next_all[:, lanes(group, width * cores)]
    node_next[...] = jnp.where(core == 0, mine[:, :width], mine[:, width:])
    cot = extra[half : half + nodes].astype(f32)
    dy = norm_back(cot * gain, normed, inverse).astype(bf16)
    hidden = to_hidden(dy, out_mine[...], out_other[...])
    hidden = (hidden * swish_slope(node_pre[...])).astype(bf16)
    dpre[...] = hidden
    out = from_hidden(hidden, in_mine[:, features:], in_other[:, features:])
    part[...] = out
    sent[...] = out.astype(bf16)


def turn_edges(groups, *refs):
    parts = refs[:groups]
    take, pick, extra, normed, inverse, edge_pre, node_dpre = refs[groups : groups + 7]
    e_mine, e_other, out_mine, out_other, in_mine, in_other, kept, *sents, grads = refs[groups + 7 :]
    group, _ = place()
    nodes, half = take.shape
    features = extra.shape[1]
    width = kept.shape[1]
    high, low = split(total(parts))
    edge_total = extra[:half].astype(f32) + dot_cols(take[...], high) + dot_cols(take[...], low)
    gain = extra[half + nodes :].astype(f32)[0:1]
    dy = norm_back(edge_total * gain, normed[...], inverse[...]).astype(bf16)
    hidden = to_hidden(dy, out_mine[...], out_other[...])
    dpre = (hidden * swish_slope(edge_pre[...])).astype(bf16)

    def weighted(values, first):
        columns = slice(first * features, (first + 1) * features)
        return from_hidden(values, e_mine[:, columns], e_other[:, columns])

    grads[:half] = weighted(dpre, 0)
    high, low = split(dot(pick[...], dpre))
    grads[half:] = weighted(high, 1) + weighted(low, 1)
    high, low = split(dot(take[...], dpre))
    home = weighted(high, 2) + weighted(low, 2)
    home = home + 0.5 * from_hidden(node_dpre[...], in_mine[:, :features], in_other[:, :features])
    grads[half : half + nodes] += home
    for step, sent in enumerate(sents, 1):
        sent[...] = grads[:, lanes(group ^ step, width)].astype(bf16)
    grads[:half] += edge_total
    kept[...] = grads[:, lanes(group, width)]


def add_groups(groups, *refs):
    parts, (rows, table, sent) = refs[:groups], refs[groups:]
    _, core = place()
    half, width = rows.shape
    value = total(parts)
    mine = jnp.where(core == 0, value[:, :width], value[:, width:])
    sent[...] = jnp.where(core == 0, value[:, width:], value[:, :width]).astype(bf16)
    rows[...] = mine[:half].astype(bf16)
    table[...] = mine[half:]


def add_cores(table, came, own, *sents):
    nodes = own.shape[0]
    half = came.shape[0] - table.shape[0]
    value = table[...] + came[half:].astype(f32)
    own[...] = value[:nodes]
    for step, sent in enumerate(sents, 1):
        sent[...] = value[step * nodes : (step + 1) * nodes].astype(bf16)


def assemble(next_mine, next_came, grad_mine, came, edge_next, edge_grad):
    _, core = place()
    half = next_mine.shape[0]
    mine = pl.ds(pl.multiple_of(core * half, half), half)
    theirs = pl.ds(pl.multiple_of((1 - core) * half, half), half)
    edge_next[mine] = next_mine[...]
    edge_next[theirs] = next_came[...]
    edge_grad[mine] = grad_mine[...]
    edge_grad[theirs] = came[:half]


def shards(
    latent,
    edge_state,
    send_rows,
    sender_slot,
    receiver_row,
    edge_in_weight,
    edge_out_weight,
    edge_gain,
    node_in_weight,
    node_out_weight,
    node_gain,
    edge_cot,
    node_cot,
):
    nodes, width = latent.shape
    edge_dev = edge_state.shape[0]
    half = edge_dev // cores
    blocks = send_rows.shape[0]
    feats = lax.axis_size("feat")
    groups = feats // cores
    features = width * feats
    wide = width * cores
    hidden = edge_in_weight.shape[0] * cores
    table = blocks * nodes

    def swapped(values, axis, bits):
        count = lax.axis_size(axis)
        return lax.ppermute(values, axis, [(i, i ^ bits) for i in range(count)])

    def over_cores(values):
        return swapped(values, "feat", 1)

    def over_groups(values):
        return [swapped(values, "feat", cores * step) for step in range(1, groups)]

    def over_nodes(values):
        return [swapped(values, "nodes", step) for step in range(1, blocks)]

    gain_e, gain_n = edge_gain.reshape(1, width), node_gain.reshape(1, width)
    slot_rows = sender_slot.reshape(cores, half)
    receiver_rows = receiver_row.reshape(cores, half)

    latent2, state2 = over_cores(latent), over_cores(edge_state)
    e_in = (edge_in_weight, over_cores(edge_in_weight))
    pack, extra_sent = stage(
        merge_inputs,
        [((nodes + half, wide), bf16), ((half + 2 * nodes, width), bf16)],
        [latent, latent2, edge_state, state2, edge_cot, node_cot, gain_e, gain_n],
    )
    packs = [pack] + over_groups(pack)
    extra2 = over_cores(extra_sent)
    full, lent = stage(
        functools.partial(lend_rows, groups),
        [((nodes + half, features), bf16), ((2 * nodes, hidden), bf16)],
        [*packs, *e_in],
    )
    tables = [lent] + over_nodes(lent)
    pre, pick, take, extra = stage(
        start_edges,
        [((half, hidden), f32), ((table, half), bf16), ((nodes, half), bf16), ((half + 2 * nodes, wide), bf16)],
        [full, *e_in, extra2, edge_cot, node_cot, gain_e, gain_n, slot_rows, receiver_rows, send_rows],
        scalars=1,
    )
    extras = [extra] + over_groups(extra)
    e_out = (edge_out_weight, over_cores(edge_out_weight))
    edge_pre, part, sent = stage(
        functools.partial(finish_edges, blocks),
        [((half, hidden), f32), ((half, features), f32), ((half, features), bf16)],
        [*tables, pre, pick, *e_out],
    )
    parts = [part] + over_groups(sent)
    normed, inverse, next_mine, next_sent, aggregate, extra_full, _ = stage(
        functools.partial(update_edges, groups),
        [
            ((half, features), f32),
            ((half, 1), f32),
            ((half, width), bf16),
            ((half, width), bf16),
            ((nodes, features), f32),
            ((half + 2 * nodes, features), bf16),
            ((half, features), bf16),
        ],
        [*parts, *extras, full, take],
    )
    aggregate2 = over_cores(aggregate)
    next_came = over_cores(next_sent)
    n_in = (node_in_weight, over_cores(node_in_weight))
    n_out = (node_out_weight, over_cores(node_out_weight))
    node_pre, part, sent = stage(
        start_nodes,
        [((nodes, hidden), f32), ((nodes, features), f32), ((nodes, features), bf16)],
        [aggregate, aggregate2, full, *n_in, *n_out],
    )
    parts = [part] + over_groups(sent)
    node_next, node_dpre, part, sent, _ = stage(
        functools.partial(turn_nodes, groups),
        [
            ((nodes, width), bf16),
            ((nodes, hidden), bf16),
            ((nodes, features), f32),
            ((nodes, features), bf16),
            ((nodes, features), bf16),
        ],
        [*parts, full, extra_full, node_pre, *n_in, *n_out],
    )
    parts = [part] + over_groups(sent)
    kept, *sents, _ = stage(
        functools.partial(turn_edges, groups),
        [((half + table, wide), f32)]
        + [((half + table, wide), bf16)] * (groups - 1)
        + [((half + table, features), f32)],
        [*parts, take, pick, extra_full, normed, inverse, edge_pre, node_dpre, *e_in, *e_out, *n_in],
    )
    parts = [kept] + [swapped(s, "feat", cores * k) for k, s in enumerate(sents, 1)]
    grad_mine, table_mine, sent = stage(
        functools.partial(add_groups, groups),
        [((half, width), bf16), ((table, width), f32), ((half + table, width), bf16)],
        parts,
    )
    came = over_cores(sent)
    own, *sents = stage(
        add_cores,
        [((nodes, width), f32)] + [((nodes, width), bf16)] * (blocks - 1),
        [table_mine, came],
    )
    share = own
    for step, sent in enumerate(sents, 1):
        share = share + swapped(sent, "nodes", step).astype(f32)
    edge_next, edge_grad = stage(
        assemble,
        [((edge_dev, width), bf16), ((edge_dev, width), bf16)],
        [next_mine, next_came, grad_mine, came],
    )
    node_grad = (node_cot.astype(f32) + share).astype(bf16)
    return (edge_next, node_next, edge_grad, node_grad)


def solution(mesh):
    rows = P(("groups", "nodes"), "feat")
    flat = P(("groups", "nodes"))
    matrix = P("feat", None)
    vector = P("feat")
    return jax.shard_map(
        shards,
        mesh=mesh,
        in_specs=(
            rows,
            rows,
            P("groups", None, None),
            flat,
            flat,
            matrix,
            matrix,
            vector,
            matrix,
            matrix,
            vector,
            rows,
            rows,
        ),
        out_specs=(rows, rows, rows, rows),
        check_vma=False,
    )
```

time: 92 us -> 74.8 us (0.81)
  blocking collectives: 48.6 us -> 0 us
  Pallas kernels: 0 us -> 23.2 us
  waiting for transfers between devices: 14 us -> 22.3 us
  starting transfers between devices: 13.5 us -> 19.6 us
  matrix products: 5.37 us -> 0 us
  other arithmetic: 3.47 us -> 0.6 us
  local copies, waits for them, and re-layouts: 5.58 us -> 7.89 us
    all_gather x6 -> x0, blocking collectives: 48.6 us -> none  [the longest x4 22.4 us: gather(): return lax.all_gather(values, 'feat', axis=0)]
    pallas_call x0 -> x11, Pallas kernels: none -> 23.2 us  [stage(): pl.pallas_call(kernel, out_shape=[jax.ShapeDtypeStruct(shape, kind) for s...]
    ppermute x6 -> x22, waiting for transfers between devices: 3.37 us -> 22.3 us  [swapped(): return lax.ppermute(values, axis, [(i, i ^ bits) for i in range(count)])]
    ppermute x6 -> x22, starting transfers between devices: 6.55 us -> 19.6 us  [swapped(): return lax.ppermute(values, axis, [(i, i ^ bits) for i in range(count)])]
    all_to_all x2 -> x0, waiting for transfers between devices: 10.6 us -> none  [the longest x1 5.37 us: shards(): lax.all_to_all(edge_de, 'feat', 0, 0).astype(f32)]
    all_to_all x2 -> x0, starting transfers between devices: 6.91 us -> none  [the longest x1 3.5 us: shards(): lax.all_to_all(sent, ('nodes', 'feat'), 0, 0).astype(f32)]
    unnamed x33 -> x50, local copies, waits for them, and re-layouts: 2.08 us -> 7.89 us
    dot_general x19 -> x0, matrix products: 5.37 us -> none  [the longest x13 3.83 us: dot(): return jnp.dot(left, right, preferred_element_type=f32)]
  transfers between devices with their start and end apart: 8 -> 22, of which waited for: 3 -> 9; matrix products, arithmetic and copies ran while one was open for 8% -> 0% of each run, Pallas kernels for 0% -> 18%
where the time goes in v3:
time: 74.8 us; the launch traced here: 74.3 us
  Pallas kernels  23.2 us (31%)
  waiting for transfers between devices  22.3 us (30%)
  starting transfers between devices  19.6 us (26%)
  local copies, waits for them, and re-layouts  7.89 us (11%)
  between operations  0.78 us (1%)
    pallas_call x11, Pallas kernels, stage(): pl.pallas_call(kernel, out_shape=[jax.ShapeDtypeStruct(shape, kind) for s...  23.2 us
    ppermute x22, waiting for transfers between devices, swapped(): return lax.ppermute(values, axis, [(i, i ^ bits) for i in range(count)])  22.3 us
    ppermute x22, starting transfers between devices, swapped(): return lax.ppermute(values, axis, [(i, i ^ bits) for i in range(count)])  19.6 us
    unnamed x50, local copies, waits for them, and re-layouts  7.89 us
  transfers between devices with their start and end apart: 22, of which 9 were waited for; matrix products, arithmetic and copies ran while one was open for 0% of the time, Pallas kernels for 18%

profile of v3, /device:TPU:0, one launch (start us, length us, event | category | flops | bytes accessed | tf_op | source)
XLA Modules:
  0.0 74.3 jit_solution(2973203809008654220)
XLA Ops:
  3.7 1.6 %shard_map.156 = (bf16[144,256]{1,0:T(8,128)(2,1)}, bf16[160,128]{1,0:T(8,128)(2,1)}) custom-call(bf16[16,128]{1,0:T(8,128)(2,1)} %latent.1, bf16[16,128]{1,0:T(8,128)(2,1)} %copy-done.22, bf16[256,128]{1,0:T(8,128)(2,1)} %state.1, bf16[256,128]{1,0:T(8,128)(2,1)} %copy-done.11, bf16[256,128]{1,0:T(8,128)(2,1)} %edge_cot.3, bf16[16,128]{1,0:T(8,128)(2,1)} %node_cot.3, ...), custom_call_target="tpu_custom_call" | custom-call | flops 16777216 | bytes 209408 | tf_op jit(solution)/shard_map/pallas_call | solution.py:88
  5.3 2.8 %collective-permute-start.2 = (bf16[144,256]{1,0:T(8,128)(2,1)}, bf16[144,256]{1,0:T(8,128)(2,1)S(1)}, u32[]{:S(2)}, u32[]{:S(2)}) collective-permute-start(bf16[144,256]{1,0:T(8,128)(2,1)} %get-tuple-element.39.refs_0_), channel_id=1, source_target_pairs={{0,2},{1,3},{2,0},{3,1},{4,6},{5,7},{6,4},{7,5},{8,10},{9,11},{10,... | collective-permute-start | bytes 221192 | tf_op jit(solution)/shard_map/ppermute | solution.py:328
  8.1 2.8 %collective-permute-done.2.refs_1_ = bf16[144,256]{1,0:T(8,128)(2,1)S(1)} collective-permute-done((bf16[144,256]{1,0:T(8,128)(2,1)}, bf16[144,256]{1,0:T(8,128)(2,1)S(1)}, u32[]{:S(2)}, u32[]{:S(2)}) %collective-permute-start.2) | collective-permute-done | bytes 73760 | tf_op jit(solution)/shard_map/ppermute | solution.py:328
  12.3 2.0 %shard_map.157 = (bf16[144,512]{1,0:T(8,128)(2,1)}, bf16[32,256]{1,0:T(8,128)(2,1)}) custom-call(bf16[144,256]{1,0:T(8,128)(2,1)} %get-tuple-element.39.refs_0_, bf16[144,256]{1,0:T(8,128)(2,1)} %copy-done.10, bf16[128,1536]{1,0:T(8,128)(2,1)} %refs_9_.1, bf16[128,1536]{1,0:T(8,128)(2,1)} %copy-done), custom_call_target="tpu_custom_call" | custom-call | flops 16777216 | bytes 933888 | tf_op jit(solution)/shard_map/pallas_call | solution.py:88
  14.3 1.8 %collective-permute-start.4 = (bf16[32,256]{1,0:T(8,128)(2,1)}, bf16[32,256]{1,0:T(8,128)(2,1)S(1)}, u32[]{:S(2)}, u32[]{:S(2)}) collective-permute-start(bf16[32,256]{1,0:T(8,128)(2,1)} %get-tuple-element.40.refs_0_), channel_id=1, source_target_pairs={{0,4},{4,0},{8,12},{12,8},{1,5},{5,1},{9,13},{13,9},{2,6},{6,2},{1... | collective-permute-start | bytes 49160 | tf_op jit(solution)/shard_map/ppermute | solution.py:328
  16.1 2.6 %collective-permute-start.5 = (bf16[32,256]{1,0:T(8,128)(2,1)}, bf16[32,256]{1,0:T(8,128)(2,1)S(1)}, u32[]{:S(2)}, u32[]{:S(2)}) collective-permute-start(bf16[32,256]{1,0:T(8,128)(2,1)} %get-tuple-element.40.refs_0_), channel_id=1, source_target_pairs={{0,8},{4,12},{8,0},{12,4},{1,9},{5,13},{9,1},{13,5},{2,10},{6,14},... | collective-permute-start | bytes 49160 | tf_op jit(solution)/shard_map/ppermute | solution.py:328
  19.3 2.3 %shard_map.158 = (f32[128,256]{1,0:T(8,128)}, bf16[64,128]{1,0:T(8,128)(2,1)}, bf16[16,128]{1,0:T(8,128)(2,1)}, bf16[160,256]{1,0:T(8,128)(2,1)}) custom-call(bf16[144,512]{1,0:T(8,128)(2,1)} %get-tuple-element.41.full.refs_4_.refs_2_, bf16[128,1536]{1,0:T(8,128)(2,1)} %refs_9_.1, bf16[128,1536]{1,0:T(8,128)(2,1)} %copy-done, bf16[160,128]{1,0:T(8,128)(2,1)} %copy-done.12, ...), custom_call_target="tpu_custom_call" | custom-call | flops 16777216 | bytes 1047552 | tf_op jit(solution)/shard_map/pallas_call | solution.py:88
  21.6 2.8 %collective-permute-done.6.refs_3_ = bf16[32,256]{1,0:T(8,128)(2,1)S(1)} collective-permute-done((bf16[32,256]{1,0:T(8,128)(2,1)}, bf16[32,256]{1,0:T(8,128)(2,1)S(1)}, u32[]{:S(2)}, u32[]{:S(2)}) %collective-permute-start.6) | collective-permute-done | bytes 16416 | tf_op jit(solution)/shard_map/ppermute | solution.py:328
  25.1 2.4 %shard_map.159 = (f32[128,256]{1,0:T(8,128)}, f32[128,512]{1,0:T(8,128)}, bf16[128,512]{1,0:T(8,128)(2,1)}) custom-call(bf16[32,256]{1,0:T(8,128)(2,1)} %get-tuple-element.40.refs_0_, bf16[32,256]{1,0:T(8,128)(2,1)} %copy-done.18, bf16[32,256]{1,0:T(8,128)(2,1)} %copy-done.19, bf16[32,256]{1,0:T(8,128)(2,1)} %copy-done.20, ...), custom_call_target="tpu_custom_call" | custom-call | flops 16777216 | bytes 475136 | tf_op jit(solution)/shard_map/pallas_call | solution.py:88
  27.4 1.5 %collective-permute-start.9 = (bf16[128,512]{1,0:T(8,128)(2,1)}, bf16[128,512]{1,0:T(8,128)(2,1)S(1)}, u32[]{:S(2)}, u32[]{:S(2)}) collective-permute-start(bf16[128,512]{1,0:T(8,128)(2,1)} %get-tuple-element.46), channel_id=1, source_target_pairs={{0,2},{1,3},{2,0},{3,1},{4,6},{5,7},{6,4},{7,5},{8,10},{9,11},{10,... | collective-permute-start | bytes 393224 | tf_op jit(solution)/shard_map/ppermute | solution.py:328
  29.5 4.8 %collective-permute-done.10.refs_3_ = bf16[160,256]{1,0:T(8,128)(2,1)S(1)} collective-permute-done((bf16[160,256]{1,0:T(8,128)(2,1)S(1)}, bf16[160,256]{1,0:T(8,128)(2,1)S(1)}, u32[]{:S(2)}, u32[]{:S(2)}) %collective-permute-start.10) | collective-permute-done | bytes 81952 | tf_op jit(solution)/shard_map/ppermute | solution.py:328
  35.1 2.1 %shard_map.160 = (f32[128,512]{1,0:T(8,128)}, f32[128,1]{1,0:T(8,128)}, bf16[128,128]{1,0:T(8,128)(2,1)}, bf16[128,128]{1,0:T(8,128)(2,1)}, f32[16,512]{1,0:T(8,...) custom-call(f32[128,512]{1,0:T(8,128)} %get-tuple-element.45.refs_0_, bf16[128,512]{1,0:T(8,128)(2,1)} %copy-done.6, ...), custom_call_target="tpu_custom_call" | custom-call | flops 16777216 | bytes 708608 | tf_op jit(solution)/shard_map/pallas_call | solution.py:88
  37.2 1.4 %collective-permute-done.12.aggregate2 = f32[16,512]{1,0:T(8,128)S(1)} collective-permute-done((f32[16,512]{1,0:T(8,128)}, f32[16,512]{1,0:T(8,128)S(1)}, u32[]{:S(2)}, u32[]{:S(2)}) %collective-permute-start.12) | collective-permute-done | bytes 32800 | tf_op jit(solution)/shard_map/ppermute | solution.py:328
  39.1 2.2 %shard_map.161 = (f32[16,256]{1,0:T(8,128)}, f32[16,512]{1,0:T(8,128)}, bf16[16,512]{1,0:T(8,128)(2,1)}) custom-call(f32[16,512]{1,0:T(8,128)} %get-tuple-element.51.aggregate, f32[16,512]{1,0:T(8,128)} %copy-done.14, bf16[144,512]{1,0:T(8,128)(2,1)} %get-tuple-element.41.full.refs_4_.refs_2_, bf16[128,1024]{1,0:T(8,128)(2,1)} %refs_13_.1, ...), custom_call_target="tpu_custom_call" | custom-call | flops 16777216 | bytes 999424 | tf_op jit(solution)/shard_map/pallas_call | solution.py:88
  42.8 2.6 %collective-permute-done.15.refs_1_ = bf16[16,512]{1,0:T(8,128)(2,1)S(1)} collective-permute-done((bf16[16,512]{1,0:T(8,128)(2,1)}, bf16[16,512]{1,0:T(8,128)(2,1)S(1)}, u32[]{:S(2)}, u32[]{:S(2)}) %collective-permute-start.15) | collective-permute-done | bytes 16416 | tf_op jit(solution)/shard_map/ppermute | solution.py:328
  46.0 2.4 %shard_map.162 = (bf16[16,128]{1,0:T(8,128)(2,1)}, bf16[16,256]{1,0:T(8,128)(2,1)}, f32[16,512]{1,0:T(8,128)}, bf16[16,512]{1,0:T(8,128)(2,1)}, bf16[16,512]{1,0:T(8,128)(2,1)}) custom-call(f32[16,512]{1,0:T(8,128)} %get-tuple-element.52.refs_0_, bf16[16,512]{1,0:T(8,128)(2,1)} %copy-done.17, bf16[144,512]{1,0:T(8,128)(2,1)} %get-tuple-element.41.full.refs_4_.refs_2_, ...), custom_call_target="tpu_custom_call" | custom-call | flops 16777216 | bytes 1163264 | tf_op jit(solution)/shard_map/pallas_call | solution.py:88
  49.7 2.6 %collective-permute-done.16.refs_1_ = bf16[16,512]{1,0:T(8,128)(2,1)S(1)} collective-permute-done((bf16[16,512]{1,0:T(8,128)(2,1)}, bf16[16,512]{1,0:T(8,128)(2,1)S(1)}, u32[]{:S(2)}, u32[]{:S(2)}) %collective-permute-start.16) | collective-permute-done | bytes 16416 | tf_op jit(solution)/shard_map/ppermute | solution.py:328
  52.9 3.6 %shard_map.163 = (f32[192,256]{1,0:T(8,128)}, bf16[192,256]{1,0:T(8,128)(2,1)}, f32[192,512]{1,0:T(8,128)}) custom-call(f32[16,512]{1,0:T(8,128)} %get-tuple-element.56.refs_0_, bf16[16,512]{1,0:T(8,128)(2,1)} %copy-done.16, bf16[16,128]{1,0:T(8,128)(2,1)} %get-tuple-element.48.refs_5_.refs_2_, bf16[64,128]{1,0:T(8,128)(2,1)} %get-tuple-element.44.refs_5_.refs_3_, ...), custom_call_target="tpu_custom_call" | custom-call | flops 16777216 | bytes 2208256 | tf_op jit(solution)/shard_map/pallas_call | solution.py:88
  56.5 1.4 %collective-permute-start.17 = (bf16[192,256]{1,0:T(8,128)(2,1)}, bf16[192,256]{1,0:T(8,128)(2,1)S(1)}, u32[]{:S(2)}, u32[]{:S(2)}) collective-permute-start(bf16[192,256]{1,0:T(8,128)(2,1)} %get-tuple-element.63), channel_id=1, source_target_pairs={{0,2},{1,3},{2,0},{3,1},{4,6},{5,7},{6,4},{7,5},{8,10},{9,11},{10,... | collective-permute-start | bytes 294920 | tf_op jit(solution)/shard_map/ppermute | solution.py:328
  57.9 3.5 %collective-permute-done.17.refs_1_ = bf16[192,256]{1,0:T(8,128)(2,1)S(1)} collective-permute-done((bf16[192,256]{1,0:T(8,128)(2,1)}, bf16[192,256]{1,0:T(8,128)(2,1)S(1)}, u32[]{:S(2)}, u32[]{:S(2)}) %collective-permute-start.17) | collective-permute-done | bytes 98336 | tf_op jit(solution)/shard_map/ppermute | solution.py:328
  62.0 1.6 %shard_map.164 = (bf16[128,128]{1,0:T(8,128)(2,1)}, f32[64,128]{1,0:T(8,128)}, bf16[192,128]{1,0:T(8,128)(2,1)}) custom-call(f32[192,256]{1,0:T(8,128)} %get-tuple-element.62.refs_0_, bf16[192,256]{1,0:T(8,128)(2,1)} %copy-done.7), custom_call_target="tpu_custom_call" | custom-call | flops 16777216 | bytes 294912 | tf_op jit(solution)/shard_map/pallas_call | solution.py:88
  65.7 1.4 %shard_map.166 = (f32[16,128]{1,0:T(8,128)}, bf16[16,128]{1,0:T(8,128)(2,1)}, bf16[16,128]{1,0:T(8,128)(2,1)}, bf16[16,128]{1,0:T(8,128)(2,1)}) custom-call(f32[64,128]{1,0:T(8,128)} %get-tuple-element.69.table, bf16[192,128]{1,0:T(8,128)(2,1)} %copy-done.5), custom_call_target="tpu_custom_call" | custom-call | flops 16777216 | bytes 81920 | tf_op jit(solution)/shard_map/pallas_call | solution.py:88
  67.8 3.7 %collective-permute-start.19 = (bf16[16,128]{1,0:T(8,128)(2,1)S(1)}, bf16[16,128]{1,0:T(8,128)(2,1)S(1)}, u32[]{:S(2)}, u32[]{:S(2)}) collective-permute-start(bf16[16,128]{1,0:T(8,128)(2,1)S(1)} %copy-done.24), channel_id=1, source_target_pairs={{0,4},{4,0},{8,12},{12,8},{1,5},{5,1},{9,13},{13,9},{2,6},{6,2},{1... | collective-permute-start | bytes 12296 | tf_op jit(solution)/shard_map/ppermute | solution.py:328
  72.1 1.5 %shard_map.165 = (bf16[256,128]{1,0:T(8,128)(2,1)}, bf16[256,128]{1,0:T(8,128)(2,1)}) custom-call(bf16[128,128]{1,0:T(8,128)(2,1)} %get-tuple-element.49.next_mine, bf16[128,128]{1,0:T(8,128)(2,1)} %copy-done.15, bf16[128,128]{1,0:T(8,128)(2,1)} %get-tuple-element.64.grad_mine, bf16[192,128]{1,0:T(8,128)(2,1)} %copy-done.5), custom_call_target="tpu_custom_call" | custom-call | flops 16777216 | bytes 147456 | tf_op jit(solution)/shard_map/pallas_call | solution.py:88
  (82 shorter events, 16.1 us)
Async XLA Ops:
  0.6 10.3 %collective-permute-start.3 = (bf16[128,1536]{1,0:T(8,128)(2,1)}, bf16[128,1536]{1,0:T(8,128)(2,1)S(1)}, u32[]{:S(2)}, u32[]{:S(2)}) collective-permute-start(bf16[128,1536]{1,0:T(8,128)(2,1)} %refs_9_.1), channel_id=1, source_target_pairs={{0,1},{1,0},{2,3},{3,2},{4,5},{5,4},{6,7},{7,6},{8,9},{9,8},{10,11... | collective-permute-start | bytes 1179656 | tf_op jit(solution)/shard_map/ppermute | solution.py:328
  1.1 1.9 %collective-permute-start.1 = (bf16[256,128]{1,0:T(8,128)(2,1)}, bf16[256,128]{1,0:T(8,128)(2,1)S(1)}, u32[]{:S(2)}, u32[]{:S(2)}) collective-permute-start(bf16[256,128]{1,0:T(8,128)(2,1)} %state.1), channel_id=1, source_target_pairs={{0,1},{1,0},{2,3},{3,2},{4,5},{5,4},{6,7},{7,6},{8,9},{9,8},{10,11... | collective-permute-start | bytes 196616 | tf_op jit(solution)/shard_map/ppermute | solution.py:328
  1.2 20.4 %collective-permute-start.8 = (bf16[128,512]{1,0:T(8,128)(2,1)}, bf16[128,512]{1,0:T(8,128)(2,1)S(1)}, u32[]{:S(2)}, u32[]{:S(2)}) collective-permute-start(bf16[128,512]{1,0:T(8,128)(2,1)} %refs_11_.1), channel_id=1, source_target_pairs={{0,1},{1,0},{2,3},{3,2},{4,5},{5,4},{6,7},{7,6},{8,9},{9,8},{10,11... | collective-permute-start | bytes 393224 | tf_op jit(solution)/shard_map/ppermute | solution.py:328
  1.7 1.4 %collective-permute-start = (bf16[16,128]{1,0:T(8,128)(2,1)}, bf16[16,128]{1,0:T(8,128)(2,1)S(1)}, u32[]{:S(2)}, u32[]{:S(2)}) collective-permute-start(bf16[16,128]{1,0:T(8,128)(2,1)} %latent.1), channel_id=1, source_target_pairs={{0,1},{1,0},{2,3},{3,2},{4,5},{5,4},{6,7},{7,6},{8,9},{9,8},{10,11... | collective-permute-start | bytes 12296 | tf_op jit(solution)/shard_map/ppermute | solution.py:328
  1.7 35.4 %collective-permute-start.13 = (bf16[128,1024]{1,0:T(8,128)(2,1)}, bf16[128,1024]{1,0:T(8,128)(2,1)S(1)}, u32[]{:S(2)}, u32[]{:S(2)}) collective-permute-start(bf16[128,1024]{1,0:T(8,128)(2,1)} %refs_13_.1), channel_id=1, source_target_pairs={{0,1},{1,0},{2,3},{3,2},{4,5},{5,4},{6,7},{7,6},{8,9},{9,8},{10,11... | collective-permute-start | bytes 786440 | tf_op jit(solution)/shard_map/ppermute | solution.py:328
  5.3 5.6 %collective-permute-start.2 = (bf16[144,256]{1,0:T(8,128)(2,1)}, bf16[144,256]{1,0:T(8,128)(2,1)S(1)}, u32[]{:S(2)}, u32[]{:S(2)}) collective-permute-start(bf16[144,256]{1,0:T(8,128)(2,1)} %get-tuple-element.39.refs_0_), channel_id=1, source_target_pairs={{0,2},{1,3},{2,0},{3,1},{4,6},{5,7},{6,4},{7,5},{8,10},{9,11},{10,... | collective-permute-start | bytes 221192 | tf_op jit(solution)/shard_map/ppermute | solution.py:328
  8.1 10.6 %collective-permute-start.7 = (bf16[160,128]{1,0:T(8,128)(2,1)}, bf16[160,128]{1,0:T(8,128)(2,1)S(1)}, u32[]{:S(2)}, u32[]{:S(2)}) collective-permute-start(bf16[160,128]{1,0:T(8,128)(2,1)} %get-tuple-element.42), channel_id=1, source_target_pairs={{0,1},{1,0},{2,3},{3,2},{4,5},{5,4},{6,7},{7,6},{8,9},{9,8},{10,11... | collective-permute-start | bytes 122888 | tf_op jit(solution)/shard_map/ppermute | solution.py:328
  14.3 7.3 %collective-permute-start.4 = (bf16[32,256]{1,0:T(8,128)(2,1)}, bf16[32,256]{1,0:T(8,128)(2,1)S(1)}, u32[]{:S(2)}, u32[]{:S(2)}) collective-permute-start(bf16[32,256]{1,0:T(8,128)(2,1)} %get-tuple-element.40.refs_0_), channel_id=1, source_target_pairs={{0,4},{4,0},{8,12},{12,8},{1,5},{5,1},{9,13},{13,9},{2,6},{6,2},{1... | collective-permute-start | bytes 49160 | tf_op jit(solution)/shard_map/ppermute | solution.py:328
  16.1 5.5 %collective-permute-start.5 = (bf16[32,256]{1,0:T(8,128)(2,1)}, bf16[32,256]{1,0:T(8,128)(2,1)S(1)}, u32[]{:S(2)}, u32[]{:S(2)}) collective-permute-start(bf16[32,256]{1,0:T(8,128)(2,1)} %get-tuple-element.40.refs_0_), channel_id=1, source_target_pairs={{0,8},{4,12},{8,0},{12,4},{1,9},{5,13},{9,1},{13,5},{2,10},{6,14},... | collective-permute-start | bytes 49160 | tf_op jit(solution)/shard_map/ppermute | solution.py:328
  18.7 5.7 %collective-permute-start.6 = (bf16[32,256]{1,0:T(8,128)(2,1)}, bf16[32,256]{1,0:T(8,128)(2,1)S(1)}, u32[]{:S(2)}, u32[]{:S(2)}) collective-permute-start(bf16[32,256]{1,0:T(8,128)(2,1)} %get-tuple-element.40.refs_0_), channel_id=1, source_target_pairs={{0,12},{4,8},{8,4},{12,0},{1,13},{5,9},{9,5},{13,1},{2,14},{6,10},... | collective-permute-start | bytes 49160 | tf_op jit(solution)/shard_map/ppermute | solution.py:328
  25.1 3.9 %copy-start.2 = (bf16[128,512]{1,0:T(8,128)(2,1)S(1)}, bf16[128,512]{1,0:T(8,128)(2,1)}, u32[]{:S(2)}) copy-start(bf16[128,512]{1,0:T(8,128)(2,1)} %refs_7_.1) | copy-start | bytes 393220
  25.1 3.9 %copy-start.8 = (bf16[160,256]{1,0:T(8,128)(2,1)S(1)}, bf16[160,256]{1,0:T(8,128)(2,1)}, u32[]{:S(2)}) copy-start(bf16[160,256]{1,0:T(8,128)(2,1)} %get-tuple-element.47.refs_2_) | copy-start | bytes 245764
  27.4 6.9 %collective-permute-start.9 = (bf16[128,512]{1,0:T(8,128)(2,1)}, bf16[128,512]{1,0:T(8,128)(2,1)S(1)}, u32[]{:S(2)}, u32[]{:S(2)}) collective-permute-start(bf16[128,512]{1,0:T(8,128)(2,1)} %get-tuple-element.46), channel_id=1, source_target_pairs={{0,2},{1,3},{2,0},{3,1},{4,6},{5,7},{6,4},{7,5},{8,10},{9,11},{10,... | collective-permute-start | bytes 393224 | tf_op jit(solution)/shard_map/ppermute | solution.py:328
  28.9 8.2 %collective-permute-start.14 = (bf16[128,512]{1,0:T(8,128)(2,1)S(1)}, bf16[128,512]{1,0:T(8,128)(2,1)S(1)}, u32[]{:S(2)}, u32[]{:S(2)}) collective-permute-start(bf16[128,512]{1,0:T(8,128)(2,1)S(1)} %copy-done.2), channel_id=1, source_target_pairs={{0,1},{1,0},{2,3},{3,2},{4,5},{5,4},{6,7},{7,6},{8,9},{9,8},{10,11... | collective-permute-start | bytes 393224 | tf_op jit(solution)/shard_map/ppermute | solution.py:328
  28.9 5.4 %collective-permute-start.10 = (bf16[160,256]{1,0:T(8,128)(2,1)S(1)}, bf16[160,256]{1,0:T(8,128)(2,1)S(1)}, u32[]{:S(2)}, u32[]{:S(2)}) collective-permute-start(bf16[160,256]{1,0:T(8,128)(2,1)S(1)} %copy-done.8), channel_id=1, source_target_pairs={{0,2},{1,3},{2,0},{3,1},{4,6},{5,7},{6,4},{7,5},{8,10},{9,11},{10,... | collective-permute-start | bytes 245768 | tf_op jit(solution)/shard_map/ppermute | solution.py:328
  37.1 1.4 %collective-permute-start.12 = (f32[16,512]{1,0:T(8,128)}, f32[16,512]{1,0:T(8,128)S(1)}, u32[]{:S(2)}, u32[]{:S(2)}) collective-permute-start(f32[16,512]{1,0:T(8,128)} %get-tuple-element.51.aggregate), channel_id=1, source_target_pairs={{0,1},{1,0},{2,3},{3,2},{4,5},{5,4},{6,7},{7,6},{8,9},{9,8},{10,11... | collective-permute-start | bytes 98312 | tf_op jit(solution)/shard_map/ppermute | solution.py:328
  41.4 3.9 %collective-permute-start.15 = (bf16[16,512]{1,0:T(8,128)(2,1)}, bf16[16,512]{1,0:T(8,128)(2,1)S(1)}, u32[]{:S(2)}, u32[]{:S(2)}) collective-permute-start(bf16[16,512]{1,0:T(8,128)(2,1)} %get-tuple-element.53), channel_id=1, source_target_pairs={{0,2},{1,3},{2,0},{3,1},{4,6},{5,7},{6,4},{7,5},{8,10},{9,11},{10,... | collective-permute-start | bytes 49160 | tf_op jit(solution)/shard_map/ppermute | solution.py:328
  48.3 3.9 %collective-permute-start.16 = (bf16[16,512]{1,0:T(8,128)(2,1)}, bf16[16,512]{1,0:T(8,128)(2,1)S(1)}, u32[]{:S(2)}, u32[]{:S(2)}) collective-permute-start(bf16[16,512]{1,0:T(8,128)(2,1)} %get-tuple-element.57), channel_id=1, source_target_pairs={{0,2},{1,3},{2,0},{3,1},{4,6},{5,7},{6,4},{7,5},{8,10},{9,11},{10,... | collective-permute-start | bytes 49160 | tf_op jit(solution)/shard_map/ppermute | solution.py:328
  56.5 4.8 %collective-permute-start.17 = (bf16[192,256]{1,0:T(8,128)(2,1)}, bf16[192,256]{1,0:T(8,128)(2,1)S(1)}, u32[]{:S(2)}, u32[]{:S(2)}) collective-permute-start(bf16[192,256]{1,0:T(8,128)(2,1)} %get-tuple-element.63), channel_id=1, source_target_pairs={{0,2},{1,3},{2,0},{3,1},{4,6},{5,7},{6,4},{7,5},{8,10},{9,11},{10,... | collective-permute-start | bytes 294920 | tf_op jit(solution)/shard_map/ppermute | solution.py:328
  63.7 1.4 %collective-permute-start.18 = (bf16[192,128]{1,0:T(8,128)(2,1)}, bf16[192,128]{1,0:T(8,128)(2,1)S(1)}, u32[]{:S(2)}, u32[]{:S(2)}) collective-permute-start(bf16[192,128]{1,0:T(8,128)(2,1)} %get-tuple-element.65), channel_id=1, source_target_pairs={{0,1},{1,0},{2,3},{3,2},{4,5},{5,4},{6,7},{7,6},{8,9},{9,8},{10,11... | collective-permute-start | bytes 147464 | tf_op jit(solution)/shard_map/ppermute | solution.py:328
  63.7 7.9 %collective-permute-start.11 = (bf16[128,128]{1,0:T(8,128)(2,1)S(1)}, bf16[128,128]{1,0:T(8,128)(2,1)S(1)}, u32[]{:S(2)}, u32[]{:S(2)}) collective-permute-start(bf16[128,128]{1,0:T(8,128)(2,1)S(1)} %copy-done.23), channel_id=1, source_target_pairs={{0,1},{1,0},{2,3},{3,2},{4,5},{5,4},{6,7},{7,6},{8,9},{9,8},{10,11... | collective-permute-start | bytes 98312 | tf_op jit(solution)/shard_map/ppermute | solution.py:328
  67.2 6.5 %collective-permute-start.21 = (bf16[16,128]{1,0:T(8,128)(2,1)}, bf16[16,128]{1,0:T(8,128)(2,1)S(1)}, u32[]{:S(2)}, u32[]{:S(2)}) collective-permute-start(bf16[16,128]{1,0:T(8,128)(2,1)} %get-tuple-element.73), channel_id=1, source_target_pairs={{0,12},{4,8},{8,4},{12,0},{1,13},{5,9},{9,5},{13,1},{2,14},{6,10},... | collective-permute-start | bytes 12296 | tf_op jit(solution)/shard_map/ppermute | solution.py:328
  67.6 6.1 %collective-permute-start.20 = (bf16[16,128]{1,0:T(8,128)(2,1)}, bf16[16,128]{1,0:T(8,128)(2,1)S(1)}, u32[]{:S(2)}, u32[]{:S(2)}) collective-permute-start(bf16[16,128]{1,0:T(8,128)(2,1)} %get-tuple-element.72), channel_id=1, source_target_pairs={{0,8},{4,12},{8,0},{12,4},{1,9},{5,13},{9,1},{13,5},{2,10},{6,14},... | collective-permute-start | bytes 12296 | tf_op jit(solution)/shard_map/ppermute | solution.py:328
  67.8 5.9 %collective-permute-start.19 = (bf16[16,128]{1,0:T(8,128)(2,1)S(1)}, bf16[16,128]{1,0:T(8,128)(2,1)S(1)}, u32[]{:S(2)}, u32[]{:S(2)}) collective-permute-start(bf16[16,128]{1,0:T(8,128)(2,1)S(1)} %copy-done.24), channel_id=1, source_target_pairs={{0,4},{4,0},{8,12},{12,8},{1,5},{5,1},{9,13},{13,9},{2,6},{6,2},{1... | collective-permute-start | bytes 12296 | tf_op jit(solution)/shard_map/ppermute | solution.py:328
  (23 other events, 25.7 us)

commit v4 on v3

--- a/solution.py
+++ b/solution.py
@@ -11,6 +11,7 @@
 f32 = jnp.float32
 bf16 = jnp.bfloat16
 cores = 2
+kernel_vmem = 8 << 20
 
 
 def dot(left, right):
@@ -91,6 +92,7 @@
         in_specs=specs,
         out_specs=[pl.BlockSpec(memory_space=pltpu.VMEM)] * len(outs),
         cost_estimate=pl.CostEstimate(flops=flops, bytes_accessed=moved, transcendentals=0),
+        compiler_params=pltpu.CompilerParams(vmem_limit_bytes=kernel_vmem),
     )(*operands)
 
 

time: 74.8 us -> 56.3 us (0.75)
  Pallas kernels: 23.2 us -> 6.4 us
  local copies, waits for them, and re-layouts: 7.89 us -> 5.38 us
  starting transfers between devices: 19.6 us -> 20.4 us
    pallas_call x11, Pallas kernels: 23.2 us -> 6.4 us  [stage(): pl.pallas_call(kernel, out_shape=[jax.ShapeDtypeStruct(shape, kind) for s...]
    unnamed x50 -> x32, local copies, waits for them, and re-layouts: 7.89 us -> 5.38 us
    ppermute x22, starting transfers between devices: 19.6 us -> 20.4 us  [swapped(): return lax.ppermute(values, axis, [(i, i ^ bits) for i in range(count)])]
  transfers between devices with their start and end apart: 22 -> 22, of which waited for: 9 -> 12; matrix products, arithmetic and copies ran while one was open for 0% -> 0% of each run, Pallas kernels for 18% -> 6%
where the time goes in v4:
time: 56.3 us; the launch traced here: 56 us
  waiting for transfers between devices  22.5 us (40%)
  starting transfers between devices  20.4 us (36%)
  Pallas kernels  6.4 us (11%)
  local copies, waits for them, and re-layouts  5.38 us (10%)
  between operations  0.76 us (1%)
  other arithmetic  0.6 us (1%)
    ppermute x22, waiting for transfers between devices, swapped(): return lax.ppermute(values, axis, [(i, i ^ bits) for i in range(count)])  22.5 us
    ppermute x22, starting transfers between devices, swapped(): return lax.ppermute(values, axis, [(i, i ^ bits) for i in range(count)])  20.4 us
    pallas_call x11, Pallas kernels, stage(): pl.pallas_call(kernel, out_shape=[jax.ShapeDtypeStruct(shape, kind) for s...  6.4 us
    unnamed x32, local copies, waits for them, and re-layouts  5.38 us
  transfers between devices with their start and end apart: 22, of which 12 were waited for; matrix products, arithmetic and copies ran while one was open for 0% of the time, Pallas kernels for 6%

profile of v4, /device:TPU:0, one launch (start us, length us, event | category | flops | bytes accessed | tf_op | source)
XLA Modules:
  0.0 56.0 jit_solution(17910898867181852497)
XLA Ops:
  2.2 0.9 %collective-permute-done.latent2 = bf16[16,128]{1,0:T(8,128)(2,1)S(1)} collective-permute-done((bf16[16,128]{1,0:T(8,128)(2,1)}, bf16[16,128]{1,0:T(8,128)(2,1)S(1)}, u32[]{:S(2)}, u32[]{:S(2)}) %collective-permute-start) | collective-permute-done | bytes 4128 | tf_op jit(solution)/shard_map/ppermute | solution.py:330
  3.7 0.8 %copy-done.5 = bf16[256,128]{1,0:T(8,128)(2,1)S(1)} copy-done((bf16[256,128]{1,0:T(8,128)(2,1)S(1)}, bf16[256,128]{1,0:T(8,128)(2,1)}, u32[]{:S(2)}) %copy-start.5) | copy-done | bytes 65560
  4.6 0.8 %copy-done.7 = bf16[256,128]{1,0:T(8,128)(2,1)S(1)} copy-done((bf16[256,128]{1,0:T(8,128)(2,1)S(1)}, bf16[256,128]{1,0:T(8,128)(2,1)}, u32[]{:S(2)}) %copy-start.7) | copy-done | bytes 65560
  6.8 2.9 %collective-permute-start.2 = (bf16[144,256]{1,0:T(8,128)(2,1)S(1)}, bf16[144,256]{1,0:T(8,128)(2,1)S(1)}, u32[]{:S(2)}, u32[]{:S(2)}) collective-permute-start(bf16[144,256]{1,0:T(8,128)(2,1)S(1)} %get-tuple-element.39.refs_0_), channel_id=1, source_target_pairs={{0,2},{1,3},{2,0},{3,1},{4,6},{5,7},{6,4},{7,5},{8,10},{9,11},{10,... | collective-permute-start | bytes 221192 | tf_op jit(solution)/shard_map/ppermute | solution.py:330
  9.7 2.6 %collective-permute-done.2.refs_1_ = bf16[144,256]{1,0:T(8,128)(2,1)S(1)} collective-permute-done((bf16[144,256]{1,0:T(8,128)(2,1)S(1)}, bf16[144,256]{1,0:T(8,128)(2,1)S(1)}, u32[]{:S(2)}, u32[]{:S(2)}) %collective-permute-start.2) | collective-permute-done | bytes 73760 | tf_op jit(solution)/shard_map/ppermute | solution.py:330
  12.3 1.0 %copy-done = bf16[128,1536]{1,0:T(8,128)(2,1)S(1)} copy-done((bf16[128,1536]{1,0:T(8,128)(2,1)S(1)}, bf16[128,1536]{1,0:T(8,128)(2,1)}, u32[]{:S(2)}) %copy-start) | copy-done | bytes 393240
  13.5 1.8 %collective-permute-start.4 = (bf16[32,256]{1,0:T(8,128)(2,1)S(1)}, bf16[32,256]{1,0:T(8,128)(2,1)S(1)}, u32[]{:S(2)}, u32[]{:S(2)}) collective-permute-start(bf16[32,256]{1,0:T(8,128)(2,1)S(1)} %get-tuple-element.40.refs_0_), channel_id=1, source_target_pairs={{0,4},{4,0},{8,12},{12,8},{1,5},{5,1},{9,13},{13,9},{2,6},{6,2},{1... | collective-permute-start | bytes 49160 | tf_op jit(solution)/shard_map/ppermute | solution.py:330
  15.3 2.6 %collective-permute-start.5 = (bf16[32,256]{1,0:T(8,128)(2,1)S(1)}, bf16[32,256]{1,0:T(8,128)(2,1)S(1)}, u32[]{:S(2)}, u32[]{:S(2)}) collective-permute-start(bf16[32,256]{1,0:T(8,128)(2,1)S(1)} %get-tuple-element.40.refs_0_), channel_id=1, source_target_pairs={{0,8},{4,12},{8,0},{12,4},{1,9},{5,13},{9,1},{13,5},{2,10},{6,14},... | collective-permute-start | bytes 49160 | tf_op jit(solution)/shard_map/ppermute | solution.py:330
  18.6 1.0 %shard_map.158 = (f32[128,256]{1,0:T(8,128)S(1)}, bf16[64,128]{1,0:T(8,128)(2,1)S(1)}, bf16[16,128]{1,0:T(8,128)(2,1)S(1)}, bf16[160,256]{1,0:T(8,128)(2,1)S(1)}) custom-call(bf16[144,512]{1,0:T(8,128)(2,1)S(1)} %get-tuple-element.41.full.refs_4_.refs_2_, bf16[128,1536]{1,0:T(8,128)(2,1)S(1)} %copy-done.1, ...), custom_call_target="tpu_custom_call" | custom-call | flops 16777216 | bytes 1047552 | tf_op jit(solution)/shard_map/pallas_call | solution.py:89
  20.0 3.5 %collective-permute-done.6.refs_3_ = bf16[32,256]{1,0:T(8,128)(2,1)S(1)} collective-permute-done((bf16[32,256]{1,0:T(8,128)(2,1)S(1)}, bf16[32,256]{1,0:T(8,128)(2,1)S(1)}, u32[]{:S(2)}, u32[]{:S(2)}) %collective-permute-start.6) | collective-permute-done | bytes 16416 | tf_op jit(solution)/shard_map/ppermute | solution.py:330
  23.9 1.6 %collective-permute-start.9 = (bf16[128,512]{1,0:T(8,128)(2,1)S(1)}, bf16[128,512]{1,0:T(8,128)(2,1)S(1)}, u32[]{:S(2)}, u32[]{:S(2)}) collective-permute-start(bf16[128,512]{1,0:T(8,128)(2,1)S(1)} %get-tuple-element.46), channel_id=1, source_target_pairs={{0,2},{1,3},{2,0},{3,1},{4,6},{5,7},{6,4},{7,5},{8,10},{9,11},{10,... | collective-permute-start | bytes 393224 | tf_op jit(solution)/shard_map/ppermute | solution.py:330
  26.0 4.7 %collective-permute-done.10.refs_3_ = bf16[160,256]{1,0:T(8,128)(2,1)S(1)} collective-permute-done((bf16[160,256]{1,0:T(8,128)(2,1)S(1)}, bf16[160,256]{1,0:T(8,128)(2,1)S(1)}, u32[]{:S(2)}, u32[]{:S(2)}) %collective-permute-start.10) | collective-permute-done | bytes 81952 | tf_op jit(solution)/shard_map/ppermute | solution.py:330
  30.7 0.8 %shard_map.160 = (f32[128,512]{1,0:T(8,128)S(1)}, f32[128,1]{1,0:T(8,128)S(1)}, bf16[128,128]{1,0:T(8,128)(2,1)S(1)}, bf16[128,128]{1,0:T(8,128)(2,1)S(1)}, f32[...) custom-call(f32[128,512]{1,0:T(8,128)S(1)} %get-tuple-element.45.refs_0_, ...), custom_call_target="tpu_custom_call" | custom-call | flops 16777216 | bytes 708608 | tf_op jit(solution)/shard_map/pallas_call | solution.py:89
  31.5 1.2 %collective-permute-done.12.aggregate2 = f32[16,512]{1,0:T(8,128)S(1)} collective-permute-done((f32[16,512]{1,0:T(8,128)S(1)}, f32[16,512]{1,0:T(8,128)S(1)}, u32[]{:S(2)}, u32[]{:S(2)}) %collective-permute-start.12) | collective-permute-done | bytes 32800 | tf_op jit(solution)/shard_map/ppermute | solution.py:330
  33.1 1.5 %collective-permute-start.15 = (bf16[16,512]{1,0:T(8,128)(2,1)S(1)}, bf16[16,512]{1,0:T(8,128)(2,1)S(1)}, u32[]{:S(2)}, u32[]{:S(2)}) collective-permute-start(bf16[16,512]{1,0:T(8,128)(2,1)S(1)} %get-tuple-element.53), channel_id=1, source_target_pairs={{0,2},{1,3},{2,0},{3,1},{4,6},{5,7},{6,4},{7,5},{8,10},{9,11},{10,... | collective-permute-start | bytes 49160 | tf_op jit(solution)/shard_map/ppermute | solution.py:330
  34.6 2.2 %collective-permute-done.15.refs_1_ = bf16[16,512]{1,0:T(8,128)(2,1)S(1)} collective-permute-done((bf16[16,512]{1,0:T(8,128)(2,1)S(1)}, bf16[16,512]{1,0:T(8,128)(2,1)S(1)}, u32[]{:S(2)}, u32[]{:S(2)}) %collective-permute-start.15) | collective-permute-done | bytes 16416 | tf_op jit(solution)/shard_map/ppermute | solution.py:330
  36.9 0.9 %shard_map.162 = (bf16[16,128]{1,0:T(8,128)(2,1)}, bf16[16,256]{1,0:T(8,128)(2,1)S(1)}, f32[16,512]{1,0:T(8,128)S(1)}, bf16[16,512]{1,0:T(8,128)(2,1)S(1)}, bf16[16,512]{1,0:T(8,128)(2,1)}) custom-call(f32[16,512]{1,0:T(8,128)S(1)} %get-tuple-element.52.refs_0_, bf16[16,512]{1,0:T(8,128)(2,1)S(1)} %collective-permute-done.15.refs_1_, ...), custom_call_target="tpu_custom_call" | custom-call | flops 16777216 | bytes 1163264 | tf_op jit(solution)/shard_map/pallas_call | solution.py:89
  37.8 1.5 %collective-permute-start.16 = (bf16[16,512]{1,0:T(8,128)(2,1)S(1)}, bf16[16,512]{1,0:T(8,128)(2,1)S(1)}, u32[]{:S(2)}, u32[]{:S(2)}) collective-permute-start(bf16[16,512]{1,0:T(8,128)(2,1)S(1)} %get-tuple-element.57), channel_id=1, source_target_pairs={{0,2},{1,3},{2,0},{3,1},{4,6},{5,7},{6,4},{7,5},{8,10},{9,11},{10,... | collective-permute-start | bytes 49160 | tf_op jit(solution)/shard_map/ppermute | solution.py:330
  39.3 2.2 %collective-permute-done.16.refs_1_ = bf16[16,512]{1,0:T(8,128)(2,1)S(1)} collective-permute-done((bf16[16,512]{1,0:T(8,128)(2,1)S(1)}, bf16[16,512]{1,0:T(8,128)(2,1)S(1)}, u32[]{:S(2)}, u32[]{:S(2)}) %collective-permute-start.16) | collective-permute-done | bytes 16416 | tf_op jit(solution)/shard_map/ppermute | solution.py:330
  41.6 1.9 %shard_map.163 = (f32[192,256]{1,0:T(8,128)S(1)}, bf16[192,256]{1,0:T(8,128)(2,1)S(1)}, f32[192,512]{1,0:T(8,128)}) custom-call(f32[16,512]{1,0:T(8,128)S(1)} %get-tuple-element.56.refs_0_, bf16[16,512]{1,0:T(8,128)(2,1)S(1)} %collective-permute-done.16.refs_1_, bf16[16,128]{1,0:T(8,128)(2,1)S(1)} %get-tuple-element.48.refs_5_.refs_2_, ...), custom_call_target="tpu_custom_call" | custom-call | flops 16777216 | bytes 2208256 | tf_op jit(solution)/shard_map/pallas_call | solution.py:89
  43.5 1.5 %collective-permute-start.17 = (bf16[192,256]{1,0:T(8,128)(2,1)S(1)}, bf16[192,256]{1,0:T(8,128)(2,1)S(1)}, u32[]{:S(2)}, u32[]{:S(2)}) collective-permute-start(bf16[192,256]{1,0:T(8,128)(2,1)S(1)} %get-tuple-element.63), channel_id=1, source_target_pairs={{0,2},{1,3},{2,0},{3,1},{4,6},{5,7},{6,4},{7,5},{8,10},{9,11},{10,... | collective-permute-start | bytes 294920 | tf_op jit(solution)/shard_map/ppermute | solution.py:330
  45.0 3.1 %collective-permute-done.17.refs_1_ = bf16[192,256]{1,0:T(8,128)(2,1)S(1)} collective-permute-done((bf16[192,256]{1,0:T(8,128)(2,1)S(1)}, bf16[192,256]{1,0:T(8,128)(2,1)S(1)}, u32[]{:S(2)}, u32[]{:S(2)}) %collective-permute-start.17) | collective-permute-done | bytes 98336 | tf_op jit(solution)/shard_map/ppermute | solution.py:330
  48.7 0.7 %collective-permute-done.18.came = bf16[192,128]{1,0:T(8,128)(2,1)S(1)} collective-permute-done((bf16[192,128]{1,0:T(8,128)(2,1)S(1)}, bf16[192,128]{1,0:T(8,128)(2,1)S(1)}, u32[]{:S(2)}, u32[]{:S(2)}) %collective-permute-start.18) | collective-permute-done | bytes 49184 | tf_op jit(solution)/shard_map/ppermute | solution.py:330
  49.6 4.2 %collective-permute-start.19 = (bf16[16,128]{1,0:T(8,128)(2,1)S(1)}, bf16[16,128]{1,0:T(8,128)(2,1)S(1)}, u32[]{:S(2)}, u32[]{:S(2)}) collective-permute-start(bf16[16,128]{1,0:T(8,128)(2,1)S(1)} %get-tuple-element.71), channel_id=1, source_target_pairs={{0,4},{4,0},{8,12},{12,8},{1,5},{5,1},{9,13},{13,9},{2,6},{6,2},{1... | collective-permute-start | bytes 12296 | tf_op jit(solution)/shard_map/ppermute | solution.py:330
  (64 shorter events, 9.1 us)
Async XLA Ops:
  0.6 11.7 %collective-permute-start.3 = (bf16[128,1536]{1,0:T(8,128)(2,1)}, bf16[128,1536]{1,0:T(8,128)(2,1)S(1)}, u32[]{:S(2)}, u32[]{:S(2)}) collective-permute-start(bf16[128,1536]{1,0:T(8,128)(2,1)} %refs_9_.1), channel_id=1, source_target_pairs={{0,1},{1,0},{2,3},{3,2},{4,5},{5,4},{6,7},{7,6},{8,9},{9,8},{10,11... | collective-permute-start | bytes 1179656 | tf_op jit(solution)/shard_map/ppermute | solution.py:330
  1.1 1.9 %collective-permute-start.1 = (bf16[256,128]{1,0:T(8,128)(2,1)}, bf16[256,128]{1,0:T(8,128)(2,1)S(1)}, u32[]{:S(2)}, u32[]{:S(2)}) collective-permute-start(bf16[256,128]{1,0:T(8,128)(2,1)} %state.1), channel_id=1, source_target_pairs={{0,1},{1,0},{2,3},{3,2},{4,5},{5,4},{6,7},{7,6},{8,9},{9,8},{10,11... | collective-permute-start | bytes 196616 | tf_op jit(solution)/shard_map/ppermute | solution.py:330
  1.2 18.4 %collective-permute-start.8 = (bf16[128,512]{1,0:T(8,128)(2,1)}, bf16[128,512]{1,0:T(8,128)(2,1)S(1)}, u32[]{:S(2)}, u32[]{:S(2)}) collective-permute-start(bf16[128,512]{1,0:T(8,128)(2,1)} %refs_11_.1), channel_id=1, source_target_pairs={{0,1},{1,0},{2,3},{3,2},{4,5},{5,4},{6,7},{7,6},{8,9},{9,8},{10,11... | collective-permute-start | bytes 393224 | tf_op jit(solution)/shard_map/ppermute | solution.py:330
  1.7 1.4 %collective-permute-start = (bf16[16,128]{1,0:T(8,128)(2,1)}, bf16[16,128]{1,0:T(8,128)(2,1)S(1)}, u32[]{:S(2)}, u32[]{:S(2)}) collective-permute-start(bf16[16,128]{1,0:T(8,128)(2,1)} %latent.1), channel_id=1, source_target_pairs={{0,1},{1,0},{2,3},{3,2},{4,5},{5,4},{6,7},{7,6},{8,9},{9,8},{10,11... | collective-permute-start | bytes 12296 | tf_op jit(solution)/shard_map/ppermute | solution.py:330
  1.7 29.8 %collective-permute-start.13 = (bf16[128,1024]{1,0:T(8,128)(2,1)}, bf16[128,1024]{1,0:T(8,128)(2,1)S(1)}, u32[]{:S(2)}, u32[]{:S(2)}) collective-permute-start(bf16[128,1024]{1,0:T(8,128)(2,1)} %refs_13_.1), channel_id=1, source_target_pairs={{0,1},{1,0},{2,3},{3,2},{4,5},{5,4},{6,7},{7,6},{8,9},{9,8},{10,11... | collective-permute-start | bytes 786440 | tf_op jit(solution)/shard_map/ppermute | solution.py:330
  6.8 5.5 %collective-permute-start.2 = (bf16[144,256]{1,0:T(8,128)(2,1)S(1)}, bf16[144,256]{1,0:T(8,128)(2,1)S(1)}, u32[]{:S(2)}, u32[]{:S(2)}) collective-permute-start(bf16[144,256]{1,0:T(8,128)(2,1)S(1)} %get-tuple-element.39.refs_0_), channel_id=1, source_target_pairs={{0,2},{1,3},{2,0},{3,1},{4,6},{5,7},{6,4},{7,5},{8,10},{9,11},{10,... | collective-permute-start | bytes 221192 | tf_op jit(solution)/shard_map/ppermute | solution.py:330
  9.7 8.2 %collective-permute-start.7 = (bf16[160,128]{1,0:T(8,128)(2,1)S(1)}, bf16[160,128]{1,0:T(8,128)(2,1)S(1)}, u32[]{:S(2)}, u32[]{:S(2)}) collective-permute-start(bf16[160,128]{1,0:T(8,128)(2,1)S(1)} %get-tuple-element.42), channel_id=1, source_target_pairs={{0,1},{1,0},{2,3},{3,2},{4,5},{5,4},{6,7},{7,6},{8,9},{9,8},{10,11... | collective-permute-start | bytes 122888 | tf_op jit(solution)/shard_map/ppermute | solution.py:330
  13.3 4.7 %copy-start.15 = (s32[256]{0:T(256)S(1)}, s32[256]{0:T(256)}, u32[]{:S(2)}) copy-start(s32[256]{0:T(256)} %param.17) | copy-start | bytes 3076
  13.5 6.1 %collective-permute-start.4 = (bf16[32,256]{1,0:T(8,128)(2,1)S(1)}, bf16[32,256]{1,0:T(8,128)(2,1)S(1)}, u32[]{:S(2)}, u32[]{:S(2)}) collective-permute-start(bf16[32,256]{1,0:T(8,128)(2,1)S(1)} %get-tuple-element.40.refs_0_), channel_id=1, source_target_pairs={{0,4},{4,0},{8,12},{12,8},{1,5},{5,1},{9,13},{13,9},{2,6},{6,2},{1... | collective-permute-start | bytes 49160 | tf_op jit(solution)/shard_map/ppermute | solution.py:330
  15.3 4.6 %collective-permute-start.5 = (bf16[32,256]{1,0:T(8,128)(2,1)S(1)}, bf16[32,256]{1,0:T(8,128)(2,1)S(1)}, u32[]{:S(2)}, u32[]{:S(2)}) collective-permute-start(bf16[32,256]{1,0:T(8,128)(2,1)S(1)} %get-tuple-element.40.refs_0_), channel_id=1, source_target_pairs={{0,8},{4,12},{8,0},{12,4},{1,9},{5,13},{9,1},{13,5},{2,10},{6,14},... | collective-permute-start | bytes 49160 | tf_op jit(solution)/shard_map/ppermute | solution.py:330
  17.9 5.5 %collective-permute-start.6 = (bf16[32,256]{1,0:T(8,128)(2,1)S(1)}, bf16[32,256]{1,0:T(8,128)(2,1)S(1)}, u32[]{:S(2)}, u32[]{:S(2)}) collective-permute-start(bf16[32,256]{1,0:T(8,128)(2,1)S(1)} %get-tuple-element.40.refs_0_), channel_id=1, source_target_pairs={{0,12},{4,8},{8,4},{12,0},{1,13},{5,9},{9,5},{13,1},{2,14},{6,10},... | collective-permute-start | bytes 49160 | tf_op jit(solution)/shard_map/ppermute | solution.py:330
  18.6 4.9 %copy-start.4 = (bf16[128,512]{1,0:T(8,128)(2,1)S(1)}, bf16[128,512]{1,0:T(8,128)(2,1)}, u32[]{:S(2)}) copy-start(bf16[128,512]{1,0:T(8,128)(2,1)} %refs_11_.1) | copy-start | bytes 393220
  23.9 6.8 %collective-permute-start.9 = (bf16[128,512]{1,0:T(8,128)(2,1)S(1)}, bf16[128,512]{1,0:T(8,128)(2,1)S(1)}, u32[]{:S(2)}, u32[]{:S(2)}) collective-permute-start(bf16[128,512]{1,0:T(8,128)(2,1)S(1)} %get-tuple-element.46), channel_id=1, source_target_pairs={{0,2},{1,3},{2,0},{3,1},{4,6},{5,7},{6,4},{7,5},{8,10},{9,11},{10,... | collective-permute-start | bytes 393224 | tf_op jit(solution)/shard_map/ppermute | solution.py:330
  25.5 6.1 %collective-permute-start.14 = (bf16[128,512]{1,0:T(8,128)(2,1)S(1)}, bf16[128,512]{1,0:T(8,128)(2,1)S(1)}, u32[]{:S(2)}, u32[]{:S(2)}) collective-permute-start(bf16[128,512]{1,0:T(8,128)(2,1)S(1)} %copy-done.3), channel_id=1, source_target_pairs={{0,1},{1,0},{2,3},{3,2},{4,5},{5,4},{6,7},{7,6},{8,9},{9,8},{10,11... | collective-permute-start | bytes 393224 | tf_op jit(solution)/shard_map/ppermute | solution.py:330
  25.5 5.2 %collective-permute-start.10 = (bf16[160,256]{1,0:T(8,128)(2,1)S(1)}, bf16[160,256]{1,0:T(8,128)(2,1)S(1)}, u32[]{:S(2)}, u32[]{:S(2)}) collective-permute-start(bf16[160,256]{1,0:T(8,128)(2,1)S(1)} %get-tuple-element.47.refs_2_), channel_id=1, source_target_pairs={{0,2},{1,3},{2,0},{3,1},{4,6},{5,7},{6,4},{7,5},{8,10},{9,11},{10,... | collective-permute-start | bytes 245768 | tf_op jit(solution)/shard_map/ppermute | solution.py:330
  31.5 1.2 %collective-permute-start.12 = (f32[16,512]{1,0:T(8,128)S(1)}, f32[16,512]{1,0:T(8,128)S(1)}, u32[]{:S(2)}, u32[]{:S(2)}) collective-permute-start(f32[16,512]{1,0:T(8,128)S(1)} %get-tuple-element.51.aggregate), channel_id=1, source_target_pairs={{0,1},{1,0},{2,3},{3,2},{4,5},{5,4},{6,7},{7,6},{8,9},{9,8},{10,11... | collective-permute-start | bytes 98312 | tf_op jit(solution)/shard_map/ppermute | solution.py:330
  33.1 3.8 %collective-permute-start.15 = (bf16[16,512]{1,0:T(8,128)(2,1)S(1)}, bf16[16,512]{1,0:T(8,128)(2,1)S(1)}, u32[]{:S(2)}, u32[]{:S(2)}) collective-permute-start(bf16[16,512]{1,0:T(8,128)(2,1)S(1)} %get-tuple-element.53), channel_id=1, source_target_pairs={{0,2},{1,3},{2,0},{3,1},{4,6},{5,7},{6,4},{7,5},{8,10},{9,11},{10,... | collective-permute-start | bytes 49160 | tf_op jit(solution)/shard_map/ppermute | solution.py:330
  37.8 3.7 %collective-permute-start.16 = (bf16[16,512]{1,0:T(8,128)(2,1)S(1)}, bf16[16,512]{1,0:T(8,128)(2,1)S(1)}, u32[]{:S(2)}, u32[]{:S(2)}) collective-permute-start(bf16[16,512]{1,0:T(8,128)(2,1)S(1)} %get-tuple-element.57), channel_id=1, source_target_pairs={{0,2},{1,3},{2,0},{3,1},{4,6},{5,7},{6,4},{7,5},{8,10},{9,11},{10,... | collective-permute-start | bytes 49160 | tf_op jit(solution)/shard_map/ppermute | solution.py:330
  43.5 4.6 %collective-permute-start.17 = (bf16[192,256]{1,0:T(8,128)(2,1)S(1)}, bf16[192,256]{1,0:T(8,128)(2,1)S(1)}, u32[]{:S(2)}, u32[]{:S(2)}) collective-permute-start(bf16[192,256]{1,0:T(8,128)(2,1)S(1)} %get-tuple-element.63), channel_id=1, source_target_pairs={{0,2},{1,3},{2,0},{3,1},{4,6},{5,7},{6,4},{7,5},{8,10},{9,11},{10,... | collective-permute-start | bytes 294920 | tf_op jit(solution)/shard_map/ppermute | solution.py:330
  48.1 1.3 %collective-permute-start.18 = (bf16[192,128]{1,0:T(8,128)(2,1)S(1)}, bf16[192,128]{1,0:T(8,128)(2,1)S(1)}, u32[]{:S(2)}, u32[]{:S(2)}) collective-permute-start(bf16[192,128]{1,0:T(8,128)(2,1)S(1)} %get-tuple-element.65), channel_id=1, source_target_pairs={{0,1},{1,0},{2,3},{3,2},{4,5},{5,4},{6,7},{7,6},{8,9},{9,8},{10,11... | collective-permute-start | bytes 147464 | tf_op jit(solution)/shard_map/ppermute | solution.py:330
  48.2 5.6 %collective-permute-start.11 = (bf16[128,128]{1,0:T(8,128)(2,1)S(1)}, bf16[128,128]{1,0:T(8,128)(2,1)S(1)}, u32[]{:S(2)}, u32[]{:S(2)}) collective-permute-start(bf16[128,128]{1,0:T(8,128)(2,1)S(1)} %get-tuple-element.50), channel_id=1, source_target_pairs={{0,1},{1,0},{2,3},{3,2},{4,5},{5,4},{6,7},{7,6},{8,9},{9,8},{10,11... | collective-permute-start | bytes 98312 | tf_op jit(solution)/shard_map/ppermute | solution.py:330
  49.4 5.4 %collective-permute-start.21 = (bf16[16,128]{1,0:T(8,128)(2,1)S(1)}, bf16[16,128]{1,0:T(8,128)(2,1)S(1)}, u32[]{:S(2)}, u32[]{:S(2)}) collective-permute-start(bf16[16,128]{1,0:T(8,128)(2,1)S(1)} %get-tuple-element.73), channel_id=1, source_target_pairs={{0,12},{4,8},{8,4},{12,0},{1,13},{5,9},{9,5},{13,1},{2,14},{6,10},... | collective-permute-start | bytes 12296 | tf_op jit(solution)/shard_map/ppermute | solution.py:330
  49.6 5.2 %collective-permute-start.20 = (bf16[16,128]{1,0:T(8,128)(2,1)S(1)}, bf16[16,128]{1,0:T(8,128)(2,1)S(1)}, u32[]{:S(2)}, u32[]{:S(2)}) collective-permute-start(bf16[16,128]{1,0:T(8,128)(2,1)S(1)} %get-tuple-element.72), channel_id=1, source_target_pairs={{0,8},{4,12},{8,0},{12,4},{1,9},{5,13},{9,1},{13,5},{2,10},{6,14},... | collective-permute-start | bytes 12296 | tf_op jit(solution)/shard_map/ppermute | solution.py:330
  49.6 5.8 %collective-permute-start.19 = (bf16[16,128]{1,0:T(8,128)(2,1)S(1)}, bf16[16,128]{1,0:T(8,128)(2,1)S(1)}, u32[]{:S(2)}, u32[]{:S(2)}) collective-permute-start(bf16[16,128]{1,0:T(8,128)(2,1)S(1)} %get-tuple-element.71), channel_id=1, source_target_pairs={{0,4},{4,0},{8,12},{12,8},{1,5},{5,1},{9,13},{13,9},{2,6},{6,2},{1... | collective-permute-start | bytes 12296 | tf_op jit(solution)/shard_map/ppermute | solution.py:330
  (14 other events, 28.5 us)

commit v5 on v1

v5 whole, which is shorter than its diff:
```python
import functools

import jax
import jax.numpy as jnp
from jax import lax
from jax.experimental import pallas as pl
from jax.experimental.pallas import tpu as pltpu
from jax.sharding import PartitionSpec as P

epsilon = 1e-05
f32 = jnp.float32
bf16 = jnp.bfloat16
cores = 2
kernel_vmem = 8 << 20


def dot(left, right):
    return jnp.dot(left, right, preferred_element_type=f32)


def dot_rows(left, right):
    return lax.dot_general(left, right, (((1,), (1,)), ((), ())), preferred_element_type=f32)


def dot_cols(left, right):
    return lax.dot_general(left, right, (((0,), (0,)), ((), ())), preferred_element_type=f32)


def split(values):
    high = values.astype(bf16)
    return high, (values - high.astype(f32)).astype(bf16)


def sigmoid(values):
    return 1.0 / (1.0 + jnp.exp(-values))


def swish_slope(pre_act):
    sigma = sigmoid(pre_act)
    return sigma * (1.0 + pre_act * (1.0 - sigma))


def normalize(values):
    mean = jnp.mean(values, axis=1, keepdims=True)
    square = jnp.mean(values * values, axis=1, keepdims=True)
    inverse = lax.rsqrt(square - mean * mean + epsilon)
    return (values - mean) * inverse, inverse


def norm_back(grad, normed, inverse):
    total = jnp.mean(grad, axis=1, keepdims=True)
    cross = jnp.mean(grad * normed, axis=1, keepdims=True)
    return inverse * (grad - total - normed * cross)


def place():
    feat = lax.axis_index("feat")
    return feat // cores, feat % cores


def pair(mine, other, core):
    return jnp.where(core == 0, jnp.concatenate([mine, other], 1), jnp.concatenate([other, mine], 1))


def lanes(group, width):
    return pl.ds(pl.multiple_of(group * width, width), width)


def put_groups(full_ref, parts):
    group, _ = place()
    width = parts[0].shape[1]
    for step, part in enumerate(parts):
        full_ref[:, lanes(group ^ step, width)] = part[...]


def stage(kernel, outs, operands, scalars=0, in_hbm=0, scratch=(), flops=1 << 24):
    specs = [pl.BlockSpec(memory_space=pltpu.HBM)] * in_hbm
    specs += [pl.BlockSpec(memory_space=pltpu.VMEM)] * (len(operands) - scalars - in_hbm)
    specs += [pl.BlockSpec(memory_space=pltpu.SMEM)] * scalars
    moved = sum(o.size * o.dtype.itemsize for o in operands)
    return pl.pallas_call(
        kernel,
        out_shape=[jax.ShapeDtypeStruct(shape, kind) for shape, kind in outs],
        in_specs=specs,
        out_specs=[pl.BlockSpec(memory_space=pltpu.VMEM)] * len(outs),
        scratch_shapes=scratch,
        cost_estimate=pl.CostEstimate(flops=flops, bytes_accessed=moved, transcendentals=0),
        compiler_params=pltpu.CompilerParams(vmem_limit_bytes=kernel_vmem),
    )(*operands)


def gains(gain_e, gain_n, rows):
    shape = (rows, gain_e.shape[1])
    row = lax.broadcasted_iota(jnp.int32, shape, 0)
    e = jnp.broadcast_to(gain_e[...].astype(f32), shape)
    n = jnp.broadcast_to(gain_n[...].astype(f32), shape)
    return jnp.where(row == 0, e, n).astype(bf16)


def total(refs):
    value = refs[0][...]
    for ref in refs[1:]:
        value = value + ref[...].astype(f32)
    return value


def merge_inputs(state, edge_cot, node_cot, state2, gain_e, gain_n, pack, extra, extra_sent, held, cots, node, sems):
    _, core = place()
    half = pack.shape[0]
    nodes = node.shape[0]
    mine = pl.ds(pl.multiple_of(core * half, half), half)
    theirs = pl.ds(pl.multiple_of((1 - core) * half, half), half)
    copies = [
        pltpu.make_async_copy(state.at[mine], held, sems.at[0]),
        pltpu.make_async_copy(edge_cot, cots, sems.at[1]),
        pltpu.make_async_copy(node_cot, node, sems.at[2]),
    ]
    for copy in copies:
        copy.start()
    for copy in copies:
        copy.wait()
    pack[...] = pair(held[...], state2[mine], core)
    for rows, ref in ((mine, extra), (theirs, extra_sent)):
        ref[:half] = cots[rows]
        ref[half : half + nodes] = node[...]
        ref[half + nodes :] = gains(gain_e, gain_n, nodes)


def prepare_edges(groups, *refs):
    packs = refs[:groups]
    mine, other, extra_mine, extra2, slot, receiver, send_rows, state, pre, pick, take, extra = refs[groups:]
    _, core = place()
    block = lax.axis_index("nodes")
    features = state.shape[1]
    nodes, half = take.shape
    blocks, _, slots = send_rows.shape
    put_groups(state, packs)
    extra[...] = pair(extra_mine[...], extra2[...], core)

    slot_row = slot[pl.ds(core, 1)]
    sender = block * nodes + slot_row
    for source in range(blocks):
        for k in range(slots):
            row = source * nodes + send_rows[source, block, k]
            sender = jnp.where(slot_row == nodes + source * slots + k, row, sender)
    pick[...] = (lax.broadcasted_iota(jnp.int32, pick.shape, 0) == sender).astype(f32).astype(bf16)
    here = receiver[pl.ds(core, 1)]
    take[...] = (lax.broadcasted_iota(jnp.int32, take.shape, 0) == here).astype(f32).astype(bf16)
    weight = jnp.concatenate([mine[:, :features], other[:, :features]], axis=0)
    pre[...] = dot_rows(state[...], weight)


def finish_edges(came, pre, pick, take, mine, other, out_mine, out_other, n_mine, n_other, edge_pre, part, sent, own, lat, table):
    block = lax.axis_index("nodes")
    count, nodes, width = came.shape
    rows, features = table.shape
    half, hidden = pre.shape
    feats = features // width
    for source in range(count):
        first, column = source // feats * nodes, source % feats * width
        table[first : first + nodes, column : column + width] = came[source]
    latent = table[pl.ds(pl.multiple_of(block * nodes, nodes), nodes)]
    own[...] = latent

    def weight(index):
        columns = slice(index * features, (index + 1) * features)
        return jnp.concatenate([mine[:, columns], other[:, columns]], axis=0)

    high, low = split(dot_rows(table[...], weight(1)))
    here_high, here_low = split(dot_rows(latent, weight(2)))
    chosen = jnp.concatenate([pick[...], pick[...], take[...], take[...]], axis=0)
    value = pre[...] + dot_cols(chosen, jnp.concatenate([high, low, here_high, here_low], axis=0))
    edge_pre[...] = value
    act = (value * sigmoid(value)).astype(bf16)
    out = dot(act, jnp.concatenate([out_mine[...], out_other[...]], axis=0))
    part[...] = out
    sent[:half] = out.astype(bf16)
    nodes_pre = dot_rows(latent, jnp.concatenate([n_mine[:, :features], n_other[:, :features]], axis=0))
    lat[...] = nodes_pre
    high, low = split(nodes_pre)
    sent[half:] = jnp.zeros((nodes, features), bf16)
    sent[half:, :hidden] = high
    sent[half:, hidden : 2 * hidden] = low


def update_edges(groups, *refs):
    part, lat, came, extras = refs[0], refs[1], refs[2 : groups + 1], refs[groups + 1 : 2 * groups + 1]
    state, take, normed, inverse, kept, lent, aggregate, extra, lat_all, next_all = refs[2 * groups + 1 :]
    group, core = place()
    put_groups(extra, extras)
    nodes, half = take.shape
    width = kept.shape[1]
    hidden = lat.shape[1]
    value = part[...]
    lat_all[:, :hidden] = lat[...]
    for step, ref in enumerate(came, 1):
        value = value + ref[:half].astype(f32)
        high, low = ref[half:, :hidden], ref[half:, hidden : 2 * hidden]
        lat_all[:, step * hidden : (step + 1) * hidden] = high.astype(f32) + low.astype(f32)
    normed_rows, inverse_rows = normalize(value)
    normed[...] = normed_rows
    inverse[...] = inverse_rows
    gain = extra[half + nodes :].astype(f32)[0:1]
    rows = (state[...].astype(f32) + normed_rows * gain).astype(bf16)
    aggregate[...] = dot(take[...], rows)
    next_all[...] = rows
    mine = next_all[:, lanes(group, width * cores)]
    kept[...] = jnp.where(core == 0, mine[:, :width], mine[:, width:])
    lent[...] = jnp.where(core == 0, mine[:, width:], mine[:, :width])


def turn(groups, *refs):
    far, refs = refs[: 2 * (groups - 1)], refs[2 * (groups - 1) :]
    aggregate, aggregate2, own, lat_all, extra, take, pick, normed, inverse, edge_pre = refs[:10]
    e_mine, e_other, out_mine, out_other, in_mine, in_other, n_mine, n_other = refs[10:18]
    node_next, kept, *sents, spread, next_all, grads = refs[18:]
    group, core = place()
    block = lax.axis_index("nodes")
    nodes, half = take.shape
    features = extra.shape[1]
    hidden = edge_pre.shape[1]
    wide = kept.shape[1]
    width = node_next.shape[1]
    gain_rows = extra[half + nodes :].astype(f32)
    edge_gain, node_gain = gain_rows[0:1], gain_rows[1:2]

    from_agg = jnp.concatenate(
        [in_mine[:, features:], in_other[:, features:]] + [f[:, :features] for f in far], axis=0
    )
    to_out = jnp.concatenate([n_mine[...], n_other[...]] + [f[:, features:] for f in far], axis=0)
    together = (aggregate[...] + aggregate2[...]).astype(bf16)
    pre = lat_all[...] + dot_rows(together, from_agg)
    act = (pre * sigmoid(pre)).astype(bf16)
    node_normed, node_inverse = normalize(dot(act, to_out))
    next_all[...] = (own[...].astype(f32) + node_normed * node_gain).astype(bf16)
    mine = next_all[:, lanes(group, wide)]
    node_next[...] = jnp.where(core == 0, mine[:, :width], mine[:, width:])
    cot = extra[half : half + nodes].astype(f32)
    node_dy = norm_back(cot * node_gain, node_normed, node_inverse).astype(bf16)
    node_dpre = (dot_rows(node_dy, to_out) * swish_slope(pre)).astype(bf16)
    high, low = split(dot(node_dpre, from_agg))

    taken = take[...]
    edge_total = extra[:half].astype(f32) + dot_cols(
        jnp.concatenate([taken, taken], axis=0), jnp.concatenate([high, low], axis=0)
    )
    dy = norm_back(edge_total * edge_gain, normed[...], inverse[...]).astype(bf16)
    back = dot_rows(dy, jnp.concatenate([out_mine[...], out_other[...]], axis=0))
    dpre = (back * swish_slope(edge_pre[...])).astype(bf16)

    def weight(index):
        columns = slice(index * features, (index + 1) * features)
        return jnp.concatenate([e_mine[:, columns], e_other[:, columns]], axis=0)

    def weighted(values, index):
        both = dot(jnp.concatenate(split(values), axis=0), weight(index))
        return both[: values.shape[0]] + both[values.shape[0] :]

    rows = spread.shape[0] * nodes // (features // width)
    grads[:half] = dot(dpre, weight(0))
    for step, sent in enumerate(sents, 1):
        sent[...] = grads[:half, lanes(group ^ step, wide)].astype(bf16)
    grads[:half] += edge_total
    kept[...] = grads[:half, lanes(group, wide)]
    grads[half : half + rows] = weighted(dot(pick[...], dpre), 1)
    home = weighted(dot(taken, dpre), 2)
    node_weight = jnp.concatenate([in_mine[:, :features], in_other[:, :features]], axis=0)
    home = home + 0.5 * dot(node_dpre[:, :hidden], node_weight)
    grads[pl.ds(pl.multiple_of(half + block * nodes, nodes), nodes)] += home
    feats = features // width
    for target in range(spread.shape[0]):
        first, column = half + target // feats * nodes, target % feats * width
        spread[target] = grads[first : first + nodes, column : column + width].astype(bf16)


def add_groups(groups, *refs):
    parts, (kept, sent) = refs[:groups], refs[groups:]
    _, core = place()
    width = kept.shape[1]
    value = total(parts)
    kept[...] = jnp.where(core == 0, value[:, :width], value[:, width:]).astype(bf16)
    sent[...] = jnp.where(core == 0, value[:, width:], value[:, :width]).astype(bf16)


def assemble(next_mine, next_came, grad_mine, grad_came, edge_next, edge_grad):
    _, core = place()
    half = next_mine.shape[0]
    mine = pl.ds(pl.multiple_of(core * half, half), half)
    theirs = pl.ds(pl.multiple_of((1 - core) * half, half), half)
    edge_next[mine] = next_mine[...]
    edge_next[theirs] = next_came[...]
    edge_grad[mine] = grad_mine[...]
    edge_grad[theirs] = grad_came[...]


def shards(
    latent,
    edge_state,
    send_rows,
    sender_slot,
    receiver_row,
    edge_in_weight,
    edge_out_weight,
    edge_gain,
    node_in_weight,
    node_out_weight,
    node_gain,
    edge_cot,
    node_cot,
):
    nodes, width = latent.shape
    edge_dev = edge_state.shape[0]
    half = edge_dev // cores
    blocks = send_rows.shape[0]
    feats = lax.axis_size("feat")
    groups = feats // cores
    features = width * feats
    wide = width * cores
    hidden = edge_in_weight.shape[0] * cores
    table = blocks * nodes
    everyone = ("nodes", "feat")

    def swapped(values, bits):
        return lax.ppermute(values, "feat", [(i, i ^ bits) for i in range(feats)])

    def over_cores(values):
        return swapped(values, 1)

    def over_groups(values):
        return [swapped(values, cores * step) for step in range(1, groups)]

    gain_e, gain_n = edge_gain.reshape(1, width), node_gain.reshape(1, width)
    slot_rows = sender_slot.reshape(cores, half)
    receiver_rows = receiver_row.reshape(cores, half)

    state2 = over_cores(edge_state)
    latents = lax.all_to_all(
        jnp.broadcast_to(latent[None], (blocks * feats, nodes, width)), everyone, 0, 0
    )
    e_in = (edge_in_weight, over_cores(edge_in_weight))
    e_out = (edge_out_weight, over_cores(edge_out_weight))
    n_in = (node_in_weight, over_cores(node_in_weight))
    n_out = (node_out_weight, over_cores(node_out_weight))
    pack, extra_mine, extra_sent = stage(
        merge_inputs,
        [((half, wide), bf16), ((half + 2 * nodes, width), bf16), ((half + 2 * nodes, width), bf16)],
        [edge_state, edge_cot, node_cot, state2, gain_e, gain_n],
        in_hbm=3,
        scratch=[
            pltpu.VMEM((half, width), bf16),
            pltpu.VMEM((edge_dev, width), bf16),
            pltpu.VMEM((nodes, width), bf16),
            pltpu.SemaphoreType.DMA((3,)),
        ],
    )
    packs = [pack] + over_groups(pack)
    far = []
    for came in over_groups(jnp.concatenate([node_in_weight[:, features:], node_out_weight], axis=1)):
        far += [came, over_cores(came)]
    extra2 = over_cores(extra_sent)
    state, pre, pick, take, extra = stage(
        functools.partial(prepare_edges, groups),
        [
            ((half, features), bf16),
            ((half, hidden), f32),
            ((table, half), bf16),
            ((nodes, half), bf16),
            ((half + 2 * nodes, wide), bf16),
        ],
        [*packs, *e_in, extra_mine, extra2, slot_rows, receiver_rows, send_rows],
        scalars=1,
    )
    extras = [extra] + over_groups(extra)
    edge_pre, part, sent, own, lat, _ = stage(
        finish_edges,
        [
            ((half, hidden), f32),
            ((half, features), f32),
            ((half + nodes, features), bf16),
            ((nodes, features), bf16),
            ((nodes, hidden), f32),
            ((table, features), bf16),
        ],
        [latents, pre, pick, take, *e_in, *e_out, *n_in],
    )
    normed, inverse, next_mine, next_sent, aggregate, extra_full, lat_all, _ = stage(
        functools.partial(update_edges, groups),
        [
            ((half, features), f32),
            ((half, 1), f32),
            ((half, width), bf16),
            ((half, width), bf16),
            ((nodes, features), f32),
            ((half + 2 * nodes, features), bf16),
            ((nodes, features), f32),
            ((half, features), bf16),
        ],
        [part, lat, *over_groups(sent), *extras, state, take],
    )
    aggregate2 = over_cores(aggregate)
    next_came = over_cores(next_sent)
    node_next, kept, *sents, spread, _, _ = stage(
        functools.partial(turn, groups),
        [((nodes, width), bf16), ((half, wide), f32)]
        + [((half, wide), bf16)] * (groups - 1)
        + [
            ((blocks * feats, nodes, width), bf16),
            ((nodes, features), bf16),
            ((half + table, features), f32),
        ],
        [*far, aggregate, aggregate2, own, lat_all, extra_full, take, pick, normed, inverse, edge_pre]
        + [*e_in, *e_out, *n_in, *n_out],
    )
    shares = lax.all_to_all(spread, everyone, 0, 0)
    grad_mine, grad_sent = stage(
        functools.partial(add_groups, groups),
        [((half, width), bf16), ((half, width), bf16)],
        [kept] + [swapped(s, cores * k) for k, s in enumerate(sents, 1)],
    )
    edge_next, edge_grad = stage(
        assemble,
        [((edge_dev, width), bf16), ((edge_dev, width), bf16)],
        [next_mine, next_came, grad_mine, over_cores(grad_sent)],
    )
    node_grad = (node_cot.astype(f32) + jnp.sum(shares.astype(f32), axis=0)).astype(bf16)
    return (edge_next, node_next, edge_grad, node_grad)


def solution(mesh):
    rows = P(("groups", "nodes"), "feat")
    flat = P(("groups", "nodes"))
    matrix = P("feat", None)
    vector = P("feat")
    return jax.shard_map(
        shards,
        mesh=mesh,
        in_specs=(
            rows,
            rows,
            P("groups", None, None),
            flat,
            flat,
            matrix,
            matrix,
            vector,
            matrix,
            matrix,
            vector,
            rows,
            rows,
        ),
        out_specs=(rows, rows, rows, rows),
        check_vma=False,
    )
```

time: 92 us -> 45.4 us (0.49)
  blocking collectives: 48.6 us -> 0 us
  starting transfers between devices: 13.5 us -> 20.9 us
  Pallas kernels: 0 us -> 6.14 us
  matrix products: 5.37 us -> 0 us
  local copies, waits for them, and re-layouts: 5.58 us -> 2.42 us
  other arithmetic: 3.47 us -> 0.64 us
    all_gather x6 -> x0, blocking collectives: 48.6 us -> none  [the longest x4 22.4 us: gather(): return lax.all_gather(values, 'feat', axis=0)]
    ppermute x6 -> x15, waiting for transfers between devices: 3.37 us -> 14.1 us  [swapped(): return lax.ppermute(values, 'feat', [(i, i ^ bits) for i in range(feats)])]
    all_to_all x2, waiting for transfers between devices: 10.6 us -> 0.05 us  [the longest x1 0.05 us: shards(): shares = lax.all_to_all(spread, everyone, 0, 0)]
    pallas_call x0 -> x7, Pallas kernels: none -> 6.14 us  [stage(): pl.pallas_call(kernel, out_shape=[jax.ShapeDtypeStruct(shape, kind) for s...]
    dot_general x19 -> x0, matrix products: 5.37 us -> none  [the longest x13 3.83 us: dot(): return jnp.dot(left, right, preferred_element_type=f32)]
    ppermute x6 -> x15, starting transfers between devices: 6.55 us -> 10.6 us  [swapped(): return lax.ppermute(values, 'feat', [(i, i ^ bits) for i in range(feats)])]
    all_to_all x2, starting transfers between devices: 6.91 us -> 10.3 us  [the longest x1 5.28 us: shards(): shares = lax.all_to_all(spread, everyone, 0, 0)]
    convert_element_type x5 -> x1, other arithmetic: 2.11 us -> 0.6 us  [shards(): (node_cot.astype(f32) + jnp.sum(shares.astype(f32), axis=0)).astype(bf16)]
  transfers between devices with their start and end apart: 8 -> 17, of which waited for: 3 -> 6; matrix products, arithmetic and copies ran while one was open for 8% -> 3% of each run, Pallas kernels for 0% -> 8%
where the time goes in v5:
time: 45.4 us; the launch traced here: 45 us
  starting transfers between devices  20.9 us (46%)
  waiting for transfers between devices  14.1 us (31%)
  Pallas kernels  6.14 us (14%)
  local copies, waits for them, and re-layouts  2.42 us (5%)
  between operations  0.87 us (2%)
  other arithmetic  0.64 us (1%)
    ppermute x15, waiting for transfers between devices, swapped(): return lax.ppermute(values, 'feat', [(i, i ^ bits) for i in range(feats)])  14.1 us
    ppermute x15, starting transfers between devices, swapped(): return lax.ppermute(values, 'feat', [(i, i ^ bits) for i in range(feats)])  10.6 us
    pallas_call x7, Pallas kernels, stage(): pl.pallas_call(kernel, out_shape=[jax.ShapeDtypeStruct(shape, kind) for s...  6.14 us
    all_to_all x1, starting transfers between devices, shards(): shares = lax.all_to_all(spread, everyone, 0, 0)  5.28 us
    all_to_all x1, starting transfers between devices, shards(): lax.all_to_all(jnp.broadcast_to(latent[None], (blocks * feats, nodes, wid...  5.03 us
    broadcast_in_dim x1, local copies, waits for them, and re-layouts, shards(): jnp.broadcast_to(latent[None], (blocks * feats, nodes, width))  1.32 us
  transfers between devices with their start and end apart: 17, of which 6 were waited for; matrix products, arithmetic and copies ran while one was open for 3% of the time, Pallas kernels for 8%

profile of v5, /device:TPU:0, one launch (start us, length us, event | category | flops | bytes accessed | tf_op | source)
XLA Modules:
  0.0 45.0 jit_solution(18284967218278527657)
XLA Ops:
  0.7 0.5 %collective-permute-start.2 = (bf16[128,1536]{1,0:T(8,128)(2,1)}, bf16[128,1536]{1,0:T(8,128)(2,1)S(1)}, u32[]{:S(2)}, u32[]{:S(2)}) collective-permute-start(bf16[128,1536]{1,0:T(8,128)(2,1)} %refs_12_.1), channel_id=1, source_target_pairs={{0,1},{1,0},{2,3},{3,2},{4,5},{5,4},{6,7},{7,6},{8,9},{9,8},{10,11... | collective-permute-start | bytes 1179656 | tf_op jit(solution)/shard_map/ppermute | solution.py:324
  1.6 3.0 %collective-permute-start.9 = (bf16[128,1024]{1,0:T(8,128)(2,1)S(1)}, bf16[128,1024]{1,0:T(8,128)(2,1)S(1)}, u32[]{:S(2)}, u32[]{:S(2)}) collective-permute-start(bf16[128,1024]{1,0:T(8,128)(2,1)S(1)} %pad_maximum_fusion), channel_id=1, source_target_pairs={{0,2},{1,3},{2,0},{3,1},{4,6},{5,7},{6,4},{7,5},{8,10},{9,11},{10,... | collective-permute-start | bytes 786440 | tf_op jit(solution)/shard_map/ppermute | solution.py:324
  4.6 0.5 %collective-permute-start = (bf16[256,128]{1,0:T(8,128)(2,1)S(1)}, bf16[256,128]{1,0:T(8,128)(2,1)S(1)}, u32[]{:S(2)}, u32[]{:S(2)}) collective-permute-start(bf16[256,128]{1,0:T(8,128)(2,1)S(1)} %copy-done.4), channel_id=1, source_target_pairs={{0,1},{1,0},{2,3},{3,2},{4,5},{5,4},{6,7},{7,6},{8,9},{9,8},{10,11... | collective-permute-start | bytes 196616 | tf_op jit(solution)/shard_map/ppermute | solution.py:324
  5.2 1.3 %broadcast_in_dim.2 = bf16[16,16,128]{2,1,0:T(8,128)(2,1)} broadcast(bf16[16,128]{1,0:T(8,128)(2,1)} %param.13), dimensions={1,2} | broadcast | bytes 69632 | tf_op jit(solution)/shard_map/broadcast_in_dim | solution.py:338
  6.6 5.0 %all-to-all-start = ((bf16[16,16,128]{2,1,0:T(8,128)(2,1)}), bf16[16,16,128]{2,1,0:T(8,128)(2,1)S(1)}, u32[]{:S(2)}, u32[]{:S(2)}) async-start(bf16[16,16,128]{2,1,0:T(8,128)(2,1)} %broadcast_in_dim.2), calls=%async_computation | async-start | bytes 131072 | tf_op jit(solution)/shard_map/all_to_all | solution.py:337
  11.9 0.5 %collective-permute-start.3 = (bf16[160,128]{1,0:T(8,128)(2,1)S(1)}, bf16[160,128]{1,0:T(8,128)(2,1)S(1)}, u32[]{:S(2)}, u32[]{:S(2)}) collective-permute-start(bf16[160,128]{1,0:T(8,128)(2,1)S(1)} %get-tuple-element.34), channel_id=1, source_target_pairs={{0,1},{1,0},{2,3},{3,2},{4,5},{5,4},{6,7},{7,6},{8,9},{9,8},{10,11... | collective-permute-start | bytes 122888 | tf_op jit(solution)/shard_map/ppermute | solution.py:324
  12.4 0.8 %collective-permute-done.3.refs_5_ = bf16[160,128]{1,0:T(8,128)(2,1)S(1)} collective-permute-done((bf16[160,128]{1,0:T(8,128)(2,1)S(1)}, bf16[160,128]{1,0:T(8,128)(2,1)S(1)}, u32[]{:S(2)}, u32[]{:S(2)}) %collective-permute-start.3) | collective-permute-done | bytes 40992 | tf_op jit(solution)/shard_map/ppermute | solution.py:324
  13.2 1.9 %collective-permute-start.1 = (bf16[128,256]{1,0:T(8,128)(2,1)S(1)}, bf16[128,256]{1,0:T(8,128)(2,1)S(1)}, u32[]{:S(2)}, u32[]{:S(2)}) collective-permute-start(bf16[128,256]{1,0:T(8,128)(2,1)S(1)} %get-tuple-element.32.refs_0_), channel_id=1, source_target_pairs={{0,2},{1,3},{2,0},{3,1},{4,6},{5,7},{6,4},{7,5},{8,10},{9,11},{10,... | collective-permute-start | bytes 196616 | tf_op jit(solution)/shard_map/ppermute | solution.py:324
  15.1 2.8 %collective-permute-done.1.refs_1_ = bf16[128,256]{1,0:T(8,128)(2,1)S(1)} collective-permute-done((bf16[128,256]{1,0:T(8,128)(2,1)S(1)}, bf16[128,256]{1,0:T(8,128)(2,1)S(1)}, u32[]{:S(2)}, u32[]{:S(2)}) %collective-permute-start.1) | collective-permute-done | bytes 65568 | tf_op jit(solution)/shard_map/ppermute | solution.py:324
  17.9 0.7 %copy-done.8 = s32[256]{0:T(256)S(1)} copy-done((s32[256]{0:T(256)S(1)}, s32[256]{0:T(256)}, u32[]{:S(2)}) %copy-start.8) | copy-done | bytes 1048
  18.5 0.9 %shard_map.157 = (bf16[128,512]{1,0:T(8,128)(2,1)S(1)}, f32[128,256]{1,0:T(8,128)S(1)}, bf16[64,128]{1,0:T(8,128)(2,1)S(1)}, bf16[16,128]{1,0:T(8,128)(2,1)S(1)}, bf16[160,256]{1,0:T(8,128)(2,1)S(1)}) custom-call(bf16[128,256]{1,0:T(8,128)(2,1)S(1)} %get-tuple-element.32.refs_0_, bf16[128,256]{1,0:T(8,128)(2,1)S(1)} %collective-permute-done.1.refs_1_, ...), custom_call_target="tpu_custom_call" | custom-call | flops 16777216 | bytes 1001984 | tf_op jit(solution)/shard_map/pallas_call | solution.py:81
  19.5 0.9 %shard_map.158 = (f32[128,256]{1,0:T(8,128)S(1)}, f32[128,512]{1,0:T(8,128)S(1)}, bf16[144,512]{1,0:T(8,128)(2,1)S(1)}, bf16[16,512]{1,0:T(8,128)(2,1)S(1)}, f32...) custom-call(bf16[16,16,128]{2,1,0:T(8,128)(2,1)S(1)} %all-to-all-done.came, f32[128,256]{1,0:T(8,128)S(1)} %get-tuple-element.35.pre, ...), custom_call_target="tpu_custom_call" | custom-call | flops 16777216 | bytes 1789952 | tf_op jit(solution)/shard_map/pallas_call | solution.py:81
  20.4 1.6 %collective-permute-start.6 = (bf16[144,512]{1,0:T(8,128)(2,1)S(1)}, bf16[144,512]{1,0:T(8,128)(2,1)S(1)}, u32[]{:S(2)}, u32[]{:S(2)}) collective-permute-start(bf16[144,512]{1,0:T(8,128)(2,1)S(1)} %get-tuple-element.40), channel_id=1, source_target_pairs={{0,2},{1,3},{2,0},{3,1},{4,6},{5,7},{6,4},{7,5},{8,10},{9,11},{10,... | collective-permute-start | bytes 442376 | tf_op jit(solution)/shard_map/ppermute | solution.py:324
  22.0 0.4 collective-permute-start.7
  22.4 5.2 %collective-permute-done.7.refs_4_ = bf16[160,256]{1,0:T(8,128)(2,1)S(1)} collective-permute-done((bf16[160,256]{1,0:T(8,128)(2,1)S(1)}, bf16[160,256]{1,0:T(8,128)(2,1)S(1)}, u32[]{:S(2)}, u32[]{:S(2)}) %collective-permute-start.7) | collective-permute-done | bytes 81952 | tf_op jit(solution)/shard_map/ppermute | solution.py:324
  27.6 0.8 %shard_map.159 = (f32[128,512]{1,0:T(8,128)S(1)}, f32[128,1]{1,0:T(8,128)S(1)}, bf16[128,128]{1,0:T(8,128)(2,1)S(1)}, bf16[128,128]{1,0:T(8,128)(2,1)S(1)}, f32[...) custom-call(f32[128,512]{1,0:T(8,128)S(1)} %get-tuple-element.38.refs_0_, ...), custom_call_target="tpu_custom_call" | custom-call | flops 16777216 | bytes 724992 | tf_op jit(solution)/shard_map/pallas_call | solution.py:81
  28.4 1.2 %collective-permute-done.11.refs_3_ = f32[16,512]{1,0:T(8,128)S(1)} collective-permute-done((f32[16,512]{1,0:T(8,128)S(1)}, f32[16,512]{1,0:T(8,128)S(1)}, u32[]{:S(2)}, u32[]{:S(2)}) %collective-permute-start.11) | collective-permute-done | bytes 32800 | tf_op jit(solution)/shard_map/ppermute | solution.py:324
  29.6 2.7 %shard_map.160 = (bf16[16,128]{1,0:T(8,128)(2,1)}, f32[128,256]{1,0:T(8,128)S(1)}, bf16[128,256]{1,0:T(8,128)(2,1)S(1)}, bf16[16,16,128]{2,1,0:T(8,128)(2,1)}, b...) custom-call(bf16[128,1024]{1,0:T(8,128)(2,1)S(1)} %collective-permute-done.9.refs_0_, ...), custom_call_target="tpu_custom_call" | custom-call | flops 16777216 | bytes 3052032 | tf_op jit(solution)/shard_map/pallas_call | solution.py:81
  32.2 5.3 %all-to-all-start.1 = ((bf16[16,16,128]{2,1,0:T(8,128)(2,1)}), bf16[16,16,128]{2,1,0:T(8,128)(2,1)S(1)}, u32[]{:S(2)}, u32[]{:S(2)}) async-start(bf16[16,16,128]{2,1,0:T(8,128)(2,1)} %get-tuple-element.59), calls=%async_computation.1 | async-start | bytes 131072 | tf_op jit(solution)/shard_map/all_to_all | solution.py:414
  37.5 1.9 %collective-permute-start.13 = (bf16[128,256]{1,0:T(8,128)(2,1)S(1)}, bf16[128,256]{1,0:T(8,128)(2,1)S(1)}, u32[]{:S(2)}, u32[]{:S(2)}) collective-permute-start(bf16[128,256]{1,0:T(8,128)(2,1)S(1)} %get-tuple-element.53), channel_id=1, source_target_pairs={{0,2},{1,3},{2,0},{3,1},{4,6},{5,7},{6,4},{7,5},{8,10},{9,11},{10,... | collective-permute-start | bytes 196616 | tf_op jit(solution)/shard_map/ppermute | solution.py:324
  39.5 3.0 %collective-permute-done.13.refs_1_ = bf16[128,256]{1,0:T(8,128)(2,1)S(1)} collective-permute-done((bf16[128,256]{1,0:T(8,128)(2,1)S(1)}, bf16[128,256]{1,0:T(8,128)(2,1)S(1)}, u32[]{:S(2)}, u32[]{:S(2)}) %collective-permute-start.13) | collective-permute-done | bytes 65568 | tf_op jit(solution)/shard_map/ppermute | solution.py:324
  42.5 1.2 %collective-permute-done.14.grad_came = bf16[128,128]{1,0:T(8,128)(2,1)S(1)} collective-permute-done((bf16[128,128]{1,0:T(8,128)(2,1)S(1)}, bf16[128,128]{1,0:T(8,128)(2,1)S(1)}, u32[]{:S(2)}, u32[]{:S(2)}) %collective-permute-start.14) | collective-permute-done | bytes 32800 | tf_op jit(solution)/shard_map/ppermute | solution.py:324
  43.7 0.7 %shard_map.162 = (bf16[256,128]{1,0:T(8,128)(2,1)}, bf16[256,128]{1,0:T(8,128)(2,1)}) custom-call(bf16[128,128]{1,0:T(8,128)(2,1)S(1)} %get-tuple-element.43.next_mine, bf16[128,128]{1,0:T(8,128)(2,1)S(1)} %collective-permute-done.8.next_came, bf16[128,128]{1,0:T(8,128)(2,1)S(1)} %get-tuple-element.54.grad_mine, ...), custom_call_target="tpu_custom_call" | custom-call | flops 16777216 | bytes 131072 | tf_op jit(solution)/shard_map/pallas_call | solution.py:81
  44.4 0.6 %add_convert_fusion = bf16[16,128]{1,0:T(8,128)(2,1)} fusion(f32[16,128]{1,0:T(8,128)S(1)} %convert_reduce_fusion, bf16[16,128]{1,0:T(8,128)(2,1)S(1)} %copy-done.6), kind=kLoop, calls=%fused_computation.2 | loop fusion | flops 6144 | bytes 16384 | tf_op jit(solution)/shard_map/convert_element_type | solution.py:425
  (47 shorter events, 1.0 us)
Async XLA Ops:
  0.7 17.2 %collective-permute-start.2 = (bf16[128,1536]{1,0:T(8,128)(2,1)}, bf16[128,1536]{1,0:T(8,128)(2,1)S(1)}, u32[]{:S(2)}, u32[]{:S(2)}) collective-permute-start(bf16[128,1536]{1,0:T(8,128)(2,1)} %refs_12_.1), channel_id=1, source_target_pairs={{0,1},{1,0},{2,3},{3,2},{4,5},{5,4},{6,7},{7,6},{8,9},{9,8},{10,11... | collective-permute-start | bytes 1179656 | tf_op jit(solution)/shard_map/ppermute | solution.py:324
  1.2 10.4 %copy-start.5 = (bf16[256,128]{1,0:T(8,128)(2,1)S(1)}, bf16[256,128]{1,0:T(8,128)(2,1)}, u32[]{:S(2)}) copy-start(bf16[256,128]{1,0:T(8,128)(2,1)} %edge_cot.1) | copy-start | bytes 196612
  1.2 10.4 %copy-start.6 = (bf16[16,128]{1,0:T(8,128)(2,1)S(1)}, bf16[16,128]{1,0:T(8,128)(2,1)}, u32[]{:S(2)}) copy-start(bf16[16,128]{1,0:T(8,128)(2,1)} %node_cot.1) | copy-start | bytes 12292
  1.2 10.4 %copy-start.10 = (bf16[128]{0:T(256)(128)(2,1)S(1)}, bf16[128]{0:T(256)(128)(2,1)}, u32[]{:S(2)}) copy-start(bf16[128]{0:T(256)(128)(2,1)} %param.20) | copy-start | bytes 772
  1.2 10.4 %copy-start.11 = (bf16[128]{0:T(256)(128)(2,1)S(1)}, bf16[128]{0:T(256)(128)(2,1)}, u32[]{:S(2)}) copy-start(bf16[128]{0:T(256)(128)(2,1)} %param.23) | copy-start | bytes 772
  1.6 16.3 %copy-start = (bf16[128,1536]{1,0:T(8,128)(2,1)S(1)}, bf16[128,1536]{1,0:T(8,128)(2,1)}, u32[]{:S(2)}) copy-start(bf16[128,1536]{1,0:T(8,128)(2,1)} %refs_12_.1) | copy-start | bytes 1179652
  1.6 10.7 %collective-permute-start.9 = (bf16[128,1024]{1,0:T(8,128)(2,1)S(1)}, bf16[128,1024]{1,0:T(8,128)(2,1)S(1)}, u32[]{:S(2)}, u32[]{:S(2)}) collective-permute-start(bf16[128,1024]{1,0:T(8,128)(2,1)S(1)} %pad_maximum_fusion), channel_id=1, source_target_pairs={{0,2},{1,3},{2,0},{3,1},{4,6},{5,7},{6,4},{7,5},{8,10},{9,11},{10,... | collective-permute-start | bytes 786440 | tf_op jit(solution)/shard_map/ppermute | solution.py:324
  4.6 14.8 %collective-permute-start.5 = (bf16[128,1024]{1,0:T(8,128)(2,1)S(1)}, bf16[128,1024]{1,0:T(8,128)(2,1)S(1)}, u32[]{:S(2)}, u32[]{:S(2)}) collective-permute-start(bf16[128,1024]{1,0:T(8,128)(2,1)S(1)} %copy-done.1), channel_id=1, source_target_pairs={{0,1},{1,0},{2,3},{3,2},{4,5},{5,4},{6,7},{7,6},{8,9},{9,8},{10,11... | collective-permute-start | bytes 786440 | tf_op jit(solution)/shard_map/ppermute | solution.py:324
  4.6 6.9 %collective-permute-start = (bf16[256,128]{1,0:T(8,128)(2,1)S(1)}, bf16[256,128]{1,0:T(8,128)(2,1)S(1)}, u32[]{:S(2)}, u32[]{:S(2)}) collective-permute-start(bf16[256,128]{1,0:T(8,128)(2,1)S(1)} %copy-done.4), channel_id=1, source_target_pairs={{0,1},{1,0},{2,3},{3,2},{4,5},{5,4},{6,7},{7,6},{8,9},{9,8},{10,11... | collective-permute-start | bytes 196616 | tf_op jit(solution)/shard_map/ppermute | solution.py:324
  5.2 14.3 %collective-permute-start.4 = (bf16[128,512]{1,0:T(8,128)(2,1)S(1)}, bf16[128,512]{1,0:T(8,128)(2,1)S(1)}, u32[]{:S(2)}, u32[]{:S(2)}) collective-permute-start(bf16[128,512]{1,0:T(8,128)(2,1)S(1)} %copy-done.2), channel_id=1, source_target_pairs={{0,1},{1,0},{2,3},{3,2},{4,5},{5,4},{6,7},{7,6},{8,9},{9,8},{10,11... | collective-permute-start | bytes 393224 | tf_op jit(solution)/shard_map/ppermute | solution.py:324
  6.6 12.9 %all-to-all-start = ((bf16[16,16,128]{2,1,0:T(8,128)(2,1)}), bf16[16,16,128]{2,1,0:T(8,128)(2,1)S(1)}, u32[]{:S(2)}, u32[]{:S(2)}) async-start(bf16[16,16,128]{2,1,0:T(8,128)(2,1)} %broadcast_in_dim.2), calls=%async_computation | async-start | bytes 131072 | tf_op jit(solution)/shard_map/all_to_all | solution.py:337
  11.6 6.2 %copy-start.9 = (s32[256]{0:T(256)S(1)}, s32[256]{0:T(256)}, u32[]{:S(2)}) copy-start(s32[256]{0:T(256)} %param.17) | copy-start | bytes 3076
  11.8 6.0 %copy-start.7 = (s32[4,4,8]{2,1,0:T(4,128)S(1)}, s32[4,4,8]{2,1,0:T(4,128)}, u32[]{:S(2)}) copy-start(s32[4,4,8]{2,1,0:T(4,128)} %refs_8_.1) | copy-start | bytes 1540
  11.9 1.3 %collective-permute-start.3 = (bf16[160,128]{1,0:T(8,128)(2,1)S(1)}, bf16[160,128]{1,0:T(8,128)(2,1)S(1)}, u32[]{:S(2)}, u32[]{:S(2)}) collective-permute-start(bf16[160,128]{1,0:T(8,128)(2,1)S(1)} %get-tuple-element.34), channel_id=1, source_target_pairs={{0,1},{1,0},{2,3},{3,2},{4,5},{5,4},{6,7},{7,6},{8,9},{9,8},{10,11... | collective-permute-start | bytes 122888 | tf_op jit(solution)/shard_map/ppermute | solution.py:324
  12.3 16.0 %collective-permute-start.10 = (bf16[128,1024]{1,0:T(8,128)(2,1)S(1)}, bf16[128,1024]{1,0:T(8,128)(2,1)S(1)}, u32[]{:S(2)}, u32[]{:S(2)}) collective-permute-start(bf16[128,1024]{1,0:T(8,128)(2,1)S(1)} %collective-permute-done.9.refs_0_), channel_id=1, source_target_pairs={{0,1},{1,0},{2,3},{3,2},{4,5},{5,4},{6,7},{7,6},{8,9},{9,8},{10,11... | collective-permute-start | bytes 786440 | tf_op jit(solution)/shard_map/ppermute | solution.py:324
  13.2 4.7 %collective-permute-start.1 = (bf16[128,256]{1,0:T(8,128)(2,1)S(1)}, bf16[128,256]{1,0:T(8,128)(2,1)S(1)}, u32[]{:S(2)}, u32[]{:S(2)}) collective-permute-start(bf16[128,256]{1,0:T(8,128)(2,1)S(1)} %get-tuple-element.32.refs_0_), channel_id=1, source_target_pairs={{0,2},{1,3},{2,0},{3,1},{4,6},{5,7},{6,4},{7,5},{8,10},{9,11},{10,... | collective-permute-start | bytes 196616 | tf_op jit(solution)/shard_map/ppermute | solution.py:324
  20.4 7.2 %collective-permute-start.6 = (bf16[144,512]{1,0:T(8,128)(2,1)S(1)}, bf16[144,512]{1,0:T(8,128)(2,1)S(1)}, u32[]{:S(2)}, u32[]{:S(2)}) collective-permute-start(bf16[144,512]{1,0:T(8,128)(2,1)S(1)} %get-tuple-element.40), channel_id=1, source_target_pairs={{0,2},{1,3},{2,0},{3,1},{4,6},{5,7},{6,4},{7,5},{8,10},{9,11},{10,... | collective-permute-start | bytes 442376 | tf_op jit(solution)/shard_map/ppermute | solution.py:324
  22.0 6.4 %collective-permute-start.12 = (bf16[128,512]{1,0:T(8,128)(2,1)S(1)}, bf16[128,512]{1,0:T(8,128)(2,1)S(1)}, u32[]{:S(2)}, u32[]{:S(2)}) collective-permute-start(bf16[128,512]{1,0:T(8,128)(2,1)S(1)} %copy-done.3), channel_id=1, source_target_pairs={{0,1},{1,0},{2,3},{3,2},{4,5},{5,4},{6,7},{7,6},{8,9},{9,8},{10,11... | collective-permute-start | bytes 393224 | tf_op jit(solution)/shard_map/ppermute | solution.py:324
  22.0 5.6 %collective-permute-start.7 = (bf16[160,256]{1,0:T(8,128)(2,1)S(1)}, bf16[160,256]{1,0:T(8,128)(2,1)S(1)}, u32[]{:S(2)}, u32[]{:S(2)}) collective-permute-start(bf16[160,256]{1,0:T(8,128)(2,1)S(1)} %get-tuple-element.41.refs_3_), channel_id=1, source_target_pairs={{0,2},{1,3},{2,0},{3,1},{4,6},{5,7},{6,4},{7,5},{8,10},{9,11},{10,... | collective-permute-start | bytes 245768 | tf_op jit(solution)/shard_map/ppermute | solution.py:324
  28.4 1.2 %collective-permute-start.11 = (f32[16,512]{1,0:T(8,128)S(1)}, f32[16,512]{1,0:T(8,128)S(1)}, u32[]{:S(2)}, u32[]{:S(2)}) collective-permute-start(f32[16,512]{1,0:T(8,128)S(1)} %get-tuple-element.45.refs_2_), channel_id=1, source_target_pairs={{0,1},{1,0},{2,3},{3,2},{4,5},{5,4},{6,7},{7,6},{8,9},{9,8},{10,11... | collective-permute-start | bytes 98312 | tf_op jit(solution)/shard_map/ppermute | solution.py:324
  32.2 12.2 %all-to-all-start.1 = ((bf16[16,16,128]{2,1,0:T(8,128)(2,1)}), bf16[16,16,128]{2,1,0:T(8,128)(2,1)S(1)}, u32[]{:S(2)}, u32[]{:S(2)}) async-start(bf16[16,16,128]{2,1,0:T(8,128)(2,1)} %get-tuple-element.59), calls=%async_computation.1 | async-start | bytes 131072 | tf_op jit(solution)/shard_map/all_to_all | solution.py:414
  37.5 4.9 %collective-permute-start.13 = (bf16[128,256]{1,0:T(8,128)(2,1)S(1)}, bf16[128,256]{1,0:T(8,128)(2,1)S(1)}, u32[]{:S(2)}, u32[]{:S(2)}) collective-permute-start(bf16[128,256]{1,0:T(8,128)(2,1)S(1)} %get-tuple-element.53), channel_id=1, source_target_pairs={{0,2},{1,3},{2,0},{3,1},{4,6},{5,7},{6,4},{7,5},{8,10},{9,11},{10,... | collective-permute-start | bytes 196616 | tf_op jit(solution)/shard_map/ppermute | solution.py:324
  39.5 3.1 %collective-permute-start.8 = (bf16[128,128]{1,0:T(8,128)(2,1)S(1)}, bf16[128,128]{1,0:T(8,128)(2,1)S(1)}, u32[]{:S(2)}, u32[]{:S(2)}) collective-permute-start(bf16[128,128]{1,0:T(8,128)(2,1)S(1)} %get-tuple-element.44), channel_id=1, source_target_pairs={{0,1},{1,0},{2,3},{3,2},{4,5},{5,4},{6,7},{7,6},{8,9},{9,8},{10,11... | collective-permute-start | bytes 98312 | tf_op jit(solution)/shard_map/ppermute | solution.py:324
  42.4 1.3 %collective-permute-start.14 = (bf16[128,128]{1,0:T(8,128)(2,1)S(1)}, bf16[128,128]{1,0:T(8,128)(2,1)S(1)}, u32[]{:S(2)}, u32[]{:S(2)}) collective-permute-start(bf16[128,128]{1,0:T(8,128)(2,1)S(1)} %get-tuple-element.55), channel_id=1, source_target_pairs={{0,1},{1,0},{2,3},{3,2},{4,5},{5,4},{6,7},{7,6},{8,9},{9,8},{10,11... | collective-permute-start | bytes 98312 | tf_op jit(solution)/shard_map/ppermute | solution.py:324
  (6 other events, 13.5 us)

commit v6 on v5

--- a/solution.py
+++ b/solution.py
@@ -64,13 +64,6 @@
 
 def lanes(group, width):
     return pl.ds(pl.multiple_of(group * width, width), width)
-
-
-def put_groups(full_ref, parts):
-    group, _ = place()
-    width = parts[0].shape[1]
-    for step, part in enumerate(parts):
-        full_ref[:, lanes(group ^ step, width)] = part[...]
 
 
 def stage(kernel, outs, operands, scalars=0, in_hbm=0, scratch=(), flops=1 << 24):
@@ -104,38 +97,55 @@
     return value
 
 
-def merge_inputs(state, edge_cot, node_cot, state2, gain_e, gain_n, pack, extra, extra_sent, held, cots, node, sems):
-    _, core = place()
-    half = pack.shape[0]
-    nodes = node.shape[0]
-    mine = pl.ds(pl.multiple_of(core * half, half), half)
-    theirs = pl.ds(pl.multiple_of((1 - core) * half, half), half)
+def pack_inputs(state, edge_cot, node_cot, latent, gain_e, gain_n, pack, held, sems):
+    edge_dev = state.shape[0]
+    nodes = latent.shape[0]
     copies = [
-        pltpu.make_async_copy(state.at[mine], held, sems.at[0]),
-        pltpu.make_async_copy(edge_cot, cots, sems.at[1]),
-        pltpu.make_async_copy(node_cot, node, sems.at[2]),
+        pltpu.make_async_copy(state, pack.at[pl.ds(0, edge_dev)], sems.at[0]),
+        pltpu.make_async_copy(edge_cot, pack.at[pl.ds(edge_dev, edge_dev)], sems.at[1]),
+        pltpu.make_async_copy(node_cot, pack.at[pl.ds(2 * edge_dev, nodes)], sems.at[2]),
+        pltpu.make_async_copy(latent, held, sems.at[3]),
     ]
     for copy in copies:
         copy.start()
+    pack[2 * edge_dev + nodes :] = gains(gain_e, gain_n, nodes)
     for copy in copies:
         copy.wait()
-    pack[...] = pair(held[...], state2[mine], core)
-    for rows, ref in ((mine, extra), (theirs, extra_sent)):
-        ref[:half] = cots[rows]
-        ref[half : half + nodes] = node[...]
-        ref[half + nodes :] = gains(gain_e, gain_n, nodes)
+
+
+def spread_latent(latent, spread):
+    spread[...] = jnp.broadcast_to(latent[...][None], spread.shape)
+
+
+def half_rows(pack, core, half):
+    first = pl.multiple_of(core * half, half)
+    return [pack[pl.ds(first, half)], pack[pl.ds(cores * half + first, half)], pack[2 * cores * half :]]
+
+
+def send_half(groups, *refs):
+    packs, sent = refs[:groups], refs[groups]
+    _, core = place()
+    width = packs[0].shape[1]
+    half = packs[0].shape[0] - sent.shape[0] >> 1
+    for step, pack in enumerate(packs):
+        sent[:, step * width : (step + 1) * width] = jnp.concatenate(half_rows(pack, 1 - core, half), axis=0)
 
 
 def prepare_edges(groups, *refs):
     packs = refs[:groups]
-    mine, other, extra_mine, extra2, slot, receiver, send_rows, state, pre, pick, take, extra = refs[groups:]
-    _, core = place()
+    came, mine, other, slot, receiver, send_rows, state, pre, pick, take, extra = refs[groups:]
+    group, core = place()
     block = lax.axis_index("nodes")
     features = state.shape[1]
     nodes, half = take.shape
+    width = features // (groups * cores)
     blocks, _, slots = send_rows.shape
-    put_groups(state, packs)
-    extra[...] = pair(extra_mine[...], extra2[...], core)
+    for step, pack in enumerate(packs):
+        columns = lanes(group ^ step, width * cores)
+        theirs = came[:, step * width : (step + 1) * width]
+        ours = half_rows(pack, core, half)
+        state[:, columns] = pair(ours[0], theirs[:half], core)
+        extra[:, columns] = pair(jnp.concatenate(ours[1:], axis=0), theirs[half:], core)
 
     slot_row = slot[pl.ds(core, 1)]
     sender = block * nodes + slot_row
@@ -184,10 +194,9 @@
 
 
 def update_edges(groups, *refs):
-    part, lat, came, extras = refs[0], refs[1], refs[2 : groups + 1], refs[groups + 1 : 2 * groups + 1]
-    state, take, normed, inverse, kept, lent, aggregate, extra, lat_all, next_all = refs[2 * groups + 1 :]
+    part, lat, came = refs[0], refs[1], refs[2 : groups + 1]
+    extra, state, take, normed, inverse, kept, lent, aggregate, lat_all, next_all = refs[groups + 1 :]
     group, core = place()
-    put_groups(extra, extras)
     nodes, half = take.shape
     width = kept.shape[1]
     hidden = lat.shape[1]
@@ -211,11 +220,10 @@
 
 def turn(groups, *refs):
     far, refs = refs[: 2 * (groups - 1)], refs[2 * (groups - 1) :]
-    aggregate, aggregate2, own, lat_all, extra, take, pick, normed, inverse, edge_pre = refs[:10]
-    e_mine, e_other, out_mine, out_other, in_mine, in_other, n_mine, n_other = refs[10:18]
-    node_next, kept, *sents, spread, next_all, grads = refs[18:]
+    aggregate, aggregate2, own, lat_all, extra, take, normed, inverse, edge_pre = refs[:9]
+    e_mine, e_other, out_mine, out_other, in_mine, in_other, n_mine, n_other = refs[9:17]
+    node_next, kept, *sents, dpre_ref, node_dpre_ref, next_all, grads = refs[17:]
     group, core = place()
-    block = lax.axis_index("nodes")
     nodes, half = take.shape
     features = extra.shape[1]
     hidden = edge_pre.shape[1]
@@ -248,28 +256,34 @@
     back = dot_rows(dy, jnp.concatenate([out_mine[...], out_other[...]], axis=0))
     dpre = (back * swish_slope(edge_pre[...])).astype(bf16)
 
-    def weight(index):
+    dpre_ref[...] = dpre
+    node_dpre_ref[...] = node_dpre[:, :hidden]
+    grads[...] = dot(dpre, jnp.concatenate([e_mine[:, :features], e_other[:, :features]], axis=0))
+    for step, sent in enumerate(sents, 1):
+        sent[...] = grads[:, lanes(group ^ step, wide)].astype(bf16)
+    grads[...] += edge_total
+    kept[...] = grads[:, lanes(group, wide)]
+
+
+def spread_nodes(dpre, node_dpre, pick, take, e_mine, e_other, in_mine, in_other, spread, grads):
+    block = lax.axis_index("nodes")
+    count, nodes, width = spread.shape
+    features = grads.shape[1]
+    feats = features // width
+
+    def weighted(values, index):
         columns = slice(index * features, (index + 1) * features)
-        return jnp.concatenate([e_mine[:, columns], e_other[:, columns]], axis=0)
-
-    def weighted(values, index):
-        both = dot(jnp.concatenate(split(values), axis=0), weight(index))
+        weight = jnp.concatenate([e_mine[:, columns], e_other[:, columns]], axis=0)
+        both = dot(jnp.concatenate(split(values), axis=0), weight)
         return both[: values.shape[0]] + both[values.shape[0] :]
 
-    rows = spread.shape[0] * nodes // (features // width)
-    grads[:half] = dot(dpre, weight(0))
-    for step, sent in enumerate(sents, 1):
-        sent[...] = grads[:half, lanes(group ^ step, wide)].astype(bf16)
-    grads[:half] += edge_total
-    kept[...] = grads[:half, lanes(group, wide)]
-    grads[half : half + rows] = weighted(dot(pick[...], dpre), 1)
-    home = weighted(dot(taken, dpre), 2)
+    grads[...] = weighted(dot(pick[...], dpre[...]), 1)
+    home = weighted(dot(take[...], dpre[...]), 2)
     node_weight = jnp.concatenate([in_mine[:, :features], in_other[:, :features]], axis=0)
-    home = home + 0.5 * dot(node_dpre[:, :hidden], node_weight)
-    grads[pl.ds(pl.multiple_of(half + block * nodes, nodes), nodes)] += home
-    feats = features // width
-    for target in range(spread.shape[0]):
-        first, column = half + target // feats * nodes, target % feats * width
+    home = home + 0.5 * dot(node_dpre[...], node_weight)
+    grads[pl.ds(pl.multiple_of(block * nodes, nodes), nodes)] += home
+    for target in range(count):
+        first, column = target // feats * nodes, target % feats * width
         spread[target] = grads[first : first + nodes, column : column + width].astype(bf16)
 
 
@@ -333,31 +347,29 @@
     slot_rows = sender_slot.reshape(cores, half)
     receiver_rows = receiver_row.reshape(cores, half)
 
-    state2 = over_cores(edge_state)
-    latents = lax.all_to_all(
-        jnp.broadcast_to(latent[None], (blocks * feats, nodes, width)), everyone, 0, 0
-    )
+    rows = 2 * edge_dev + 2 * nodes
+    pack, held = stage(
+        pack_inputs,
+        [((rows, width), bf16), ((nodes, width), bf16)],
+        [edge_state, edge_cot, node_cot, latent, gain_e, gain_n],
+        in_hbm=4,
+        scratch=[pltpu.SemaphoreType.DMA((4,))],
+    )
+    packs = [pack] + over_groups(pack)
+    (spread,) = stage(spread_latent, [((blocks * feats, nodes, width), bf16)], [held])
+    latents = lax.all_to_all(spread, everyone, 0, 0)
     e_in = (edge_in_weight, over_cores(edge_in_weight))
     e_out = (edge_out_weight, over_cores(edge_out_weight))
+    (sent,) = stage(
+        functools.partial(send_half, groups), [((rows - 2 * half, groups * width), bf16)], packs
+    )
+    came = over_cores(sent)
+    sent, node_in_weight, node_out_weight = lax.optimization_barrier((sent, node_in_weight, node_out_weight))
     n_in = (node_in_weight, over_cores(node_in_weight))
     n_out = (node_out_weight, over_cores(node_out_weight))
-    pack, extra_mine, extra_sent = stage(
-        merge_inputs,
-        [((half, wide), bf16), ((half + 2 * nodes, width), bf16), ((half + 2 * nodes, width), bf16)],
-        [edge_state, edge_cot, node_cot, state2, gain_e, gain_n],
-        in_hbm=3,
-        scratch=[
-            pltpu.VMEM((half, width), bf16),
-            pltpu.VMEM((edge_dev, width), bf16),
-            pltpu.VMEM((nodes, width), bf16),
-            pltpu.SemaphoreType.DMA((3,)),
-        ],
-    )
-    packs = [pack] + over_groups(pack)
     far = []
-    for came in over_groups(jnp.concatenate([node_in_weight[:, features:], node_out_weight], axis=1)):
-        far += [came, over_cores(came)]
-    extra2 = over_cores(extra_sent)
+    for weights in over_groups(jnp.concatenate([node_in_weight[:, features:], node_out_weight], axis=1)):
+        far += [weights, over_cores(weights)]
     state, pre, pick, take, extra = stage(
         functools.partial(prepare_edges, groups),
         [
@@ -365,12 +377,11 @@
             ((half, hidden), f32),
             ((table, half), bf16),
             ((nodes, half), bf16),
-            ((half + 2 * nodes, wide), bf16),
+            ((half + 2 * nodes, features), bf16),
         ],
-        [*packs, *e_in, extra_mine, extra2, slot_rows, receiver_rows, send_rows],
+        [*packs, came, *e_in, slot_rows, receiver_rows, send_rows],
         scalars=1,
     )
-    extras = [extra] + over_groups(extra)
     edge_pre, part, sent, own, lat, _ = stage(
         finish_edges,
         [
@@ -383,7 +394,7 @@
         ],
         [latents, pre, pick, take, *e_in, *e_out, *n_in],
     )
-    normed, inverse, next_mine, next_sent, aggregate, extra_full, lat_all, _ = stage(
+    normed, inverse, next_mine, next_sent, aggregate, lat_all, _ = stage(
         functools.partial(update_edges, groups),
         [
             ((half, features), f32),
@@ -391,31 +402,37 @@
             ((half, width), bf16),
             ((half, width), bf16),
             ((nodes, features), f32),
-            ((half + 2 * nodes, features), bf16),
             ((nodes, features), f32),
             ((half, features), bf16),
         ],
-        [part, lat, *over_groups(sent), *extras, state, take],
+        [part, lat, *over_groups(sent), extra, state, take],
     )
     aggregate2 = over_cores(aggregate)
     next_came = over_cores(next_sent)
-    node_next, kept, *sents, spread, _, _ = stage(
+    node_next, kept, *sents, dpre, node_dpre, _, _ = stage(
         functools.partial(turn, groups),
         [((nodes, width), bf16), ((half, wide), f32)]
         + [((half, wide), bf16)] * (groups - 1)
         + [
-            ((blocks * feats, nodes, width), bf16),
+            ((half, hidden), bf16),
+            ((nodes, hidden), bf16),
             ((nodes, features), bf16),
-            ((half + table, features), f32),
+            ((half, features), f32),
         ],
-        [*far, aggregate, aggregate2, own, lat_all, extra_full, take, pick, normed, inverse, edge_pre]
+        [*far, aggregate, aggregate2, own, lat_all, extra, take, normed, inverse, edge_pre]
         + [*e_in, *e_out, *n_in, *n_out],
+    )
+    sents = [swapped(s, cores * k) for k, s in enumerate(sents, 1)]
+    spread, _ = stage(
+        spread_nodes,
+        [((blocks * feats, nodes, width), bf16), ((table, features), f32)],
+        [dpre, node_dpre, pick, take, *e_in, *n_in],
     )
     shares = lax.all_to_all(spread, everyone, 0, 0)
     grad_mine, grad_sent = stage(
         functools.partial(add_groups, groups),
         [((half, width), bf16), ((half, width), bf16)],
-        [kept] + [swapped(s, cores * k) for k, s in enumerate(sents, 1)],
+        [kept, *sents],
     )
     edge_next, edge_grad = stage(
         assemble,

time: 45.4 us -> 51.1 us (1.13)
  waiting for transfers between devices: 14.1 us -> 19.2 us
  starting transfers between devices: 20.9 us -> 16.5 us
  local copies, waits for them, and re-layouts: 2.42 us -> 5.83 us
  Pallas kernels: 6.14 us -> 7.59 us
    unnamed x24 -> x28, local copies, waits for them, and re-layouts: 0.76 us -> 5.76 us
    all_to_all x1, waiting for transfers between devices: 0.01 us -> 4.83 us  [shards(): latents = lax.all_to_all(spread, everyone, 0, 0)]
    ppermute x15 -> x13, starting transfers between devices: 10.6 us -> 7.81 us  [swapped(): return lax.ppermute(values, 'feat', [(i, i ^ bits) for i in range(feats)])]
    all_to_all x1, starting transfers between devices: 5.28 us -> 3.49 us  [shards(): shares = lax.all_to_all(spread, everyone, 0, 0)]
    pallas_call x7 -> x10, Pallas kernels: 6.14 us -> 7.59 us  [stage(): pl.pallas_call(kernel, out_shape=[jax.ShapeDtypeStruct(shape, kind) for s...]
    broadcast_in_dim x1 -> x0, local copies, waits for them, and re-layouts: 1.32 us -> none  [shards(): jnp.broadcast_to(latent[None], (blocks * feats, nodes, width))]
    ppermute x15 -> x13, waiting for transfers between devices: 14.1 us -> 14.2 us  [swapped(): return lax.ppermute(values, 'feat', [(i, i ^ bits) for i in range(feats)])]
  transfers between devices with their start and end apart: 17 -> 15, of which waited for: 6 -> 7; matrix products, arithmetic and copies ran while one was open for 3% -> 0% of each run, Pallas kernels for 8% -> 8%
where the time goes in v6:
time: 51.1 us; the launch traced here: 50.5 us
  waiting for transfers between devices  19.2 us (38%)
  starting transfers between devices  16.5 us (32%)
  Pallas kernels  7.59 us (15%)
  local copies, waits for them, and re-layouts  5.83 us (11%)
  between operations  0.8 us (2%)
  other arithmetic  0.63 us (1%)
    ppermute x13, waiting for transfers between devices, swapped(): return lax.ppermute(values, 'feat', [(i, i ^ bits) for i in range(feats)])  14.2 us
    ppermute x13, starting transfers between devices, swapped(): return lax.ppermute(values, 'feat', [(i, i ^ bits) for i in range(feats)])  7.81 us
    pallas_call x10, Pallas kernels, stage(): pl.pallas_call(kernel, out_shape=[jax.ShapeDtypeStruct(shape, kind) for s...  7.59 us
    unnamed x28, local copies, waits for them, and re-layouts  5.76 us
    all_to_all x1, starting transfers between devices, shards(): latents = lax.all_to_all(spread, everyone, 0, 0)  5.22 us
    all_to_all x1, waiting for transfers between devices, shards(): latents = lax.all_to_all(spread, everyone, 0, 0)  4.83 us
    all_to_all x1, starting transfers between devices, shards(): shares = lax.all_to_all(spread, everyone, 0, 0)  3.49 us
  transfers between devices with their start and end apart: 15, of which 7 were waited for; matrix products, arithmetic and copies ran while one was open for 0% of the time, Pallas kernels for 8%

profile of v6, /device:TPU:0, one launch (start us, length us, event | category | flops | bytes accessed | tf_op | source)
XLA Modules:
  0.0 50.5 jit_solution(11599813431207742279)
XLA Ops:
  1.3 0.8 %copy-done.4 = bf16[256,128]{1,0:T(8,128)(2,1)S(1)} copy-done((bf16[256,128]{1,0:T(8,128)(2,1)S(1)}, bf16[256,128]{1,0:T(8,128)(2,1)}, u32[]{:S(2)}) %copy-start.4) | copy-done | bytes 65560
  2.1 0.8 %copy-done.5 = bf16[256,128]{1,0:T(8,128)(2,1)S(1)} copy-done((bf16[256,128]{1,0:T(8,128)(2,1)S(1)}, bf16[256,128]{1,0:T(8,128)(2,1)}, u32[]{:S(2)}) %copy-start.5) | copy-done | bytes 65560
  3.0 0.7 %copy-done.6 = bf16[16,128]{1,0:T(8,128)(2,1)S(1)} copy-done((bf16[16,128]{1,0:T(8,128)(2,1)S(1)}, bf16[16,128]{1,0:T(8,128)(2,1)}, u32[]{:S(2)}) %copy-start.6) | copy-done | bytes 4120
  3.7 0.7 %copy-done.9 = bf16[16,128]{1,0:T(8,128)(2,1)S(1)} copy-done((bf16[16,128]{1,0:T(8,128)(2,1)S(1)}, bf16[16,128]{1,0:T(8,128)(2,1)}, u32[]{:S(2)}) %copy-start.9) | copy-done | bytes 4120
  4.6 3.0 %collective-permute-start = (bf16[544,128]{1,0:T(8,128)(2,1)S(1)}, bf16[544,128]{1,0:T(8,128)(2,1)S(1)}, u32[]{:S(2)}, u32[]{:S(2)}) collective-permute-start(bf16[544,128]{1,0:T(8,128)(2,1)S(1)} %get-tuple-element.35.refs_0_), channel_id=1, source_target_pairs={{0,2},{1,3},{2,0},{3,1},{4,6},{5,7},{6,4},{7,5},{8,10},{9,11},{10,... | collective-permute-start | bytes 417800 | tf_op jit(solution)/shard_map/ppermute | solution.py:338
  7.6 3.7 %collective-permute-done.refs_1_ = bf16[544,128]{1,0:T(8,128)(2,1)S(1)} collective-permute-done((bf16[544,128]{1,0:T(8,128)(2,1)S(1)}, bf16[544,128]{1,0:T(8,128)(2,1)S(1)}, u32[]{:S(2)}, u32[]{:S(2)}) %collective-permute-start) | collective-permute-done | bytes 139296 | tf_op jit(solution)/shard_map/ppermute | solution.py:338
  11.3 0.8 %copy-done.3 = bf16[128,512]{1,0:T(8,128)(2,1)S(1)} copy-done((bf16[128,512]{1,0:T(8,128)(2,1)S(1)}, bf16[128,512]{1,0:T(8,128)(2,1)}, u32[]{:S(2)}) %copy-start.3) | copy-done | bytes 131096
  12.2 1.8 %collective-permute-start.7 = (bf16[128,1024]{1,0:T(8,128)(2,1)S(1)}, bf16[128,1024]{1,0:T(8,128)(2,1)S(1)}, u32[]{:S(2)}, u32[]{:S(2)}) collective-permute-start(bf16[128,1024]{1,0:T(8,128)(2,1)S(1)} %pad_maximum_fusion), channel_id=1, source_target_pairs={{0,2},{1,3},{2,0},{3,1},{4,6},{5,7},{6,4},{7,5},{8,10},{9,11},{10,... | collective-permute-start | bytes 786440 | tf_op jit(solution)/shard_map/ppermute | solution.py:338
  14.6 0.6 %shard_map.157 = bf16[16,16,128]{2,1,0:T(8,128)(2,1)} custom-call(bf16[16,128]{1,0:T(8,128)(2,1)S(1)} %get-tuple-element.34.latent), custom_call_target="tpu_custom_call" | custom-call | flops 16777216 | bytes 4096 | tf_op jit(solution)/shard_map/pallas_call | solution.py:74
  15.2 5.2 %all-to-all-start = ((bf16[16,16,128]{2,1,0:T(8,128)(2,1)}), bf16[16,16,128]{2,1,0:T(8,128)(2,1)S(1)}, u32[]{:S(2)}, u32[]{:S(2)}) async-start(bf16[16,16,128]{2,1,0:T(8,128)(2,1)} %shard_map.157), calls=%async_computation | async-start | bytes 131072 | tf_op jit(solution)/shard_map/all_to_all | solution.py:360
  21.0 0.6 %copy-done.10 = s32[256]{0:T(256)S(1)} copy-done((s32[256]{0:T(256)S(1)}, s32[256]{0:T(256)}, u32[]{:S(2)}) %copy-start.10) | copy-done | bytes 1048
  21.6 0.9 %shard_map.159 = (bf16[128,512]{1,0:T(8,128)(2,1)S(1)}, f32[128,256]{1,0:T(8,128)S(1)}, bf16[64,128]{1,0:T(8,128)(2,1)S(1)}, bf16[16,128]{1,0:T(8,128)(2,1)S(1)}, bf16[160,512]{1,0:T(8,128)(2,1)S(1)}) custom-call(bf16[544,128]{1,0:T(8,128)(2,1)S(1)} %get-tuple-element.35.refs_0_, bf16[544,128]{1,0:T(8,128)(2,1)S(1)} %collective-permute-done.refs_1_, ...), custom_call_target="tpu_custom_call" | custom-call | flops 16777216 | bytes 1214976 | tf_op jit(solution)/shard_map/pallas_call | solution.py:74
  22.5 4.8 %all-to-all-done.came = bf16[16,16,128]{2,1,0:T(8,128)(2,1)S(1)} async-done(((bf16[16,16,128]{2,1,0:T(8,128)(2,1)}), bf16[16,16,128]{2,1,0:T(8,128)(2,1)S(1)}, u32[]{:S(2)}, u32[]{:S(2)}) %all-to-all-start) | async-done | bytes 65568 | tf_op jit(solution)/shard_map/all_to_all | solution.py:360
  27.3 0.9 %shard_map.160 = (f32[128,256]{1,0:T(8,128)S(1)}, f32[128,512]{1,0:T(8,128)S(1)}, bf16[144,512]{1,0:T(8,128)(2,1)S(1)}, bf16[16,512]{1,0:T(8,128)(2,1)S(1)}, f32...) custom-call(bf16[16,16,128]{2,1,0:T(8,128)(2,1)S(1)} %all-to-all-done.came, f32[128,256]{1,0:T(8,128)S(1)} %get-tuple-element.36.pre, ...), custom_call_target="tpu_custom_call" | custom-call | flops 16777216 | bytes 1789952 | tf_op jit(solution)/shard_map/pallas_call | solution.py:74
  28.4 5.2 %collective-permute-done.5.refs_2_ = bf16[144,512]{1,0:T(8,128)(2,1)S(1)} collective-permute-done((bf16[144,512]{1,0:T(8,128)(2,1)S(1)}, bf16[144,512]{1,0:T(8,128)(2,1)S(1)}, u32[]{:S(2)}, u32[]{:S(2)}) %collective-permute-start.5) | collective-permute-done | bytes 147488 | tf_op jit(solution)/shard_map/ppermute | solution.py:338
  33.6 0.8 %shard_map.161 = (f32[128,512]{1,0:T(8,128)S(1)}, f32[128,1]{1,0:T(8,128)S(1)}, bf16[128,128]{1,0:T(8,128)(2,1)S(1)}, bf16[128,128]{1,0:T(8,128)(2,1)S(1)}, f32[...) custom-call(f32[128,512]{1,0:T(8,128)S(1)} %get-tuple-element.40.refs_0_, ...), custom_call_target="tpu_custom_call" | custom-call | flops 16777216 | bytes 724992 | tf_op jit(solution)/shard_map/pallas_call | solution.py:74
  34.4 1.2 %collective-permute-done.9.refs_3_ = f32[16,512]{1,0:T(8,128)S(1)} collective-permute-done((f32[16,512]{1,0:T(8,128)S(1)}, f32[16,512]{1,0:T(8,128)S(1)}, u32[]{:S(2)}, u32[]{:S(2)}) %collective-permute-start.9) | collective-permute-done | bytes 32800 | tf_op jit(solution)/shard_map/ppermute | solution.py:338
  35.6 2.3 %shard_map.162 = (bf16[16,128]{1,0:T(8,128)(2,1)}, f32[128,256]{1,0:T(8,128)S(1)}, bf16[128,256]{1,0:T(8,128)(2,1)S(1)}, bf16[128,256]{1,0:T(8,128)(2,1)S(1)}, b...) custom-call(bf16[128,1024]{1,0:T(8,128)(2,1)S(1)} %collective-permute-done.7.refs_0_, ...), custom_call_target="tpu_custom_call" | custom-call | flops 16777216 | bytes 3035648 | tf_op jit(solution)/shard_map/pallas_call | solution.py:74
  37.9 1.1 %shard_map.165 = (bf16[16,16,128]{2,1,0:T(8,128)(2,1)}, f32[64,512]{1,0:T(8,128)}) custom-call(bf16[128,256]{1,0:T(8,128)(2,1)S(1)} %get-tuple-element.61.dpre, bf16[16,256]{1,0:T(8,128)(2,1)S(1)} %get-tuple-element.62.node_dpre, bf16[64,128]{1,0:T(8,128)(2,1)S(1)} %get-tuple-element.37.pick, bf16[16,128]{1,0:T(8,128)(2,1)S(1)} %get-tuple-element.38.take.refs_5_.refs_7_, ...), custom_call_target="tpu_custom_call" | custom-call | flops 16777216 | bytes 1404928 | tf_op jit(solution)/shard_map/pallas_call | solution.py:74
  39.0 3.5 %all-to-all-start.1 = ((bf16[16,16,128]{2,1,0:T(8,128)(2,1)}), bf16[16,16,128]{2,1,0:T(8,128)(2,1)S(1)}, u32[]{:S(2)}, u32[]{:S(2)}) async-start(bf16[16,16,128]{2,1,0:T(8,128)(2,1)} %get-tuple-element.63), calls=%async_computation.1 | async-start | bytes 131072 | tf_op jit(solution)/shard_map/all_to_all | solution.py:431
  42.5 1.8 %collective-permute-start.11 = (bf16[128,256]{1,0:T(8,128)(2,1)S(1)}, bf16[128,256]{1,0:T(8,128)(2,1)S(1)}, u32[]{:S(2)}, u32[]{:S(2)}) collective-permute-start(bf16[128,256]{1,0:T(8,128)(2,1)S(1)} %get-tuple-element.55), channel_id=1, source_target_pairs={{0,2},{1,3},{2,0},{3,1},{4,6},{5,7},{6,4},{7,5},{8,10},{9,11},{10,... | collective-permute-start | bytes 196616 | tf_op jit(solution)/shard_map/ppermute | solution.py:338
  44.3 3.0 %collective-permute-done.11.refs_1_ = bf16[128,256]{1,0:T(8,128)(2,1)S(1)} collective-permute-done((bf16[128,256]{1,0:T(8,128)(2,1)S(1)}, bf16[128,256]{1,0:T(8,128)(2,1)S(1)}, u32[]{:S(2)}, u32[]{:S(2)}) %collective-permute-start.11) | collective-permute-done | bytes 65568 | tf_op jit(solution)/shard_map/ppermute | solution.py:338
  47.4 1.2 %collective-permute-done.12.grad_came = bf16[128,128]{1,0:T(8,128)(2,1)S(1)} collective-permute-done((bf16[128,128]{1,0:T(8,128)(2,1)S(1)}, bf16[128,128]{1,0:T(8,128)(2,1)S(1)}, u32[]{:S(2)}, u32[]{:S(2)}) %collective-permute-start.12) | collective-permute-done | bytes 32800 | tf_op jit(solution)/shard_map/ppermute | solution.py:338
  48.6 0.7 %shard_map.164 = (bf16[256,128]{1,0:T(8,128)(2,1)}, bf16[256,128]{1,0:T(8,128)(2,1)}) custom-call(bf16[128,128]{1,0:T(8,128)(2,1)S(1)} %get-tuple-element.45.next_mine, bf16[128,128]{1,0:T(8,128)(2,1)S(1)} %collective-permute-done.6.next_came, bf16[128,128]{1,0:T(8,128)(2,1)S(1)} %get-tuple-element.56.grad_mine, ...), custom_call_target="tpu_custom_call" | custom-call | flops 16777216 | bytes 131072 | tf_op jit(solution)/shard_map/pallas_call | solution.py:74
  (49 shorter events, 3.5 us)
Async XLA Ops:
  1.3 0.8 %copy-start.4 = (bf16[256,128]{1,0:T(8,128)(2,1)S(1)}, bf16[256,128]{1,0:T(8,128)(2,1)}, u32[]{:S(2)}) copy-start(bf16[256,128]{1,0:T(8,128)(2,1)} %state.1) | copy-start | bytes 196612
  2.1 0.8 %copy-start.5 = (bf16[256,128]{1,0:T(8,128)(2,1)S(1)}, bf16[256,128]{1,0:T(8,128)(2,1)}, u32[]{:S(2)}) copy-start(bf16[256,128]{1,0:T(8,128)(2,1)} %edge_cot.1) | copy-start | bytes 196612
  4.6 6.7 %collective-permute-start = (bf16[544,128]{1,0:T(8,128)(2,1)S(1)}, bf16[544,128]{1,0:T(8,128)(2,1)S(1)}, u32[]{:S(2)}, u32[]{:S(2)}) collective-permute-start(bf16[544,128]{1,0:T(8,128)(2,1)S(1)} %get-tuple-element.35.refs_0_), channel_id=1, source_target_pairs={{0,2},{1,3},{2,0},{3,1},{4,6},{5,7},{6,4},{7,5},{8,10},{9,11},{10,... | collective-permute-start | bytes 417800 | tf_op jit(solution)/shard_map/ppermute | solution.py:338
  7.6 13.4 %collective-permute-start.2 = (bf16[128,1536]{1,0:T(8,128)(2,1)}, bf16[128,1536]{1,0:T(8,128)(2,1)S(1)}, u32[]{:S(2)}, u32[]{:S(2)}) collective-permute-start(bf16[128,1536]{1,0:T(8,128)(2,1)} %e_mine.1), channel_id=1, source_target_pairs={{0,1},{1,0},{2,3},{3,2},{4,5},{5,4},{6,7},{7,6},{8,9},{9,8},{10,11... | collective-permute-start | bytes 1179656 | tf_op jit(solution)/shard_map/ppermute | solution.py:338
  11.2 0.9 %copy-start.3 = (bf16[128,512]{1,0:T(8,128)(2,1)S(1)}, bf16[128,512]{1,0:T(8,128)(2,1)}, u32[]{:S(2)}) copy-start(bf16[128,512]{1,0:T(8,128)(2,1)} %refs_17_) | copy-start | bytes 393220
  11.3 0.9 %slice-start = ((bf16[128,1024]{1,0:T(8,128)(2,1)}), bf16[128,512]{1,0:T(8,128)(2,1)S(1)}, s32[]{:S(2)}) async-start(bf16[128,1024]{1,0:T(8,128)(2,1)} %in_mine), calls=%async_computation.2 | async-start | bytes 262144 | tf_op jit(solution)/shard_map/slice | solution.py:371
  11.3 2.8 %copy-start.1 = (bf16[128,1024]{1,0:T(8,128)(2,1)S(1)}, bf16[128,1024]{1,0:T(8,128)(2,1)}, u32[]{:S(2)}) copy-start(bf16[128,1024]{1,0:T(8,128)(2,1)} %in_mine) | copy-start | bytes 786436
  11.3 3.3 %copy-start.2 = (bf16[128,512]{1,0:T(8,128)(2,1)S(1)}, bf16[128,512]{1,0:T(8,128)(2,1)}, u32[]{:S(2)}) copy-start(bf16[128,512]{1,0:T(8,128)(2,1)} %refs_13_.1) | copy-start | bytes 393220
  12.2 8.7 %copy-start = (bf16[128,1536]{1,0:T(8,128)(2,1)S(1)}, bf16[128,1536]{1,0:T(8,128)(2,1)}, u32[]{:S(2)}) copy-start(bf16[128,1536]{1,0:T(8,128)(2,1)} %e_mine.1) | copy-start | bytes 1179652
  12.2 8.2 %collective-permute-start.7 = (bf16[128,1024]{1,0:T(8,128)(2,1)S(1)}, bf16[128,1024]{1,0:T(8,128)(2,1)S(1)}, u32[]{:S(2)}, u32[]{:S(2)}) collective-permute-start(bf16[128,1024]{1,0:T(8,128)(2,1)S(1)} %pad_maximum_fusion), channel_id=1, source_target_pairs={{0,2},{1,3},{2,0},{3,1},{4,6},{5,7},{6,4},{7,5},{8,10},{9,11},{10,... | collective-permute-start | bytes 786440 | tf_op jit(solution)/shard_map/ppermute | solution.py:338
  14.0 13.3 %collective-permute-start.4 = (bf16[128,1024]{1,0:T(8,128)(2,1)S(1)}, bf16[128,1024]{1,0:T(8,128)(2,1)S(1)}, u32[]{:S(2)}, u32[]{:S(2)}) collective-permute-start(bf16[128,1024]{1,0:T(8,128)(2,1)S(1)} %copy-done.1), channel_id=1, source_target_pairs={{0,1},{1,0},{2,3},{3,2},{4,5},{5,4},{6,7},{7,6},{8,9},{9,8},{10,11... | collective-permute-start | bytes 786440 | tf_op jit(solution)/shard_map/ppermute | solution.py:338
  14.1 6.9 %collective-permute-start.1 = (bf16[288,256]{1,0:T(8,128)(2,1)S(1)}, bf16[288,256]{1,0:T(8,128)(2,1)S(1)}, u32[]{:S(2)}, u32[]{:S(2)}) collective-permute-start(bf16[288,256]{1,0:T(8,128)(2,1)S(1)} %shard_map.158), channel_id=1, source_target_pairs={{0,1},{1,0},{2,3},{3,2},{4,5},{5,4},{6,7},{7,6},{8,9},{9,8},{10,11... | collective-permute-start | bytes 442376 | tf_op jit(solution)/shard_map/ppermute | solution.py:338
  14.6 12.8 %collective-permute-start.3 = (bf16[128,512]{1,0:T(8,128)(2,1)S(1)}, bf16[128,512]{1,0:T(8,128)(2,1)S(1)}, u32[]{:S(2)}, u32[]{:S(2)}) collective-permute-start(bf16[128,512]{1,0:T(8,128)(2,1)S(1)} %copy-done.2), channel_id=1, source_target_pairs={{0,1},{1,0},{2,3},{3,2},{4,5},{5,4},{6,7},{7,6},{8,9},{9,8},{10,11... | collective-permute-start | bytes 393224 | tf_op jit(solution)/shard_map/ppermute | solution.py:338
  15.2 5.7 %copy-start.8 = (s32[4,4,8]{2,1,0:T(4,128)S(1)}, s32[4,4,8]{2,1,0:T(4,128)}, u32[]{:S(2)}) copy-start(s32[4,4,8]{2,1,0:T(4,128)} %refs_7_.1) | copy-start | bytes 1540
  15.2 5.7 %copy-start.11 = (s32[256]{0:T(256)S(1)}, s32[256]{0:T(256)}, u32[]{:S(2)}) copy-start(s32[256]{0:T(256)} %param.17) | copy-start | bytes 3076
  15.2 12.1 %all-to-all-start = ((bf16[16,16,128]{2,1,0:T(8,128)(2,1)}), bf16[16,16,128]{2,1,0:T(8,128)(2,1)S(1)}, u32[]{:S(2)}, u32[]{:S(2)}) async-start(bf16[16,16,128]{2,1,0:T(8,128)(2,1)} %shard_map.157), calls=%async_computation | async-start | bytes 131072 | tf_op jit(solution)/shard_map/all_to_all | solution.py:360
  20.5 15.1 %collective-permute-start.8 = (bf16[128,1024]{1,0:T(8,128)(2,1)S(1)}, bf16[128,1024]{1,0:T(8,128)(2,1)S(1)}, u32[]{:S(2)}, u32[]{:S(2)}) collective-permute-start(bf16[128,1024]{1,0:T(8,128)(2,1)S(1)} %collective-permute-done.7.refs_0_), channel_id=1, source_target_pairs={{0,1},{1,0},{2,3},{3,2},{4,5},{5,4},{6,7},{7,6},{8,9},{9,8},{10,11... | collective-permute-start | bytes 786440 | tf_op jit(solution)/shard_map/ppermute | solution.py:338
  28.3 5.3 %collective-permute-start.5 = (bf16[144,512]{1,0:T(8,128)(2,1)S(1)}, bf16[144,512]{1,0:T(8,128)(2,1)S(1)}, u32[]{:S(2)}, u32[]{:S(2)}) collective-permute-start(bf16[144,512]{1,0:T(8,128)(2,1)S(1)} %get-tuple-element.42), channel_id=1, source_target_pairs={{0,2},{1,3},{2,0},{3,1},{4,6},{5,7},{6,4},{7,5},{8,10},{9,11},{10,... | collective-permute-start | bytes 442376 | tf_op jit(solution)/shard_map/ppermute | solution.py:338
  28.4 6.0 %collective-permute-start.10 = (bf16[128,512]{1,0:T(8,128)(2,1)S(1)}, bf16[128,512]{1,0:T(8,128)(2,1)S(1)}, u32[]{:S(2)}, u32[]{:S(2)}) collective-permute-start(bf16[128,512]{1,0:T(8,128)(2,1)S(1)} %copy-done.3), channel_id=1, source_target_pairs={{0,1},{1,0},{2,3},{3,2},{4,5},{5,4},{6,7},{7,6},{8,9},{9,8},{10,11... | collective-permute-start | bytes 393224 | tf_op jit(solution)/shard_map/ppermute | solution.py:338
  34.4 1.2 %collective-permute-start.9 = (f32[16,512]{1,0:T(8,128)S(1)}, f32[16,512]{1,0:T(8,128)S(1)}, u32[]{:S(2)}, u32[]{:S(2)}) collective-permute-start(f32[16,512]{1,0:T(8,128)S(1)} %get-tuple-element.48.refs_2_), channel_id=1, source_target_pairs={{0,1},{1,0},{2,3},{3,2},{4,5},{5,4},{6,7},{7,6},{8,9},{9,8},{10,11... | collective-permute-start | bytes 98312 | tf_op jit(solution)/shard_map/ppermute | solution.py:338
  39.0 10.4 %all-to-all-start.1 = ((bf16[16,16,128]{2,1,0:T(8,128)(2,1)}), bf16[16,16,128]{2,1,0:T(8,128)(2,1)S(1)}, u32[]{:S(2)}, u32[]{:S(2)}) async-start(bf16[16,16,128]{2,1,0:T(8,128)(2,1)} %get-tuple-element.63), calls=%async_computation.1 | async-start | bytes 131072 | tf_op jit(solution)/shard_map/all_to_all | solution.py:431
  42.5 4.8 %collective-permute-start.11 = (bf16[128,256]{1,0:T(8,128)(2,1)S(1)}, bf16[128,256]{1,0:T(8,128)(2,1)S(1)}, u32[]{:S(2)}, u32[]{:S(2)}) collective-permute-start(bf16[128,256]{1,0:T(8,128)(2,1)S(1)} %get-tuple-element.55), channel_id=1, source_target_pairs={{0,2},{1,3},{2,0},{3,1},{4,6},{5,7},{6,4},{7,5},{8,10},{9,11},{10,... | collective-permute-start | bytes 196616 | tf_op jit(solution)/shard_map/ppermute | solution.py:338
  44.3 3.1 %collective-permute-start.6 = (bf16[128,128]{1,0:T(8,128)(2,1)S(1)}, bf16[128,128]{1,0:T(8,128)(2,1)S(1)}, u32[]{:S(2)}, u32[]{:S(2)}) collective-permute-start(bf16[128,128]{1,0:T(8,128)(2,1)S(1)} %get-tuple-element.46), channel_id=1, source_target_pairs={{0,1},{1,0},{2,3},{3,2},{4,5},{5,4},{6,7},{7,6},{8,9},{9,8},{10,11... | collective-permute-start | bytes 98312 | tf_op jit(solution)/shard_map/ppermute | solution.py:338
  47.3 1.3 %collective-permute-start.12 = (bf16[128,128]{1,0:T(8,128)(2,1)S(1)}, bf16[128,128]{1,0:T(8,128)(2,1)S(1)}, u32[]{:S(2)}, u32[]{:S(2)}) collective-permute-start(bf16[128,128]{1,0:T(8,128)(2,1)S(1)} %get-tuple-element.57), channel_id=1, source_target_pairs={{0,1},{1,0},{2,3},{3,2},{4,5},{5,4},{6,7},{7,6},{8,9},{9,8},{10,11... | collective-permute-start | bytes 98312 | tf_op jit(solution)/shard_map/ppermute | solution.py:338
  (6 other events, 4.1 us)

commit v7 on v6

--- a/solution.py
+++ b/solution.py
@@ -66,9 +66,8 @@
     return pl.ds(pl.multiple_of(group * width, width), width)
 
 
-def stage(kernel, outs, operands, scalars=0, in_hbm=0, scratch=(), flops=1 << 24):
-    specs = [pl.BlockSpec(memory_space=pltpu.HBM)] * in_hbm
-    specs += [pl.BlockSpec(memory_space=pltpu.VMEM)] * (len(operands) - scalars - in_hbm)
+def stage(kernel, outs, operands, scalars=0, flops=1 << 24):
+    specs = [pl.BlockSpec(memory_space=pltpu.VMEM)] * (len(operands) - scalars)
     specs += [pl.BlockSpec(memory_space=pltpu.SMEM)] * scalars
     moved = sum(o.size * o.dtype.itemsize for o in operands)
     return pl.pallas_call(
@@ -76,7 +75,6 @@
         out_shape=[jax.ShapeDtypeStruct(shape, kind) for shape, kind in outs],
         in_specs=specs,
         out_specs=[pl.BlockSpec(memory_space=pltpu.VMEM)] * len(outs),
-        scratch_shapes=scratch,
         cost_estimate=pl.CostEstimate(flops=flops, bytes_accessed=moved, transcendentals=0),
         compiler_params=pltpu.CompilerParams(vmem_limit_bytes=kernel_vmem),
     )(*operands)
@@ -97,55 +95,40 @@
     return value
 
 
-def pack_inputs(state, edge_cot, node_cot, latent, gain_e, gain_n, pack, held, sems):
-    edge_dev = state.shape[0]
-    nodes = latent.shape[0]
-    copies = [
-        pltpu.make_async_copy(state, pack.at[pl.ds(0, edge_dev)], sems.at[0]),
-        pltpu.make_async_copy(edge_cot, pack.at[pl.ds(edge_dev, edge_dev)], sems.at[1]),
-        pltpu.make_async_copy(node_cot, pack.at[pl.ds(2 * edge_dev, nodes)], sems.at[2]),
-        pltpu.make_async_copy(latent, held, sems.at[3]),
-    ]
-    for copy in copies:
-        copy.start()
-    pack[2 * edge_dev + nodes :] = gains(gain_e, gain_n, nodes)
-    for copy in copies:
-        copy.wait()
-
-
-def spread_latent(latent, spread):
-    spread[...] = jnp.broadcast_to(latent[...][None], spread.shape)
+def pack_extra(edge_cot, node_cot, gain_e, gain_n, pack):
+    edge_dev = edge_cot.shape[0]
+    nodes = node_cot.shape[0]
+    pack[:edge_dev] = edge_cot[...]
+    pack[edge_dev : edge_dev + nodes] = node_cot[...]
+    pack[edge_dev + nodes :] = gains(gain_e, gain_n, nodes)
 
 
 def half_rows(pack, core, half):
     first = pl.multiple_of(core * half, half)
-    return [pack[pl.ds(first, half)], pack[pl.ds(cores * half + first, half)], pack[2 * cores * half :]]
+    return jnp.concatenate([pack[pl.ds(first, half)], pack[cores * half :]], axis=0)
 
 
 def send_half(groups, *refs):
     packs, sent = refs[:groups], refs[groups]
     _, core = place()
     width = packs[0].shape[1]
-    half = packs[0].shape[0] - sent.shape[0] >> 1
+    half = packs[0].shape[0] - sent.shape[0]
     for step, pack in enumerate(packs):
-        sent[:, step * width : (step + 1) * width] = jnp.concatenate(half_rows(pack, 1 - core, half), axis=0)
-
-
-def prepare_edges(groups, *refs):
-    packs = refs[:groups]
-    came, mine, other, slot, receiver, send_rows, state, pre, pick, take, extra = refs[groups:]
+        sent[:, step * width : (step + 1) * width] = half_rows(pack, 1 - core, half)
+
+
+def prepare_edges(feats, *refs):
+    states = refs[:feats]
+    mine, other, slot, receiver, send_rows, state, pre, pick, take = refs[feats:]
     group, core = place()
     block = lax.axis_index("nodes")
     features = state.shape[1]
     nodes, half = take.shape
-    width = features // (groups * cores)
     blocks, _, slots = send_rows.shape
-    for step, pack in enumerate(packs):
-        columns = lanes(group ^ step, width * cores)
-        theirs = came[:, step * width : (step + 1) * width]
-        ours = half_rows(pack, core, half)
-        state[:, columns] = pair(ours[0], theirs[:half], core)
-        extra[:, columns] = pair(jnp.concatenate(ours[1:], axis=0), theirs[half:], core)
+    rows = pl.ds(pl.multiple_of(core * half, half), half)
+    for step in range(feats // cores):
+        ours, theirs = states[cores * step][rows], states[cores * step + 1][rows]
+        state[:, lanes(group ^ step, features * cores // feats)] = pair(ours, theirs, core)
 
     slot_row = slot[pl.ds(core, 1)]
     sender = block * nodes + slot_row
@@ -194,12 +177,15 @@
 
 
 def update_edges(groups, *refs):
-    part, lat, came = refs[0], refs[1], refs[2 : groups + 1]
-    extra, state, take, normed, inverse, kept, lent, aggregate, lat_all, next_all = refs[groups + 1 :]
+    part, lat, came, packs = refs[0], refs[1], refs[2 : groups + 1], refs[groups + 1 : 2 * groups + 1]
+    theirs, state, take, normed, inverse, kept, lent, aggregate, lat_all, extra, next_all = refs[2 * groups + 1 :]
     group, core = place()
     nodes, half = take.shape
     width = kept.shape[1]
     hidden = lat.shape[1]
+    for step, pack in enumerate(packs):
+        both = pair(half_rows(pack, core, half), theirs[:, step * width : (step + 1) * width], core)
+        extra[:, lanes(group ^ step, width * cores)] = both
     value = part[...]
     lat_all[:, :hidden] = lat[...]
     for step, ref in enumerate(came, 1):
@@ -294,6 +280,13 @@
     value = total(parts)
     kept[...] = jnp.where(core == 0, value[:, :width], value[:, width:]).astype(bf16)
     sent[...] = jnp.where(core == 0, value[:, width:], value[:, :width]).astype(bf16)
+
+
+def add_nodes(shares, node_cot, node_grad):
+    value = node_cot[...].astype(f32)
+    for source in range(shares.shape[0]):
+        value = value + shares[source].astype(f32)
+    node_grad[...] = value.astype(bf16)
 
 
 def assemble(next_mine, next_came, grad_mine, grad_came, edge_next, edge_grad):
@@ -347,41 +340,31 @@
     slot_rows = sender_slot.reshape(cores, half)
     receiver_rows = receiver_row.reshape(cores, half)
 
-    rows = 2 * edge_dev + 2 * nodes
-    pack, held = stage(
-        pack_inputs,
-        [((rows, width), bf16), ((nodes, width), bf16)],
-        [edge_state, edge_cot, node_cot, latent, gain_e, gain_n],
-        in_hbm=4,
-        scratch=[pltpu.SemaphoreType.DMA((4,))],
-    )
-    packs = [pack] + over_groups(pack)
-    (spread,) = stage(spread_latent, [((blocks * feats, nodes, width), bf16)], [held])
-    latents = lax.all_to_all(spread, everyone, 0, 0)
+    latents = lax.all_to_all(
+        jnp.broadcast_to(latent[None], (blocks * feats, nodes, width)), everyone, 0, 0
+    )
+    states = [edge_state] + [swapped(edge_state, step) for step in range(1, feats)]
     e_in = (edge_in_weight, over_cores(edge_in_weight))
+    state, pre, pick, take = stage(
+        functools.partial(prepare_edges, feats),
+        [((half, features), bf16), ((half, hidden), f32), ((table, half), bf16), ((nodes, half), bf16)],
+        [*states, *e_in, slot_rows, receiver_rows, send_rows],
+        scalars=1,
+    )
+    pre, node_in_weight, node_out_weight, edge_out_weight, edge_cot = lax.optimization_barrier(
+        (pre, node_in_weight, node_out_weight, edge_out_weight, edge_cot)
+    )
     e_out = (edge_out_weight, over_cores(edge_out_weight))
-    (sent,) = stage(
-        functools.partial(send_half, groups), [((rows - 2 * half, groups * width), bf16)], packs
-    )
-    came = over_cores(sent)
-    sent, node_in_weight, node_out_weight = lax.optimization_barrier((sent, node_in_weight, node_out_weight))
-    n_in = (node_in_weight, over_cores(node_in_weight))
-    n_out = (node_out_weight, over_cores(node_out_weight))
     far = []
     for weights in over_groups(jnp.concatenate([node_in_weight[:, features:], node_out_weight], axis=1)):
         far += [weights, over_cores(weights)]
-    state, pre, pick, take, extra = stage(
-        functools.partial(prepare_edges, groups),
-        [
-            ((half, features), bf16),
-            ((half, hidden), f32),
-            ((table, half), bf16),
-            ((nodes, half), bf16),
-            ((half + 2 * nodes, features), bf16),
-        ],
-        [*packs, came, *e_in, slot_rows, receiver_rows, send_rows],
-        scalars=1,
-    )
+    rows = edge_dev + 2 * nodes
+    (pack,) = stage(pack_extra, [((rows, width), bf16)], [edge_cot, node_cot, gain_e, gain_n])
+    packs = [pack] + over_groups(pack)
+    (sent,) = stage(functools.partial(send_half, groups), [((rows - half, groups * width), bf16)], packs)
+    extra_came = over_cores(sent)
+    n_in = (node_in_weight, over_cores(node_in_weight))
+    n_out = (node_out_weight, over_cores(node_out_weight))
     edge_pre, part, sent, own, lat, _ = stage(
         finish_edges,
         [
@@ -394,7 +377,7 @@
         ],
         [latents, pre, pick, take, *e_in, *e_out, *n_in],
     )
-    normed, inverse, next_mine, next_sent, aggregate, lat_all, _ = stage(
+    normed, inverse, next_mine, next_sent, aggregate, lat_all, extra, _ = stage(
         functools.partial(update_edges, groups),
         [
             ((half, features), f32),
@@ -403,9 +386,10 @@
             ((half, width), bf16),
             ((nodes, features), f32),
             ((nodes, features), f32),
+            ((half + 2 * nodes, features), bf16),
             ((half, features), bf16),
         ],
-        [part, lat, *over_groups(sent), extra, state, take],
+        [part, lat, *over_groups(sent), *packs, extra_came, state, take],
     )
     aggregate2 = over_cores(aggregate)
     next_came = over_cores(next_sent)
@@ -439,7 +423,7 @@
         [((edge_dev, width), bf16), ((edge_dev, width), bf16)],
         [next_mine, next_came, grad_mine, over_cores(grad_sent)],
     )
-    node_grad = (node_cot.astype(f32) + jnp.sum(shares.astype(f32), axis=0)).astype(bf16)
+    (node_grad,) = stage(add_nodes, [((nodes, width), bf16)], [shares, node_cot])
     return (edge_next, node_next, edge_grad, node_grad)
 
 

time: 51.1 us -> 51.8 us (1.014)
  starting transfers between devices: 16.5 us -> 18.4 us
  other arithmetic: 0.63 us -> 0.02 us
    unnamed x28, local copies, waits for them, and re-layouts: 5.76 us -> 3.91 us
    ppermute x13 -> x16, starting transfers between devices: 7.81 us -> 8.75 us  [swapped(): return lax.ppermute(values, 'feat', [(i, i ^ bits) for i in range(feats)])]
    all_to_all x1, starting transfers between devices: 5.22 us -> 6.16 us  [shards(): lax.all_to_all(jnp.broadcast_to(latent[None], (blocks * feats, nodes, wid...]
    slice x2, local copies, waits for them, and re-layouts: 0.08 us -> 1.01 us  [shards(): node_in_weight[:, features:]]
    ppermute x13 -> x16, waiting for transfers between devices: 14.2 us -> 15.1 us  [swapped(): return lax.ppermute(values, 'feat', [(i, i ^ bits) for i in range(feats)])]
    all_to_all x1, waiting for transfers between devices: 4.83 us -> 3.99 us  [shards(): lax.all_to_all(jnp.broadcast_to(latent[None], (blocks * feats, nodes, wid...]
    broadcast_in_dim x0 -> x1, local copies, waits for them, and re-layouts: none -> 0.64 us  [shards(): jnp.broadcast_to(latent[None], (blocks * feats, nodes, width))]
    convert_element_type x1 -> x0, other arithmetic: 0.6 us -> none  [shards(): (node_cot.astype(f32) + jnp.sum(shares.astype(f32), axis=0)).astype(bf16)]
  transfers between devices with their start and end apart: 15 -> 18, of which waited for: 7 -> 10; matrix products, arithmetic and copies ran while one was open for 0% -> 1% of each run, Pallas kernels for 8% -> 5%
where the time goes in v7:
time: 51.8 us; the launch traced here: 51.3 us
  waiting for transfers between devices  19.2 us (37%)
  starting transfers between devices  18.4 us (36%)
  Pallas kernels  7.38 us (14%)
  local copies, waits for them, and re-layouts  5.56 us (11%)
  between operations  0.78 us (2%)
    ppermute x16, waiting for transfers between devices, swapped(): return lax.ppermute(values, 'feat', [(i, i ^ bits) for i in range(feats)])  15.1 us
    ppermute x16, starting transfers between devices, swapped(): return lax.ppermute(values, 'feat', [(i, i ^ bits) for i in range(feats)])  8.75 us
    pallas_call x10, Pallas kernels, stage(): pl.pallas_call(kernel, out_shape=[jax.ShapeDtypeStruct(shape, kind) for s...  7.38 us
    all_to_all x1, starting transfers between devices, shards(): lax.all_to_all(jnp.broadcast_to(latent[None], (blocks * feats, nodes, wid...  6.16 us
    all_to_all x1, waiting for transfers between devices, shards(): lax.all_to_all(jnp.broadcast_to(latent[None], (blocks * feats, nodes, wid...  3.99 us
    unnamed x28, local copies, waits for them, and re-layouts  3.91 us
    all_to_all x1, starting transfers between devices, shards(): shares = lax.all_to_all(spread, everyone, 0, 0)  3.49 us
  transfers between devices with their start and end apart: 18, of which 10 were waited for; matrix products, arithmetic and copies ran while one was open for 1% of the time, Pallas kernels for 5%

profile of v7, /device:TPU:0, one launch (start us, length us, event | category | flops | bytes accessed | tf_op | source)
XLA Modules:
  0.0 51.3 jit_solution(13434840728235096305)
XLA Ops:
  1.2 2.9 %collective-permute-start.1 = (bf16[256,128]{1,0:T(8,128)(2,1)}, bf16[256,128]{1,0:T(8,128)(2,1)S(1)}, u32[]{:S(2)}, u32[]{:S(2)}) collective-permute-start(bf16[256,128]{1,0:T(8,128)(2,1)} %refs_0_.1), channel_id=1, source_target_pairs={{0,2},{1,3},{2,0},{3,1},{4,6},{5,7},{6,4},{7,5},{8,10},{9,11},{10,... | collective-permute-start | bytes 196616 | tf_op jit(solution)/shard_map/ppermute | solution.py:331
  4.2 2.6 %collective-permute-done.1.refs_2_ = bf16[256,128]{1,0:T(8,128)(2,1)S(1)} collective-permute-done((bf16[256,128]{1,0:T(8,128)(2,1)}, bf16[256,128]{1,0:T(8,128)(2,1)S(1)}, u32[]{:S(2)}, u32[]{:S(2)}) %collective-permute-start.1) | collective-permute-done | bytes 65568 | tf_op jit(solution)/shard_map/ppermute | solution.py:331
  6.8 2.0 %collective-permute-done.2.refs_3_ = bf16[256,128]{1,0:T(8,128)(2,1)S(1)} collective-permute-done((bf16[256,128]{1,0:T(8,128)(2,1)}, bf16[256,128]{1,0:T(8,128)(2,1)S(1)}, u32[]{:S(2)}, u32[]{:S(2)}) %collective-permute-start.2) | collective-permute-done | bytes 65568 | tf_op jit(solution)/shard_map/ppermute | solution.py:331
  8.7 0.7 %copy-done.10 = s32[256]{0:T(256)S(1)} copy-done((s32[256]{0:T(256)S(1)}, s32[256]{0:T(256)}, u32[]{:S(2)}) %copy-start.10) | copy-done | bytes 1048
  9.4 1.0 %copy-done = bf16[128,1536]{1,0:T(8,128)(2,1)S(1)} copy-done((bf16[128,1536]{1,0:T(8,128)(2,1)S(1)}, bf16[128,1536]{1,0:T(8,128)(2,1)}, u32[]{:S(2)}) %copy-start) | copy-done | bytes 393240
  10.4 0.8 %copy-done.5 = bf16[256,128]{1,0:T(8,128)(2,1)S(1)} copy-done((bf16[256,128]{1,0:T(8,128)(2,1)S(1)}, bf16[256,128]{1,0:T(8,128)(2,1)}, u32[]{:S(2)}) %copy-start.5) | copy-done | bytes 65560
  11.3 0.7 %copy-done.8 = s32[4,4,8]{2,1,0:T(4,128)S(1)} copy-done((s32[4,4,8]{2,1,0:T(4,128)S(1)}, s32[4,4,8]{2,1,0:T(4,128)}, u32[]{:S(2)}) %copy-start.8) | copy-done | bytes 536
  12.0 0.9 %shard_map.156 = (bf16[128,512]{1,0:T(8,128)(2,1)S(1)}, f32[128,256]{1,0:T(8,128)S(1)}, bf16[64,128]{1,0:T(8,128)(2,1)S(1)}, bf16[16,128]{1,0:T(8,128)(2,1)S(1)}) custom-call(bf16[256,128]{1,0:T(8,128)(2,1)S(1)} %copy-done.5, bf16[256,128]{1,0:T(8,128)(2,1)S(1)} %collective-permute-done.refs_1_, bf16[256,128]{1,0:T(8,128)(2,1)S(1)} %collective-permute-done.1.refs_2_, ...), custom_call_target="tpu_custom_call" | custom-call | flops 16777216 | bytes 1051136 | tf_op jit(solution)/shard_map/pallas_call | solution.py:73
  12.9 1.0 %slice-done = bf16[128,512]{1,0:T(8,128)(2,1)S(1)} async-done(((bf16[128,1024]{1,0:T(8,128)(2,1)}), bf16[128,512]{1,0:T(8,128)(2,1)S(1)}, s32[]{:S(2)}) %slice-start) | async-done | bytes 131096 | tf_op jit(solution)/shard_map/slice | solution.py:359
  15.6 6.2 %all-to-all-start = ((bf16[16,16,128]{2,1,0:T(8,128)(2,1)}), bf16[16,16,128]{2,1,0:T(8,128)(2,1)S(1)}, u32[]{:S(2)}, u32[]{:S(2)}) async-start(bf16[16,16,128]{2,1,0:T(8,128)(2,1)} %broadcast_in_dim.2), calls=%async_computation | async-start | bytes 131072 | tf_op jit(solution)/shard_map/all_to_all | solution.py:343
  23.0 1.7 %collective-permute-start.7 = (bf16[288,128]{1,0:T(8,128)(2,1)S(1)}, bf16[288,128]{1,0:T(8,128)(2,1)S(1)}, u32[]{:S(2)}, u32[]{:S(2)}) collective-permute-start(bf16[288,128]{1,0:T(8,128)(2,1)S(1)} %shard_map.158.refs_0_.refs_3_), channel_id=1, source_target_pairs={{0,2},{1,3},{2,0},{3,1},{4,6},{5,7},{6,4},{7,5},{8,10},{9,11},{10,... | collective-permute-start | bytes 221192 | tf_op jit(solution)/shard_map/ppermute | solution.py:331
  24.7 4.0 %all-to-all-done.came = bf16[16,16,128]{2,1,0:T(8,128)(2,1)S(1)} async-done(((bf16[16,16,128]{2,1,0:T(8,128)(2,1)}), bf16[16,16,128]{2,1,0:T(8,128)(2,1)S(1)}, u32[]{:S(2)}, u32[]{:S(2)}) %all-to-all-start) | async-done | bytes 65568 | tf_op jit(solution)/shard_map/all_to_all | solution.py:343
  28.7 0.9 %shard_map.157 = (f32[128,256]{1,0:T(8,128)S(1)}, f32[128,512]{1,0:T(8,128)S(1)}, bf16[144,512]{1,0:T(8,128)(2,1)S(1)}, bf16[16,512]{1,0:T(8,128)(2,1)S(1)}, f32...) custom-call(bf16[16,16,128]{2,1,0:T(8,128)(2,1)S(1)} %all-to-all-done.came, f32[128,256]{1,0:T(8,128)S(1)} %get-tuple-element.36.pre, ...), custom_call_target="tpu_custom_call" | custom-call | flops 16777216 | bytes 1789952 | tf_op jit(solution)/shard_map/pallas_call | solution.py:73
  30.3 0.9 %collective-permute-done.8.refs_5_ = bf16[160,256]{1,0:T(8,128)(2,1)S(1)} collective-permute-done((bf16[160,256]{1,0:T(8,128)(2,1)S(1)}, bf16[160,256]{1,0:T(8,128)(2,1)S(1)}, u32[]{:S(2)}, u32[]{:S(2)}) %collective-permute-start.8) | collective-permute-done | bytes 81952 | tf_op jit(solution)/shard_map/ppermute | solution.py:331
  31.2 3.7 %collective-permute-done.6.refs_2_ = bf16[144,512]{1,0:T(8,128)(2,1)S(1)} collective-permute-done((bf16[144,512]{1,0:T(8,128)(2,1)S(1)}, bf16[144,512]{1,0:T(8,128)(2,1)S(1)}, u32[]{:S(2)}, u32[]{:S(2)}) %collective-permute-start.6) | collective-permute-done | bytes 147488 | tf_op jit(solution)/shard_map/ppermute | solution.py:331
  34.9 0.8 %shard_map.160 = (f32[128,512]{1,0:T(8,128)S(1)}, f32[128,1]{1,0:T(8,128)S(1)}, bf16[128,128]{1,0:T(8,128)(2,1)S(1)}, bf16[128,128]{1,0:T(8,128)(2,1)S(1)}, f32[...) custom-call(f32[128,512]{1,0:T(8,128)S(1)} %get-tuple-element.41.refs_0_, ...), custom_call_target="tpu_custom_call" | custom-call | flops 16777216 | bytes 790528 | tf_op jit(solution)/shard_map/pallas_call | solution.py:73
  35.7 1.2 %collective-permute-done.12.refs_3_ = f32[16,512]{1,0:T(8,128)S(1)} collective-permute-done((f32[16,512]{1,0:T(8,128)S(1)}, f32[16,512]{1,0:T(8,128)S(1)}, u32[]{:S(2)}, u32[]{:S(2)}) %collective-permute-start.12) | collective-permute-done | bytes 32800 | tf_op jit(solution)/shard_map/ppermute | solution.py:331
  36.9 2.3 %shard_map.161 = (bf16[16,128]{1,0:T(8,128)(2,1)}, f32[128,256]{1,0:T(8,128)S(1)}, bf16[128,256]{1,0:T(8,128)(2,1)S(1)}, bf16[128,256]{1,0:T(8,128)(2,1)S(1)}, b...) custom-call(bf16[128,1024]{1,0:T(8,128)(2,1)S(1)} %collective-permute-done.10.refs_0_, ...), custom_call_target="tpu_custom_call" | custom-call | flops 16777216 | bytes 3035648 | tf_op jit(solution)/shard_map/pallas_call | solution.py:73
  39.2 1.1 %shard_map.164 = (bf16[16,16,128]{2,1,0:T(8,128)(2,1)}, f32[64,512]{1,0:T(8,128)}) custom-call(bf16[128,256]{1,0:T(8,128)(2,1)S(1)} %get-tuple-element.63.dpre, bf16[16,256]{1,0:T(8,128)(2,1)S(1)} %get-tuple-element.64.node_dpre, bf16[64,128]{1,0:T(8,128)(2,1)S(1)} %get-tuple-element.37.pick, bf16[16,128]{1,0:T(8,128)(2,1)S(1)} %get-tuple-element.38.take.refs_7_, ...), custom_call_target="tpu_custom_call" | custom-call | flops 16777216 | bytes 1404928 | tf_op jit(solution)/shard_map/pallas_call | solution.py:73
  40.4 3.5 %all-to-all-start.1 = ((bf16[16,16,128]{2,1,0:T(8,128)(2,1)}), bf16[16,16,128]{2,1,0:T(8,128)(2,1)S(1)}, u32[]{:S(2)}, u32[]{:S(2)}) async-start(bf16[16,16,128]{2,1,0:T(8,128)(2,1)} %get-tuple-element.65), calls=%async_computation.1 | async-start | bytes 131072 | tf_op jit(solution)/shard_map/all_to_all | solution.py:415
  43.8 1.8 %collective-permute-start.14 = (bf16[128,256]{1,0:T(8,128)(2,1)S(1)}, bf16[128,256]{1,0:T(8,128)(2,1)S(1)}, u32[]{:S(2)}, u32[]{:S(2)}) collective-permute-start(bf16[128,256]{1,0:T(8,128)(2,1)S(1)} %get-tuple-element.57), channel_id=1, source_target_pairs={{0,2},{1,3},{2,0},{3,1},{4,6},{5,7},{6,4},{7,5},{8,10},{9,11},{10,... | collective-permute-start | bytes 196616 | tf_op jit(solution)/shard_map/ppermute | solution.py:331
  45.7 3.0 %collective-permute-done.14.refs_1_ = bf16[128,256]{1,0:T(8,128)(2,1)S(1)} collective-permute-done((bf16[128,256]{1,0:T(8,128)(2,1)S(1)}, bf16[128,256]{1,0:T(8,128)(2,1)S(1)}, u32[]{:S(2)}, u32[]{:S(2)}) %collective-permute-start.14) | collective-permute-done | bytes 65568 | tf_op jit(solution)/shard_map/ppermute | solution.py:331
  48.7 1.2 %collective-permute-done.15.grad_came = bf16[128,128]{1,0:T(8,128)(2,1)S(1)} collective-permute-done((bf16[128,128]{1,0:T(8,128)(2,1)S(1)}, bf16[128,128]{1,0:T(8,128)(2,1)S(1)}, u32[]{:S(2)}, u32[]{:S(2)}) %collective-permute-start.15) | collective-permute-done | bytes 32800 | tf_op jit(solution)/shard_map/ppermute | solution.py:331
  49.9 0.7 %shard_map.163 = (bf16[256,128]{1,0:T(8,128)(2,1)}, bf16[256,128]{1,0:T(8,128)(2,1)}) custom-call(bf16[128,128]{1,0:T(8,128)(2,1)S(1)} %get-tuple-element.46.next_mine, bf16[128,128]{1,0:T(8,128)(2,1)S(1)} %collective-permute-done.9.next_came, bf16[128,128]{1,0:T(8,128)(2,1)S(1)} %get-tuple-element.58.grad_mine, ...), custom_call_target="tpu_custom_call" | custom-call | flops 16777216 | bytes 131072 | tf_op jit(solution)/shard_map/pallas_call | solution.py:73
  (54 shorter events, 5.1 us)
Async XLA Ops:
  0.6 8.1 %collective-permute-start.3 = (bf16[128,1536]{1,0:T(8,128)(2,1)}, bf16[128,1536]{1,0:T(8,128)(2,1)S(1)}, u32[]{:S(2)}, u32[]{:S(2)}) collective-permute-start(bf16[128,1536]{1,0:T(8,128)(2,1)} %e_mine.1), channel_id=1, source_target_pairs={{0,1},{1,0},{2,3},{3,2},{4,5},{5,4},{6,7},{7,6},{8,9},{9,8},{10,11... | collective-permute-start | bytes 1179656 | tf_op jit(solution)/shard_map/ppermute | solution.py:331
  1.2 3.0 %collective-permute-start = (bf16[256,128]{1,0:T(8,128)(2,1)}, bf16[256,128]{1,0:T(8,128)(2,1)S(1)}, u32[]{:S(2)}, u32[]{:S(2)}) collective-permute-start(bf16[256,128]{1,0:T(8,128)(2,1)} %refs_0_.1), channel_id=1, source_target_pairs={{0,1},{1,0},{2,3},{3,2},{4,5},{5,4},{6,7},{7,6},{8,9},{9,8},{10,11... | collective-permute-start | bytes 196616 | tf_op jit(solution)/shard_map/ppermute | solution.py:331
  1.2 5.5 %collective-permute-start.1 = (bf16[256,128]{1,0:T(8,128)(2,1)}, bf16[256,128]{1,0:T(8,128)(2,1)S(1)}, u32[]{:S(2)}, u32[]{:S(2)}) collective-permute-start(bf16[256,128]{1,0:T(8,128)(2,1)} %refs_0_.1), channel_id=1, source_target_pairs={{0,2},{1,3},{2,0},{3,1},{4,6},{5,7},{6,4},{7,5},{8,10},{9,11},{10,... | collective-permute-start | bytes 196616 | tf_op jit(solution)/shard_map/ppermute | solution.py:331
  4.1 4.6 %collective-permute-start.2 = (bf16[256,128]{1,0:T(8,128)(2,1)}, bf16[256,128]{1,0:T(8,128)(2,1)S(1)}, u32[]{:S(2)}, u32[]{:S(2)}) collective-permute-start(bf16[256,128]{1,0:T(8,128)(2,1)} %refs_0_.1), channel_id=1, source_target_pairs={{0,3},{1,2},{2,1},{3,0},{4,7},{5,6},{6,5},{7,4},{8,11},{9,10},{10,... | collective-permute-start | bytes 196616 | tf_op jit(solution)/shard_map/ppermute | solution.py:331
  12.0 3.0 %copy-start.13 = (bf16[16,128]{1,0:T(8,128)(2,1)S(1)}, bf16[16,128]{1,0:T(8,128)(2,1)}, u32[]{:S(2)}) copy-start(bf16[16,128]{1,0:T(8,128)(2,1)} %param.13) | copy-start | bytes 12292
  12.9 1.5 %copy-start.2 = (bf16[128,1024]{1,0:T(8,128)(2,1)S(1)}, bf16[128,1024]{1,0:T(8,128)(2,1)}, u32[]{:S(2)}) copy-start(bf16[128,1024]{1,0:T(8,128)(2,1)} %in_mine) | copy-start | bytes 786436
  12.9 1.8 %copy-start.3 = (bf16[128,512]{1,0:T(8,128)(2,1)S(1)}, bf16[128,512]{1,0:T(8,128)(2,1)}, u32[]{:S(2)}) copy-start(bf16[128,512]{1,0:T(8,128)(2,1)} %refs_13_) | copy-start | bytes 393220
  13.9 14.7 %copy-start.1 = (bf16[128,1536]{1,0:T(8,128)(2,1)S(1)}, bf16[128,1536]{1,0:T(8,128)(2,1)}, u32[]{:S(2)}) copy-start(bf16[128,1536]{1,0:T(8,128)(2,1)} %e_mine.1) | copy-start | bytes 1179652
  13.9 8.4 %collective-permute-start.10 = (bf16[128,1024]{1,0:T(8,128)(2,1)S(1)}, bf16[128,1024]{1,0:T(8,128)(2,1)S(1)}, u32[]{:S(2)}, u32[]{:S(2)}) collective-permute-start(bf16[128,1024]{1,0:T(8,128)(2,1)S(1)} %pad_maximum_fusion), channel_id=1, source_target_pairs={{0,2},{1,3},{2,0},{3,1},{4,6},{5,7},{6,4},{7,5},{8,10},{9,11},{10,... | collective-permute-start | bytes 786440 | tf_op jit(solution)/shard_map/ppermute | solution.py:331
  14.4 14.2 %collective-permute-start.5 = (bf16[128,1024]{1,0:T(8,128)(2,1)S(1)}, bf16[128,1024]{1,0:T(8,128)(2,1)S(1)}, u32[]{:S(2)}, u32[]{:S(2)}) collective-permute-start(bf16[128,1024]{1,0:T(8,128)(2,1)S(1)} %copy-done.2), channel_id=1, source_target_pairs={{0,1},{1,0},{2,3},{3,2},{4,5},{5,4},{6,7},{7,6},{8,9},{9,8},{10,11... | collective-permute-start | bytes 786440 | tf_op jit(solution)/shard_map/ppermute | solution.py:331
  14.7 14.0 %collective-permute-start.4 = (bf16[128,512]{1,0:T(8,128)(2,1)S(1)}, bf16[128,512]{1,0:T(8,128)(2,1)S(1)}, u32[]{:S(2)}, u32[]{:S(2)}) collective-permute-start(bf16[128,512]{1,0:T(8,128)(2,1)S(1)} %copy-done.3), channel_id=1, source_target_pairs={{0,1},{1,0},{2,3},{3,2},{4,5},{5,4},{6,7},{7,6},{8,9},{9,8},{10,11... | collective-permute-start | bytes 393224 | tf_op jit(solution)/shard_map/ppermute | solution.py:331
  15.6 6.7 %copy-start.6 = (bf16[256,128]{1,0:T(8,128)(2,1)S(1)}, bf16[256,128]{1,0:T(8,128)(2,1)}, u32[]{:S(2)}) copy-start(bf16[256,128]{1,0:T(8,128)(2,1)} %edge_cot) | copy-start | bytes 196612
  15.6 6.7 %copy-start.7 = (bf16[16,128]{1,0:T(8,128)(2,1)S(1)}, bf16[16,128]{1,0:T(8,128)(2,1)}, u32[]{:S(2)}) copy-start(bf16[16,128]{1,0:T(8,128)(2,1)} %node_cot.3) | copy-start | bytes 12292
  15.6 13.1 %all-to-all-start = ((bf16[16,16,128]{2,1,0:T(8,128)(2,1)}), bf16[16,16,128]{2,1,0:T(8,128)(2,1)S(1)}, u32[]{:S(2)}, u32[]{:S(2)}) async-start(bf16[16,16,128]{2,1,0:T(8,128)(2,1)} %broadcast_in_dim.2), calls=%async_computation | async-start | bytes 131072 | tf_op jit(solution)/shard_map/all_to_all | solution.py:343
  22.3 14.6 %collective-permute-start.11 = (bf16[128,1024]{1,0:T(8,128)(2,1)S(1)}, bf16[128,1024]{1,0:T(8,128)(2,1)S(1)}, u32[]{:S(2)}, u32[]{:S(2)}) collective-permute-start(bf16[128,1024]{1,0:T(8,128)(2,1)S(1)} %collective-permute-done.10.refs_0_), channel_id=1, source_target_pairs={{0,1},{1,0},{2,3},{3,2},{4,5},{5,4},{6,7},{7,6},{8,9},{9,8},{10,11... | collective-permute-start | bytes 786440 | tf_op jit(solution)/shard_map/ppermute | solution.py:331
  23.0 6.7 %collective-permute-start.7 = (bf16[288,128]{1,0:T(8,128)(2,1)S(1)}, bf16[288,128]{1,0:T(8,128)(2,1)S(1)}, u32[]{:S(2)}, u32[]{:S(2)}) collective-permute-start(bf16[288,128]{1,0:T(8,128)(2,1)S(1)} %shard_map.158.refs_0_.refs_3_), channel_id=1, source_target_pairs={{0,2},{1,3},{2,0},{3,1},{4,6},{5,7},{6,4},{7,5},{8,10},{9,11},{10,... | collective-permute-start | bytes 221192 | tf_op jit(solution)/shard_map/ppermute | solution.py:331
  29.6 5.3 %collective-permute-start.6 = (bf16[144,512]{1,0:T(8,128)(2,1)S(1)}, bf16[144,512]{1,0:T(8,128)(2,1)S(1)}, u32[]{:S(2)}, u32[]{:S(2)}) collective-permute-start(bf16[144,512]{1,0:T(8,128)(2,1)S(1)} %get-tuple-element.43), channel_id=1, source_target_pairs={{0,2},{1,3},{2,0},{3,1},{4,6},{5,7},{6,4},{7,5},{8,10},{9,11},{10,... | collective-permute-start | bytes 442376 | tf_op jit(solution)/shard_map/ppermute | solution.py:331
  29.7 6.0 %collective-permute-start.13 = (bf16[128,512]{1,0:T(8,128)(2,1)S(1)}, bf16[128,512]{1,0:T(8,128)(2,1)S(1)}, u32[]{:S(2)}, u32[]{:S(2)}) collective-permute-start(bf16[128,512]{1,0:T(8,128)(2,1)S(1)} %copy-done.4), channel_id=1, source_target_pairs={{0,1},{1,0},{2,3},{3,2},{4,5},{5,4},{6,7},{7,6},{8,9},{9,8},{10,11... | collective-permute-start | bytes 393224 | tf_op jit(solution)/shard_map/ppermute | solution.py:331
  29.7 1.5 %collective-permute-start.8 = (bf16[160,256]{1,0:T(8,128)(2,1)S(1)}, bf16[160,256]{1,0:T(8,128)(2,1)S(1)}, u32[]{:S(2)}, u32[]{:S(2)}) collective-permute-start(bf16[160,256]{1,0:T(8,128)(2,1)S(1)} %shard_map.159), channel_id=1, source_target_pairs={{0,1},{1,0},{2,3},{3,2},{4,5},{5,4},{6,7},{7,6},{8,9},{9,8},{10,11... | collective-permute-start | bytes 245768 | tf_op jit(solution)/shard_map/ppermute | solution.py:331
  35.7 1.2 %collective-permute-start.12 = (f32[16,512]{1,0:T(8,128)S(1)}, f32[16,512]{1,0:T(8,128)S(1)}, u32[]{:S(2)}, u32[]{:S(2)}) collective-permute-start(f32[16,512]{1,0:T(8,128)S(1)} %get-tuple-element.49.refs_2_), channel_id=1, source_target_pairs={{0,1},{1,0},{2,3},{3,2},{4,5},{5,4},{6,7},{7,6},{8,9},{9,8},{10,11... | collective-permute-start | bytes 98312 | tf_op jit(solution)/shard_map/ppermute | solution.py:331
  40.4 10.4 %all-to-all-start.1 = ((bf16[16,16,128]{2,1,0:T(8,128)(2,1)}), bf16[16,16,128]{2,1,0:T(8,128)(2,1)S(1)}, u32[]{:S(2)}, u32[]{:S(2)}) async-start(bf16[16,16,128]{2,1,0:T(8,128)(2,1)} %get-tuple-element.65), calls=%async_computation.1 | async-start | bytes 131072 | tf_op jit(solution)/shard_map/all_to_all | solution.py:415
  43.8 4.8 %collective-permute-start.14 = (bf16[128,256]{1,0:T(8,128)(2,1)S(1)}, bf16[128,256]{1,0:T(8,128)(2,1)S(1)}, u32[]{:S(2)}, u32[]{:S(2)}) collective-permute-start(bf16[128,256]{1,0:T(8,128)(2,1)S(1)} %get-tuple-element.57), channel_id=1, source_target_pairs={{0,2},{1,3},{2,0},{3,1},{4,6},{5,7},{6,4},{7,5},{8,10},{9,11},{10,... | collective-permute-start | bytes 196616 | tf_op jit(solution)/shard_map/ppermute | solution.py:331
  45.7 3.1 %collective-permute-start.9 = (bf16[128,128]{1,0:T(8,128)(2,1)S(1)}, bf16[128,128]{1,0:T(8,128)(2,1)S(1)}, u32[]{:S(2)}, u32[]{:S(2)}) collective-permute-start(bf16[128,128]{1,0:T(8,128)(2,1)S(1)} %get-tuple-element.47), channel_id=1, source_target_pairs={{0,1},{1,0},{2,3},{3,2},{4,5},{5,4},{6,7},{7,6},{8,9},{9,8},{10,11... | collective-permute-start | bytes 98312 | tf_op jit(solution)/shard_map/ppermute | solution.py:331
  48.6 1.3 %collective-permute-start.15 = (bf16[128,128]{1,0:T(8,128)(2,1)S(1)}, bf16[128,128]{1,0:T(8,128)(2,1)S(1)}, u32[]{:S(2)}, u32[]{:S(2)}) collective-permute-start(bf16[128,128]{1,0:T(8,128)(2,1)S(1)} %get-tuple-element.59), channel_id=1, source_target_pairs={{0,1},{1,0},{2,3},{3,2},{4,5},{5,4},{6,7},{7,6},{8,9},{9,8},{10,11... | collective-permute-start | bytes 98312 | tf_op jit(solution)/shard_map/ppermute | solution.py:331
  (9 other events, 7.2 us)

commit v8 on v7

v8 whole, which is shorter than its diff:
```python
import functools

import jax
import jax.numpy as jnp
from jax import lax
from jax.experimental import pallas as pl
from jax.experimental.pallas import tpu as pltpu
from jax.sharding import PartitionSpec as P

epsilon = 1e-05
f32 = jnp.float32
bf16 = jnp.bfloat16
cores = 2
kernel_vmem = 8 << 20


def dot(left, right):
    return jnp.dot(left, right, preferred_element_type=f32)


def dot_rows(left, right):
    return lax.dot_general(left, right, (((1,), (1,)), ((), ())), preferred_element_type=f32)


def dot_cols(left, right):
    return lax.dot_general(left, right, (((0,), (0,)), ((), ())), preferred_element_type=f32)


def split(values):
    high = values.astype(bf16)
    return high, (values - high.astype(f32)).astype(bf16)


def sigmoid(values):
    return 1.0 / (1.0 + jnp.exp(-values))


def swish_slope(pre_act):
    sigma = sigmoid(pre_act)
    return sigma * (1.0 + pre_act * (1.0 - sigma))


def normalize(values):
    mean = jnp.mean(values, axis=1, keepdims=True)
    square = jnp.mean(values * values, axis=1, keepdims=True)
    inverse = lax.rsqrt(square - mean * mean + epsilon)
    return (values - mean) * inverse, inverse


def norm_back(grad, normed, inverse):
    total = jnp.mean(grad, axis=1, keepdims=True)
    cross = jnp.mean(grad * normed, axis=1, keepdims=True)
    return inverse * (grad - total - normed * cross)


def place():
    feat = lax.axis_index("feat")
    return feat // cores, feat % cores


def pair(mine, other, core):
    return jnp.where(core == 0, jnp.concatenate([mine, other], 1), jnp.concatenate([other, mine], 1))


def lanes(group, width):
    return pl.ds(pl.multiple_of(group * width, width), width)


def stage(kernel, outs, operands, scalars=0, scratch=(), flops=1 << 24):
    specs = [pl.BlockSpec(memory_space=pltpu.VMEM)] * (len(operands) - scalars)
    specs += [pl.BlockSpec(memory_space=pltpu.SMEM)] * scalars
    moved = sum(o.size * o.dtype.itemsize for o in operands)
    return pl.pallas_call(
        kernel,
        out_shape=[jax.ShapeDtypeStruct(shape, kind) for shape, kind in outs],
        in_specs=specs,
        out_specs=[pl.BlockSpec(memory_space=pltpu.VMEM)] * len(outs),
        scratch_shapes=[pltpu.VMEM(shape, kind) for shape, kind in scratch],
        cost_estimate=pl.CostEstimate(flops=flops, bytes_accessed=moved, transcendentals=0),
        compiler_params=pltpu.CompilerParams(vmem_limit_bytes=kernel_vmem),
    )(*operands)


def gains(gain_e, gain_n, rows):
    shape = (rows, gain_e.shape[1])
    row = lax.broadcasted_iota(jnp.int32, shape, 0)
    e = jnp.broadcast_to(gain_e[...].astype(f32), shape)
    n = jnp.broadcast_to(gain_n[...].astype(f32), shape)
    return jnp.where(row == 0, e, n).astype(bf16)


def total(refs):
    value = refs[0][...]
    for ref in refs[1:]:
        value = value + ref[...].astype(f32)
    return value


def pack_extra(edge_cot, node_cot, pack):
    edge_dev = edge_cot.shape[0]
    nodes = node_cot.shape[0]
    pack[:edge_dev] = edge_cot[...]
    pack[edge_dev:] = node_cot[...]


def join_weights(edge_in, edge_out, node_in, node_out, wall, far):
    features = node_out.shape[1]
    wall[:, : 3 * features] = edge_in[...]
    wall[:, 3 * features : 4 * features] = edge_out[...]
    wall[:, 4 * features : 6 * features] = node_in[...]
    wall[:, 6 * features :] = node_out[...]
    far[:, :features] = node_in[:, features:]
    far[:, features:] = node_out[...]


def chip_weights(walls, index, features):
    return jnp.concatenate([wall[:, index * features : (index + 1) * features] for wall in walls], axis=0)


def half_rows(pack, core, half):
    rows = pack[pl.ds(pl.multiple_of(core * half, half), half)]
    if pack.shape[0] == cores * half:
        return rows
    return jnp.concatenate([rows, pack[cores * half :]], axis=0)


def stack_tables(*refs):
    *parts, gain_e, gain_n, table = refs
    nodes = parts[0].shape[0]
    table[...] = jnp.concatenate([part[...] for part in parts] + [gains(gain_e, gain_n, nodes)], axis=0)


def join_groups(*refs):
    *parts, joined = refs
    joined[...] = jnp.concatenate([part[...] for part in parts], axis=1)


def send_half(groups, *refs):
    packs, sent = refs[:groups], refs[groups]
    _, core = place()
    width = packs[0].shape[1]
    half = packs[0].shape[0] - sent.shape[0] if packs[0].shape[0] < cores * sent.shape[0] else sent.shape[0]
    for step, pack in enumerate(packs):
        sent[:, step * width : (step + 1) * width] = half_rows(pack, 1 - core, half)


def prepare_edges(groups, *refs):
    packs = refs[:groups]
    theirs, *walls, slot, receiver, send_rows, state, pre, pick, take = refs[groups:]
    group, core = place()
    block = lax.axis_index("nodes")
    features = state.shape[1]
    nodes, half = take.shape
    width = packs[0].shape[1]
    blocks, _, slots = send_rows.shape
    for step, pack in enumerate(packs):
        both = pair(half_rows(pack, core, half), theirs[:, step * width : (step + 1) * width], core)
        state[:, lanes(group ^ step, width * cores)] = both

    slot_row = slot[pl.ds(core, 1)]
    sender = slot_row
    for source in range(blocks):
        for k in range(slots):
            row = (source ^ block) * nodes + send_rows[source, block, k]
            sender = jnp.where(slot_row == nodes + source * slots + k, row, sender)
    pick[...] = (lax.broadcasted_iota(jnp.int32, pick.shape, 0) == sender).astype(f32).astype(bf16)
    here = receiver[pl.ds(core, 1)]
    take[...] = (lax.broadcasted_iota(jnp.int32, take.shape, 0) == here).astype(f32).astype(bf16)
    pre[...] = dot_rows(state[...], chip_weights(walls, 0, features))


def finish_edges(groups, *refs):
    tables = refs[:groups]
    theirs, pre, pick, take, *walls, edge_pre, part, sent, own, lat, gain, table = refs[groups:]
    group, core = place()
    features = table.shape[1]
    nodes = own.shape[0]
    half, hidden = pre.shape
    width = tables[0].shape[1]
    for step, ours in enumerate(tables):
        both = pair(ours[...], theirs[:, step * width : (step + 1) * width], core)
        table[:, lanes(group ^ step, cores * width)] = both
    latent = table[:nodes]
    own[...] = latent
    count = table.shape[0] - nodes
    gain[...] = table[count:]

    def weight(index):
        return chip_weights(walls, index, features)

    high, low = split(dot_rows(table[:count], weight(1)))
    here_high, here_low = split(dot_rows(latent, weight(2)))
    chosen = jnp.concatenate([pick[...], pick[...], take[...], take[...]], axis=0)
    value = pre[...] + dot_cols(chosen, jnp.concatenate([high, low, here_high, here_low], axis=0))
    edge_pre[...] = value
    act = (value * sigmoid(value)).astype(bf16)
    out = dot(act, weight(3))
    part[...] = out
    sent[:half] = out.astype(bf16)
    nodes_pre = dot_rows(latent, weight(4))
    lat[...] = nodes_pre
    high, low = split(nodes_pre)
    sent[half:] = jnp.zeros((nodes, features), bf16)
    sent[half:, :hidden] = high
    sent[half:, hidden : 2 * hidden] = low


def update_edges(groups, *refs):
    part, lat, came = refs[0], refs[1], refs[2 : groups + 1]
    gain, state, take, normed, inverse, kept, lent, aggregate, lat_all, next_all = refs[groups + 1 :]
    group, core = place()
    nodes, half = take.shape
    width = kept.shape[1]
    hidden = lat.shape[1]
    value = part[...]
    lat_all[:, :hidden] = lat[...]
    for step, ref in enumerate(came, 1):
        value = value + ref[:half].astype(f32)
        high, low = ref[half:, :hidden], ref[half:, hidden : 2 * hidden]
        lat_all[:, step * hidden : (step + 1) * hidden] = high.astype(f32) + low.astype(f32)
    normed_rows, inverse_rows = normalize(value)
    normed[...] = normed_rows
    inverse[...] = inverse_rows
    rows = (state[...].astype(f32) + normed_rows * gain[...].astype(f32)[0:1]).astype(bf16)
    aggregate[...] = dot(take[...], rows)
    next_all[...] = rows
    mine = next_all[:, lanes(group, width * cores)]
    kept[...] = jnp.where(core == 0, mine[:, :width], mine[:, width:])
    lent[...] = jnp.where(core == 0, mine[:, width:], mine[:, :width])


def turn(groups, *refs):
    far, refs = refs[: 2 * (groups - 1)], refs[2 * (groups - 1) :]
    packs, refs = refs[:groups], refs[groups:]
    theirs, aggregate, aggregate2, own, lat_all, gain, take, normed, inverse, edge_pre = refs[:10]
    walls = refs[10:12]
    node_next, kept, *sents, dpre_ref, node_dpre_ref, next_all, grads, extra = refs[12:]
    group, core = place()
    nodes, half = take.shape
    features = gain.shape[1]
    hidden = edge_pre.shape[1]
    wide = kept.shape[1]
    width = node_next.shape[1]
    gain_rows = gain[...].astype(f32)
    edge_gain, node_gain = gain_rows[0:1], gain_rows[1:2]
    for step, pack in enumerate(packs):
        both = pair(half_rows(pack, core, half), theirs[:, step * width : (step + 1) * width], core)
        extra[:, lanes(group ^ step, wide)] = both

    from_agg = jnp.concatenate([chip_weights(walls, 5, features)] + [f[:, :features] for f in far], axis=0)
    to_out = jnp.concatenate([chip_weights(walls, 6, features)] + [f[:, features:] for f in far], axis=0)
    together = (aggregate[...] + aggregate2[...]).astype(bf16)
    pre = lat_all[...] + dot_rows(together, from_agg)
    act = (pre * sigmoid(pre)).astype(bf16)
    node_normed, node_inverse = normalize(dot(act, to_out))
    next_all[...] = (own[...].astype(f32) + node_normed * node_gain).astype(bf16)
    mine = next_all[:, lanes(group, wide)]
    node_next[...] = jnp.where(core == 0, mine[:, :width], mine[:, width:])
    cot = extra[half:].astype(f32)
    node_dy = norm_back(cot * node_gain, node_normed, node_inverse).astype(bf16)
    node_dpre = (dot_rows(node_dy, to_out) * swish_slope(pre)).astype(bf16)
    high, low = split(dot(node_dpre, from_agg))

    taken = take[...]
    edge_total = extra[:half].astype(f32) + dot_cols(
        jnp.concatenate([taken, taken], axis=0), jnp.concatenate([high, low], axis=0)
    )
    dy = norm_back(edge_total * edge_gain, normed[...], inverse[...]).astype(bf16)
    back = dot_rows(dy, chip_weights(walls, 3, features))
    dpre = (back * swish_slope(edge_pre[...])).astype(bf16)

    dpre_ref[...] = dpre
    node_dpre_ref[...] = node_dpre[:, :hidden]
    grads[...] = dot(dpre, chip_weights(walls, 0, features))
    for step, sent in enumerate(sents, 1):
        sent[...] = grads[:, lanes(group ^ step, wide)].astype(bf16)
    grads[...] += edge_total
    kept[...] = grads[:, lanes(group, wide)]


def spread_nodes(dpre, node_dpre, pick, take, *refs):
    *walls, spread, grads = refs
    block = lax.axis_index("nodes")
    count, nodes, width = spread.shape
    features = grads.shape[1]
    feats = features // width

    def weighted(values, index):
        both = dot(jnp.concatenate(split(values), axis=0), chip_weights(walls, index, features))
        return both[: values.shape[0]] + both[values.shape[0] :]

    grads[...] = weighted(dot(pick[...], dpre[...]), 1)
    home = weighted(dot(take[...], dpre[...]), 2)
    home = home + 0.5 * dot(node_dpre[...], chip_weights(walls, 4, features))
    grads[:nodes] += home
    for target in range(count):
        first = pl.multiple_of((target // feats ^ block) * nodes, nodes)
        column = target % feats * width
        spread[target] = grads[pl.ds(first, nodes), column : column + width].astype(bf16)


def add_groups(groups, *refs):
    parts, (kept, sent) = refs[:groups], refs[groups:]
    _, core = place()
    width = kept.shape[1]
    value = total(parts)
    kept[...] = jnp.where(core == 0, value[:, :width], value[:, width:]).astype(bf16)
    sent[...] = jnp.where(core == 0, value[:, width:], value[:, :width]).astype(bf16)


def add_nodes(shares, node_cot, node_grad):
    value = node_cot[...].astype(f32)
    for source in range(shares.shape[0]):
        value = value + shares[source].astype(f32)
    node_grad[...] = value.astype(bf16)


def assemble(next_mine, next_came, grad_mine, grad_came, edge_next, edge_grad):
    _, core = place()
    half = next_mine.shape[0]
    mine = pl.ds(pl.multiple_of(core * half, half), half)
    theirs = pl.ds(pl.multiple_of((1 - core) * half, half), half)
    edge_next[mine] = next_mine[...]
    edge_next[theirs] = next_came[...]
    edge_grad[mine] = grad_mine[...]
    edge_grad[theirs] = grad_came[...]


def shards(
    latent,
    edge_state,
    send_rows,
    sender_slot,
    receiver_row,
    edge_in_weight,
    edge_out_weight,
    edge_gain,
    node_in_weight,
    node_out_weight,
    node_gain,
    edge_cot,
    node_cot,
):
    nodes, width = latent.shape
    edge_dev = edge_state.shape[0]
    half = edge_dev // cores
    blocks = send_rows.shape[0]
    feats = lax.axis_size("feat")
    groups = feats // cores
    features = width * feats
    wide = width * cores
    hidden = edge_in_weight.shape[0] * cores
    table = blocks * nodes
    everyone = ("nodes", "feat")

    def swapped(values, bits):
        return lax.ppermute(values, "feat", [(i, i ^ bits) for i in range(feats)])

    def over_cores(values):
        return swapped(values, 1)

    def over_groups(values):
        return [swapped(values, cores * step) for step in range(1, groups)]

    gain_e, gain_n = edge_gain.reshape(1, width), node_gain.reshape(1, width)
    slot_rows = sender_slot.reshape(cores, half)
    receiver_rows = receiver_row.reshape(cores, half)

    def over_nodes(values, step):
        return lax.ppermute(values, "nodes", [(i, i ^ step) for i in range(blocks)])

    hid = edge_in_weight.shape[0]
    tables = [over_nodes(latent, step) for step in range(1, blocks)]
    states = over_groups(edge_state)
    wall, far = stage(
        join_weights,
        [((hid, 7 * features), bf16), ((hid, 2 * features), bf16)],
        [edge_in_weight, edge_out_weight, node_in_weight, node_out_weight],
    )
    far = over_groups(far)
    walls = [wall, over_cores(wall)]
    tables, states = lax.optimization_barrier((tables, states))
    (mine,) = stage(stack_tables, [((table + nodes, width), bf16)], [latent, *tables, gain_e, gain_n])
    tables = [mine] + over_groups(mine)
    states = [edge_state] + states
    (sent,) = stage(functools.partial(send_half, groups), [((half, groups * width), bf16)], states)
    state, pre, pick, take = stage(
        functools.partial(prepare_edges, groups),
        [((half, features), bf16), ((half, hidden), f32), ((table, half), bf16), ((nodes, half), bf16)],
        [*states, over_cores(sent), *walls, slot_rows, receiver_rows, send_rows],
        scalars=1,
    )
    (joined,) = stage(join_groups, [((table + nodes, groups * width), bf16)], tables)
    edge_pre, part, sent, own, lat, gain = stage(
        functools.partial(finish_edges, groups),
        [
            ((half, hidden), f32),
            ((half, features), f32),
            ((half + nodes, features), bf16),
            ((nodes, features), bf16),
            ((nodes, hidden), f32),
            ((nodes, features), bf16),
        ],
        [*tables, over_cores(joined), pre, pick, take, *walls],
        scratch=[((table + nodes, features), bf16)],
    )
    sent, edge_cot, far = lax.optimization_barrier((sent, edge_cot, far))
    far = [weights for came in far for weights in (came, over_cores(came))]
    (pack,) = stage(pack_extra, [((edge_dev + nodes, width), bf16)], [edge_cot, node_cot])
    packs = [pack] + over_groups(pack)
    (extra_sent,) = stage(
        functools.partial(send_half, groups), [((half + nodes, groups * width), bf16)], packs
    )
    extra_came = over_cores(extra_sent)
    normed, inverse, next_mine, next_sent, aggregate, lat_all = stage(
        functools.partial(update_edges, groups),
        [
            ((half, features), f32),
            ((half, 1), f32),
            ((half, width), bf16),
            ((half, width), bf16),
            ((nodes, features), f32),
            ((nodes, features), f32),
        ],
        [part, lat, *over_groups(sent), gain, state, take],
        scratch=[((half, features), bf16)],
    )
    aggregate2 = over_cores(aggregate)
    next_came = over_cores(next_sent)
    node_next, kept, *sents, dpre, node_dpre = stage(
        functools.partial(turn, groups),
        [((nodes, width), bf16), ((half, wide), f32)]
        + [((half, wide), bf16)] * (groups - 1)
        + [((half, hidden), bf16), ((nodes, hidden), bf16)],
        [*far, *packs, extra_came, aggregate, aggregate2, own, lat_all, gain, take, normed, inverse, edge_pre]
        + walls,
        scratch=[((nodes, features), bf16), ((half, features), f32), ((half + nodes, features), bf16)],
    )
    sents = [swapped(s, cores * k) for k, s in enumerate(sents, 1)]
    (spread,) = stage(
        spread_nodes,
        [((blocks * feats, nodes, width), bf16)],
        [dpre, node_dpre, pick, take, *walls],
        scratch=[((table, features), f32)],
    )
    shares = lax.all_to_all(spread, everyone, 0, 0)
    grad_mine, grad_sent = stage(
        functools.partial(add_groups, groups),
        [((half, width), bf16), ((half, width), bf16)],
        [kept, *sents],
    )
    edge_next, edge_grad = stage(
        assemble,
        [((edge_dev, width), bf16), ((edge_dev, width), bf16)],
        [next_mine, next_came, grad_mine, over_cores(grad_sent)],
    )
    (node_grad,) = stage(add_nodes, [((nodes, width), bf16)], [shares, node_cot])
    return (edge_next, node_next, edge_grad, node_grad)


def solution(mesh):
    rows = P(("groups", "nodes"), "feat")
    flat = P(("groups", "nodes"))
    matrix = P("feat", None)
    vector = P("feat")
    return jax.shard_map(
        shards,
        mesh=mesh,
        in_specs=(
            rows,
            rows,
            P("groups", None, None),
            flat,
            flat,
            matrix,
            matrix,
            vector,
            matrix,
            matrix,
            vector,
            rows,
            rows,
        ),
        out_specs=(rows, rows, rows, rows),
        check_vma=False,
    )
```

time: 51.8 us -> 51.5 us (level)
  starting transfers between devices: 18.4 us -> 24.1 us
  waiting for transfers between devices: 19.2 us -> 14.8 us
  Pallas kernels: 7.38 us -> 6.32 us
    ppermute x0 -> x3, starting transfers between devices: none -> 7.77 us  [over_nodes(): return lax.ppermute(values, 'nodes', [(i, i ^ step) for i in range(blocks)])]
    all_to_all x1 -> x0, starting transfers between devices: 6.16 us -> none  [shards(): lax.all_to_all(jnp.broadcast_to(latent[None], (blocks * feats, nodes, wid...]
    all_to_all x1 -> x0, waiting for transfers between devices: 3.99 us -> none  [shards(): lax.all_to_all(jnp.broadcast_to(latent[None], (blocks * feats, nodes, wid...]
    ppermute x16 -> x14, waiting for transfers between devices: 15.1 us -> 12.6 us  [swapped(): return lax.ppermute(values, 'feat', [(i, i ^ bits) for i in range(feats)])]
    all_to_all x1, starting transfers between devices: 3.49 us -> 5.83 us  [shards(): shares = lax.all_to_all(spread, everyone, 0, 0)]
    ppermute x0 -> x3, waiting for transfers between devices: none -> 2.14 us  [over_nodes(): return lax.ppermute(values, 'nodes', [(i, i ^ step) for i in range(blocks)])]
    ppermute x16 -> x14, starting transfers between devices: 8.75 us -> 10.5 us  [swapped(): return lax.ppermute(values, 'feat', [(i, i ^ bits) for i in range(feats)])]
    unnamed x28 -> x26, local copies, waits for them, and re-layouts: 3.91 us -> 5.1 us
  transfers between devices with their start and end apart: 18 -> 18, of which waited for: 10 -> 8; matrix products, arithmetic and copies ran while one was open for 1% -> 0% of each run, Pallas kernels for 5% -> 5%
where the time goes in v8:
time: 51.5 us; the launch traced here: 51.2 us
  starting transfers between devices  24.1 us (47%)
  waiting for transfers between devices  14.8 us (29%)
  Pallas kernels  6.32 us (12%)
  local copies, waits for them, and re-layouts  5.1 us (10%)
  between operations  0.83 us (2%)
    ppermute x14, waiting for transfers between devices, swapped(): return lax.ppermute(values, 'feat', [(i, i ^ bits) for i in range(feats)])  12.6 us
    ppermute x14, starting transfers between devices, swapped(): return lax.ppermute(values, 'feat', [(i, i ^ bits) for i in range(feats)])  10.5 us
    ppermute x3, starting transfers between devices, over_nodes(): return lax.ppermute(values, 'nodes', [(i, i ^ step) for i in range(blocks)])  7.77 us
    pallas_call x14, Pallas kernels, stage(): pl.pallas_call(kernel, out_shape=[jax.ShapeDtypeStruct(shape, kind) for s...  6.32 us
    all_to_all x1, starting transfers between devices, shards(): shares = lax.all_to_all(spread, everyone, 0, 0)  5.83 us
    unnamed x26, local copies, waits for them, and re-layouts  5.1 us
    ppermute x3, waiting for transfers between devices, over_nodes(): return lax.ppermute(values, 'nodes', [(i, i ^ step) for i in range(blocks)])  2.14 us
  transfers between devices with their start and end apart: 18, of which 8 were waited for; matrix products, arithmetic and copies ran while one was open for 0% of the time, Pallas kernels for 5%

profile of v8, /device:TPU:0, one launch (start us, length us, event | category | flops | bytes accessed | tf_op | source)
XLA Modules:
  0.0 51.2 jit_solution(9457244486245594689)
XLA Ops:
  0.6 1.0 %copy-done = bf16[128,1536]{1,0:T(8,128)(2,1)S(1)} copy-done((bf16[128,1536]{1,0:T(8,128)(2,1)S(1)}, bf16[128,1536]{1,0:T(8,128)(2,1)}, u32[]{:S(2)}) %copy-start) | copy-done | bytes 393240
  1.6 0.9 %copy-done.1 = bf16[128,1024]{1,0:T(8,128)(2,1)S(1)} copy-done((bf16[128,1024]{1,0:T(8,128)(2,1)S(1)}, bf16[128,1024]{1,0:T(8,128)(2,1)}, u32[]{:S(2)}) %copy-start.1) | copy-done | bytes 262168
  2.6 0.9 %copy-done.3 = bf16[128,512]{1,0:T(8,128)(2,1)S(1)} copy-done((bf16[128,512]{1,0:T(8,128)(2,1)S(1)}, bf16[128,512]{1,0:T(8,128)(2,1)}, u32[]{:S(2)}) %copy-start.3) | copy-done | bytes 131096
  3.5 0.9 %copy-done.4 = bf16[128,512]{1,0:T(8,128)(2,1)S(1)} copy-done((bf16[128,512]{1,0:T(8,128)(2,1)S(1)}, bf16[128,512]{1,0:T(8,128)(2,1)}, u32[]{:S(2)}) %copy-start.4) | copy-done | bytes 131096
  5.0 2.6 %collective-permute-start.8 = (bf16[128,1024]{1,0:T(8,128)(2,1)S(1)}, bf16[128,1024]{1,0:T(8,128)(2,1)S(1)}, u32[]{:S(2)}, u32[]{:S(2)}) collective-permute-start(bf16[128,1024]{1,0:T(8,128)(2,1)S(1)} %get-tuple-element.49), channel_id=1, source_target_pairs={{0,2},{1,3},{2,0},{3,1},{4,6},{5,7},{6,4},{7,5},{8,10},{9,11},{10,... | collective-permute-start | bytes 786440 | tf_op jit(solution)/shard_map/ppermute | solution.py:357
  8.2 2.6 %collective-permute-start.1 = (bf16[16,128]{1,0:T(8,128)(2,1)S(1)}, bf16[16,128]{1,0:T(8,128)(2,1)S(1)}, u32[]{:S(2)}, u32[]{:S(2)}) collective-permute-start(bf16[16,128]{1,0:T(8,128)(2,1)S(1)} %copy-done.10), channel_id=1, source_target_pairs={{0,8},{4,12},{8,0},{12,4},{1,9},{5,13},{9,1},{13,5},{2,10},{6,14},... | collective-permute-start | bytes 12296 | tf_op jit(solution)/shard_map/ppermute | solution.py:370
  10.8 1.6 %collective-permute-start = (bf16[16,128]{1,0:T(8,128)(2,1)S(1)}, bf16[16,128]{1,0:T(8,128)(2,1)S(1)}, u32[]{:S(2)}, u32[]{:S(2)}) collective-permute-start(bf16[16,128]{1,0:T(8,128)(2,1)S(1)} %copy-done.10), channel_id=1, source_target_pairs={{0,4},{4,0},{8,12},{12,8},{1,5},{5,1},{9,13},{13,9},{2,6},{6,2},{1... | collective-permute-start | bytes 12296 | tf_op jit(solution)/shard_map/ppermute | solution.py:370
  12.7 3.6 %collective-permute-start.2 = (bf16[16,128]{1,0:T(8,128)(2,1)S(1)}, bf16[16,128]{1,0:T(8,128)(2,1)S(1)}, u32[]{:S(2)}, u32[]{:S(2)}) collective-permute-start(bf16[16,128]{1,0:T(8,128)(2,1)S(1)} %copy-done.10), channel_id=1, source_target_pairs={{0,12},{4,8},{8,4},{12,0},{1,13},{5,9},{9,5},{13,1},{2,14},{6,10},... | collective-permute-start | bytes 12296 | tf_op jit(solution)/shard_map/ppermute | solution.py:370
  16.3 1.8 %collective-permute-done.2.refs_3_ = bf16[16,128]{1,0:T(8,128)(2,1)S(1)} collective-permute-done((bf16[16,128]{1,0:T(8,128)(2,1)S(1)}, bf16[16,128]{1,0:T(8,128)(2,1)S(1)}, u32[]{:S(2)}, u32[]{:S(2)}) %collective-permute-start.2) | collective-permute-done | bytes 4128 | tf_op jit(solution)/shard_map/ppermute | solution.py:370
  18.2 0.6 %copy-done.11 = bf16[128]{0:T(256)(128)(2,1)S(1)} copy-done((bf16[128]{0:T(256)(128)(2,1)S(1)}, bf16[128]{0:T(256)(128)(2,1)}, u32[]{:S(2)}) %copy-start.11) | copy-done | bytes 280
  18.9 1.5 %collective-permute-start.4 = (bf16[80,128]{1,0:T(8,128)(2,1)S(1)}, bf16[80,128]{1,0:T(8,128)(2,1)S(1)}, u32[]{:S(2)}, u32[]{:S(2)}) collective-permute-start(bf16[80,128]{1,0:T(8,128)(2,1)S(1)} %shard_map.156.refs_0_), channel_id=1, source_target_pairs={{0,2},{1,3},{2,0},{3,1},{4,6},{5,7},{6,4},{7,5},{8,10},{9,11},{10,... | collective-permute-start | bytes 61448 | tf_op jit(solution)/shard_map/ppermute | solution.py:357
  20.4 2.4 %collective-permute-done.4.refs_1_ = bf16[80,128]{1,0:T(8,128)(2,1)S(1)} collective-permute-done((bf16[80,128]{1,0:T(8,128)(2,1)S(1)}, bf16[80,128]{1,0:T(8,128)(2,1)S(1)}, u32[]{:S(2)}, u32[]{:S(2)}) %collective-permute-start.4) | collective-permute-done | bytes 20512 | tf_op jit(solution)/shard_map/ppermute | solution.py:357
  23.5 0.9 %shard_map.160 = (bf16[128,512]{1,0:T(8,128)(2,1)S(1)}, f32[128,256]{1,0:T(8,128)S(1)}, bf16[64,128]{1,0:T(8,128)(2,1)S(1)}, bf16[16,128]{1,0:T(8,128)(2,1)S(1)}) custom-call(bf16[256,128]{1,0:T(8,128)(2,1)S(1)} %copy-done.2, bf16[256,128]{1,0:T(8,128)(2,1)S(1)} %collective-permute-done.3.refs_1_, bf16[128,256]{1,0:T(8,128)(2,1)S(1)} %collective-permute-done.6.refs_2_, ...), custom_call_target="tpu_custom_call" | custom-call | flops 16777216 | bytes 2034176 | tf_op jit(solution)/shard_map/pallas_call | solution.py:73
  24.4 0.6 %shard_map.161 = (f32[128,256]{1,0:T(8,128)S(1)}, f32[128,512]{1,0:T(8,128)S(1)}, bf16[144,512]{1,0:T(8,128)(2,1)S(1)}, bf16[16,512]{1,0:T(8,128)(2,1)S(1)}, f32...) custom-call(bf16[80,128]{1,0:T(8,128)(2,1)S(1)} %shard_map.156.refs_0_, ...), custom_call_target="tpu_custom_call" | custom-call | flops 16777216 | bytes 2068480 | tf_op jit(solution)/shard_map/pallas_call | solution.py:73
  25.6 1.4 %collective-permute-start.9 = (bf16[144,512]{1,0:T(8,128)(2,1)S(1)}, bf16[144,512]{1,0:T(8,128)(2,1)S(1)}, u32[]{:S(2)}, u32[]{:S(2)}) collective-permute-start(bf16[144,512]{1,0:T(8,128)(2,1)S(1)} %get-tuple-element.50), channel_id=1, source_target_pairs={{0,2},{1,3},{2,0},{3,1},{4,6},{5,7},{6,4},{7,5},{8,10},{9,11},{10,... | collective-permute-start | bytes 442376 | tf_op jit(solution)/shard_map/ppermute | solution.py:357
  27.1 0.7 %collective-permute-start.12 = (bf16[272,128]{1,0:T(8,128)(2,1)S(1)}, bf16[272,128]{1,0:T(8,128)(2,1)S(1)}, u32[]{:S(2)}, u32[]{:S(2)}) collective-permute-start(bf16[272,128]{1,0:T(8,128)(2,1)S(1)} %shard_map.163.refs_0_.refs_2_), channel_id=1, source_target_pairs={{0,2},{1,3},{2,0},{3,1},{4,6},{5,7},{6,4},{7,5},{8,10},{9,11},{10,... | collective-permute-start | bytes 208904 | tf_op jit(solution)/shard_map/ppermute | solution.py:357
  27.7 5.2 %collective-permute-done.12.refs_1_.refs_3_ = bf16[272,128]{1,0:T(8,128)(2,1)S(1)} collective-permute-done((bf16[272,128]{1,0:T(8,128)(2,1)S(1)}, bf16[272,128]{1,0:T(8,128)(2,1)S(1)}, u32[]{:S(2)}, u32[]{:S(2)}) %collective-permute-start.12) | collective-permute-done | bytes 69664 | tf_op jit(solution)/shard_map/ppermute | solution.py:357
  34.7 2.0 %shard_map.165 = (bf16[16,128]{1,0:T(8,128)(2,1)}, f32[128,256]{1,0:T(8,128)S(1)}, bf16[128,256]{1,0:T(8,128)(2,1)S(1)}, bf16[128,256]{1,0:T(8,128)(2,1)S(1)}, bf16[16,256]{1,0:T(8,128)(2,1)S(1)}) custom-call(bf16[128,1024]{1,0:T(8,128)(2,1)S(1)} %collective-permute-done.8.refs_0_, bf16[128,1024]{1,0:T(8,128)(2,1)S(1)} %collective-permute-done.11.refs_1_, ...), custom_call_target="tpu_custom_call" | custom-call | flops 16777216 | bytes 3101184 | tf_op jit(solution)/shard_map/pallas_call | solution.py:73
  36.7 1.1 %shard_map.168 = bf16[16,16,128]{2,1,0:T(8,128)(2,1)} custom-call(bf16[128,256]{1,0:T(8,128)(2,1)S(1)} %get-tuple-element.70.dpre, bf16[16,256]{1,0:T(8,128)(2,1)S(1)} %get-tuple-element.71.node_dpre, bf16[64,128]{1,0:T(8,128)(2,1)S(1)} %get-tuple-element.44.refs_4_.pick, bf16[16,128]{1,0:T(8,128)(2,1)S(1)} %get-tuple-element.45.refs_5_.refs_10_.take, ...), custom_call_target="tpu_custom_call" | custom-call | flops 16777216 | bytes 1929216 | tf_op jit(solution)/shard_map/pallas_call | solution.py:73
  37.8 5.8 %all-to-all-start = ((bf16[16,16,128]{2,1,0:T(8,128)(2,1)}), bf16[16,16,128]{2,1,0:T(8,128)(2,1)S(1)}, u32[]{:S(2)}, u32[]{:S(2)}) async-start(bf16[16,16,128]{2,1,0:T(8,128)(2,1)} %shard_map.168), calls=%async_computation | async-start | bytes 131072 | tf_op jit(solution)/shard_map/all_to_all | solution.py:446
  43.6 1.9 %collective-permute-start.15 = (bf16[128,256]{1,0:T(8,128)(2,1)S(1)}, bf16[128,256]{1,0:T(8,128)(2,1)S(1)}, u32[]{:S(2)}, u32[]{:S(2)}) collective-permute-start(bf16[128,256]{1,0:T(8,128)(2,1)S(1)} %get-tuple-element.64), channel_id=1, source_target_pairs={{0,2},{1,3},{2,0},{3,1},{4,6},{5,7},{6,4},{7,5},{8,10},{9,11},{10,... | collective-permute-start | bytes 196616 | tf_op jit(solution)/shard_map/ppermute | solution.py:357
  45.6 3.0 %collective-permute-done.15.refs_1_ = bf16[128,256]{1,0:T(8,128)(2,1)S(1)} collective-permute-done((bf16[128,256]{1,0:T(8,128)(2,1)S(1)}, bf16[128,256]{1,0:T(8,128)(2,1)S(1)}, u32[]{:S(2)}, u32[]{:S(2)}) %collective-permute-start.15) | collective-permute-done | bytes 65568 | tf_op jit(solution)/shard_map/ppermute | solution.py:357
  48.6 1.2 %collective-permute-done.16.grad_came = bf16[128,128]{1,0:T(8,128)(2,1)S(1)} collective-permute-done((bf16[128,128]{1,0:T(8,128)(2,1)S(1)}, bf16[128,128]{1,0:T(8,128)(2,1)S(1)}, u32[]{:S(2)}, u32[]{:S(2)}) %collective-permute-start.16) | collective-permute-done | bytes 32800 | tf_op jit(solution)/shard_map/ppermute | solution.py:357
  49.8 0.7 %shard_map.167 = (bf16[256,128]{1,0:T(8,128)(2,1)}, bf16[256,128]{1,0:T(8,128)(2,1)}) custom-call(bf16[128,128]{1,0:T(8,128)(2,1)S(1)} %get-tuple-element.53.next_mine, bf16[128,128]{1,0:T(8,128)(2,1)S(1)} %collective-permute-done.10.next_came, bf16[128,128]{1,0:T(8,128)(2,1)S(1)} %get-tuple-element.65.grad_mine, ...), custom_call_target="tpu_custom_call" | custom-call | flops 16777216 | bytes 131072 | tf_op jit(solution)/shard_map/pallas_call | solution.py:73
  (52 shorter events, 5.5 us)
Async XLA Ops:
  0.6 1.0 %copy-start = (bf16[128,1536]{1,0:T(8,128)(2,1)S(1)}, bf16[128,1536]{1,0:T(8,128)(2,1)}, u32[]{:S(2)}) copy-start(bf16[128,1536]{1,0:T(8,128)(2,1)} %edge_in.1) | copy-start | bytes 1179652
  1.6 0.9 %copy-start.1 = (bf16[128,1024]{1,0:T(8,128)(2,1)S(1)}, bf16[128,1024]{1,0:T(8,128)(2,1)}, u32[]{:S(2)}) copy-start(bf16[128,1024]{1,0:T(8,128)(2,1)} %node_in.1) | copy-start | bytes 786436
  4.4 3.2 %copy-start.2 = (bf16[256,128]{1,0:T(8,128)(2,1)S(1)}, bf16[256,128]{1,0:T(8,128)(2,1)}, u32[]{:S(2)}) copy-start(bf16[256,128]{1,0:T(8,128)(2,1)} %refs_0_.5) | copy-start | bytes 196612
  4.4 3.8 %copy-start.10 = (bf16[16,128]{1,0:T(8,128)(2,1)S(1)}, bf16[16,128]{1,0:T(8,128)(2,1)}, u32[]{:S(2)}) copy-start(bf16[16,128]{1,0:T(8,128)(2,1)} %refs_0_.3) | copy-start | bytes 12292
  4.5 18.3 %collective-permute-start.7 = (bf16[128,3584]{1,0:T(8,128)(2,1)S(1)}, bf16[128,3584]{1,0:T(8,128)(2,1)S(1)}, u32[]{:S(2)}, u32[]{:S(2)}) collective-permute-start(bf16[128,3584]{1,0:T(8,128)(2,1)S(1)} %get-tuple-element.42.refs_3_.refs_6_.refs_14_.refs_0_), channel_id=1, source_target_pairs={{0,1},{1,0},{2,3},{3,2},{4,5},{5,4},{6,7},{7,6},{8,9},{9,8},{10,11... | collective-permute-start | bytes 2752520 | tf_op jit(solution)/shard_map/ppermute | solution.py:357
  5.0 20.1 %collective-permute-start.8 = (bf16[128,1024]{1,0:T(8,128)(2,1)S(1)}, bf16[128,1024]{1,0:T(8,128)(2,1)S(1)}, u32[]{:S(2)}, u32[]{:S(2)}) collective-permute-start(bf16[128,1024]{1,0:T(8,128)(2,1)S(1)} %get-tuple-element.49), channel_id=1, source_target_pairs={{0,2},{1,3},{2,0},{3,1},{4,6},{5,7},{6,4},{7,5},{8,10},{9,11},{10,... | collective-permute-start | bytes 786440 | tf_op jit(solution)/shard_map/ppermute | solution.py:357
  7.6 10.5 %collective-permute-start.3 = (bf16[256,128]{1,0:T(8,128)(2,1)S(1)}, bf16[256,128]{1,0:T(8,128)(2,1)S(1)}, u32[]{:S(2)}, u32[]{:S(2)}) collective-permute-start(bf16[256,128]{1,0:T(8,128)(2,1)S(1)} %copy-done.2), channel_id=1, source_target_pairs={{0,2},{1,3},{2,0},{3,1},{4,6},{5,7},{6,4},{7,5},{8,10},{9,11},{10,... | collective-permute-start | bytes 196616 | tf_op jit(solution)/shard_map/ppermute | solution.py:357
  8.2 4.5 %collective-permute-start.1 = (bf16[16,128]{1,0:T(8,128)(2,1)S(1)}, bf16[16,128]{1,0:T(8,128)(2,1)S(1)}, u32[]{:S(2)}, u32[]{:S(2)}) collective-permute-start(bf16[16,128]{1,0:T(8,128)(2,1)S(1)} %copy-done.10), channel_id=1, source_target_pairs={{0,8},{4,12},{8,0},{12,4},{1,9},{5,13},{9,1},{13,5},{2,10},{6,14},... | collective-permute-start | bytes 12296 | tf_op jit(solution)/shard_map/ppermute | solution.py:370
  10.8 5.5 %collective-permute-start = (bf16[16,128]{1,0:T(8,128)(2,1)S(1)}, bf16[16,128]{1,0:T(8,128)(2,1)S(1)}, u32[]{:S(2)}, u32[]{:S(2)}) collective-permute-start(bf16[16,128]{1,0:T(8,128)(2,1)S(1)} %copy-done.10), channel_id=1, source_target_pairs={{0,4},{4,0},{8,12},{12,8},{1,5},{5,1},{9,13},{13,9},{2,6},{6,2},{1... | collective-permute-start | bytes 12296 | tf_op jit(solution)/shard_map/ppermute | solution.py:370
  12.7 5.4 %collective-permute-start.2 = (bf16[16,128]{1,0:T(8,128)(2,1)S(1)}, bf16[16,128]{1,0:T(8,128)(2,1)S(1)}, u32[]{:S(2)}, u32[]{:S(2)}) collective-permute-start(bf16[16,128]{1,0:T(8,128)(2,1)S(1)} %copy-done.10), channel_id=1, source_target_pairs={{0,12},{4,8},{8,4},{12,0},{1,13},{5,9},{9,5},{13,1},{2,14},{6,10},... | collective-permute-start | bytes 12296 | tf_op jit(solution)/shard_map/ppermute | solution.py:370
  18.1 4.7 %collective-permute-start.6 = (bf16[128,256]{1,0:T(8,128)(2,1)S(1)}, bf16[128,256]{1,0:T(8,128)(2,1)S(1)}, u32[]{:S(2)}, u32[]{:S(2)}) collective-permute-start(bf16[128,256]{1,0:T(8,128)(2,1)S(1)} %shard_map.158), channel_id=1, source_target_pairs={{0,1},{1,0},{2,3},{3,2},{4,5},{5,4},{6,7},{7,6},{8,9},{9,8},{10,11... | collective-permute-start | bytes 196616 | tf_op jit(solution)/shard_map/ppermute | solution.py:357
  18.9 3.8 %collective-permute-start.4 = (bf16[80,128]{1,0:T(8,128)(2,1)S(1)}, bf16[80,128]{1,0:T(8,128)(2,1)S(1)}, u32[]{:S(2)}, u32[]{:S(2)}) collective-permute-start(bf16[80,128]{1,0:T(8,128)(2,1)S(1)} %shard_map.156.refs_0_), channel_id=1, source_target_pairs={{0,2},{1,3},{2,0},{3,1},{4,6},{5,7},{6,4},{7,5},{8,10},{9,11},{10,... | collective-permute-start | bytes 61448 | tf_op jit(solution)/shard_map/ppermute | solution.py:357
  22.7 1.7 %collective-permute-start.5 = (bf16[80,256]{1,0:T(8,128)(2,1)S(1)}, bf16[80,256]{1,0:T(8,128)(2,1)S(1)}, u32[]{:S(2)}, u32[]{:S(2)}) collective-permute-start(bf16[80,256]{1,0:T(8,128)(2,1)S(1)} %shard_map.157), channel_id=1, source_target_pairs={{0,1},{1,0},{2,3},{3,2},{4,5},{5,4},{6,7},{7,6},{8,9},{9,8},{10,11... | collective-permute-start | bytes 122888 | tf_op jit(solution)/shard_map/ppermute | solution.py:357
  24.4 2.6 %copy-start.5 = (bf16[256,128]{1,0:T(8,128)(2,1)S(1)}, bf16[256,128]{1,0:T(8,128)(2,1)}, u32[]{:S(2)}) copy-start(bf16[256,128]{1,0:T(8,128)(2,1)} %edge_cot) | copy-start | bytes 196612
  24.4 2.6 %copy-start.6 = (bf16[16,128]{1,0:T(8,128)(2,1)S(1)}, bf16[16,128]{1,0:T(8,128)(2,1)}, u32[]{:S(2)}) copy-start(bf16[16,128]{1,0:T(8,128)(2,1)} %node_cot.3) | copy-start | bytes 12292
  25.1 9.6 %collective-permute-start.11 = (bf16[128,1024]{1,0:T(8,128)(2,1)S(1)}, bf16[128,1024]{1,0:T(8,128)(2,1)S(1)}, u32[]{:S(2)}, u32[]{:S(2)}) collective-permute-start(bf16[128,1024]{1,0:T(8,128)(2,1)S(1)} %collective-permute-done.8.refs_0_), channel_id=1, source_target_pairs={{0,1},{1,0},{2,3},{3,2},{4,5},{5,4},{6,7},{7,6},{8,9},{9,8},{10,11... | collective-permute-start | bytes 786440 | tf_op jit(solution)/shard_map/ppermute | solution.py:357
  25.6 7.4 %collective-permute-start.9 = (bf16[144,512]{1,0:T(8,128)(2,1)S(1)}, bf16[144,512]{1,0:T(8,128)(2,1)S(1)}, u32[]{:S(2)}, u32[]{:S(2)}) collective-permute-start(bf16[144,512]{1,0:T(8,128)(2,1)S(1)} %get-tuple-element.50), channel_id=1, source_target_pairs={{0,2},{1,3},{2,0},{3,1},{4,6},{5,7},{6,4},{7,5},{8,10},{9,11},{10,... | collective-permute-start | bytes 442376 | tf_op jit(solution)/shard_map/ppermute | solution.py:357
  27.1 5.9 %collective-permute-start.12 = (bf16[272,128]{1,0:T(8,128)(2,1)S(1)}, bf16[272,128]{1,0:T(8,128)(2,1)S(1)}, u32[]{:S(2)}, u32[]{:S(2)}) collective-permute-start(bf16[272,128]{1,0:T(8,128)(2,1)S(1)} %shard_map.163.refs_0_.refs_2_), channel_id=1, source_target_pairs={{0,2},{1,3},{2,0},{3,1},{4,6},{5,7},{6,4},{7,5},{8,10},{9,11},{10,... | collective-permute-start | bytes 208904 | tf_op jit(solution)/shard_map/ppermute | solution.py:357
  33.0 1.3 %collective-permute-start.13 = (bf16[144,256]{1,0:T(8,128)(2,1)S(1)}, bf16[144,256]{1,0:T(8,128)(2,1)S(1)}, u32[]{:S(2)}, u32[]{:S(2)}) collective-permute-start(bf16[144,256]{1,0:T(8,128)(2,1)S(1)} %shard_map.164), channel_id=1, source_target_pairs={{0,1},{1,0},{2,3},{3,2},{4,5},{5,4},{6,7},{7,6},{8,9},{9,8},{10,11... | collective-permute-start | bytes 221192 | tf_op jit(solution)/shard_map/ppermute | solution.py:357
  33.3 1.4 %collective-permute-start.14 = (f32[16,512]{1,0:T(8,128)S(1)}, f32[16,512]{1,0:T(8,128)S(1)}, u32[]{:S(2)}, u32[]{:S(2)}) collective-permute-start(f32[16,512]{1,0:T(8,128)S(1)} %get-tuple-element.57.refs_5_), channel_id=1, source_target_pairs={{0,1},{1,0},{2,3},{3,2},{4,5},{5,4},{6,7},{7,6},{8,9},{9,8},{10,11... | collective-permute-start | bytes 98312 | tf_op jit(solution)/shard_map/ppermute | solution.py:357
  37.8 12.7 %all-to-all-start = ((bf16[16,16,128]{2,1,0:T(8,128)(2,1)}), bf16[16,16,128]{2,1,0:T(8,128)(2,1)S(1)}, u32[]{:S(2)}, u32[]{:S(2)}) async-start(bf16[16,16,128]{2,1,0:T(8,128)(2,1)} %shard_map.168), calls=%async_computation | async-start | bytes 131072 | tf_op jit(solution)/shard_map/all_to_all | solution.py:446
  43.6 4.9 %collective-permute-start.15 = (bf16[128,256]{1,0:T(8,128)(2,1)S(1)}, bf16[128,256]{1,0:T(8,128)(2,1)S(1)}, u32[]{:S(2)}, u32[]{:S(2)}) collective-permute-start(bf16[128,256]{1,0:T(8,128)(2,1)S(1)} %get-tuple-element.64), channel_id=1, source_target_pairs={{0,2},{1,3},{2,0},{3,1},{4,6},{5,7},{6,4},{7,5},{8,10},{9,11},{10,... | collective-permute-start | bytes 196616 | tf_op jit(solution)/shard_map/ppermute | solution.py:357
  45.6 3.1 %collective-permute-start.10 = (bf16[128,128]{1,0:T(8,128)(2,1)S(1)}, bf16[128,128]{1,0:T(8,128)(2,1)S(1)}, u32[]{:S(2)}, u32[]{:S(2)}) collective-permute-start(bf16[128,128]{1,0:T(8,128)(2,1)S(1)} %get-tuple-element.54), channel_id=1, source_target_pairs={{0,1},{1,0},{2,3},{3,2},{4,5},{5,4},{6,7},{7,6},{8,9},{9,8},{10,11... | collective-permute-start | bytes 98312 | tf_op jit(solution)/shard_map/ppermute | solution.py:357
  48.6 1.3 %collective-permute-start.16 = (bf16[128,128]{1,0:T(8,128)(2,1)S(1)}, bf16[128,128]{1,0:T(8,128)(2,1)S(1)}, u32[]{:S(2)}, u32[]{:S(2)}) collective-permute-start(bf16[128,128]{1,0:T(8,128)(2,1)S(1)} %get-tuple-element.66), channel_id=1, source_target_pairs={{0,1},{1,0},{2,3},{3,2},{4,5},{5,4},{6,7},{7,6},{8,9},{9,8},{10,11... | collective-permute-start | bytes 98312 | tf_op jit(solution)/shard_map/ppermute | solution.py:357
  (7 other events, 5.2 us)

commit v9 on v7

--- a/solution.py
+++ b/solution.py
@@ -66,7 +66,7 @@
     return pl.ds(pl.multiple_of(group * width, width), width)
 
 
-def stage(kernel, outs, operands, scalars=0, flops=1 << 24):
+def stage(kernel, outs, operands, scalars=0, scratch=(), flops=1 << 24):
     specs = [pl.BlockSpec(memory_space=pltpu.VMEM)] * (len(operands) - scalars)
     specs += [pl.BlockSpec(memory_space=pltpu.SMEM)] * scalars
     moved = sum(o.size * o.dtype.itemsize for o in operands)
@@ -75,6 +75,7 @@
         out_shape=[jax.ShapeDtypeStruct(shape, kind) for shape, kind in outs],
         in_specs=specs,
         out_specs=[pl.BlockSpec(memory_space=pltpu.VMEM)] * len(outs),
+        scratch_shapes=[pltpu.VMEM(shape, kind) for shape, kind in scratch],
         cost_estimate=pl.CostEstimate(flops=flops, bytes_accessed=moved, transcendentals=0),
         compiler_params=pltpu.CompilerParams(vmem_limit_bytes=kernel_vmem),
     )(*operands)
@@ -95,40 +96,42 @@
     return value
 
 
-def pack_extra(edge_cot, node_cot, gain_e, gain_n, pack):
-    edge_dev = edge_cot.shape[0]
-    nodes = node_cot.shape[0]
-    pack[:edge_dev] = edge_cot[...]
-    pack[edge_dev : edge_dev + nodes] = node_cot[...]
-    pack[edge_dev + nodes :] = gains(gain_e, gain_n, nodes)
+def spread_inputs(latent, node_cot, gain_e, gain_n, spread):
+    nodes = latent.shape[0]
+    rows = jnp.concatenate([latent[...], node_cot[...], gains(gain_e, gain_n, nodes)], axis=0)
+    spread[...] = jnp.broadcast_to(rows[None], spread.shape)
 
 
 def half_rows(pack, core, half):
     first = pl.multiple_of(core * half, half)
-    return jnp.concatenate([pack[pl.ds(first, half)], pack[cores * half :]], axis=0)
+    return pack[pl.ds(first, half)], pack[pl.ds(cores * half + first, half)]
 
 
 def send_half(groups, *refs):
     packs, sent = refs[:groups], refs[groups]
     _, core = place()
     width = packs[0].shape[1]
-    half = packs[0].shape[0] - sent.shape[0]
+    half = sent.shape[0] // 2
     for step, pack in enumerate(packs):
-        sent[:, step * width : (step + 1) * width] = half_rows(pack, 1 - core, half)
-
-
-def prepare_edges(feats, *refs):
-    states = refs[:feats]
-    mine, other, slot, receiver, send_rows, state, pre, pick, take = refs[feats:]
+        columns = slice(step * width, (step + 1) * width)
+        sent[:half, columns], sent[half:, columns] = half_rows(pack, 1 - core, half)
+
+
+def prepare_edges(groups, *refs):
+    packs = refs[:groups]
+    theirs, mine, other, slot, receiver, send_rows, state, cot, pre, pick, take = refs[groups:]
     group, core = place()
     block = lax.axis_index("nodes")
     features = state.shape[1]
     nodes, half = take.shape
+    width = packs[0].shape[1]
     blocks, _, slots = send_rows.shape
-    rows = pl.ds(pl.multiple_of(core * half, half), half)
-    for step in range(feats // cores):
-        ours, theirs = states[cores * step][rows], states[cores * step + 1][rows]
-        state[:, lanes(group ^ step, features * cores // feats)] = pair(ours, theirs, core)
+    for step, pack in enumerate(packs):
+        columns = slice(step * width, (step + 1) * width)
+        wide = lanes(group ^ step, width * cores)
+        my_state, my_cot = half_rows(pack, core, half)
+        state[:, wide] = pair(my_state, theirs[:half, columns], core)
+        cot[:, wide] = pair(my_cot, theirs[half:, columns], core)
 
     slot_row = slot[pl.ds(core, 1)]
     sender = block * nodes + slot_row
@@ -143,17 +146,24 @@
     pre[...] = dot_rows(state[...], weight)
 
 
-def finish_edges(came, pre, pick, take, mine, other, out_mine, out_other, n_mine, n_other, edge_pre, part, sent, own, lat, table):
+def finish_edges(came, pre, pick, take, *refs):
+    mine, other, out_mine, out_other, n_mine, n_other, edge_pre, part, sent, own, node_cot, gain, lat, table = refs
     block = lax.axis_index("nodes")
-    count, nodes, width = came.shape
-    rows, features = table.shape
+    count, _, width = came.shape
+    features = table.shape[1]
+    nodes = own.shape[0]
     half, hidden = pre.shape
     feats = features // width
     for source in range(count):
         first, column = source // feats * nodes, source % feats * width
-        table[first : first + nodes, column : column + width] = came[source]
-    latent = table[pl.ds(pl.multiple_of(block * nodes, nodes), nodes)]
-    own[...] = latent
+        table[first : first + nodes, column : column + width] = came[source, :nodes]
+    for feat in range(feats):
+        columns = slice(feat * width, (feat + 1) * width)
+        here = came[block * feats + feat]
+        own[:, columns] = here[:nodes]
+        node_cot[:, columns] = here[nodes : 2 * nodes]
+        gain[:, columns] = here[2 * nodes :]
+    latent = own[...]
 
     def weight(index):
         columns = slice(index * features, (index + 1) * features)
@@ -177,15 +187,12 @@
 
 
 def update_edges(groups, *refs):
-    part, lat, came, packs = refs[0], refs[1], refs[2 : groups + 1], refs[groups + 1 : 2 * groups + 1]
-    theirs, state, take, normed, inverse, kept, lent, aggregate, lat_all, extra, next_all = refs[2 * groups + 1 :]
+    part, lat, came = refs[0], refs[1], refs[2 : groups + 1]
+    gain, state, take, normed, inverse, kept, lent, aggregate, lat_all, next_all = refs[groups + 1 :]
     group, core = place()
     nodes, half = take.shape
     width = kept.shape[1]
     hidden = lat.shape[1]
-    for step, pack in enumerate(packs):
-        both = pair(half_rows(pack, core, half), theirs[:, step * width : (step + 1) * width], core)
-        extra[:, lanes(group ^ step, width * cores)] = both
     value = part[...]
     lat_all[:, :hidden] = lat[...]
     for step, ref in enumerate(came, 1):
@@ -195,8 +202,7 @@
     normed_rows, inverse_rows = normalize(value)
     normed[...] = normed_rows
     inverse[...] = inverse_rows
-    gain = extra[half + nodes :].astype(f32)[0:1]
-    rows = (state[...].astype(f32) + normed_rows * gain).astype(bf16)
+    rows = (state[...].astype(f32) + normed_rows * gain[...].astype(f32)[0:1]).astype(bf16)
     aggregate[...] = dot(take[...], rows)
     next_all[...] = rows
     mine = next_all[:, lanes(group, width * cores)]
@@ -206,16 +212,16 @@
 
 def turn(groups, *refs):
     far, refs = refs[: 2 * (groups - 1)], refs[2 * (groups - 1) :]
-    aggregate, aggregate2, own, lat_all, extra, take, normed, inverse, edge_pre = refs[:9]
-    e_mine, e_other, out_mine, out_other, in_mine, in_other, n_mine, n_other = refs[9:17]
-    node_next, kept, *sents, dpre_ref, node_dpre_ref, next_all, grads = refs[17:]
+    aggregate, aggregate2, own, lat_all, gain, node_cot, edge_cot, take, normed, inverse, edge_pre = refs[:11]
+    e_mine, e_other, out_mine, out_other, in_mine, in_other, n_mine, n_other = refs[11:19]
+    node_next, kept, *sents, dpre_ref, node_dpre_ref, next_all, grads = refs[19:]
     group, core = place()
     nodes, half = take.shape
-    features = extra.shape[1]
+    features = gain.shape[1]
     hidden = edge_pre.shape[1]
     wide = kept.shape[1]
     width = node_next.shape[1]
-    gain_rows = extra[half + nodes :].astype(f32)
+    gain_rows = gain[...].astype(f32)
     edge_gain, node_gain = gain_rows[0:1], gain_rows[1:2]
 
     from_agg = jnp.concatenate(
@@ -229,13 +235,12 @@
     next_all[...] = (own[...].astype(f32) + node_normed * node_gain).astype(bf16)
     mine = next_all[:, lanes(group, wide)]
     node_next[...] = jnp.where(core == 0, mine[:, :width], mine[:, width:])
-    cot = extra[half : half + nodes].astype(f32)
-    node_dy = norm_back(cot * node_gain, node_normed, node_inverse).astype(bf16)
+    node_dy = norm_back(node_cot[...].astype(f32) * node_gain, node_normed, node_inverse).astype(bf16)
     node_dpre = (dot_rows(node_dy, to_out) * swish_slope(pre)).astype(bf16)
     high, low = split(dot(node_dpre, from_agg))
 
     taken = take[...]
-    edge_total = extra[:half].astype(f32) + dot_cols(
+    edge_total = edge_cot[...].astype(f32) + dot_cols(
         jnp.concatenate([taken, taken], axis=0), jnp.concatenate([high, low], axis=0)
     )
     dy = norm_back(edge_total * edge_gain, normed[...], inverse[...]).astype(bf16)
@@ -340,44 +345,47 @@
     slot_rows = sender_slot.reshape(cores, half)
     receiver_rows = receiver_row.reshape(cores, half)
 
-    latents = lax.all_to_all(
-        jnp.broadcast_to(latent[None], (blocks * feats, nodes, width)), everyone, 0, 0
-    )
-    states = [edge_state] + [swapped(edge_state, step) for step in range(1, feats)]
-    e_in = (edge_in_weight, over_cores(edge_in_weight))
-    state, pre, pick, take = stage(
-        functools.partial(prepare_edges, feats),
-        [((half, features), bf16), ((half, hidden), f32), ((table, half), bf16), ((nodes, half), bf16)],
-        [*states, *e_in, slot_rows, receiver_rows, send_rows],
-        scalars=1,
-    )
-    pre, node_in_weight, node_out_weight, edge_out_weight, edge_cot = lax.optimization_barrier(
-        (pre, node_in_weight, node_out_weight, edge_out_weight, edge_cot)
-    )
-    e_out = (edge_out_weight, over_cores(edge_out_weight))
     far = []
     for weights in over_groups(jnp.concatenate([node_in_weight[:, features:], node_out_weight], axis=1)):
         far += [weights, over_cores(weights)]
-    rows = edge_dev + 2 * nodes
-    (pack,) = stage(pack_extra, [((rows, width), bf16)], [edge_cot, node_cot, gain_e, gain_n])
-    packs = [pack] + over_groups(pack)
-    (sent,) = stage(functools.partial(send_half, groups), [((rows - half, groups * width), bf16)], packs)
-    extra_came = over_cores(sent)
+    e_in = (edge_in_weight, over_cores(edge_in_weight))
+    e_out = (edge_out_weight, over_cores(edge_out_weight))
     n_in = (node_in_weight, over_cores(node_in_weight))
     n_out = (node_out_weight, over_cores(node_out_weight))
-    edge_pre, part, sent, own, lat, _ = stage(
+    pack = jnp.concatenate([edge_state, edge_cot])
+    packs = [pack] + over_groups(pack)
+    (spread,) = stage(
+        spread_inputs, [((blocks * feats, 3 * nodes, width), bf16)], [latent, node_cot, gain_e, gain_n]
+    )
+    came = lax.all_to_all(spread, everyone, 0, 0)
+    (sent,) = stage(functools.partial(send_half, groups), [((edge_dev, groups * width), bf16)], packs)
+    state, cot, pre, pick, take = stage(
+        functools.partial(prepare_edges, groups),
+        [
+            ((half, features), bf16),
+            ((half, features), bf16),
+            ((half, hidden), f32),
+            ((table, half), bf16),
+            ((nodes, half), bf16),
+        ],
+        [*packs, over_cores(sent), *e_in, slot_rows, receiver_rows, send_rows],
+        scalars=1,
+    )
+    edge_pre, part, sent, own, full_node_cot, gain, lat = stage(
         finish_edges,
         [
             ((half, hidden), f32),
             ((half, features), f32),
             ((half + nodes, features), bf16),
             ((nodes, features), bf16),
+            ((nodes, features), bf16),
+            ((nodes, features), bf16),
             ((nodes, hidden), f32),
-            ((table, features), bf16),
         ],
-        [latents, pre, pick, take, *e_in, *e_out, *n_in],
-    )
-    normed, inverse, next_mine, next_sent, aggregate, lat_all, extra, _ = stage(
+        [came, pre, pick, take, *e_in, *e_out, *n_in],
+        scratch=[((table, features), bf16)],
+    )
+    normed, inverse, next_mine, next_sent, aggregate, lat_all = stage(
         functools.partial(update_edges, groups),
         [
             ((half, features), f32),
@@ -386,31 +394,27 @@
             ((half, width), bf16),
             ((nodes, features), f32),
             ((nodes, features), f32),
-            ((half + 2 * nodes, features), bf16),
-            ((half, features), bf16),
         ],
-        [part, lat, *over_groups(sent), *packs, extra_came, state, take],
+        [part, lat, *over_groups(sent), gain, state, take],
+        scratch=[((half, features), bf16)],
     )
     aggregate2 = over_cores(aggregate)
     next_came = over_cores(next_sent)
-    node_next, kept, *sents, dpre, node_dpre, _, _ = stage(
+    node_next, kept, *sents, dpre, node_dpre = stage(
         functools.partial(turn, groups),
         [((nodes, width), bf16), ((half, wide), f32)]
         + [((half, wide), bf16)] * (groups - 1)
-        + [
-            ((half, hidden), bf16),
-            ((nodes, hidden), bf16),
-            ((nodes, features), bf16),
-            ((half, features), f32),
-        ],
-        [*far, aggregate, aggregate2, own, lat_all, extra, take, normed, inverse, edge_pre]
+        + [((half, hidden), bf16), ((nodes, hidden), bf16)],
+        [*far, aggregate, aggregate2, own, lat_all, gain, full_node_cot, cot, take, normed, inverse, edge_pre]
         + [*e_in, *e_out, *n_in, *n_out],
+        scratch=[((nodes, features), bf16), ((half, features), f32)],
     )
     sents = [swapped(s, cores * k) for k, s in enumerate(sents, 1)]
-    spread, _ = stage(
+    (spread,) = stage(
         spread_nodes,
-        [((blocks * feats, nodes, width), bf16), ((table, features), f32)],
+        [((blocks * feats, nodes, width), bf16)],
         [dpre, node_dpre, pick, take, *e_in, *n_in],
+        scratch=[((table, features), f32)],
     )
     shares = lax.all_to_all(spread, everyone, 0, 0)
     grad_mine, grad_sent = stage(

time: 51.8 us -> 52.6 us (1.015)
  waiting for transfers between devices: 19.2 us -> 20.9 us
  local copies, waits for them, and re-layouts: 5.56 us -> 3.93 us
  starting transfers between devices: 18.4 us -> 19.5 us
    ppermute x16 -> x13, waiting for transfers between devices: 15.1 us -> 20.9 us  [swapped(): return lax.ppermute(values, 'feat', [(i, i ^ bits) for i in range(feats)])]
    all_to_all x1, waiting for transfers between devices: 3.99 us -> 0.01 us  [shards(): came = lax.all_to_all(spread, everyone, 0, 0)]
    ppermute x16 -> x13, starting transfers between devices: 8.75 us -> 7.23 us  [swapped(): return lax.ppermute(values, 'feat', [(i, i ^ bits) for i in range(feats)])]
    all_to_all x1, starting transfers between devices: 3.49 us -> 4.89 us  [shards(): shares = lax.all_to_all(spread, everyone, 0, 0)]
    all_to_all x1, starting transfers between devices: 6.16 us -> 7.36 us  [shards(): came = lax.all_to_all(spread, everyone, 0, 0)]
    broadcast_in_dim x1 -> x0, local copies, waits for them, and re-layouts: 0.64 us -> none  [shards(): jnp.broadcast_to(latent[None], (blocks * feats, nodes, width))]
    slice x2, local copies, waits for them, and re-layouts: 1.01 us -> 0.42 us  [shards(): node_in_weight[:, features:]]
    unnamed x28 -> x29, local copies, waits for them, and re-layouts: 3.91 us -> 3.5 us
  transfers between devices with their start and end apart: 18 -> 15, of which waited for: 10 -> 6; matrix products, arithmetic and copies ran while one was open for 1% -> 0% of each run, Pallas kernels for 5% -> 5%
where the time goes in v9:
time: 52.6 us; the launch traced here: 52.1 us
  waiting for transfers between devices  20.9 us (40%)
  starting transfers between devices  19.5 us (37%)
  Pallas kernels  6.91 us (13%)
  local copies, waits for them, and re-layouts  3.93 us (7%)
  between operations  0.84 us (2%)
    ppermute x13, waiting for transfers between devices, swapped(): return lax.ppermute(values, 'feat', [(i, i ^ bits) for i in range(feats)])  20.9 us
    all_to_all x1, starting transfers between devices, shards(): came = lax.all_to_all(spread, everyone, 0, 0)  7.36 us
    ppermute x13, starting transfers between devices, swapped(): return lax.ppermute(values, 'feat', [(i, i ^ bits) for i in range(feats)])  7.23 us
    pallas_call x10, Pallas kernels, stage(): pl.pallas_call(kernel, out_shape=[jax.ShapeDtypeStruct(shape, kind) for s...  6.91 us
    all_to_all x1, starting transfers between devices, shards(): shares = lax.all_to_all(spread, everyone, 0, 0)  4.89 us
    unnamed x29, local copies, waits for them, and re-layouts  3.5 us
  transfers between devices with their start and end apart: 15, of which 6 were waited for; matrix products, arithmetic and copies ran while one was open for 0% of the time, Pallas kernels for 5%

profile of v9, /device:TPU:0, one launch (start us, length us, event | category | flops | bytes accessed | tf_op | source)
XLA Modules:
  0.0 52.1 jit_solution(4192703482330327034)
XLA Ops:
  0.7 0.7 %copy-done.4 = bf16[16,128]{1,0:T(8,128)(2,1)S(1)} copy-done((bf16[16,128]{1,0:T(8,128)(2,1)S(1)}, bf16[16,128]{1,0:T(8,128)(2,1)}, u32[]{:S(2)}) %copy-start.4) | copy-done | bytes 4120
  1.4 0.7 %copy-done.7 = bf16[16,128]{1,0:T(8,128)(2,1)S(1)} copy-done((bf16[16,128]{1,0:T(8,128)(2,1)S(1)}, bf16[16,128]{1,0:T(8,128)(2,1)}, u32[]{:S(2)}) %copy-start.7) | copy-done | bytes 4120
  2.1 0.7 %copy-done.10 = bf16[128]{0:T(256)(128)(2,1)S(1)} copy-done((bf16[128]{0:T(256)(128)(2,1)S(1)}, bf16[128]{0:T(256)(128)(2,1)}, u32[]{:S(2)}) %copy-start.10) | copy-done | bytes 280
  2.7 0.7 %copy-done.11 = bf16[128]{0:T(256)(128)(2,1)S(1)} copy-done((bf16[128]{0:T(256)(128)(2,1)S(1)}, bf16[128]{0:T(256)(128)(2,1)}, u32[]{:S(2)}) %copy-start.11) | copy-done | bytes 280
  3.4 0.7 %shard_map.156 = bf16[16,48,128]{2,1,0:T(8,128)(2,1)} custom-call(bf16[16,128]{1,0:T(8,128)(2,1)S(1)} %copy-done.7, bf16[16,128]{1,0:T(8,128)(2,1)S(1)} %copy-done.4, bf16[1,128]{1,0:T(2,128)(2,1)S(1)} %bitcast.6, bf16[1,128]{1,0:T(2,128)(2,1)S(1)} %bitcast.7), custom_call_target="tpu_custom_call" | custom-call | flops 16777216 | bytes 8704 | tf_op jit(solution)/shard_map/pallas_call | solution.py:73
  4.1 7.4 %all-to-all-start = ((bf16[16,48,128]{2,1,0:T(8,128)(2,1)}), bf16[16,48,128]{2,1,0:T(8,128)(2,1)S(1)}, u32[]{:S(2)}, u32[]{:S(2)}) async-start(bf16[16,48,128]{2,1,0:T(8,128)(2,1)} %shard_map.156), calls=%async_computation | async-start | bytes 393216 | tf_op jit(solution)/shard_map/all_to_all | solution.py:360
  12.5 2.0 %collective-permute-start.7 = (bf16[128,1024]{1,0:T(8,128)(2,1)S(1)}, bf16[128,1024]{1,0:T(8,128)(2,1)S(1)}, u32[]{:S(2)}, u32[]{:S(2)}) collective-permute-start(bf16[128,1024]{1,0:T(8,128)(2,1)S(1)} %pad_maximum_fusion), channel_id=1, source_target_pairs={{0,2},{1,3},{2,0},{3,1},{4,6},{5,7},{6,4},{7,5},{8,10},{9,11},{10,... | collective-permute-start | bytes 786440 | tf_op jit(solution)/shard_map/ppermute | solution.py:336
  14.5 0.8 %collective-permute-start = (bf16[512,128]{1,0:T(8,128)(2,1)S(1)}, bf16[512,128]{1,0:T(8,128)(2,1)S(1)}, u32[]{:S(2)}, u32[]{:S(2)}) collective-permute-start(bf16[512,128]{1,0:T(8,128)(2,1)S(1)} %constant_dynamic-update-slice_fusion.refs_0_), channel_id=1, source_target_pairs={{0,2},{1,3},{2,0},{3,1},{4,6},{5,7},{6,4},{7,5},{8,10},{9,11},{10,... | collective-permute-start | bytes 393224 | tf_op jit(solution)/shard_map/ppermute | solution.py:336
  15.4 10.1 %collective-permute-done.refs_1_ = bf16[512,128]{1,0:T(8,128)(2,1)S(1)} collective-permute-done((bf16[512,128]{1,0:T(8,128)(2,1)S(1)}, bf16[512,128]{1,0:T(8,128)(2,1)S(1)}, u32[]{:S(2)}, u32[]{:S(2)}) %collective-permute-start) | collective-permute-done | bytes 131104 | tf_op jit(solution)/shard_map/ppermute | solution.py:336
  26.2 0.7 %collective-permute-done.1.refs_2_ = bf16[256,256]{1,0:T(8,128)(2,1)S(1)} collective-permute-done((bf16[256,256]{1,0:T(8,128)(2,1)S(1)}, bf16[256,256]{1,0:T(8,128)(2,1)S(1)}, u32[]{:S(2)}, u32[]{:S(2)}) %collective-permute-start.1) | collective-permute-done | bytes 131104 | tf_op jit(solution)/shard_map/ppermute | solution.py:336
  26.9 0.7 %copy-done.8 = s32[256]{0:T(256)S(1)} copy-done((s32[256]{0:T(256)S(1)}, s32[256]{0:T(256)}, u32[]{:S(2)}) %copy-start.8) | copy-done | bytes 1048
  27.6 0.9 %shard_map.158 = (bf16[128,512]{1,0:T(8,128)(2,1)S(1)}, bf16[128,512]{1,0:T(8,128)(2,1)S(1)}, f32[128,256]{1,0:T(8,128)S(1)}, bf16[64,128]{1,0:T(8,128)(2,1)S(1)}, bf16[16,128]{1,0:T(8,128)(2,1)S(1)}) custom-call(bf16[512,128]{1,0:T(8,128)(2,1)S(1)} %constant_dynamic-update-slice_fusion.refs_0_, bf16[512,128]{1,0:T(8,128)(2,1)S(1)} %collective-permute-done.refs_1_, ...), custom_call_target="tpu_custom_call" | custom-call | flops 16777216 | bytes 1182208 | tf_op jit(solution)/shard_map/pallas_call | solution.py:73
  28.5 0.6 %shard_map.159 = (f32[128,256]{1,0:T(8,128)S(1)}, f32[128,512]{1,0:T(8,128)S(1)}, bf16[144,512]{1,0:T(8,128)(2,1)S(1)}, bf16[16,512]{1,0:T(8,128)(2,1)S(1)}, bf1...) custom-call(bf16[16,48,128]{2,1,0:T(8,128)(2,1)S(1)} %all-to-all-done.came, ...), custom_call_target="tpu_custom_call" | custom-call | flops 16777216 | bytes 1921024 | tf_op jit(solution)/shard_map/pallas_call | solution.py:73
  29.2 1.3 %collective-permute-start.5 = (bf16[144,512]{1,0:T(8,128)(2,1)S(1)}, bf16[144,512]{1,0:T(8,128)(2,1)S(1)}, u32[]{:S(2)}, u32[]{:S(2)}) collective-permute-start(bf16[144,512]{1,0:T(8,128)(2,1)S(1)} %get-tuple-element.36), channel_id=1, source_target_pairs={{0,2},{1,3},{2,0},{3,1},{4,6},{5,7},{6,4},{7,5},{8,10},{9,11},{10,... | collective-permute-start | bytes 442376 | tf_op jit(solution)/shard_map/ppermute | solution.py:336
  30.4 4.7 %collective-permute-done.5.refs_2_ = bf16[144,512]{1,0:T(8,128)(2,1)S(1)} collective-permute-done((bf16[144,512]{1,0:T(8,128)(2,1)S(1)}, bf16[144,512]{1,0:T(8,128)(2,1)S(1)}, u32[]{:S(2)}, u32[]{:S(2)}) %collective-permute-start.5) | collective-permute-done | bytes 147488 | tf_op jit(solution)/shard_map/ppermute | solution.py:336
  35.4 1.2 %collective-permute-done.9.refs_3_ = f32[16,512]{1,0:T(8,128)S(1)} collective-permute-done((f32[16,512]{1,0:T(8,128)S(1)}, f32[16,512]{1,0:T(8,128)S(1)}, u32[]{:S(2)}, u32[]{:S(2)}) %collective-permute-start.9) | collective-permute-done | bytes 32800 | tf_op jit(solution)/shard_map/ppermute | solution.py:336
  36.6 2.0 %shard_map.161 = (bf16[16,128]{1,0:T(8,128)(2,1)}, f32[128,256]{1,0:T(8,128)S(1)}, bf16[128,256]{1,0:T(8,128)(2,1)S(1)}, bf16[128,256]{1,0:T(8,128)(2,1)S(1)}, bf16[16,256]{1,0:T(8,128)(2,1)S(1)}) custom-call(bf16[128,1024]{1,0:T(8,128)(2,1)S(1)} %collective-permute-done.7.refs_0_, bf16[128,1024]{1,0:T(8,128)(2,1)S(1)} %collective-permute-done.8.refs_1_, ...), custom_call_target="tpu_custom_call" | custom-call | flops 16777216 | bytes 3035648 | tf_op jit(solution)/shard_map/pallas_call | solution.py:73
  38.6 1.1 %shard_map.164 = bf16[16,16,128]{2,1,0:T(8,128)(2,1)} custom-call(bf16[128,256]{1,0:T(8,128)(2,1)S(1)} %get-tuple-element.56.dpre, bf16[16,256]{1,0:T(8,128)(2,1)S(1)} %get-tuple-element.57.node_dpre, bf16[64,128]{1,0:T(8,128)(2,1)S(1)} %get-tuple-element.32.pick, bf16[16,128]{1,0:T(8,128)(2,1)S(1)} %get-tuple-element.33.take.refs_5_.refs_9_, ...), custom_call_target="tpu_custom_call" | custom-call | flops 16777216 | bytes 1404928 | tf_op jit(solution)/shard_map/pallas_call | solution.py:73
  39.7 4.9 %all-to-all-start.1 = ((bf16[16,16,128]{2,1,0:T(8,128)(2,1)}), bf16[16,16,128]{2,1,0:T(8,128)(2,1)S(1)}, u32[]{:S(2)}, u32[]{:S(2)}) async-start(bf16[16,16,128]{2,1,0:T(8,128)(2,1)} %shard_map.164), calls=%async_computation.1 | async-start | bytes 131072 | tf_op jit(solution)/shard_map/all_to_all | solution.py:419
  44.6 1.9 %collective-permute-start.11 = (bf16[128,256]{1,0:T(8,128)(2,1)S(1)}, bf16[128,256]{1,0:T(8,128)(2,1)S(1)}, u32[]{:S(2)}, u32[]{:S(2)}) collective-permute-start(bf16[128,256]{1,0:T(8,128)(2,1)S(1)} %get-tuple-element.50), channel_id=1, source_target_pairs={{0,2},{1,3},{2,0},{3,1},{4,6},{5,7},{6,4},{7,5},{8,10},{9,11},{10,... | collective-permute-start | bytes 196616 | tf_op jit(solution)/shard_map/ppermute | solution.py:336
  46.5 3.0 %collective-permute-done.11.refs_1_ = bf16[128,256]{1,0:T(8,128)(2,1)S(1)} collective-permute-done((bf16[128,256]{1,0:T(8,128)(2,1)S(1)}, bf16[128,256]{1,0:T(8,128)(2,1)S(1)}, u32[]{:S(2)}, u32[]{:S(2)}) %collective-permute-start.11) | collective-permute-done | bytes 65568 | tf_op jit(solution)/shard_map/ppermute | solution.py:336
  49.6 1.2 %collective-permute-done.12.grad_came = bf16[128,128]{1,0:T(8,128)(2,1)S(1)} collective-permute-done((bf16[128,128]{1,0:T(8,128)(2,1)S(1)}, bf16[128,128]{1,0:T(8,128)(2,1)S(1)}, u32[]{:S(2)}, u32[]{:S(2)}) %collective-permute-start.12) | collective-permute-done | bytes 32800 | tf_op jit(solution)/shard_map/ppermute | solution.py:336
  50.8 0.7 %shard_map.163 = (bf16[256,128]{1,0:T(8,128)(2,1)}, bf16[256,128]{1,0:T(8,128)(2,1)}) custom-call(bf16[128,128]{1,0:T(8,128)(2,1)S(1)} %get-tuple-element.39.next_mine, bf16[128,128]{1,0:T(8,128)(2,1)S(1)} %collective-permute-done.6.next_came, bf16[128,128]{1,0:T(8,128)(2,1)S(1)} %get-tuple-element.51.grad_mine, ...), custom_call_target="tpu_custom_call" | custom-call | flops 16777216 | bytes 131072 | tf_op jit(solution)/shard_map/pallas_call | solution.py:73
  51.5 0.6 %shard_map.165 = bf16[16,128]{1,0:T(8,128)(2,1)} custom-call(bf16[16,16,128]{2,1,0:T(8,128)(2,1)S(1)} %all-to-all-done.1.shares, bf16[16,128]{1,0:T(8,128)(2,1)S(1)} %copy-done.5), custom_call_target="tpu_custom_call" | custom-call | flops 16777216 | bytes 69632 | tf_op jit(solution)/shard_map/pallas_call | solution.py:73
  (49 shorter events, 2.2 us)
Async XLA Ops:
  0.6 10.8 %copy-start = (bf16[128,1536]{1,0:T(8,128)(2,1)S(1)}, bf16[128,1536]{1,0:T(8,128)(2,1)}, u32[]{:S(2)}) copy-start(bf16[128,1536]{1,0:T(8,128)(2,1)} %e_mine.1) | copy-start | bytes 1179652
  4.1 24.4 %all-to-all-start = ((bf16[16,48,128]{2,1,0:T(8,128)(2,1)}), bf16[16,48,128]{2,1,0:T(8,128)(2,1)S(1)}, u32[]{:S(2)}, u32[]{:S(2)}) async-start(bf16[16,48,128]{2,1,0:T(8,128)(2,1)} %shard_map.156), calls=%async_computation | async-start | bytes 393216 | tf_op jit(solution)/shard_map/all_to_all | solution.py:360
  11.4 0.9 %slice-start = ((bf16[128,1024]{1,0:T(8,128)(2,1)}), bf16[128,512]{1,0:T(8,128)(2,1)S(1)}, s32[]{:S(2)}) async-start(bf16[128,1024]{1,0:T(8,128)(2,1)} %in_mine.1), calls=%async_computation.2 | async-start | bytes 262144 | tf_op jit(solution)/shard_map/slice | solution.py:349
  11.5 1.0 %copy-start.2 = (bf16[128,512]{1,0:T(8,128)(2,1)S(1)}, bf16[128,512]{1,0:T(8,128)(2,1)}, u32[]{:S(2)}) copy-start(bf16[128,512]{1,0:T(8,128)(2,1)} %refs_19_.1) | copy-start | bytes 393220
  11.5 15.4 %collective-permute-start.2 = (bf16[128,1536]{1,0:T(8,128)(2,1)S(1)}, bf16[128,1536]{1,0:T(8,128)(2,1)S(1)}, u32[]{:S(2)}, u32[]{:S(2)}) collective-permute-start(bf16[128,1536]{1,0:T(8,128)(2,1)S(1)} %copy-done), channel_id=1, source_target_pairs={{0,1},{1,0},{2,3},{3,2},{4,5},{5,4},{6,7},{7,6},{8,9},{9,8},{10,11... | collective-permute-start | bytes 1179656 | tf_op jit(solution)/shard_map/ppermute | solution.py:336
  12.4 2.0 %copy-start.12 = (bf16[256,128]{1,0:T(8,128)(2,1)S(1)}, bf16[256,128]{1,0:T(8,128)(2,1)}, u32[]{:S(2)}) copy-start(bf16[256,128]{1,0:T(8,128)(2,1)} %param.14) | copy-start | bytes 196612
  12.4 2.9 %copy-start.1 = (bf16[128,1024]{1,0:T(8,128)(2,1)S(1)}, bf16[128,1024]{1,0:T(8,128)(2,1)}, u32[]{:S(2)}) copy-start(bf16[128,1024]{1,0:T(8,128)(2,1)} %in_mine.1) | copy-start | bytes 786436
  12.5 2.0 %copy-start.13 = (bf16[256,128]{1,0:T(8,128)(2,1)S(1)}, bf16[256,128]{1,0:T(8,128)(2,1)}, u32[]{:S(2)}) copy-start(bf16[256,128]{1,0:T(8,128)(2,1)} %param.24) | copy-start | bytes 196612
  12.5 13.6 %collective-permute-start.7 = (bf16[128,1024]{1,0:T(8,128)(2,1)S(1)}, bf16[128,1024]{1,0:T(8,128)(2,1)S(1)}, u32[]{:S(2)}, u32[]{:S(2)}) collective-permute-start(bf16[128,1024]{1,0:T(8,128)(2,1)S(1)} %pad_maximum_fusion), channel_id=1, source_target_pairs={{0,2},{1,3},{2,0},{3,1},{4,6},{5,7},{6,4},{7,5},{8,10},{9,11},{10,... | collective-permute-start | bytes 786440 | tf_op jit(solution)/shard_map/ppermute | solution.py:336
  14.5 11.1 %copy-start.3 = (bf16[128,512]{1,0:T(8,128)(2,1)S(1)}, bf16[128,512]{1,0:T(8,128)(2,1)}, u32[]{:S(2)}) copy-start(bf16[128,512]{1,0:T(8,128)(2,1)} %refs_15_.1) | copy-start | bytes 393220
  14.5 11.0 %collective-permute-start = (bf16[512,128]{1,0:T(8,128)(2,1)S(1)}, bf16[512,128]{1,0:T(8,128)(2,1)S(1)}, u32[]{:S(2)}, u32[]{:S(2)}) collective-permute-start(bf16[512,128]{1,0:T(8,128)(2,1)S(1)} %constant_dynamic-update-slice_fusion.refs_0_), channel_id=1, source_target_pairs={{0,2},{1,3},{2,0},{3,1},{4,6},{5,7},{6,4},{7,5},{8,10},{9,11},{10,... | collective-permute-start | bytes 393224 | tf_op jit(solution)/shard_map/ppermute | solution.py:336
  15.4 13.2 %collective-permute-start.4 = (bf16[128,1024]{1,0:T(8,128)(2,1)S(1)}, bf16[128,1024]{1,0:T(8,128)(2,1)S(1)}, u32[]{:S(2)}, u32[]{:S(2)}) collective-permute-start(bf16[128,1024]{1,0:T(8,128)(2,1)S(1)} %copy-done.1), channel_id=1, source_target_pairs={{0,1},{1,0},{2,3},{3,2},{4,5},{5,4},{6,7},{7,6},{8,9},{9,8},{10,11... | collective-permute-start | bytes 786440 | tf_op jit(solution)/shard_map/ppermute | solution.py:336
  25.5 1.5 %copy-start.6 = (s32[4,4,8]{2,1,0:T(4,128)S(1)}, s32[4,4,8]{2,1,0:T(4,128)}, u32[]{:S(2)}) copy-start(s32[4,4,8]{2,1,0:T(4,128)} %refs_7_.1) | copy-start | bytes 1540
  25.5 1.5 %copy-start.9 = (s32[256]{0:T(256)S(1)}, s32[256]{0:T(256)}, u32[]{:S(2)}) copy-start(s32[256]{0:T(256)} %param.17) | copy-start | bytes 3076
  25.5 1.4 %collective-permute-start.1 = (bf16[256,256]{1,0:T(8,128)(2,1)S(1)}, bf16[256,256]{1,0:T(8,128)(2,1)S(1)}, u32[]{:S(2)}, u32[]{:S(2)}) collective-permute-start(bf16[256,256]{1,0:T(8,128)(2,1)S(1)} %shard_map.157), channel_id=1, source_target_pairs={{0,1},{1,0},{2,3},{3,2},{4,5},{5,4},{6,7},{7,6},{8,9},{9,8},{10,11... | collective-permute-start | bytes 393224 | tf_op jit(solution)/shard_map/ppermute | solution.py:336
  25.6 2.9 %collective-permute-start.3 = (bf16[128,512]{1,0:T(8,128)(2,1)S(1)}, bf16[128,512]{1,0:T(8,128)(2,1)S(1)}, u32[]{:S(2)}, u32[]{:S(2)}) collective-permute-start(bf16[128,512]{1,0:T(8,128)(2,1)S(1)} %copy-done.3), channel_id=1, source_target_pairs={{0,1},{1,0},{2,3},{3,2},{4,5},{5,4},{6,7},{7,6},{8,9},{9,8},{10,11... | collective-permute-start | bytes 393224 | tf_op jit(solution)/shard_map/ppermute | solution.py:336
  26.1 9.3 %collective-permute-start.8 = (bf16[128,1024]{1,0:T(8,128)(2,1)S(1)}, bf16[128,1024]{1,0:T(8,128)(2,1)S(1)}, u32[]{:S(2)}, u32[]{:S(2)}) collective-permute-start(bf16[128,1024]{1,0:T(8,128)(2,1)S(1)} %collective-permute-done.7.refs_0_), channel_id=1, source_target_pairs={{0,1},{1,0},{2,3},{3,2},{4,5},{5,4},{6,7},{7,6},{8,9},{9,8},{10,11... | collective-permute-start | bytes 786440 | tf_op jit(solution)/shard_map/ppermute | solution.py:336
  29.2 5.9 %collective-permute-start.5 = (bf16[144,512]{1,0:T(8,128)(2,1)S(1)}, bf16[144,512]{1,0:T(8,128)(2,1)S(1)}, u32[]{:S(2)}, u32[]{:S(2)}) collective-permute-start(bf16[144,512]{1,0:T(8,128)(2,1)S(1)} %get-tuple-element.36), channel_id=1, source_target_pairs={{0,2},{1,3},{2,0},{3,1},{4,6},{5,7},{6,4},{7,5},{8,10},{9,11},{10,... | collective-permute-start | bytes 442376 | tf_op jit(solution)/shard_map/ppermute | solution.py:336
  30.4 4.9 %collective-permute-start.10 = (bf16[128,512]{1,0:T(8,128)(2,1)S(1)}, bf16[128,512]{1,0:T(8,128)(2,1)S(1)}, u32[]{:S(2)}, u32[]{:S(2)}) collective-permute-start(bf16[128,512]{1,0:T(8,128)(2,1)S(1)} %copy-done.2), channel_id=1, source_target_pairs={{0,1},{1,0},{2,3},{3,2},{4,5},{5,4},{6,7},{7,6},{8,9},{9,8},{10,11... | collective-permute-start | bytes 393224 | tf_op jit(solution)/shard_map/ppermute | solution.py:336
  35.4 1.2 %collective-permute-start.9 = (f32[16,512]{1,0:T(8,128)S(1)}, f32[16,512]{1,0:T(8,128)S(1)}, u32[]{:S(2)}, u32[]{:S(2)}) collective-permute-start(f32[16,512]{1,0:T(8,128)S(1)} %get-tuple-element.41.refs_2_), channel_id=1, source_target_pairs={{0,1},{1,0},{2,3},{3,2},{4,5},{5,4},{6,7},{7,6},{8,9},{9,8},{10,11... | collective-permute-start | bytes 98312 | tf_op jit(solution)/shard_map/ppermute | solution.py:336
  39.7 11.8 %all-to-all-start.1 = ((bf16[16,16,128]{2,1,0:T(8,128)(2,1)}), bf16[16,16,128]{2,1,0:T(8,128)(2,1)S(1)}, u32[]{:S(2)}, u32[]{:S(2)}) async-start(bf16[16,16,128]{2,1,0:T(8,128)(2,1)} %shard_map.164), calls=%async_computation.1 | async-start | bytes 131072 | tf_op jit(solution)/shard_map/all_to_all | solution.py:419
  44.6 4.9 %collective-permute-start.11 = (bf16[128,256]{1,0:T(8,128)(2,1)S(1)}, bf16[128,256]{1,0:T(8,128)(2,1)S(1)}, u32[]{:S(2)}, u32[]{:S(2)}) collective-permute-start(bf16[128,256]{1,0:T(8,128)(2,1)S(1)} %get-tuple-element.50), channel_id=1, source_target_pairs={{0,2},{1,3},{2,0},{3,1},{4,6},{5,7},{6,4},{7,5},{8,10},{9,11},{10,... | collective-permute-start | bytes 196616 | tf_op jit(solution)/shard_map/ppermute | solution.py:336
  46.5 3.1 %collective-permute-start.6 = (bf16[128,128]{1,0:T(8,128)(2,1)S(1)}, bf16[128,128]{1,0:T(8,128)(2,1)S(1)}, u32[]{:S(2)}, u32[]{:S(2)}) collective-permute-start(bf16[128,128]{1,0:T(8,128)(2,1)S(1)} %get-tuple-element.40), channel_id=1, source_target_pairs={{0,1},{1,0},{2,3},{3,2},{4,5},{5,4},{6,7},{7,6},{8,9},{9,8},{10,11... | collective-permute-start | bytes 98312 | tf_op jit(solution)/shard_map/ppermute | solution.py:336
  49.5 1.3 %collective-permute-start.12 = (bf16[128,128]{1,0:T(8,128)(2,1)S(1)}, bf16[128,128]{1,0:T(8,128)(2,1)S(1)}, u32[]{:S(2)}, u32[]{:S(2)}) collective-permute-start(bf16[128,128]{1,0:T(8,128)(2,1)S(1)} %get-tuple-element.52), channel_id=1, source_target_pairs={{0,1},{1,0},{2,3},{3,2},{4,5},{5,4},{6,7},{7,6},{8,9},{9,8},{10,11... | collective-permute-start | bytes 98312 | tf_op jit(solution)/shard_map/ppermute | solution.py:336
  (6 other events, 4.1 us)

commit v10 on v7

--- a/solution.py
+++ b/solution.py
@@ -66,7 +66,7 @@
     return pl.ds(pl.multiple_of(group * width, width), width)
 
 
-def stage(kernel, outs, operands, scalars=0, flops=1 << 24):
+def stage(kernel, outs, operands, scalars=0, scratch=(), flops=1 << 24):
     specs = [pl.BlockSpec(memory_space=pltpu.VMEM)] * (len(operands) - scalars)
     specs += [pl.BlockSpec(memory_space=pltpu.SMEM)] * scalars
     moved = sum(o.size * o.dtype.itemsize for o in operands)
@@ -75,6 +75,7 @@
         out_shape=[jax.ShapeDtypeStruct(shape, kind) for shape, kind in outs],
         in_specs=specs,
         out_specs=[pl.BlockSpec(memory_space=pltpu.VMEM)] * len(outs),
+        scratch_shapes=[pltpu.VMEM(shape, kind) for shape, kind in scratch],
         cost_estimate=pl.CostEstimate(flops=flops, bytes_accessed=moved, transcendentals=0),
         compiler_params=pltpu.CompilerParams(vmem_limit_bytes=kernel_vmem),
     )(*operands)
@@ -104,8 +105,10 @@
 
 
 def half_rows(pack, core, half):
-    first = pl.multiple_of(core * half, half)
-    return jnp.concatenate([pack[pl.ds(first, half)], pack[cores * half :]], axis=0)
+    rows = pack[pl.ds(pl.multiple_of(core * half, half), half)]
+    if pack.shape[0] == cores * half:
+        return rows
+    return jnp.concatenate([rows, pack[cores * half :]], axis=0)
 
 
 def send_half(groups, *refs):
@@ -117,18 +120,18 @@
         sent[:, step * width : (step + 1) * width] = half_rows(pack, 1 - core, half)
 
 
-def prepare_edges(feats, *refs):
-    states = refs[:feats]
-    mine, other, slot, receiver, send_rows, state, pre, pick, take = refs[feats:]
+def prepare_edges(groups, *refs):
+    packs = refs[:groups]
+    theirs, mine, other, slot, receiver, send_rows, state, pre, pick, take = refs[groups:]
     group, core = place()
     block = lax.axis_index("nodes")
     features = state.shape[1]
     nodes, half = take.shape
+    width = packs[0].shape[1]
     blocks, _, slots = send_rows.shape
-    rows = pl.ds(pl.multiple_of(core * half, half), half)
-    for step in range(feats // cores):
-        ours, theirs = states[cores * step][rows], states[cores * step + 1][rows]
-        state[:, lanes(group ^ step, features * cores // feats)] = pair(ours, theirs, core)
+    for step, pack in enumerate(packs):
+        both = pair(half_rows(pack, core, half), theirs[:, step * width : (step + 1) * width], core)
+        state[:, lanes(group ^ step, width * cores)] = both
 
     slot_row = slot[pl.ds(core, 1)]
     sender = block * nodes + slot_row
@@ -343,29 +346,27 @@
     latents = lax.all_to_all(
         jnp.broadcast_to(latent[None], (blocks * feats, nodes, width)), everyone, 0, 0
     )
-    states = [edge_state] + [swapped(edge_state, step) for step in range(1, feats)]
+    states = [edge_state] + over_groups(edge_state)
     e_in = (edge_in_weight, over_cores(edge_in_weight))
-    state, pre, pick, take = stage(
-        functools.partial(prepare_edges, feats),
-        [((half, features), bf16), ((half, hidden), f32), ((table, half), bf16), ((nodes, half), bf16)],
-        [*states, *e_in, slot_rows, receiver_rows, send_rows],
-        scalars=1,
-    )
-    pre, node_in_weight, node_out_weight, edge_out_weight, edge_cot = lax.optimization_barrier(
-        (pre, node_in_weight, node_out_weight, edge_out_weight, edge_cot)
-    )
     e_out = (edge_out_weight, over_cores(edge_out_weight))
+    n_in = (node_in_weight, over_cores(node_in_weight))
+    n_out = (node_out_weight, over_cores(node_out_weight))
     far = []
     for weights in over_groups(jnp.concatenate([node_in_weight[:, features:], node_out_weight], axis=1)):
         far += [weights, over_cores(weights)]
+    (sent,) = stage(functools.partial(send_half, groups), [((half, groups * width), bf16)], states)
+    state, pre, pick, take = stage(
+        functools.partial(prepare_edges, groups),
+        [((half, features), bf16), ((half, hidden), f32), ((table, half), bf16), ((nodes, half), bf16)],
+        [*states, over_cores(sent), *e_in, slot_rows, receiver_rows, send_rows],
+        scalars=1,
+    )
     rows = edge_dev + 2 * nodes
     (pack,) = stage(pack_extra, [((rows, width), bf16)], [edge_cot, node_cot, gain_e, gain_n])
     packs = [pack] + over_groups(pack)
     (sent,) = stage(functools.partial(send_half, groups), [((rows - half, groups * width), bf16)], packs)
     extra_came = over_cores(sent)
-    n_in = (node_in_weight, over_cores(node_in_weight))
-    n_out = (node_out_weight, over_cores(node_out_weight))
-    edge_pre, part, sent, own, lat, _ = stage(
+    edge_pre, part, sent, own, lat = stage(
         finish_edges,
         [
             ((half, hidden), f32),
@@ -373,11 +374,11 @@
             ((half + nodes, features), bf16),
             ((nodes, features), bf16),
             ((nodes, hidden), f32),
-            ((table, features), bf16),
         ],
         [latents, pre, pick, take, *e_in, *e_out, *n_in],
-    )
-    normed, inverse, next_mine, next_sent, aggregate, lat_all, extra, _ = stage(
+        scratch=[((table, features), bf16)],
+    )
+    normed, inverse, next_mine, next_sent, aggregate, lat_all, extra = stage(
         functools.partial(update_edges, groups),
         [
             ((half, features), f32),
@@ -387,30 +388,27 @@
             ((nodes, features), f32),
             ((nodes, features), f32),
             ((half + 2 * nodes, features), bf16),
-            ((half, features), bf16),
         ],
         [part, lat, *over_groups(sent), *packs, extra_came, state, take],
+        scratch=[((half, features), bf16)],
     )
     aggregate2 = over_cores(aggregate)
     next_came = over_cores(next_sent)
-    node_next, kept, *sents, dpre, node_dpre, _, _ = stage(
+    node_next, kept, *sents, dpre, node_dpre = stage(
         functools.partial(turn, groups),
         [((nodes, width), bf16), ((half, wide), f32)]
         + [((half, wide), bf16)] * (groups - 1)
-        + [
-            ((half, hidden), bf16),
-            ((nodes, hidden), bf16),
-            ((nodes, features), bf16),
-            ((half, features), f32),
-        ],
+        + [((half, hidden), bf16), ((nodes, hidden), bf16)],
         [*far, aggregate, aggregate2, own, lat_all, extra, take, normed, inverse, edge_pre]
         + [*e_in, *e_out, *n_in, *n_out],
+        scratch=[((nodes, features), bf16), ((half, features), f32)],
     )
     sents = [swapped(s, cores * k) for k, s in enumerate(sents, 1)]
-    spread, _ = stage(
+    (spread,) = stage(
         spread_nodes,
-        [((blocks * feats, nodes, width), bf16), ((table, features), f32)],
+        [((blocks * feats, nodes, width), bf16)],
         [dpre, node_dpre, pick, take, *e_in, *n_in],
+        scratch=[((table, features), f32)],
     )
     shares = lax.all_to_all(spread, everyone, 0, 0)
     grad_mine, grad_sent = stage(

time: 51.8 us -> 41.5 us (0.80)
  waiting for transfers between devices: 19.2 us -> 12.2 us
  local copies, waits for them, and re-layouts: 5.56 us -> 3.12 us
  Pallas kernels: 7.38 us -> 6.25 us
    ppermute x16 -> x15, waiting for transfers between devices: 15.1 us -> 10.4 us  [swapped(): return lax.ppermute(values, 'feat', [(i, i ^ bits) for i in range(feats)])]
    unnamed x28 -> x24, local copies, waits for them, and re-layouts: 3.91 us -> 1.42 us
    all_to_all x1, waiting for transfers between devices: 3.99 us -> 1.69 us  [shards(): lax.all_to_all(jnp.broadcast_to(latent[None], (blocks * feats, nodes, wid...]
    pallas_call x10 -> x11, Pallas kernels: 7.38 us -> 6.25 us  [stage(): pl.pallas_call(kernel, out_shape=[jax.ShapeDtypeStruct(shape, kind) for s...]
    ppermute x16 -> x15, starting transfers between devices: 8.75 us -> 9.64 us  [swapped(): return lax.ppermute(values, 'feat', [(i, i ^ bits) for i in range(feats)])]
    broadcast_in_dim x1, local copies, waits for them, and re-layouts: 0.64 us -> 1.32 us  [shards(): jnp.broadcast_to(latent[None], (blocks * feats, nodes, width))]
    slice x2, local copies, waits for them, and re-layouts: 1.01 us -> 0.37 us  [shards(): node_in_weight[:, features:]]
    all_to_all x1, starting transfers between devices: 6.16 us -> 5.61 us  [shards(): lax.all_to_all(jnp.broadcast_to(latent[None], (blocks * feats, nodes, wid...]
  transfers between devices with their start and end apart: 18 -> 17, of which waited for: 10 -> 8; matrix products, arithmetic and copies ran while one was open for 1% -> 3% of each run, Pallas kernels for 5% -> 6%
where the time goes in v10:
time: 41.5 us; the launch traced here: 41.1 us
  starting transfers between devices  18.7 us (45%)
  waiting for transfers between devices  12.2 us (29%)
  Pallas kernels  6.25 us (15%)
  local copies, waits for them, and re-layouts  3.12 us (8%)
  between operations  0.79 us (2%)
    ppermute x15, waiting for transfers between devices, swapped(): return lax.ppermute(values, 'feat', [(i, i ^ bits) for i in range(feats)])  10.4 us
    ppermute x15, starting transfers between devices, swapped(): return lax.ppermute(values, 'feat', [(i, i ^ bits) for i in range(feats)])  9.64 us
    pallas_call x11, Pallas kernels, stage(): pl.pallas_call(kernel, out_shape=[jax.ShapeDtypeStruct(shape, kind) for s...  6.25 us
    all_to_all x1, starting transfers between devices, shards(): lax.all_to_all(jnp.broadcast_to(latent[None], (blocks * feats, nodes, wid...  5.61 us
    all_to_all x1, starting transfers between devices, shards(): shares = lax.all_to_all(spread, everyone, 0, 0)  3.49 us
    all_to_all x1, waiting for transfers between devices, shards(): lax.all_to_all(jnp.broadcast_to(latent[None], (blocks * feats, nodes, wid...  1.69 us
    unnamed x24, local copies, waits for them, and re-layouts  1.42 us
    broadcast_in_dim x1, local copies, waits for them, and re-layouts, shards(): jnp.broadcast_to(latent[None], (blocks * feats, nodes, width))  1.32 us
  transfers between devices with their start and end apart: 17, of which 8 were waited for; matrix products, arithmetic and copies ran while one was open for 3% of the time, Pallas kernels for 6%

profile of v10, /device:TPU:0, one launch (start us, length us, event | category | flops | bytes accessed | tf_op | source)
XLA Modules:
  0.0 41.1 jit_solution(16442062370060796754)
XLA Ops:
  0.7 0.5 %collective-permute-start.2 = (bf16[128,1536]{1,0:T(8,128)(2,1)}, bf16[128,1536]{1,0:T(8,128)(2,1)S(1)}, u32[]{:S(2)}, u32[]{:S(2)}) collective-permute-start(bf16[128,1536]{1,0:T(8,128)(2,1)} %e_mine.1), channel_id=1, source_target_pairs={{0,1},{1,0},{2,3},{3,2},{4,5},{5,4},{6,7},{7,6},{8,9},{9,8},{10,11... | collective-permute-start | bytes 1179656 | tf_op jit(solution)/shard_map/ppermute | solution.py:334
  1.7 3.0 %collective-permute-start.9 = (bf16[128,1024]{1,0:T(8,128)(2,1)S(1)}, bf16[128,1024]{1,0:T(8,128)(2,1)S(1)}, u32[]{:S(2)}, u32[]{:S(2)}) collective-permute-start(bf16[128,1024]{1,0:T(8,128)(2,1)S(1)} %pad_maximum_fusion), channel_id=1, source_target_pairs={{0,2},{1,3},{2,0},{3,1},{4,6},{5,7},{6,4},{7,5},{8,10},{9,11},{10,... | collective-permute-start | bytes 786440 | tf_op jit(solution)/shard_map/ppermute | solution.py:334
  4.7 0.8 %collective-permute-start = (bf16[256,128]{1,0:T(8,128)(2,1)S(1)}, bf16[256,128]{1,0:T(8,128)(2,1)S(1)}, u32[]{:S(2)}, u32[]{:S(2)}) collective-permute-start(bf16[256,128]{1,0:T(8,128)(2,1)S(1)} %copy-done.4), channel_id=1, source_target_pairs={{0,2},{1,3},{2,0},{3,1},{4,6},{5,7},{6,4},{7,5},{8,10},{9,11},{10,... | collective-permute-start | bytes 196616 | tf_op jit(solution)/shard_map/ppermute | solution.py:334
  5.7 1.3 %broadcast_in_dim.2 = bf16[16,16,128]{2,1,0:T(8,128)(2,1)} broadcast(bf16[16,128]{1,0:T(8,128)(2,1)} %param.13), dimensions={1,2} | broadcast | bytes 69632 | tf_op jit(solution)/shard_map/broadcast_in_dim | solution.py:347
  7.1 5.6 %all-to-all-start = ((bf16[16,16,128]{2,1,0:T(8,128)(2,1)}), bf16[16,16,128]{2,1,0:T(8,128)(2,1)S(1)}, u32[]{:S(2)}, u32[]{:S(2)}) async-start(bf16[16,16,128]{2,1,0:T(8,128)(2,1)} %broadcast_in_dim.2), calls=%async_computation | async-start | bytes 131072 | tf_op jit(solution)/shard_map/all_to_all | solution.py:346
  12.7 0.5 %collective-permute-start.10 = (bf16[128,1024]{1,0:T(8,128)(2,1)S(1)}, bf16[128,1024]{1,0:T(8,128)(2,1)S(1)}, u32[]{:S(2)}, u32[]{:S(2)}) collective-permute-start(bf16[128,1024]{1,0:T(8,128)(2,1)S(1)} %collective-permute-done.9.refs_0_), channel_id=1, source_target_pairs={{0,1},{1,0},{2,3},{3,2},{4,5},{5,4},{6,7},{7,6},{8,9},{9,8},{10,11... | collective-permute-start | bytes 786440 | tf_op jit(solution)/shard_map/ppermute | solution.py:334
  13.4 0.5 %copy-done.6 = bf16[16,128]{1,0:T(8,128)(2,1)S(1)} copy-done((bf16[16,128]{1,0:T(8,128)(2,1)S(1)}, bf16[16,128]{1,0:T(8,128)(2,1)}, u32[]{:S(2)}) %copy-start.6) | copy-done | bytes 4120
  14.5 1.8 %collective-permute-start.6 = (bf16[288,128]{1,0:T(8,128)(2,1)S(1)}, bf16[288,128]{1,0:T(8,128)(2,1)S(1)}, u32[]{:S(2)}, u32[]{:S(2)}) collective-permute-start(bf16[288,128]{1,0:T(8,128)(2,1)S(1)} %shard_map.159.refs_0_.refs_3_), channel_id=1, source_target_pairs={{0,2},{1,3},{2,0},{3,1},{4,6},{5,7},{6,4},{7,5},{8,10},{9,11},{10,... | collective-permute-start | bytes 221192 | tf_op jit(solution)/shard_map/ppermute | solution.py:334
  16.3 0.7 %copy-done.8 = s32[256]{0:T(256)S(1)} copy-done((s32[256]{0:T(256)S(1)}, s32[256]{0:T(256)}, u32[]{:S(2)}) %copy-start.8) | copy-done | bytes 1048
  17.0 0.9 %shard_map.157 = (bf16[128,512]{1,0:T(8,128)(2,1)S(1)}, f32[128,256]{1,0:T(8,128)S(1)}, bf16[64,128]{1,0:T(8,128)(2,1)S(1)}, bf16[16,128]{1,0:T(8,128)(2,1)S(1)}) custom-call(bf16[256,128]{1,0:T(8,128)(2,1)S(1)} %copy-done.4, bf16[256,128]{1,0:T(8,128)(2,1)S(1)} %collective-permute-done.refs_1_, bf16[128,256]{1,0:T(8,128)(2,1)S(1)} %collective-permute-done.1.refs_2_, ...), custom_call_target="tpu_custom_call" | custom-call | flops 16777216 | bytes 985600 | tf_op jit(solution)/shard_map/pallas_call | solution.py:73
  17.9 1.7 %all-to-all-done.came = bf16[16,16,128]{2,1,0:T(8,128)(2,1)S(1)} async-done(((bf16[16,16,128]{2,1,0:T(8,128)(2,1)}), bf16[16,16,128]{2,1,0:T(8,128)(2,1)S(1)}, u32[]{:S(2)}, u32[]{:S(2)}) %all-to-all-start) | async-done | bytes 65568 | tf_op jit(solution)/shard_map/all_to_all | solution.py:346
  19.6 0.6 %shard_map.158 = (f32[128,256]{1,0:T(8,128)S(1)}, f32[128,512]{1,0:T(8,128)S(1)}, bf16[144,512]{1,0:T(8,128)(2,1)S(1)}, bf16[16,512]{1,0:T(8,128)(2,1)S(1)}, f32[16,256]{1,0:T(8,128)S(1)}) custom-call(bf16[16,16,128]{2,1,0:T(8,128)(2,1)S(1)} %all-to-all-done.came, f32[128,256]{1,0:T(8,128)S(1)} %get-tuple-element.29.pre, ...), custom_call_target="tpu_custom_call" | custom-call | flops 16777216 | bytes 1789952 | tf_op jit(solution)/shard_map/pallas_call | solution.py:73
  20.4 0.6 %collective-permute-start.7 = (bf16[160,256]{1,0:T(8,128)(2,1)S(1)}, bf16[160,256]{1,0:T(8,128)(2,1)S(1)}, u32[]{:S(2)}, u32[]{:S(2)}) collective-permute-start(bf16[160,256]{1,0:T(8,128)(2,1)S(1)} %shard_map.160), channel_id=1, source_target_pairs={{0,1},{1,0},{2,3},{3,2},{4,5},{5,4},{6,7},{7,6},{8,9},{9,8},{10,11... | collective-permute-start | bytes 245768 | tf_op jit(solution)/shard_map/ppermute | solution.py:334
  21.0 0.9 %collective-permute-done.7.refs_5_ = bf16[160,256]{1,0:T(8,128)(2,1)S(1)} collective-permute-done((bf16[160,256]{1,0:T(8,128)(2,1)S(1)}, bf16[160,256]{1,0:T(8,128)(2,1)S(1)}, u32[]{:S(2)}, u32[]{:S(2)}) %collective-permute-start.7) | collective-permute-done | bytes 81952 | tf_op jit(solution)/shard_map/ppermute | solution.py:334
  21.9 3.7 %collective-permute-done.5.refs_2_ = bf16[144,512]{1,0:T(8,128)(2,1)S(1)} collective-permute-done((bf16[144,512]{1,0:T(8,128)(2,1)S(1)}, bf16[144,512]{1,0:T(8,128)(2,1)S(1)}, u32[]{:S(2)}, u32[]{:S(2)}) %collective-permute-start.5) | collective-permute-done | bytes 147488 | tf_op jit(solution)/shard_map/ppermute | solution.py:334
  25.8 1.2 %collective-permute-done.11.refs_3_ = f32[16,512]{1,0:T(8,128)S(1)} collective-permute-done((f32[16,512]{1,0:T(8,128)S(1)}, f32[16,512]{1,0:T(8,128)S(1)}, u32[]{:S(2)}, u32[]{:S(2)}) %collective-permute-start.11) | collective-permute-done | bytes 32800 | tf_op jit(solution)/shard_map/ppermute | solution.py:334
  27.0 2.0 %shard_map.162 = (bf16[16,128]{1,0:T(8,128)(2,1)}, f32[128,256]{1,0:T(8,128)S(1)}, bf16[128,256]{1,0:T(8,128)(2,1)S(1)}, bf16[128,256]{1,0:T(8,128)(2,1)S(1)}, bf16[16,256]{1,0:T(8,128)(2,1)S(1)}) custom-call(bf16[128,1024]{1,0:T(8,128)(2,1)S(1)} %collective-permute-done.9.refs_0_, bf16[128,1024]{1,0:T(8,128)(2,1)S(1)} %collective-permute-done.10.refs_1_, ...), custom_call_target="tpu_custom_call" | custom-call | flops 16777216 | bytes 3035648 | tf_op jit(solution)/shard_map/pallas_call | solution.py:73
  29.1 1.1 %shard_map.165 = bf16[16,16,128]{2,1,0:T(8,128)(2,1)} custom-call(bf16[128,256]{1,0:T(8,128)(2,1)S(1)} %get-tuple-element.52.dpre, bf16[16,256]{1,0:T(8,128)(2,1)S(1)} %get-tuple-element.53.node_dpre, bf16[64,128]{1,0:T(8,128)(2,1)S(1)} %get-tuple-element.30.pick, bf16[16,128]{1,0:T(8,128)(2,1)S(1)} %get-tuple-element.31.take.refs_7_, ...), custom_call_target="tpu_custom_call" | custom-call | flops 16777216 | bytes 1404928 | tf_op jit(solution)/shard_map/pallas_call | solution.py:73
  30.2 3.5 %all-to-all-start.1 = ((bf16[16,16,128]{2,1,0:T(8,128)(2,1)}), bf16[16,16,128]{2,1,0:T(8,128)(2,1)S(1)}, u32[]{:S(2)}, u32[]{:S(2)}) async-start(bf16[16,16,128]{2,1,0:T(8,128)(2,1)} %shard_map.165), calls=%async_computation.1 | async-start | bytes 131072 | tf_op jit(solution)/shard_map/all_to_all | solution.py:413
  33.7 1.8 %collective-permute-start.13 = (bf16[128,256]{1,0:T(8,128)(2,1)S(1)}, bf16[128,256]{1,0:T(8,128)(2,1)S(1)}, u32[]{:S(2)}, u32[]{:S(2)}) collective-permute-start(bf16[128,256]{1,0:T(8,128)(2,1)S(1)} %get-tuple-element.46), channel_id=1, source_target_pairs={{0,2},{1,3},{2,0},{3,1},{4,6},{5,7},{6,4},{7,5},{8,10},{9,11},{10,... | collective-permute-start | bytes 196616 | tf_op jit(solution)/shard_map/ppermute | solution.py:334
  35.5 3.0 %collective-permute-done.13.refs_1_ = bf16[128,256]{1,0:T(8,128)(2,1)S(1)} collective-permute-done((bf16[128,256]{1,0:T(8,128)(2,1)S(1)}, bf16[128,256]{1,0:T(8,128)(2,1)S(1)}, u32[]{:S(2)}, u32[]{:S(2)}) %collective-permute-start.13) | collective-permute-done | bytes 65568 | tf_op jit(solution)/shard_map/ppermute | solution.py:334
  38.5 1.2 %collective-permute-done.14.grad_came = bf16[128,128]{1,0:T(8,128)(2,1)S(1)} collective-permute-done((bf16[128,128]{1,0:T(8,128)(2,1)S(1)}, bf16[128,128]{1,0:T(8,128)(2,1)S(1)}, u32[]{:S(2)}, u32[]{:S(2)}) %collective-permute-start.14) | collective-permute-done | bytes 32800 | tf_op jit(solution)/shard_map/ppermute | solution.py:334
  39.7 0.7 %shard_map.164 = (bf16[256,128]{1,0:T(8,128)(2,1)}, bf16[256,128]{1,0:T(8,128)(2,1)}) custom-call(bf16[128,128]{1,0:T(8,128)(2,1)S(1)} %get-tuple-element.36.next_mine, bf16[128,128]{1,0:T(8,128)(2,1)S(1)} %collective-permute-done.8.next_came, bf16[128,128]{1,0:T(8,128)(2,1)S(1)} %get-tuple-element.47.grad_mine, ...), custom_call_target="tpu_custom_call" | custom-call | flops 16777216 | bytes 131072 | tf_op jit(solution)/shard_map/pallas_call | solution.py:73
  40.5 0.6 %shard_map.166 = bf16[16,128]{1,0:T(8,128)(2,1)} custom-call(bf16[16,16,128]{2,1,0:T(8,128)(2,1)S(1)} %all-to-all-done.1.shares, bf16[16,128]{1,0:T(8,128)(2,1)S(1)} %copy-done.6), custom_call_target="tpu_custom_call" | custom-call | flops 16777216 | bytes 69632 | tf_op jit(solution)/shard_map/pallas_call | solution.py:73
  (49 shorter events, 2.2 us)
Async XLA Ops:
  0.7 15.7 %collective-permute-start.2 = (bf16[128,1536]{1,0:T(8,128)(2,1)}, bf16[128,1536]{1,0:T(8,128)(2,1)S(1)}, u32[]{:S(2)}, u32[]{:S(2)}) collective-permute-start(bf16[128,1536]{1,0:T(8,128)(2,1)} %e_mine.1), channel_id=1, source_target_pairs={{0,1},{1,0},{2,3},{3,2},{4,5},{5,4},{6,7},{7,6},{8,9},{9,8},{10,11... | collective-permute-start | bytes 1179656 | tf_op jit(solution)/shard_map/ppermute | solution.py:334
  1.6 3.1 %copy-start.1 = (bf16[128,1024]{1,0:T(8,128)(2,1)S(1)}, bf16[128,1024]{1,0:T(8,128)(2,1)}, u32[]{:S(2)}) copy-start(bf16[128,1024]{1,0:T(8,128)(2,1)} %in_mine.1) | copy-start | bytes 786436
  1.6 3.1 %copy-start.4 = (bf16[256,128]{1,0:T(8,128)(2,1)S(1)}, bf16[256,128]{1,0:T(8,128)(2,1)}, u32[]{:S(2)}) copy-start(bf16[256,128]{1,0:T(8,128)(2,1)} %refs_0_.3) | copy-start | bytes 196612
  1.6 3.9 %copy-start.2 = (bf16[128,512]{1,0:T(8,128)(2,1)S(1)}, bf16[128,512]{1,0:T(8,128)(2,1)}, u32[]{:S(2)}) copy-start(bf16[128,512]{1,0:T(8,128)(2,1)} %refs_13_.1) | copy-start | bytes 393220
  1.6 11.7 %copy-start.5 = (bf16[256,128]{1,0:T(8,128)(2,1)S(1)}, bf16[256,128]{1,0:T(8,128)(2,1)}, u32[]{:S(2)}) copy-start(bf16[256,128]{1,0:T(8,128)(2,1)} %edge_cot.1) | copy-start | bytes 196612
  1.6 14.7 %copy-start = (bf16[128,1536]{1,0:T(8,128)(2,1)S(1)}, bf16[128,1536]{1,0:T(8,128)(2,1)}, u32[]{:S(2)}) copy-start(bf16[128,1536]{1,0:T(8,128)(2,1)} %e_mine.1) | copy-start | bytes 1179652
  1.7 11.0 %collective-permute-start.9 = (bf16[128,1024]{1,0:T(8,128)(2,1)S(1)}, bf16[128,1024]{1,0:T(8,128)(2,1)S(1)}, u32[]{:S(2)}, u32[]{:S(2)}) collective-permute-start(bf16[128,1024]{1,0:T(8,128)(2,1)S(1)} %pad_maximum_fusion), channel_id=1, source_target_pairs={{0,2},{1,3},{2,0},{3,1},{4,6},{5,7},{6,4},{7,5},{8,10},{9,11},{10,... | collective-permute-start | bytes 786440 | tf_op jit(solution)/shard_map/ppermute | solution.py:334
  4.7 14.9 %collective-permute-start.4 = (bf16[128,1024]{1,0:T(8,128)(2,1)S(1)}, bf16[128,1024]{1,0:T(8,128)(2,1)S(1)}, u32[]{:S(2)}, u32[]{:S(2)}) collective-permute-start(bf16[128,1024]{1,0:T(8,128)(2,1)S(1)} %copy-done.1), channel_id=1, source_target_pairs={{0,1},{1,0},{2,3},{3,2},{4,5},{5,4},{6,7},{7,6},{8,9},{9,8},{10,11... | collective-permute-start | bytes 786440 | tf_op jit(solution)/shard_map/ppermute | solution.py:334
  4.7 8.5 %collective-permute-start = (bf16[256,128]{1,0:T(8,128)(2,1)S(1)}, bf16[256,128]{1,0:T(8,128)(2,1)S(1)}, u32[]{:S(2)}, u32[]{:S(2)}) collective-permute-start(bf16[256,128]{1,0:T(8,128)(2,1)S(1)} %copy-done.4), channel_id=1, source_target_pairs={{0,2},{1,3},{2,0},{3,1},{4,6},{5,7},{6,4},{7,5},{8,10},{9,11},{10,... | collective-permute-start | bytes 196616 | tf_op jit(solution)/shard_map/ppermute | solution.py:334
  5.5 14.1 %collective-permute-start.3 = (bf16[128,512]{1,0:T(8,128)(2,1)S(1)}, bf16[128,512]{1,0:T(8,128)(2,1)S(1)}, u32[]{:S(2)}, u32[]{:S(2)}) collective-permute-start(bf16[128,512]{1,0:T(8,128)(2,1)S(1)} %copy-done.2), channel_id=1, source_target_pairs={{0,1},{1,0},{2,3},{3,2},{4,5},{5,4},{6,7},{7,6},{8,9},{9,8},{10,11... | collective-permute-start | bytes 393224 | tf_op jit(solution)/shard_map/ppermute | solution.py:334
  7.1 12.5 %all-to-all-start = ((bf16[16,16,128]{2,1,0:T(8,128)(2,1)}), bf16[16,16,128]{2,1,0:T(8,128)(2,1)S(1)}, u32[]{:S(2)}, u32[]{:S(2)}) async-start(bf16[16,16,128]{2,1,0:T(8,128)(2,1)} %broadcast_in_dim.2), calls=%async_computation | async-start | bytes 131072 | tf_op jit(solution)/shard_map/all_to_all | solution.py:346
  12.7 13.1 %collective-permute-start.10 = (bf16[128,1024]{1,0:T(8,128)(2,1)S(1)}, bf16[128,1024]{1,0:T(8,128)(2,1)S(1)}, u32[]{:S(2)}, u32[]{:S(2)}) collective-permute-start(bf16[128,1024]{1,0:T(8,128)(2,1)S(1)} %collective-permute-done.9.refs_0_), channel_id=1, source_target_pairs={{0,1},{1,0},{2,3},{3,2},{4,5},{5,4},{6,7},{7,6},{8,9},{9,8},{10,11... | collective-permute-start | bytes 786440 | tf_op jit(solution)/shard_map/ppermute | solution.py:334
  13.2 1.3 %collective-permute-start.1 = (bf16[128,256]{1,0:T(8,128)(2,1)S(1)}, bf16[128,256]{1,0:T(8,128)(2,1)S(1)}, u32[]{:S(2)}, u32[]{:S(2)}) collective-permute-start(bf16[128,256]{1,0:T(8,128)(2,1)S(1)} %shard_map.156), channel_id=1, source_target_pairs={{0,1},{1,0},{2,3},{3,2},{4,5},{5,4},{6,7},{7,6},{8,9},{9,8},{10,11... | collective-permute-start | bytes 196616 | tf_op jit(solution)/shard_map/ppermute | solution.py:334
  14.0 2.3 %copy-start.7 = (s32[4,4,8]{2,1,0:T(4,128)S(1)}, s32[4,4,8]{2,1,0:T(4,128)}, u32[]{:S(2)}) copy-start(s32[4,4,8]{2,1,0:T(4,128)} %refs_7_.1) | copy-start | bytes 1540
  14.0 2.3 %copy-start.9 = (s32[256]{0:T(256)S(1)}, s32[256]{0:T(256)}, u32[]{:S(2)}) copy-start(s32[256]{0:T(256)} %param.17) | copy-start | bytes 3076
  14.5 5.9 %collective-permute-start.6 = (bf16[288,128]{1,0:T(8,128)(2,1)S(1)}, bf16[288,128]{1,0:T(8,128)(2,1)S(1)}, u32[]{:S(2)}, u32[]{:S(2)}) collective-permute-start(bf16[288,128]{1,0:T(8,128)(2,1)S(1)} %shard_map.159.refs_0_.refs_3_), channel_id=1, source_target_pairs={{0,2},{1,3},{2,0},{3,1},{4,6},{5,7},{6,4},{7,5},{8,10},{9,11},{10,... | collective-permute-start | bytes 221192 | tf_op jit(solution)/shard_map/ppermute | solution.py:334
  20.2 5.3 %collective-permute-start.5 = (bf16[144,512]{1,0:T(8,128)(2,1)S(1)}, bf16[144,512]{1,0:T(8,128)(2,1)S(1)}, u32[]{:S(2)}, u32[]{:S(2)}) collective-permute-start(bf16[144,512]{1,0:T(8,128)(2,1)S(1)} %get-tuple-element.34), channel_id=1, source_target_pairs={{0,2},{1,3},{2,0},{3,1},{4,6},{5,7},{6,4},{7,5},{8,10},{9,11},{10,... | collective-permute-start | bytes 442376 | tf_op jit(solution)/shard_map/ppermute | solution.py:334
  20.4 5.5 %collective-permute-start.12 = (bf16[128,512]{1,0:T(8,128)(2,1)S(1)}, bf16[128,512]{1,0:T(8,128)(2,1)S(1)}, u32[]{:S(2)}, u32[]{:S(2)}) collective-permute-start(bf16[128,512]{1,0:T(8,128)(2,1)S(1)} %copy-done.3), channel_id=1, source_target_pairs={{0,1},{1,0},{2,3},{3,2},{4,5},{5,4},{6,7},{7,6},{8,9},{9,8},{10,11... | collective-permute-start | bytes 393224 | tf_op jit(solution)/shard_map/ppermute | solution.py:334
  20.4 1.5 %collective-permute-start.7 = (bf16[160,256]{1,0:T(8,128)(2,1)S(1)}, bf16[160,256]{1,0:T(8,128)(2,1)S(1)}, u32[]{:S(2)}, u32[]{:S(2)}) collective-permute-start(bf16[160,256]{1,0:T(8,128)(2,1)S(1)} %shard_map.160), channel_id=1, source_target_pairs={{0,1},{1,0},{2,3},{3,2},{4,5},{5,4},{6,7},{7,6},{8,9},{9,8},{10,11... | collective-permute-start | bytes 245768 | tf_op jit(solution)/shard_map/ppermute | solution.py:334
  25.8 1.2 %collective-permute-start.11 = (f32[16,512]{1,0:T(8,128)S(1)}, f32[16,512]{1,0:T(8,128)S(1)}, u32[]{:S(2)}, u32[]{:S(2)}) collective-permute-start(f32[16,512]{1,0:T(8,128)S(1)} %get-tuple-element.38.refs_2_), channel_id=1, source_target_pairs={{0,1},{1,0},{2,3},{3,2},{4,5},{5,4},{6,7},{7,6},{8,9},{9,8},{10,11... | collective-permute-start | bytes 98312 | tf_op jit(solution)/shard_map/ppermute | solution.py:334
  30.2 10.4 %all-to-all-start.1 = ((bf16[16,16,128]{2,1,0:T(8,128)(2,1)}), bf16[16,16,128]{2,1,0:T(8,128)(2,1)S(1)}, u32[]{:S(2)}, u32[]{:S(2)}) async-start(bf16[16,16,128]{2,1,0:T(8,128)(2,1)} %shard_map.165), calls=%async_computation.1 | async-start | bytes 131072 | tf_op jit(solution)/shard_map/all_to_all | solution.py:413
  33.7 4.8 %collective-permute-start.13 = (bf16[128,256]{1,0:T(8,128)(2,1)S(1)}, bf16[128,256]{1,0:T(8,128)(2,1)S(1)}, u32[]{:S(2)}, u32[]{:S(2)}) collective-permute-start(bf16[128,256]{1,0:T(8,128)(2,1)S(1)} %get-tuple-element.46), channel_id=1, source_target_pairs={{0,2},{1,3},{2,0},{3,1},{4,6},{5,7},{6,4},{7,5},{8,10},{9,11},{10,... | collective-permute-start | bytes 196616 | tf_op jit(solution)/shard_map/ppermute | solution.py:334
  35.5 3.1 %collective-permute-start.8 = (bf16[128,128]{1,0:T(8,128)(2,1)S(1)}, bf16[128,128]{1,0:T(8,128)(2,1)S(1)}, u32[]{:S(2)}, u32[]{:S(2)}) collective-permute-start(bf16[128,128]{1,0:T(8,128)(2,1)S(1)} %get-tuple-element.37), channel_id=1, source_target_pairs={{0,1},{1,0},{2,3},{3,2},{4,5},{5,4},{6,7},{7,6},{8,9},{9,8},{10,11... | collective-permute-start | bytes 98312 | tf_op jit(solution)/shard_map/ppermute | solution.py:334
  38.5 1.3 %collective-permute-start.14 = (bf16[128,128]{1,0:T(8,128)(2,1)S(1)}, bf16[128,128]{1,0:T(8,128)(2,1)S(1)}, u32[]{:S(2)}, u32[]{:S(2)}) collective-permute-start(bf16[128,128]{1,0:T(8,128)(2,1)S(1)} %get-tuple-element.48), channel_id=1, source_target_pairs={{0,1},{1,0},{2,3},{3,2},{4,5},{5,4},{6,7},{7,6},{8,9},{9,8},{10,11... | collective-permute-start | bytes 98312 | tf_op jit(solution)/shard_map/ppermute | solution.py:334
  (6 other events, 4.6 us)

commit v11 on v10

--- a/solution.py
+++ b/solution.py
@@ -96,6 +96,17 @@
     return value
 
 
+def spread_latent(latent, spread):
+    spread[...] = jnp.broadcast_to(latent[...][None], spread.shape)
+
+
+def merge_state(state, state2, pack):
+    _, core = place()
+    half = pack.shape[0]
+    mine = pl.ds(pl.multiple_of(core * half, half), half)
+    pack[...] = pair(state[mine], state2[mine], core)
+
+
 def pack_extra(edge_cot, node_cot, gain_e, gain_n, pack):
     edge_dev = edge_cot.shape[0]
     nodes = node_cot.shape[0]
@@ -122,16 +133,14 @@
 
 def prepare_edges(groups, *refs):
     packs = refs[:groups]
-    theirs, mine, other, slot, receiver, send_rows, state, pre, pick, take = refs[groups:]
+    mine, other, slot, receiver, send_rows, state, pre, pick, take = refs[groups:]
     group, core = place()
     block = lax.axis_index("nodes")
     features = state.shape[1]
     nodes, half = take.shape
-    width = packs[0].shape[1]
     blocks, _, slots = send_rows.shape
     for step, pack in enumerate(packs):
-        both = pair(half_rows(pack, core, half), theirs[:, step * width : (step + 1) * width], core)
-        state[:, lanes(group ^ step, width * cores)] = both
+        state[:, lanes(group ^ step, pack.shape[1])] = pack[...]
 
     slot_row = slot[pl.ds(core, 1)]
     sender = block * nodes + slot_row
@@ -146,11 +155,11 @@
     pre[...] = dot_rows(state[...], weight)
 
 
-def finish_edges(came, pre, pick, take, mine, other, out_mine, out_other, n_mine, n_other, edge_pre, part, sent, own, lat, table):
+def finish_edges(came, pre, pick, take, mine, other, n_mine, n_other, edge_pre, sent, own, lat, table):
     block = lax.axis_index("nodes")
     count, nodes, width = came.shape
     rows, features = table.shape
-    half, hidden = pre.shape
+    half = pre.shape[0]
     feats = features // width
     for source in range(count):
         first, column = source // feats * nodes, source % feats * width
@@ -167,21 +176,16 @@
     chosen = jnp.concatenate([pick[...], pick[...], take[...], take[...]], axis=0)
     value = pre[...] + dot_cols(chosen, jnp.concatenate([high, low, here_high, here_low], axis=0))
     edge_pre[...] = value
-    act = (value * sigmoid(value)).astype(bf16)
-    out = dot(act, jnp.concatenate([out_mine[...], out_other[...]], axis=0))
-    part[...] = out
-    sent[:half] = out.astype(bf16)
+    sent[:half] = (value * sigmoid(value)).astype(bf16)
     nodes_pre = dot_rows(latent, jnp.concatenate([n_mine[:, :features], n_other[:, :features]], axis=0))
     lat[...] = nodes_pre
-    high, low = split(nodes_pre)
-    sent[half:] = jnp.zeros((nodes, features), bf16)
-    sent[half:, :hidden] = high
-    sent[half:, hidden : 2 * hidden] = low
+    sent[half:] = jnp.concatenate(split(nodes_pre), axis=0)
 
 
 def update_edges(groups, *refs):
-    part, lat, came, packs = refs[0], refs[1], refs[2 : groups + 1], refs[groups + 1 : 2 * groups + 1]
-    theirs, state, take, normed, inverse, kept, lent, aggregate, lat_all, extra, next_all = refs[2 * groups + 1 :]
+    lat, acts, packs, refs = refs[0], refs[1 : groups + 1], refs[groups + 1 : 2 * groups + 1], refs[2 * groups + 1 :]
+    far, refs = refs[: 2 * (groups - 1)], refs[2 * (groups - 1) :]
+    out_mine, out_other, theirs, state, take, normed, inverse, kept, lent, aggregate, lat_all, extra, next_all = refs
     group, core = place()
     nodes, half = take.shape
     width = kept.shape[1]
@@ -189,12 +193,13 @@
     for step, pack in enumerate(packs):
         both = pair(half_rows(pack, core, half), theirs[:, step * width : (step + 1) * width], core)
         extra[:, lanes(group ^ step, width * cores)] = both
-    value = part[...]
     lat_all[:, :hidden] = lat[...]
-    for step, ref in enumerate(came, 1):
-        value = value + ref[:half].astype(f32)
-        high, low = ref[half:, :hidden], ref[half:, hidden : 2 * hidden]
+    for step, act in enumerate(acts[1:], 1):
+        high, low = act[half : half + nodes], act[half + nodes :]
         lat_all[:, step * hidden : (step + 1) * hidden] = high.astype(f32) + low.astype(f32)
+    features = state.shape[1]
+    weight = jnp.concatenate([out_mine[...], out_other[...]] + [f[:, 2 * features :] for f in far], axis=0)
+    value = dot(jnp.concatenate([act[:half] for act in acts], axis=1), weight)
     normed_rows, inverse_rows = normalize(value)
     normed[...] = normed_rows
     inverse[...] = inverse_rows
@@ -224,7 +229,7 @@
     from_agg = jnp.concatenate(
         [in_mine[:, features:], in_other[:, features:]] + [f[:, :features] for f in far], axis=0
     )
-    to_out = jnp.concatenate([n_mine[...], n_other[...]] + [f[:, features:] for f in far], axis=0)
+    to_out = jnp.concatenate([n_mine[...], n_other[...]] + [f[:, features : 2 * features] for f in far], axis=0)
     together = (aggregate[...] + aggregate2[...]).astype(bf16)
     pre = lat_all[...] + dot_rows(together, from_agg)
     act = (pre * sigmoid(pre)).astype(bf16)
@@ -343,22 +348,22 @@
     slot_rows = sender_slot.reshape(cores, half)
     receiver_rows = receiver_row.reshape(cores, half)
 
-    latents = lax.all_to_all(
-        jnp.broadcast_to(latent[None], (blocks * feats, nodes, width)), everyone, 0, 0
-    )
-    states = [edge_state] + over_groups(edge_state)
+    (spread,) = stage(spread_latent, [((blocks * feats, nodes, width), bf16)], [latent])
+    latents = lax.all_to_all(spread, everyone, 0, 0)
+    (pack,) = stage(merge_state, [((half, wide), bf16)], [edge_state, over_cores(edge_state)])
+    pack, edge_cot = lax.optimization_barrier((pack, edge_cot))
+    states = [pack] + over_groups(pack)
     e_in = (edge_in_weight, over_cores(edge_in_weight))
     e_out = (edge_out_weight, over_cores(edge_out_weight))
     n_in = (node_in_weight, over_cores(node_in_weight))
     n_out = (node_out_weight, over_cores(node_out_weight))
     far = []
-    for weights in over_groups(jnp.concatenate([node_in_weight[:, features:], node_out_weight], axis=1)):
+    for weights in over_groups(jnp.concatenate([node_in_weight[:, features:], node_out_weight, edge_out_weight], axis=1)):
         far += [weights, over_cores(weights)]
-    (sent,) = stage(functools.partial(send_half, groups), [((half, groups * width), bf16)], states)
     state, pre, pick, take = stage(
         functools.partial(prepare_edges, groups),
         [((half, features), bf16), ((half, hidden), f32), ((table, half), bf16), ((nodes, half), bf16)],
-        [*states, over_cores(sent), *e_in, slot_rows, receiver_rows, send_rows],
+        [*states, *e_in, slot_rows, receiver_rows, send_rows],
         scalars=1,
     )
     rows = edge_dev + 2 * nodes
@@ -366,16 +371,15 @@
     packs = [pack] + over_groups(pack)
     (sent,) = stage(functools.partial(send_half, groups), [((rows - half, groups * width), bf16)], packs)
     extra_came = over_cores(sent)
-    edge_pre, part, sent, own, lat = stage(
+    edge_pre, sent, own, lat = stage(
         finish_edges,
         [
             ((half, hidden), f32),
-            ((half, features), f32),
-            ((half + nodes, features), bf16),
+            ((half + 2 * nodes, hidden), bf16),
             ((nodes, features), bf16),
             ((nodes, hidden), f32),
         ],
-        [latents, pre, pick, take, *e_in, *e_out, *n_in],
+        [latents, pre, pick, take, *e_in, *n_in],
         scratch=[((table, features), bf16)],
     )
     normed, inverse, next_mine, next_sent, aggregate, lat_all, extra = stage(
@@ -389,7 +393,7 @@
             ((nodes, features), f32),
             ((half + 2 * nodes, features), bf16),
         ],
-        [part, lat, *over_groups(sent), *packs, extra_came, state, take],
+        [lat, sent, *over_groups(sent), *packs, *far, *e_out, extra_came, state, take],
         scratch=[((half, features), bf16)],
     )
     aggregate2 = over_cores(aggregate)

time: 41.5 us -> 54.2 us (1.31)
  waiting for transfers between devices: 12.2 us -> 22.3 us
  starting transfers between devices: 18.7 us -> 20.4 us
  other arithmetic: 0.02 us -> 1 us
  local copies, waits for them, and re-layouts: 3.12 us -> 2.33 us
  Pallas kernels: 6.25 us -> 6.93 us
    ppermute x15, waiting for transfers between devices: 10.4 us -> 22.3 us  [swapped(): return lax.ppermute(values, 'feat', [(i, i ^ bits) for i in range(feats)])]
    all_to_all x1, waiting for transfers between devices: 1.69 us -> 0.01 us  [shards(): latents = lax.all_to_all(spread, everyone, 0, 0)]
    broadcast_in_dim x1 -> x0, local copies, waits for them, and re-layouts: 1.32 us -> none  [shards(): jnp.broadcast_to(latent[None], (blocks * feats, nodes, width))]
    all_to_all x1, starting transfers between devices: 3.49 us -> 4.74 us  [shards(): shares = lax.all_to_all(spread, everyone, 0, 0)]
    concatenate x1, other arithmetic: 0.02 us -> 1 us  [shards(): jnp.concatenate([node_in_weight[:, features:], node_out_weight, edge_out_...]
    all_to_all x1, starting transfers between devices: 5.61 us -> 6.33 us  [shards(): latents = lax.all_to_all(spread, everyone, 0, 0)]
    pallas_call x11 -> x12, Pallas kernels: 6.25 us -> 6.93 us  [stage(): pl.pallas_call(kernel, out_shape=[jax.ShapeDtypeStruct(shape, kind) for s...]
    unnamed x24 -> x26, local copies, waits for them, and re-layouts: 1.42 us -> 1.44 us
  transfers between devices with their start and end apart: 17 -> 17, of which waited for: 8 -> 7; matrix products, arithmetic and copies ran while one was open for 3% -> 0% of each run, Pallas kernels for 6% -> 6%
where the time goes in v11:
time: 54.2 us; the launch traced here: 53.8 us
  waiting for transfers between devices  22.3 us (41%)
  starting transfers between devices  20.4 us (38%)
  Pallas kernels  6.93 us (13%)
  local copies, waits for them, and re-layouts  2.33 us (4%)
  other arithmetic  1 us (2%)
  between operations  0.81 us (1%)
    ppermute x15, waiting for transfers between devices, swapped(): return lax.ppermute(values, 'feat', [(i, i ^ bits) for i in range(feats)])  22.3 us
    ppermute x15, starting transfers between devices, swapped(): return lax.ppermute(values, 'feat', [(i, i ^ bits) for i in range(feats)])  9.32 us
    pallas_call x12, Pallas kernels, stage(): pl.pallas_call(kernel, out_shape=[jax.ShapeDtypeStruct(shape, kind) for s...  6.93 us
    all_to_all x1, starting transfers between devices, shards(): latents = lax.all_to_all(spread, everyone, 0, 0)  6.33 us
    all_to_all x1, starting transfers between devices, shards(): shares = lax.all_to_all(spread, everyone, 0, 0)  4.74 us
    unnamed x26, local copies, waits for them, and re-layouts  1.44 us
  transfers between devices with their start and end apart: 17, of which 7 were waited for; matrix products, arithmetic and copies ran while one was open for 0% of the time, Pallas kernels for 6%

profile of v11, /device:TPU:0, one launch (start us, length us, event | category | flops | bytes accessed | tf_op | source)
XLA Modules:
  0.0 53.8 jit_solution(9660624145233129797)
XLA Ops:
  0.7 0.9 %slice-done = bf16[128,512]{1,0:T(8,128)(2,1)S(1)} async-done(((bf16[128,1024]{1,0:T(8,128)(2,1)}), bf16[128,512]{1,0:T(8,128)(2,1)S(1)}, s32[]{:S(2)}) %slice-start) | async-done | bytes 131096 | tf_op jit(solution)/shard_map/slice | solution.py:361
  1.6 1.0 %pad_maximum_fusion = bf16[128,1536]{1,0:T(8,128)(2,1)S(1)} fusion(bf16[128,512]{1,0:T(8,128)(2,1)S(1)} %copy-done.2, bf16[128,512]{1,0:T(8,128)(2,1)} %refs_17_.1, bf16[128,512]{1,0:T(8,128)(2,1)S(1)} %slice-done), kind=kLoop, calls=%fused_computation | loop fusion | flops 1179648 | bytes 786432 | tf_op jit(solution)/shard_map/concatenate | solution.py:361
  2.6 3.0 %collective-permute-start.6 = (bf16[128,1536]{1,0:T(8,128)(2,1)S(1)}, bf16[128,1536]{1,0:T(8,128)(2,1)S(1)}, u32[]{:S(2)}, u32[]{:S(2)}) collective-permute-start(bf16[128,1536]{1,0:T(8,128)(2,1)S(1)} %pad_maximum_fusion), channel_id=1, source_target_pairs={{0,2},{1,3},{2,0},{3,1},{4,6},{5,7},{6,4},{7,5},{8,10},{9,11},{10,... | collective-permute-start | bytes 1179656 | tf_op jit(solution)/shard_map/ppermute | solution.py:339
  5.6 9.1 %collective-permute-done.6.refs_5_.refs_0_ = bf16[128,1536]{1,0:T(8,128)(2,1)S(1)} collective-permute-done((bf16[128,1536]{1,0:T(8,128)(2,1)S(1)}, bf16[128,1536]{1,0:T(8,128)(2,1)S(1)}, u32[]{:S(2)}, u32[]{:S(2)}) %collective-permute-start.6) | collective-permute-done | bytes 393248 | tf_op jit(solution)/shard_map/ppermute | solution.py:339
  15.3 0.6 %shard_map.156 = bf16[16,16,128]{2,1,0:T(8,128)(2,1)} custom-call(bf16[16,128]{1,0:T(8,128)(2,1)S(1)} %copy-done.8), custom_call_target="tpu_custom_call" | custom-call | flops 16777216 | bytes 4096 | tf_op jit(solution)/shard_map/pallas_call | solution.py:73
  16.0 6.3 %all-to-all-start = ((bf16[16,16,128]{2,1,0:T(8,128)(2,1)}), bf16[16,16,128]{2,1,0:T(8,128)(2,1)S(1)}, u32[]{:S(2)}, u32[]{:S(2)}) async-start(bf16[16,16,128]{2,1,0:T(8,128)(2,1)} %shard_map.156), calls=%async_computation | async-start | bytes 131072 | tf_op jit(solution)/shard_map/all_to_all | solution.py:352
  22.4 2.0 %collective-permute-start.1 = (bf16[128,256]{1,0:T(8,128)(2,1)S(1)}, bf16[128,256]{1,0:T(8,128)(2,1)S(1)}, u32[]{:S(2)}, u32[]{:S(2)}) collective-permute-start(bf16[128,256]{1,0:T(8,128)(2,1)S(1)} %shard_map.157.refs_0_), channel_id=1, source_target_pairs={{0,2},{1,3},{2,0},{3,1},{4,6},{5,7},{6,4},{7,5},{8,10},{9,11},{10,... | collective-permute-start | bytes 196616 | tf_op jit(solution)/shard_map/ppermute | solution.py:339
  24.4 0.6 %copy-done.11 = bf16[128]{0:T(256)(128)(2,1)S(1)} copy-done((bf16[128]{0:T(256)(128)(2,1)S(1)}, bf16[128]{0:T(256)(128)(2,1)}, u32[]{:S(2)}) %copy-start.11) | copy-done | bytes 280
  25.2 2.0 %collective-permute-done.1.refs_1_ = bf16[128,256]{1,0:T(8,128)(2,1)S(1)} collective-permute-done((bf16[128,256]{1,0:T(8,128)(2,1)S(1)}, bf16[128,256]{1,0:T(8,128)(2,1)S(1)}, u32[]{:S(2)}, u32[]{:S(2)}) %collective-permute-start.1) | collective-permute-done | bytes 65568 | tf_op jit(solution)/shard_map/ppermute | solution.py:339
  27.2 2.4 %collective-permute-done.5.refs_1_.refs_4_ = bf16[288,128]{1,0:T(8,128)(2,1)S(1)} collective-permute-done((bf16[288,128]{1,0:T(8,128)(2,1)S(1)}, bf16[288,128]{1,0:T(8,128)(2,1)S(1)}, u32[]{:S(2)}, u32[]{:S(2)}) %collective-permute-start.5) | collective-permute-done | bytes 73760 | tf_op jit(solution)/shard_map/ppermute | solution.py:339
  29.6 0.5 %collective-permute-start.9 = (bf16[160,256]{1,0:T(8,128)(2,1)S(1)}, bf16[160,256]{1,0:T(8,128)(2,1)S(1)}, u32[]{:S(2)}, u32[]{:S(2)}) collective-permute-start(bf16[160,256]{1,0:T(8,128)(2,1)S(1)} %shard_map.161), channel_id=1, source_target_pairs={{0,1},{1,0},{2,3},{3,2},{4,5},{5,4},{6,7},{7,6},{8,9},{9,8},{10,11... | collective-permute-start | bytes 245768 | tf_op jit(solution)/shard_map/ppermute | solution.py:339
  30.3 0.6 %copy-done.9 = s32[256]{0:T(256)S(1)} copy-done((s32[256]{0:T(256)S(1)}, s32[256]{0:T(256)}, u32[]{:S(2)}) %copy-start.9) | copy-done | bytes 1048
  30.8 0.9 %shard_map.158 = (bf16[128,512]{1,0:T(8,128)(2,1)S(1)}, f32[128,256]{1,0:T(8,128)S(1)}, bf16[64,128]{1,0:T(8,128)(2,1)S(1)}, bf16[16,128]{1,0:T(8,128)(2,1)S(1)}) custom-call(bf16[128,256]{1,0:T(8,128)(2,1)S(1)} %shard_map.157.refs_0_, bf16[128,256]{1,0:T(8,128)(2,1)S(1)} %collective-permute-done.1.refs_1_, bf16[128,1536]{1,0:T(8,128)(2,1)S(1)} %copy-done, ...), custom_call_target="tpu_custom_call" | custom-call | flops 16777216 | bytes 920064 | tf_op jit(solution)/shard_map/pallas_call | solution.py:73
  32.2 1.0 %collective-permute-start.4 = (bf16[160,256]{1,0:T(8,128)(2,1)S(1)}, bf16[160,256]{1,0:T(8,128)(2,1)S(1)}, u32[]{:S(2)}, u32[]{:S(2)}) collective-permute-start(bf16[160,256]{1,0:T(8,128)(2,1)S(1)} %get-tuple-element.35.refs_1_), channel_id=1, source_target_pairs={{0,2},{1,3},{2,0},{3,1},{4,6},{5,7},{6,4},{7,5},{8,10},{9,11},{10,... | collective-permute-start | bytes 245768 | tf_op jit(solution)/shard_map/ppermute | solution.py:339
  33.3 3.5 %collective-permute-done.4.refs_2_ = bf16[160,256]{1,0:T(8,128)(2,1)S(1)} collective-permute-done((bf16[160,256]{1,0:T(8,128)(2,1)S(1)}, bf16[160,256]{1,0:T(8,128)(2,1)S(1)}, u32[]{:S(2)}, u32[]{:S(2)}) %collective-permute-start.4) | collective-permute-done | bytes 81952 | tf_op jit(solution)/shard_map/ppermute | solution.py:339
  37.2 1.2 %collective-permute-done.11.refs_3_ = f32[16,512]{1,0:T(8,128)S(1)} collective-permute-done((f32[16,512]{1,0:T(8,128)S(1)}, f32[16,512]{1,0:T(8,128)S(1)}, u32[]{:S(2)}, u32[]{:S(2)}) %collective-permute-start.11) | collective-permute-done | bytes 32800 | tf_op jit(solution)/shard_map/ppermute | solution.py:339
  38.4 2.0 %shard_map.163 = (bf16[16,128]{1,0:T(8,128)(2,1)}, f32[128,256]{1,0:T(8,128)S(1)}, bf16[128,256]{1,0:T(8,128)(2,1)S(1)}, bf16[128,256]{1,0:T(8,128)(2,1)S(1)}, bf16[16,256]{1,0:T(8,128)(2,1)S(1)}) custom-call(bf16[128,1536]{1,0:T(8,128)(2,1)S(1)} %collective-permute-done.6.refs_5_.refs_0_, bf16[128,1536]{1,0:T(8,128)(2,1)S(1)} %collective-permute-done.7.refs_6_.refs_1_, ...), custom_call_target="tpu_custom_call" | custom-call | flops 16777216 | bytes 3297792 | tf_op jit(solution)/shard_map/pallas_call | solution.py:73
  40.4 1.1 %shard_map.166 = bf16[16,16,128]{2,1,0:T(8,128)(2,1)} custom-call(bf16[128,256]{1,0:T(8,128)(2,1)S(1)} %get-tuple-element.54.dpre, bf16[16,256]{1,0:T(8,128)(2,1)S(1)} %get-tuple-element.55.node_dpre, bf16[64,128]{1,0:T(8,128)(2,1)S(1)} %get-tuple-element.32.pick, bf16[16,128]{1,0:T(8,128)(2,1)S(1)} %get-tuple-element.33.take.refs_11_.refs_7_, ...), custom_call_target="tpu_custom_call" | custom-call | flops 16777216 | bytes 1404928 | tf_op jit(solution)/shard_map/pallas_call | solution.py:73
  41.5 4.7 %all-to-all-start.1 = ((bf16[16,16,128]{2,1,0:T(8,128)(2,1)}), bf16[16,16,128]{2,1,0:T(8,128)(2,1)S(1)}, u32[]{:S(2)}, u32[]{:S(2)}) async-start(bf16[16,16,128]{2,1,0:T(8,128)(2,1)} %shard_map.166), calls=%async_computation.1 | async-start | bytes 131072 | tf_op jit(solution)/shard_map/all_to_all | solution.py:417
  46.3 1.9 %collective-permute-start.13 = (bf16[128,256]{1,0:T(8,128)(2,1)S(1)}, bf16[128,256]{1,0:T(8,128)(2,1)S(1)}, u32[]{:S(2)}, u32[]{:S(2)}) collective-permute-start(bf16[128,256]{1,0:T(8,128)(2,1)S(1)} %get-tuple-element.48), channel_id=1, source_target_pairs={{0,2},{1,3},{2,0},{3,1},{4,6},{5,7},{6,4},{7,5},{8,10},{9,11},{10,... | collective-permute-start | bytes 196616 | tf_op jit(solution)/shard_map/ppermute | solution.py:339
  48.2 3.0 %collective-permute-done.13.refs_1_ = bf16[128,256]{1,0:T(8,128)(2,1)S(1)} collective-permute-done((bf16[128,256]{1,0:T(8,128)(2,1)S(1)}, bf16[128,256]{1,0:T(8,128)(2,1)S(1)}, u32[]{:S(2)}, u32[]{:S(2)}) %collective-permute-start.13) | collective-permute-done | bytes 65568 | tf_op jit(solution)/shard_map/ppermute | solution.py:339
  51.3 1.2 %collective-permute-done.14.grad_came = bf16[128,128]{1,0:T(8,128)(2,1)S(1)} collective-permute-done((bf16[128,128]{1,0:T(8,128)(2,1)S(1)}, bf16[128,128]{1,0:T(8,128)(2,1)S(1)}, u32[]{:S(2)}, u32[]{:S(2)}) %collective-permute-start.14) | collective-permute-done | bytes 32800 | tf_op jit(solution)/shard_map/ppermute | solution.py:339
  52.5 0.7 %shard_map.165 = (bf16[256,128]{1,0:T(8,128)(2,1)}, bf16[256,128]{1,0:T(8,128)(2,1)}) custom-call(bf16[128,128]{1,0:T(8,128)(2,1)S(1)} %get-tuple-element.38.next_mine, bf16[128,128]{1,0:T(8,128)(2,1)S(1)} %collective-permute-done.10.next_came, bf16[128,128]{1,0:T(8,128)(2,1)S(1)} %get-tuple-element.49.grad_mine, ...), custom_call_target="tpu_custom_call" | custom-call | flops 16777216 | bytes 131072 | tf_op jit(solution)/shard_map/pallas_call | solution.py:73
  53.2 0.6 %shard_map.167 = bf16[16,128]{1,0:T(8,128)(2,1)} custom-call(bf16[16,16,128]{2,1,0:T(8,128)(2,1)S(1)} %all-to-all-done.1.shares, bf16[16,128]{1,0:T(8,128)(2,1)S(1)} %copy-done.6), custom_call_target="tpu_custom_call" | custom-call | flops 16777216 | bytes 69632 | tf_op jit(solution)/shard_map/pallas_call | solution.py:73
  (51 shorter events, 2.2 us)
Async XLA Ops:
  1.6 4.0 %copy-start = (bf16[128,1536]{1,0:T(8,128)(2,1)S(1)}, bf16[128,1536]{1,0:T(8,128)(2,1)}, u32[]{:S(2)}) copy-start(bf16[128,1536]{1,0:T(8,128)(2,1)} %e_mine.1) | copy-start | bytes 1179652
  1.6 13.1 %copy-start.1 = (bf16[128,1024]{1,0:T(8,128)(2,1)S(1)}, bf16[128,1024]{1,0:T(8,128)(2,1)}, u32[]{:S(2)}) copy-start(bf16[128,1024]{1,0:T(8,128)(2,1)} %in_mine.1) | copy-start | bytes 786436
  1.6 13.6 %copy-start.4 = (bf16[256,128]{1,0:T(8,128)(2,1)S(1)}, bf16[256,128]{1,0:T(8,128)(2,1)}, u32[]{:S(2)}) copy-start(bf16[256,128]{1,0:T(8,128)(2,1)} %state.1) | copy-start | bytes 196612
  1.6 13.7 %copy-start.8 = (bf16[16,128]{1,0:T(8,128)(2,1)S(1)}, bf16[16,128]{1,0:T(8,128)(2,1)}, u32[]{:S(2)}) copy-start(bf16[16,128]{1,0:T(8,128)(2,1)} %latent.1) | copy-start | bytes 12292
  2.6 12.1 %collective-permute-start.6 = (bf16[128,1536]{1,0:T(8,128)(2,1)S(1)}, bf16[128,1536]{1,0:T(8,128)(2,1)S(1)}, u32[]{:S(2)}, u32[]{:S(2)}) collective-permute-start(bf16[128,1536]{1,0:T(8,128)(2,1)S(1)} %pad_maximum_fusion), channel_id=1, source_target_pairs={{0,2},{1,3},{2,0},{3,1},{4,6},{5,7},{6,4},{7,5},{8,10},{9,11},{10,... | collective-permute-start | bytes 1179656 | tf_op jit(solution)/shard_map/ppermute | solution.py:339
  5.6 24.0 %collective-permute-start.2 = (bf16[128,1536]{1,0:T(8,128)(2,1)S(1)}, bf16[128,1536]{1,0:T(8,128)(2,1)S(1)}, u32[]{:S(2)}, u32[]{:S(2)}) collective-permute-start(bf16[128,1536]{1,0:T(8,128)(2,1)S(1)} %copy-done), channel_id=1, source_target_pairs={{0,1},{1,0},{2,3},{3,2},{4,5},{5,4},{6,7},{7,6},{8,9},{9,8},{10,11... | collective-permute-start | bytes 1179656 | tf_op jit(solution)/shard_map/ppermute | solution.py:339
  14.7 22.0 %collective-permute-start.7 = (bf16[128,1536]{1,0:T(8,128)(2,1)S(1)}, bf16[128,1536]{1,0:T(8,128)(2,1)S(1)}, u32[]{:S(2)}, u32[]{:S(2)}) collective-permute-start(bf16[128,1536]{1,0:T(8,128)(2,1)S(1)} %collective-permute-done.6.refs_5_.refs_0_), channel_id=1, source_target_pairs={{0,1},{1,0},{2,3},{3,2},{4,5},{5,4},{6,7},{7,6},{8,9},{9,8},{10,11... | collective-permute-start | bytes 1179656 | tf_op jit(solution)/shard_map/ppermute | solution.py:339
  14.7 17.0 %collective-permute-start.3 = (bf16[128,1024]{1,0:T(8,128)(2,1)S(1)}, bf16[128,1024]{1,0:T(8,128)(2,1)S(1)}, u32[]{:S(2)}, u32[]{:S(2)}) collective-permute-start(bf16[128,1024]{1,0:T(8,128)(2,1)S(1)} %copy-done.1), channel_id=1, source_target_pairs={{0,1},{1,0},{2,3},{3,2},{4,5},{5,4},{6,7},{7,6},{8,9},{9,8},{10,11... | collective-permute-start | bytes 786440 | tf_op jit(solution)/shard_map/ppermute | solution.py:339
  15.3 7.1 %collective-permute-start = (bf16[256,128]{1,0:T(8,128)(2,1)S(1)}, bf16[256,128]{1,0:T(8,128)(2,1)S(1)}, u32[]{:S(2)}, u32[]{:S(2)}) collective-permute-start(bf16[256,128]{1,0:T(8,128)(2,1)S(1)} %copy-done.4), channel_id=1, source_target_pairs={{0,1},{1,0},{2,3},{3,2},{4,5},{5,4},{6,7},{7,6},{8,9},{9,8},{10,11... | collective-permute-start | bytes 196616 | tf_op jit(solution)/shard_map/ppermute | solution.py:339
  16.0 8.4 %copy-start.6 = (bf16[16,128]{1,0:T(8,128)(2,1)S(1)}, bf16[16,128]{1,0:T(8,128)(2,1)}, u32[]{:S(2)}) copy-start(bf16[16,128]{1,0:T(8,128)(2,1)} %node_cot.3) | copy-start | bytes 12292
  16.0 15.8 %all-to-all-start = ((bf16[16,16,128]{2,1,0:T(8,128)(2,1)}), bf16[16,16,128]{2,1,0:T(8,128)(2,1)S(1)}, u32[]{:S(2)}, u32[]{:S(2)}) async-start(bf16[16,16,128]{2,1,0:T(8,128)(2,1)} %shard_map.156), calls=%async_computation | async-start | bytes 131072 | tf_op jit(solution)/shard_map/all_to_all | solution.py:352
  22.3 2.1 %copy-start.5 = (bf16[256,128]{1,0:T(8,128)(2,1)S(1)}, bf16[256,128]{1,0:T(8,128)(2,1)}, u32[]{:S(2)}) copy-start(bf16[256,128]{1,0:T(8,128)(2,1)} %edge_cot) | copy-start | bytes 196612
  22.3 7.2 %copy-start.3 = (bf16[128,512]{1,0:T(8,128)(2,1)S(1)}, bf16[128,512]{1,0:T(8,128)(2,1)}, u32[]{:S(2)}) copy-start(bf16[128,512]{1,0:T(8,128)(2,1)} %refs_17_.1) | copy-start | bytes 393220
  22.4 4.8 %collective-permute-start.1 = (bf16[128,256]{1,0:T(8,128)(2,1)S(1)}, bf16[128,256]{1,0:T(8,128)(2,1)S(1)}, u32[]{:S(2)}, u32[]{:S(2)}) collective-permute-start(bf16[128,256]{1,0:T(8,128)(2,1)S(1)} %shard_map.157.refs_0_), channel_id=1, source_target_pairs={{0,2},{1,3},{2,0},{3,1},{4,6},{5,7},{6,4},{7,5},{8,10},{9,11},{10,... | collective-permute-start | bytes 196616 | tf_op jit(solution)/shard_map/ppermute | solution.py:339
  25.0 4.5 %collective-permute-start.5 = (bf16[288,128]{1,0:T(8,128)(2,1)S(1)}, bf16[288,128]{1,0:T(8,128)(2,1)S(1)}, u32[]{:S(2)}, u32[]{:S(2)}) collective-permute-start(bf16[288,128]{1,0:T(8,128)(2,1)S(1)} %shard_map.160.refs_0_.refs_3_), channel_id=1, source_target_pairs={{0,2},{1,3},{2,0},{3,1},{4,6},{5,7},{6,4},{7,5},{8,10},{9,11},{10,... | collective-permute-start | bytes 221192 | tf_op jit(solution)/shard_map/ppermute | solution.py:339
  27.2 6.1 %collective-permute-start.8 = (bf16[128,512]{1,0:T(8,128)(2,1)S(1)}, bf16[128,512]{1,0:T(8,128)(2,1)S(1)}, u32[]{:S(2)}, u32[]{:S(2)}) collective-permute-start(bf16[128,512]{1,0:T(8,128)(2,1)S(1)} %copy-done.2), channel_id=1, source_target_pairs={{0,1},{1,0},{2,3},{3,2},{4,5},{5,4},{6,7},{7,6},{8,9},{9,8},{10,11... | collective-permute-start | bytes 393224 | tf_op jit(solution)/shard_map/ppermute | solution.py:339
  29.6 7.7 %collective-permute-start.12 = (bf16[128,512]{1,0:T(8,128)(2,1)S(1)}, bf16[128,512]{1,0:T(8,128)(2,1)S(1)}, u32[]{:S(2)}, u32[]{:S(2)}) collective-permute-start(bf16[128,512]{1,0:T(8,128)(2,1)S(1)} %copy-done.3), channel_id=1, source_target_pairs={{0,1},{1,0},{2,3},{3,2},{4,5},{5,4},{6,7},{7,6},{8,9},{9,8},{10,11... | collective-permute-start | bytes 393224 | tf_op jit(solution)/shard_map/ppermute | solution.py:339
  29.6 3.6 %collective-permute-start.9 = (bf16[160,256]{1,0:T(8,128)(2,1)S(1)}, bf16[160,256]{1,0:T(8,128)(2,1)S(1)}, u32[]{:S(2)}, u32[]{:S(2)}) collective-permute-start(bf16[160,256]{1,0:T(8,128)(2,1)S(1)} %shard_map.161), channel_id=1, source_target_pairs={{0,1},{1,0},{2,3},{3,2},{4,5},{5,4},{6,7},{7,6},{8,9},{9,8},{10,11... | collective-permute-start | bytes 245768 | tf_op jit(solution)/shard_map/ppermute | solution.py:339
  32.2 4.5 %collective-permute-start.4 = (bf16[160,256]{1,0:T(8,128)(2,1)S(1)}, bf16[160,256]{1,0:T(8,128)(2,1)S(1)}, u32[]{:S(2)}, u32[]{:S(2)}) collective-permute-start(bf16[160,256]{1,0:T(8,128)(2,1)S(1)} %get-tuple-element.35.refs_1_), channel_id=1, source_target_pairs={{0,2},{1,3},{2,0},{3,1},{4,6},{5,7},{6,4},{7,5},{8,10},{9,11},{10,... | collective-permute-start | bytes 245768 | tf_op jit(solution)/shard_map/ppermute | solution.py:339
  37.2 1.2 %collective-permute-start.11 = (f32[16,512]{1,0:T(8,128)S(1)}, f32[16,512]{1,0:T(8,128)S(1)}, u32[]{:S(2)}, u32[]{:S(2)}) collective-permute-start(f32[16,512]{1,0:T(8,128)S(1)} %get-tuple-element.40.refs_2_), channel_id=1, source_target_pairs={{0,1},{1,0},{2,3},{3,2},{4,5},{5,4},{6,7},{7,6},{8,9},{9,8},{10,11... | collective-permute-start | bytes 98312 | tf_op jit(solution)/shard_map/ppermute | solution.py:339
  41.5 11.6 %all-to-all-start.1 = ((bf16[16,16,128]{2,1,0:T(8,128)(2,1)}), bf16[16,16,128]{2,1,0:T(8,128)(2,1)S(1)}, u32[]{:S(2)}, u32[]{:S(2)}) async-start(bf16[16,16,128]{2,1,0:T(8,128)(2,1)} %shard_map.166), calls=%async_computation.1 | async-start | bytes 131072 | tf_op jit(solution)/shard_map/all_to_all | solution.py:417
  46.3 4.9 %collective-permute-start.13 = (bf16[128,256]{1,0:T(8,128)(2,1)S(1)}, bf16[128,256]{1,0:T(8,128)(2,1)S(1)}, u32[]{:S(2)}, u32[]{:S(2)}) collective-permute-start(bf16[128,256]{1,0:T(8,128)(2,1)S(1)} %get-tuple-element.48), channel_id=1, source_target_pairs={{0,2},{1,3},{2,0},{3,1},{4,6},{5,7},{6,4},{7,5},{8,10},{9,11},{10,... | collective-permute-start | bytes 196616 | tf_op jit(solution)/shard_map/ppermute | solution.py:339
  48.2 3.1 %collective-permute-start.10 = (bf16[128,128]{1,0:T(8,128)(2,1)S(1)}, bf16[128,128]{1,0:T(8,128)(2,1)S(1)}, u32[]{:S(2)}, u32[]{:S(2)}) collective-permute-start(bf16[128,128]{1,0:T(8,128)(2,1)S(1)} %get-tuple-element.39), channel_id=1, source_target_pairs={{0,1},{1,0},{2,3},{3,2},{4,5},{5,4},{6,7},{7,6},{8,9},{9,8},{10,11... | collective-permute-start | bytes 98312 | tf_op jit(solution)/shard_map/ppermute | solution.py:339
  51.2 1.3 %collective-permute-start.14 = (bf16[128,128]{1,0:T(8,128)(2,1)S(1)}, bf16[128,128]{1,0:T(8,128)(2,1)S(1)}, u32[]{:S(2)}, u32[]{:S(2)}) collective-permute-start(bf16[128,128]{1,0:T(8,128)(2,1)S(1)} %get-tuple-element.50), channel_id=1, source_target_pairs={{0,1},{1,0},{2,3},{3,2},{4,5},{5,4},{6,7},{7,6},{8,9},{9,8},{10,11... | collective-permute-start | bytes 98312 | tf_op jit(solution)/shard_map/ppermute | solution.py:339
  (7 other events, 5.3 us)

commit v12 on v10

--- a/solution.py
+++ b/solution.py
@@ -96,6 +96,17 @@
     return value
 
 
+def spread_latent(latent, spread):
+    spread[...] = jnp.broadcast_to(latent[...][None], spread.shape)
+
+
+def merge_state(state, state2, pack):
+    _, core = place()
+    half = pack.shape[0]
+    mine = pl.ds(pl.multiple_of(core * half, half), half)
+    pack[...] = pair(state[mine], state2[mine], core)
+
+
 def pack_extra(edge_cot, node_cot, gain_e, gain_n, pack):
     edge_dev = edge_cot.shape[0]
     nodes = node_cot.shape[0]
@@ -122,16 +133,14 @@
 
 def prepare_edges(groups, *refs):
     packs = refs[:groups]
-    theirs, mine, other, slot, receiver, send_rows, state, pre, pick, take = refs[groups:]
+    mine, other, slot, receiver, send_rows, state, pre, pick, take = refs[groups:]
     group, core = place()
     block = lax.axis_index("nodes")
     features = state.shape[1]
     nodes, half = take.shape
-    width = packs[0].shape[1]
     blocks, _, slots = send_rows.shape
     for step, pack in enumerate(packs):
-        both = pair(half_rows(pack, core, half), theirs[:, step * width : (step + 1) * width], core)
-        state[:, lanes(group ^ step, width * cores)] = both
+        state[:, lanes(group ^ step, pack.shape[1])] = pack[...]
 
     slot_row = slot[pl.ds(core, 1)]
     sender = block * nodes + slot_row
@@ -343,27 +352,28 @@
     slot_rows = sender_slot.reshape(cores, half)
     receiver_rows = receiver_row.reshape(cores, half)
 
-    latents = lax.all_to_all(
-        jnp.broadcast_to(latent[None], (blocks * feats, nodes, width)), everyone, 0, 0
-    )
-    states = [edge_state] + over_groups(edge_state)
+    (spread,) = stage(spread_latent, [((blocks * feats, nodes, width), bf16)], [latent])
+    latents = lax.all_to_all(spread, everyone, 0, 0)
+    (pack,) = stage(merge_state, [((half, wide), bf16)], [edge_state, over_cores(edge_state)])
+    pack, edge_cot = lax.optimization_barrier((pack, edge_cot))
+    states = [pack] + over_groups(pack)
     e_in = (edge_in_weight, over_cores(edge_in_weight))
     e_out = (edge_out_weight, over_cores(edge_out_weight))
     n_in = (node_in_weight, over_cores(node_in_weight))
     n_out = (node_out_weight, over_cores(node_out_weight))
-    far = []
-    for weights in over_groups(jnp.concatenate([node_in_weight[:, features:], node_out_weight], axis=1)):
-        far += [weights, over_cores(weights)]
-    (sent,) = stage(functools.partial(send_half, groups), [((half, groups * width), bf16)], states)
+    far = over_groups(jnp.concatenate([node_in_weight[:, features:], node_out_weight], axis=1))
     state, pre, pick, take = stage(
         functools.partial(prepare_edges, groups),
         [((half, features), bf16), ((half, hidden), f32), ((table, half), bf16), ((nodes, half), bf16)],
-        [*states, over_cores(sent), *e_in, slot_rows, receiver_rows, send_rows],
+        [*states, *e_in, slot_rows, receiver_rows, send_rows],
         scalars=1,
     )
     rows = edge_dev + 2 * nodes
     (pack,) = stage(pack_extra, [((rows, width), bf16)], [edge_cot, node_cot, gain_e, gain_n])
-    packs = [pack] + over_groups(pack)
+    packs = over_groups(pack)
+    far, packs, _ = lax.optimization_barrier((far, packs, pre))
+    far = [weights for came in far for weights in (came, over_cores(came))]
+    packs = [pack] + packs
     (sent,) = stage(functools.partial(send_half, groups), [((rows - half, groups * width), bf16)], packs)
     extra_came = over_cores(sent)
     edge_pre, part, sent, own, lat = stage(

time: 41.5 us -> 49 us (1.18)
  waiting for transfers between devices: 12.2 us -> 20.7 us
  local copies, waits for them, and re-layouts: 3.12 us -> 1.13 us
  Pallas kernels: 6.25 us -> 6.87 us
  starting transfers between devices: 18.7 us -> 19.2 us
    ppermute x15, waiting for transfers between devices: 10.4 us -> 15.7 us  [swapped(): return lax.ppermute(values, 'feat', [(i, i ^ bits) for i in range(feats)])]
    all_to_all x1, waiting for transfers between devices: 1.69 us -> 4.82 us  [shards(): latents = lax.all_to_all(spread, everyone, 0, 0)]
    broadcast_in_dim x1 -> x0, local copies, waits for them, and re-layouts: 1.32 us -> none  [shards(): jnp.broadcast_to(latent[None], (blocks * feats, nodes, width))]
    all_to_all x1, starting transfers between devices: 5.61 us -> 6.4 us  [shards(): latents = lax.all_to_all(spread, everyone, 0, 0)]
    unnamed x24 -> x26, local copies, waits for them, and re-layouts: 1.42 us -> 0.76 us
    pallas_call x11 -> x12, Pallas kernels: 6.25 us -> 6.87 us  [stage(): pl.pallas_call(kernel, out_shape=[jax.ShapeDtypeStruct(shape, kind) for s...]
  transfers between devices with their start and end apart: 17 -> 17, of which waited for: 8 -> 9; matrix products, arithmetic and copies ran while one was open for 3% -> 0% of each run, Pallas kernels for 6% -> 6%
where the time goes in v12:
time: 49 us; the launch traced here: 48.7 us
  waiting for transfers between devices  20.7 us (42%)
  starting transfers between devices  19.2 us (39%)
  Pallas kernels  6.87 us (14%)
  local copies, waits for them, and re-layouts  1.13 us (2%)
  between operations  0.85 us (2%)
    ppermute x15, waiting for transfers between devices, swapped(): return lax.ppermute(values, 'feat', [(i, i ^ bits) for i in range(feats)])  15.7 us
    ppermute x15, starting transfers between devices, swapped(): return lax.ppermute(values, 'feat', [(i, i ^ bits) for i in range(feats)])  9.28 us
    pallas_call x12, Pallas kernels, stage(): pl.pallas_call(kernel, out_shape=[jax.ShapeDtypeStruct(shape, kind) for s...  6.87 us
    all_to_all x1, starting transfers between devices, shards(): latents = lax.all_to_all(spread, everyone, 0, 0)  6.4 us
    all_to_all x1, waiting for transfers between devices, shards(): latents = lax.all_to_all(spread, everyone, 0, 0)  4.82 us
    all_to_all x1, starting transfers between devices, shards(): shares = lax.all_to_all(spread, everyone, 0, 0)  3.48 us
  transfers between devices with their start and end apart: 17, of which 9 were waited for; matrix products, arithmetic and copies ran while one was open for 0% of the time, Pallas kernels for 6%

profile of v12, /device:TPU:0, one launch (start us, length us, event | category | flops | bytes accessed | tf_op | source)
XLA Modules:
  0.0 48.7 jit_solution(14744466932640657508)
XLA Ops:
  0.7 0.5 %collective-permute-start.2 = (bf16[128,1536]{1,0:T(8,128)(2,1)}, bf16[128,1536]{1,0:T(8,128)(2,1)S(1)}, u32[]{:S(2)}, u32[]{:S(2)}) collective-permute-start(bf16[128,1536]{1,0:T(8,128)(2,1)} %e_mine.1), channel_id=1, source_target_pairs={{0,1},{1,0},{2,3},{3,2},{4,5},{5,4},{6,7},{7,6},{8,9},{9,8},{10,11... | collective-permute-start | bytes 1179656 | tf_op jit(solution)/shard_map/ppermute | solution.py:343
  1.7 3.0 %collective-permute-start.6 = (bf16[128,1024]{1,0:T(8,128)(2,1)S(1)}, bf16[128,1024]{1,0:T(8,128)(2,1)S(1)}, u32[]{:S(2)}, u32[]{:S(2)}) collective-permute-start(bf16[128,1024]{1,0:T(8,128)(2,1)S(1)} %pad_maximum_fusion), channel_id=1, source_target_pairs={{0,2},{1,3},{2,0},{3,1},{4,6},{5,7},{6,4},{7,5},{8,10},{9,11},{10,... | collective-permute-start | bytes 786440 | tf_op jit(solution)/shard_map/ppermute | solution.py:343
  5.2 0.7 %collective-permute-done.state2 = bf16[256,128]{1,0:T(8,128)(2,1)S(1)} collective-permute-done((bf16[256,128]{1,0:T(8,128)(2,1)S(1)}, bf16[256,128]{1,0:T(8,128)(2,1)S(1)}, u32[]{:S(2)}, u32[]{:S(2)}) %collective-permute-start) | collective-permute-done | bytes 65568 | tf_op jit(solution)/shard_map/ppermute | solution.py:343
  6.0 0.7 %collective-permute-start.1 = (bf16[128,256]{1,0:T(8,128)(2,1)S(1)}, bf16[128,256]{1,0:T(8,128)(2,1)S(1)}, u32[]{:S(2)}, u32[]{:S(2)}) collective-permute-start(bf16[128,256]{1,0:T(8,128)(2,1)S(1)} %shard_map.157.refs_0_), channel_id=1, source_target_pairs={{0,2},{1,3},{2,0},{3,1},{4,6},{5,7},{6,4},{7,5},{8,10},{9,11},{10,... | collective-permute-start | bytes 196616 | tf_op jit(solution)/shard_map/ppermute | solution.py:343
  6.7 1.4 %collective-permute-start.7 = (bf16[288,128]{1,0:T(8,128)(2,1)S(1)}, bf16[288,128]{1,0:T(8,128)(2,1)S(1)}, u32[]{:S(2)}, u32[]{:S(2)}) collective-permute-start(bf16[288,128]{1,0:T(8,128)(2,1)S(1)} %shard_map.160.refs_0_.refs_3_), channel_id=1, source_target_pairs={{0,2},{1,3},{2,0},{3,1},{4,6},{5,7},{6,4},{7,5},{8,10},{9,11},{10,... | collective-permute-start | bytes 221192 | tf_op jit(solution)/shard_map/ppermute | solution.py:343
  8.2 5.0 %collective-permute-done.1.refs_1_ = bf16[128,256]{1,0:T(8,128)(2,1)S(1)} collective-permute-done((bf16[128,256]{1,0:T(8,128)(2,1)S(1)}, bf16[128,256]{1,0:T(8,128)(2,1)S(1)}, u32[]{:S(2)}, u32[]{:S(2)}) %collective-permute-start.1) | collective-permute-done | bytes 65568 | tf_op jit(solution)/shard_map/ppermute | solution.py:343
  13.2 0.6 %shard_map.156 = bf16[16,16,128]{2,1,0:T(8,128)(2,1)} custom-call(bf16[16,128]{1,0:T(8,128)(2,1)S(1)} %copy-done.8), custom_call_target="tpu_custom_call" | custom-call | flops 16777216 | bytes 4096 | tf_op jit(solution)/shard_map/pallas_call | solution.py:73
  13.9 6.4 %all-to-all-start = ((bf16[16,16,128]{2,1,0:T(8,128)(2,1)}), bf16[16,16,128]{2,1,0:T(8,128)(2,1)S(1)}, u32[]{:S(2)}, u32[]{:S(2)}) async-start(bf16[16,16,128]{2,1,0:T(8,128)(2,1)} %shard_map.156), calls=%async_computation | async-start | bytes 131072 | tf_op jit(solution)/shard_map/all_to_all | solution.py:356
  20.3 0.6 %copy-done.9 = s32[256]{0:T(256)S(1)} copy-done((s32[256]{0:T(256)S(1)}, s32[256]{0:T(256)}, u32[]{:S(2)}) %copy-start.9) | copy-done | bytes 1048
  21.0 0.9 %shard_map.158 = (bf16[128,512]{1,0:T(8,128)(2,1)S(1)}, f32[128,256]{1,0:T(8,128)S(1)}, bf16[64,128]{1,0:T(8,128)(2,1)S(1)}, bf16[16,128]{1,0:T(8,128)(2,1)S(1)}) custom-call(bf16[128,256]{1,0:T(8,128)(2,1)S(1)} %shard_map.157.refs_0_, bf16[128,256]{1,0:T(8,128)(2,1)S(1)} %collective-permute-done.1.refs_1_, bf16[128,1536]{1,0:T(8,128)(2,1)S(1)} %copy-done, ...), custom_call_target="tpu_custom_call" | custom-call | flops 16777216 | bytes 920064 | tf_op jit(solution)/shard_map/pallas_call | solution.py:73
  22.3 4.8 %all-to-all-done.came = bf16[16,16,128]{2,1,0:T(8,128)(2,1)S(1)} async-done(((bf16[16,16,128]{2,1,0:T(8,128)(2,1)}), bf16[16,16,128]{2,1,0:T(8,128)(2,1)S(1)}, u32[]{:S(2)}, u32[]{:S(2)}) %all-to-all-start) | async-done | bytes 65568 | tf_op jit(solution)/shard_map/all_to_all | solution.py:356
  27.2 0.6 %shard_map.159 = (f32[128,256]{1,0:T(8,128)S(1)}, f32[128,512]{1,0:T(8,128)S(1)}, bf16[144,512]{1,0:T(8,128)(2,1)S(1)}, bf16[16,512]{1,0:T(8,128)(2,1)S(1)}, f32[16,256]{1,0:T(8,128)S(1)}) custom-call(bf16[16,16,128]{2,1,0:T(8,128)(2,1)S(1)} %all-to-all-done.came, f32[128,256]{1,0:T(8,128)S(1)} %get-tuple-element.34.pre, ...), custom_call_target="tpu_custom_call" | custom-call | flops 16777216 | bytes 1789952 | tf_op jit(solution)/shard_map/pallas_call | solution.py:73
  28.0 0.6 %collective-permute-start.8 = (bf16[160,256]{1,0:T(8,128)(2,1)S(1)}, bf16[160,256]{1,0:T(8,128)(2,1)S(1)}, u32[]{:S(2)}, u32[]{:S(2)}) collective-permute-start(bf16[160,256]{1,0:T(8,128)(2,1)S(1)} %shard_map.161), channel_id=1, source_target_pairs={{0,1},{1,0},{2,3},{3,2},{4,5},{5,4},{6,7},{7,6},{8,9},{9,8},{10,11... | collective-permute-start | bytes 245768 | tf_op jit(solution)/shard_map/ppermute | solution.py:343
  28.5 0.9 %collective-permute-done.8.refs_5_ = bf16[160,256]{1,0:T(8,128)(2,1)S(1)} collective-permute-done((bf16[160,256]{1,0:T(8,128)(2,1)S(1)}, bf16[160,256]{1,0:T(8,128)(2,1)S(1)}, u32[]{:S(2)}, u32[]{:S(2)}) %collective-permute-start.8) | collective-permute-done | bytes 81952 | tf_op jit(solution)/shard_map/ppermute | solution.py:343
  29.5 3.7 %collective-permute-done.5.refs_2_ = bf16[144,512]{1,0:T(8,128)(2,1)S(1)} collective-permute-done((bf16[144,512]{1,0:T(8,128)(2,1)S(1)}, bf16[144,512]{1,0:T(8,128)(2,1)S(1)}, u32[]{:S(2)}, u32[]{:S(2)}) %collective-permute-start.5) | collective-permute-done | bytes 147488 | tf_op jit(solution)/shard_map/ppermute | solution.py:343
  33.4 1.2 %collective-permute-done.11.refs_3_ = f32[16,512]{1,0:T(8,128)S(1)} collective-permute-done((f32[16,512]{1,0:T(8,128)S(1)}, f32[16,512]{1,0:T(8,128)S(1)}, u32[]{:S(2)}, u32[]{:S(2)}) %collective-permute-start.11) | collective-permute-done | bytes 32800 | tf_op jit(solution)/shard_map/ppermute | solution.py:343
  34.6 2.0 %shard_map.163 = (bf16[16,128]{1,0:T(8,128)(2,1)}, f32[128,256]{1,0:T(8,128)S(1)}, bf16[128,256]{1,0:T(8,128)(2,1)S(1)}, bf16[128,256]{1,0:T(8,128)(2,1)S(1)}, bf16[16,256]{1,0:T(8,128)(2,1)S(1)}) custom-call(bf16[128,1024]{1,0:T(8,128)(2,1)S(1)} %collective-permute-done.6.refs_0_, bf16[128,1024]{1,0:T(8,128)(2,1)S(1)} %collective-permute-done.10.refs_1_, ...), custom_call_target="tpu_custom_call" | custom-call | flops 16777216 | bytes 3035648 | tf_op jit(solution)/shard_map/pallas_call | solution.py:73
  36.7 1.1 %shard_map.166 = bf16[16,16,128]{2,1,0:T(8,128)(2,1)} custom-call(bf16[128,256]{1,0:T(8,128)(2,1)S(1)} %get-tuple-element.60.dpre, bf16[16,256]{1,0:T(8,128)(2,1)S(1)} %get-tuple-element.61.node_dpre, bf16[64,128]{1,0:T(8,128)(2,1)S(1)} %get-tuple-element.35.pick, bf16[16,128]{1,0:T(8,128)(2,1)S(1)} %get-tuple-element.36.take.refs_7_, ...), custom_call_target="tpu_custom_call" | custom-call | flops 16777216 | bytes 1404928 | tf_op jit(solution)/shard_map/pallas_call | solution.py:73
  37.7 3.5 %all-to-all-start.1 = ((bf16[16,16,128]{2,1,0:T(8,128)(2,1)}), bf16[16,16,128]{2,1,0:T(8,128)(2,1)S(1)}, u32[]{:S(2)}, u32[]{:S(2)}) async-start(bf16[16,16,128]{2,1,0:T(8,128)(2,1)} %shard_map.166), calls=%async_computation.1 | async-start | bytes 131072 | tf_op jit(solution)/shard_map/all_to_all | solution.py:423
  41.2 1.8 %collective-permute-start.13 = (bf16[128,256]{1,0:T(8,128)(2,1)S(1)}, bf16[128,256]{1,0:T(8,128)(2,1)S(1)}, u32[]{:S(2)}, u32[]{:S(2)}) collective-permute-start(bf16[128,256]{1,0:T(8,128)(2,1)S(1)} %get-tuple-element.54), channel_id=1, source_target_pairs={{0,2},{1,3},{2,0},{3,1},{4,6},{5,7},{6,4},{7,5},{8,10},{9,11},{10,... | collective-permute-start | bytes 196616 | tf_op jit(solution)/shard_map/ppermute | solution.py:343
  43.0 3.0 %collective-permute-done.13.refs_1_ = bf16[128,256]{1,0:T(8,128)(2,1)S(1)} collective-permute-done((bf16[128,256]{1,0:T(8,128)(2,1)S(1)}, bf16[128,256]{1,0:T(8,128)(2,1)S(1)}, u32[]{:S(2)}, u32[]{:S(2)}) %collective-permute-start.13) | collective-permute-done | bytes 65568 | tf_op jit(solution)/shard_map/ppermute | solution.py:343
  46.1 1.2 %collective-permute-done.14.grad_came = bf16[128,128]{1,0:T(8,128)(2,1)S(1)} collective-permute-done((bf16[128,128]{1,0:T(8,128)(2,1)S(1)}, bf16[128,128]{1,0:T(8,128)(2,1)S(1)}, u32[]{:S(2)}, u32[]{:S(2)}) %collective-permute-start.14) | collective-permute-done | bytes 32800 | tf_op jit(solution)/shard_map/ppermute | solution.py:343
  47.3 0.7 %shard_map.165 = (bf16[256,128]{1,0:T(8,128)(2,1)}, bf16[256,128]{1,0:T(8,128)(2,1)}) custom-call(bf16[128,128]{1,0:T(8,128)(2,1)S(1)} %get-tuple-element.43.next_mine, bf16[128,128]{1,0:T(8,128)(2,1)S(1)} %collective-permute-done.9.next_came, bf16[128,128]{1,0:T(8,128)(2,1)S(1)} %get-tuple-element.55.grad_mine, ...), custom_call_target="tpu_custom_call" | custom-call | flops 16777216 | bytes 131072 | tf_op jit(solution)/shard_map/pallas_call | solution.py:73
  48.1 0.6 %shard_map.167 = bf16[16,128]{1,0:T(8,128)(2,1)} custom-call(bf16[16,16,128]{2,1,0:T(8,128)(2,1)S(1)} %all-to-all-done.1.shares, bf16[16,128]{1,0:T(8,128)(2,1)S(1)} %copy-done.6), custom_call_target="tpu_custom_call" | custom-call | flops 16777216 | bytes 69632 | tf_op jit(solution)/shard_map/pallas_call | solution.py:73
  (51 shorter events, 2.2 us)
Async XLA Ops:
  0.7 19.6 %collective-permute-start.2 = (bf16[128,1536]{1,0:T(8,128)(2,1)}, bf16[128,1536]{1,0:T(8,128)(2,1)S(1)}, u32[]{:S(2)}, u32[]{:S(2)}) collective-permute-start(bf16[128,1536]{1,0:T(8,128)(2,1)} %e_mine.1), channel_id=1, source_target_pairs={{0,1},{1,0},{2,3},{3,2},{4,5},{5,4},{6,7},{7,6},{8,9},{9,8},{10,11... | collective-permute-start | bytes 1179656 | tf_op jit(solution)/shard_map/ppermute | solution.py:343
  1.6 5.1 %copy-start.5 = (bf16[256,128]{1,0:T(8,128)(2,1)S(1)}, bf16[256,128]{1,0:T(8,128)(2,1)}, u32[]{:S(2)}) copy-start(bf16[256,128]{1,0:T(8,128)(2,1)} %edge_cot) | copy-start | bytes 196612
  1.6 5.1 %copy-start.6 = (bf16[16,128]{1,0:T(8,128)(2,1)S(1)}, bf16[16,128]{1,0:T(8,128)(2,1)}, u32[]{:S(2)}) copy-start(bf16[16,128]{1,0:T(8,128)(2,1)} %node_cot.3) | copy-start | bytes 12292
  1.6 11.6 %copy-start.2 = (bf16[128,512]{1,0:T(8,128)(2,1)S(1)}, bf16[128,512]{1,0:T(8,128)(2,1)}, u32[]{:S(2)}) copy-start(bf16[128,512]{1,0:T(8,128)(2,1)} %refs_13_.1) | copy-start | bytes 393220
  1.6 11.6 %copy-start.8 = (bf16[16,128]{1,0:T(8,128)(2,1)S(1)}, bf16[16,128]{1,0:T(8,128)(2,1)}, u32[]{:S(2)}) copy-start(bf16[16,128]{1,0:T(8,128)(2,1)} %latent.1) | copy-start | bytes 12292
  1.7 18.6 %copy-start = (bf16[128,1536]{1,0:T(8,128)(2,1)S(1)}, bf16[128,1536]{1,0:T(8,128)(2,1)}, u32[]{:S(2)}) copy-start(bf16[128,1536]{1,0:T(8,128)(2,1)} %e_mine.1) | copy-start | bytes 1179652
  1.7 20.2 %collective-permute-start.6 = (bf16[128,1024]{1,0:T(8,128)(2,1)S(1)}, bf16[128,1024]{1,0:T(8,128)(2,1)S(1)}, u32[]{:S(2)}, u32[]{:S(2)}) collective-permute-start(bf16[128,1024]{1,0:T(8,128)(2,1)S(1)} %pad_maximum_fusion), channel_id=1, source_target_pairs={{0,2},{1,3},{2,0},{3,1},{4,6},{5,7},{6,4},{7,5},{8,10},{9,11},{10,... | collective-permute-start | bytes 786440 | tf_op jit(solution)/shard_map/ppermute | solution.py:343
  4.7 1.3 %collective-permute-start = (bf16[256,128]{1,0:T(8,128)(2,1)S(1)}, bf16[256,128]{1,0:T(8,128)(2,1)S(1)}, u32[]{:S(2)}, u32[]{:S(2)}) collective-permute-start(bf16[256,128]{1,0:T(8,128)(2,1)S(1)} %copy-done.4), channel_id=1, source_target_pairs={{0,1},{1,0},{2,3},{3,2},{4,5},{5,4},{6,7},{7,6},{8,9},{9,8},{10,11... | collective-permute-start | bytes 196616 | tf_op jit(solution)/shard_map/ppermute | solution.py:343
  4.7 22.5 %collective-permute-start.4 = (bf16[128,1024]{1,0:T(8,128)(2,1)S(1)}, bf16[128,1024]{1,0:T(8,128)(2,1)S(1)}, u32[]{:S(2)}, u32[]{:S(2)}) collective-permute-start(bf16[128,1024]{1,0:T(8,128)(2,1)S(1)} %copy-done.1), channel_id=1, source_target_pairs={{0,1},{1,0},{2,3},{3,2},{4,5},{5,4},{6,7},{7,6},{8,9},{9,8},{10,11... | collective-permute-start | bytes 786440 | tf_op jit(solution)/shard_map/ppermute | solution.py:343
  6.0 7.2 %collective-permute-start.1 = (bf16[128,256]{1,0:T(8,128)(2,1)S(1)}, bf16[128,256]{1,0:T(8,128)(2,1)S(1)}, u32[]{:S(2)}, u32[]{:S(2)}) collective-permute-start(bf16[128,256]{1,0:T(8,128)(2,1)S(1)} %shard_map.157.refs_0_), channel_id=1, source_target_pairs={{0,2},{1,3},{2,0},{3,1},{4,6},{5,7},{6,4},{7,5},{8,10},{9,11},{10,... | collective-permute-start | bytes 196616 | tf_op jit(solution)/shard_map/ppermute | solution.py:343
  6.7 15.1 %collective-permute-start.7 = (bf16[288,128]{1,0:T(8,128)(2,1)S(1)}, bf16[288,128]{1,0:T(8,128)(2,1)S(1)}, u32[]{:S(2)}, u32[]{:S(2)}) collective-permute-start(bf16[288,128]{1,0:T(8,128)(2,1)S(1)} %shard_map.160.refs_0_.refs_3_), channel_id=1, source_target_pairs={{0,2},{1,3},{2,0},{3,1},{4,6},{5,7},{6,4},{7,5},{8,10},{9,11},{10,... | collective-permute-start | bytes 221192 | tf_op jit(solution)/shard_map/ppermute | solution.py:343
  13.2 14.0 %collective-permute-start.3 = (bf16[128,512]{1,0:T(8,128)(2,1)S(1)}, bf16[128,512]{1,0:T(8,128)(2,1)S(1)}, u32[]{:S(2)}, u32[]{:S(2)}) collective-permute-start(bf16[128,512]{1,0:T(8,128)(2,1)S(1)} %copy-done.2), channel_id=1, source_target_pairs={{0,1},{1,0},{2,3},{3,2},{4,5},{5,4},{6,7},{7,6},{8,9},{9,8},{10,11... | collective-permute-start | bytes 393224 | tf_op jit(solution)/shard_map/ppermute | solution.py:343
  13.9 6.4 %copy-start.7 = (s32[4,4,8]{2,1,0:T(4,128)S(1)}, s32[4,4,8]{2,1,0:T(4,128)}, u32[]{:S(2)}) copy-start(s32[4,4,8]{2,1,0:T(4,128)} %refs_6_.1) | copy-start | bytes 1540
  13.9 6.5 %copy-start.10 = (s32[256]{0:T(256)S(1)}, s32[256]{0:T(256)}, u32[]{:S(2)}) copy-start(s32[256]{0:T(256)} %param.17) | copy-start | bytes 3076
  13.9 13.3 %all-to-all-start = ((bf16[16,16,128]{2,1,0:T(8,128)(2,1)}), bf16[16,16,128]{2,1,0:T(8,128)(2,1)S(1)}, u32[]{:S(2)}, u32[]{:S(2)}) async-start(bf16[16,16,128]{2,1,0:T(8,128)(2,1)} %shard_map.156), calls=%async_computation | async-start | bytes 131072 | tf_op jit(solution)/shard_map/all_to_all | solution.py:356
  21.9 12.8 %collective-permute-start.10 = (bf16[128,1024]{1,0:T(8,128)(2,1)S(1)}, bf16[128,1024]{1,0:T(8,128)(2,1)S(1)}, u32[]{:S(2)}, u32[]{:S(2)}) collective-permute-start(bf16[128,1024]{1,0:T(8,128)(2,1)S(1)} %collective-permute-done.6.refs_0_), channel_id=1, source_target_pairs={{0,1},{1,0},{2,3},{3,2},{4,5},{5,4},{6,7},{7,6},{8,9},{9,8},{10,11... | collective-permute-start | bytes 786440 | tf_op jit(solution)/shard_map/ppermute | solution.py:343
  27.8 5.3 %collective-permute-start.5 = (bf16[144,512]{1,0:T(8,128)(2,1)S(1)}, bf16[144,512]{1,0:T(8,128)(2,1)S(1)}, u32[]{:S(2)}, u32[]{:S(2)}) collective-permute-start(bf16[144,512]{1,0:T(8,128)(2,1)S(1)} %get-tuple-element.39), channel_id=1, source_target_pairs={{0,2},{1,3},{2,0},{3,1},{4,6},{5,7},{6,4},{7,5},{8,10},{9,11},{10,... | collective-permute-start | bytes 442376 | tf_op jit(solution)/shard_map/ppermute | solution.py:343
  27.9 5.5 %collective-permute-start.12 = (bf16[128,512]{1,0:T(8,128)(2,1)S(1)}, bf16[128,512]{1,0:T(8,128)(2,1)S(1)}, u32[]{:S(2)}, u32[]{:S(2)}) collective-permute-start(bf16[128,512]{1,0:T(8,128)(2,1)S(1)} %copy-done.3), channel_id=1, source_target_pairs={{0,1},{1,0},{2,3},{3,2},{4,5},{5,4},{6,7},{7,6},{8,9},{9,8},{10,11... | collective-permute-start | bytes 393224 | tf_op jit(solution)/shard_map/ppermute | solution.py:343
  28.0 1.5 %collective-permute-start.8 = (bf16[160,256]{1,0:T(8,128)(2,1)S(1)}, bf16[160,256]{1,0:T(8,128)(2,1)S(1)}, u32[]{:S(2)}, u32[]{:S(2)}) collective-permute-start(bf16[160,256]{1,0:T(8,128)(2,1)S(1)} %shard_map.161), channel_id=1, source_target_pairs={{0,1},{1,0},{2,3},{3,2},{4,5},{5,4},{6,7},{7,6},{8,9},{9,8},{10,11... | collective-permute-start | bytes 245768 | tf_op jit(solution)/shard_map/ppermute | solution.py:343
  33.4 1.2 %collective-permute-start.11 = (f32[16,512]{1,0:T(8,128)S(1)}, f32[16,512]{1,0:T(8,128)S(1)}, u32[]{:S(2)}, u32[]{:S(2)}) collective-permute-start(f32[16,512]{1,0:T(8,128)S(1)} %get-tuple-element.46.refs_2_), channel_id=1, source_target_pairs={{0,1},{1,0},{2,3},{3,2},{4,5},{5,4},{6,7},{7,6},{8,9},{9,8},{10,11... | collective-permute-start | bytes 98312 | tf_op jit(solution)/shard_map/ppermute | solution.py:343
  37.7 10.3 %all-to-all-start.1 = ((bf16[16,16,128]{2,1,0:T(8,128)(2,1)}), bf16[16,16,128]{2,1,0:T(8,128)(2,1)S(1)}, u32[]{:S(2)}, u32[]{:S(2)}) async-start(bf16[16,16,128]{2,1,0:T(8,128)(2,1)} %shard_map.166), calls=%async_computation.1 | async-start | bytes 131072 | tf_op jit(solution)/shard_map/all_to_all | solution.py:423
  41.2 4.8 %collective-permute-start.13 = (bf16[128,256]{1,0:T(8,128)(2,1)S(1)}, bf16[128,256]{1,0:T(8,128)(2,1)S(1)}, u32[]{:S(2)}, u32[]{:S(2)}) collective-permute-start(bf16[128,256]{1,0:T(8,128)(2,1)S(1)} %get-tuple-element.54), channel_id=1, source_target_pairs={{0,2},{1,3},{2,0},{3,1},{4,6},{5,7},{6,4},{7,5},{8,10},{9,11},{10,... | collective-permute-start | bytes 196616 | tf_op jit(solution)/shard_map/ppermute | solution.py:343
  43.0 3.1 %collective-permute-start.9 = (bf16[128,128]{1,0:T(8,128)(2,1)S(1)}, bf16[128,128]{1,0:T(8,128)(2,1)S(1)}, u32[]{:S(2)}, u32[]{:S(2)}) collective-permute-start(bf16[128,128]{1,0:T(8,128)(2,1)S(1)} %get-tuple-element.44), channel_id=1, source_target_pairs={{0,1},{1,0},{2,3},{3,2},{4,5},{5,4},{6,7},{7,6},{8,9},{9,8},{10,11... | collective-permute-start | bytes 98312 | tf_op jit(solution)/shard_map/ppermute | solution.py:343
  46.0 1.3 %collective-permute-start.14 = (bf16[128,128]{1,0:T(8,128)(2,1)S(1)}, bf16[128,128]{1,0:T(8,128)(2,1)S(1)}, u32[]{:S(2)}, u32[]{:S(2)}) collective-permute-start(bf16[128,128]{1,0:T(8,128)(2,1)S(1)} %get-tuple-element.56), channel_id=1, source_target_pairs={{0,1},{1,0},{2,3},{3,2},{4,5},{5,4},{6,7},{7,6},{8,9},{9,8},{10,11... | collective-permute-start | bytes 98312 | tf_op jit(solution)/shard_map/ppermute | solution.py:343
  (7 other events, 19.0 us)

commit v13 on v10

--- a/solution.py
+++ b/solution.py
@@ -94,6 +94,10 @@
     for ref in refs[1:]:
         value = value + ref[...].astype(f32)
     return value
+
+
+def spread_latent(latent, spread):
+    spread[...] = jnp.broadcast_to(latent[...][None], spread.shape)
 
 
 def pack_extra(edge_cot, node_cot, gain_e, gain_n, pack):
@@ -209,15 +213,16 @@
 
 def turn(groups, *refs):
     far, refs = refs[: 2 * (groups - 1)], refs[2 * (groups - 1) :]
-    aggregate, aggregate2, own, lat_all, extra, take, normed, inverse, edge_pre = refs[:9]
-    e_mine, e_other, out_mine, out_other, in_mine, in_other, n_mine, n_other = refs[9:17]
-    node_next, kept, *sents, dpre_ref, node_dpre_ref, next_all, grads = refs[17:]
+    aggregate, aggregate2, own, lat_all, extra, take, pick, normed, inverse, edge_pre = refs[:10]
+    e_mine, e_other, out_mine, out_other, in_mine, in_other, n_mine, n_other = refs[10:18]
+    node_next, dpre_ref, total_ref, spread, next_all, grads = refs[18:]
     group, core = place()
+    block = lax.axis_index("nodes")
     nodes, half = take.shape
     features = extra.shape[1]
     hidden = edge_pre.shape[1]
-    wide = kept.shape[1]
     width = node_next.shape[1]
+    wide = width * cores
     gain_rows = extra[half + nodes :].astype(f32)
     edge_gain, node_gain = gain_rows[0:1], gain_rows[1:2]
 
@@ -246,19 +251,7 @@
     dpre = (back * swish_slope(edge_pre[...])).astype(bf16)
 
     dpre_ref[...] = dpre
-    node_dpre_ref[...] = node_dpre[:, :hidden]
-    grads[...] = dot(dpre, jnp.concatenate([e_mine[:, :features], e_other[:, :features]], axis=0))
-    for step, sent in enumerate(sents, 1):
-        sent[...] = grads[:, lanes(group ^ step, wide)].astype(bf16)
-    grads[...] += edge_total
-    kept[...] = grads[:, lanes(group, wide)]
-
-
-def spread_nodes(dpre, node_dpre, pick, take, e_mine, e_other, in_mine, in_other, spread, grads):
-    block = lax.axis_index("nodes")
-    count, nodes, width = spread.shape
-    features = grads.shape[1]
-    feats = features // width
+    total_ref[...] = edge_total
 
     def weighted(values, index):
         columns = slice(index * features, (index + 1) * features)
@@ -266,14 +259,26 @@
         both = dot(jnp.concatenate(split(values), axis=0), weight)
         return both[: values.shape[0]] + both[values.shape[0] :]
 
-    grads[...] = weighted(dot(pick[...], dpre[...]), 1)
-    home = weighted(dot(take[...], dpre[...]), 2)
+    grads[...] = weighted(dot(pick[...], dpre), 1)
+    home = weighted(dot(taken, dpre), 2)
     node_weight = jnp.concatenate([in_mine[:, :features], in_other[:, :features]], axis=0)
-    home = home + 0.5 * dot(node_dpre[...], node_weight)
+    home = home + 0.5 * dot(node_dpre[:, :hidden], node_weight)
     grads[pl.ds(pl.multiple_of(block * nodes, nodes), nodes)] += home
-    for target in range(count):
+    feats = features // width
+    for target in range(spread.shape[0]):
         first, column = target // feats * nodes, target % feats * width
         spread[target] = grads[first : first + nodes, column : column + width].astype(bf16)
+
+
+def turn_edges(dpre, edge_total, e_mine, e_other, kept, *refs):
+    *sents, grads = refs
+    group, _ = place()
+    features = edge_total.shape[1]
+    wide = kept.shape[1]
+    grads[...] = dot(dpre[...], jnp.concatenate([e_mine[:, :features], e_other[:, :features]], axis=0))
+    for step, sent in enumerate(sents, 1):
+        sent[...] = grads[:, lanes(group ^ step, wide)].astype(bf16)
+    kept[...] = grads[:, lanes(group, wide)] + edge_total[:, lanes(group, wide)]
 
 
 def add_groups(groups, *refs):
@@ -343,9 +348,8 @@
     slot_rows = sender_slot.reshape(cores, half)
     receiver_rows = receiver_row.reshape(cores, half)
 
-    latents = lax.all_to_all(
-        jnp.broadcast_to(latent[None], (blocks * feats, nodes, width)), everyone, 0, 0
-    )
+    (spread,) = stage(spread_latent, [((blocks * feats, nodes, width), bf16)], [latent])
+    latents = lax.all_to_all(spread, everyone, 0, 0)
     states = [edge_state] + over_groups(edge_state)
     e_in = (edge_in_weight, over_cores(edge_in_weight))
     e_out = (edge_out_weight, over_cores(edge_out_weight))
@@ -394,22 +398,25 @@
     )
     aggregate2 = over_cores(aggregate)
     next_came = over_cores(next_sent)
-    node_next, kept, *sents, dpre, node_dpre = stage(
+    node_next, dpre, edge_total, spread = stage(
         functools.partial(turn, groups),
-        [((nodes, width), bf16), ((half, wide), f32)]
-        + [((half, wide), bf16)] * (groups - 1)
-        + [((half, hidden), bf16), ((nodes, hidden), bf16)],
-        [*far, aggregate, aggregate2, own, lat_all, extra, take, normed, inverse, edge_pre]
+        [
+            ((nodes, width), bf16),
+            ((half, hidden), bf16),
+            ((half, features), f32),
+            ((blocks * feats, nodes, width), bf16),
+        ],
+        [*far, aggregate, aggregate2, own, lat_all, extra, take, pick, normed, inverse, edge_pre]
         + [*e_in, *e_out, *n_in, *n_out],
-        scratch=[((nodes, features), bf16), ((half, features), f32)],
+        scratch=[((nodes, features), bf16), ((table, features), f32)],
+    )
+    kept, *sents = stage(
+        turn_edges,
+        [((half, wide), f32)] + [((half, wide), bf16)] * (groups - 1),
+        [dpre, edge_total, *e_in],
+        scratch=[((half, features), f32)],
     )
     sents = [swapped(s, cores * k) for k, s in enumerate(sents, 1)]
-    (spread,) = stage(
-        spread_nodes,
-        [((blocks * feats, nodes, width), bf16)],
-        [dpre, node_dpre, pick, take, *e_in, *n_in],
-        scratch=[((table, features), f32)],
-    )
     shares = lax.all_to_all(spread, everyone, 0, 0)
     grad_mine, grad_sent = stage(
         functools.partial(add_groups, groups),

time: 41.5 us -> 40.9 us (0.986)
  local copies, waits for them, and re-layouts: 3.12 us -> 2.48 us
    broadcast_in_dim x1 -> x0, local copies, waits for them, and re-layouts: 1.32 us -> none  [shards(): jnp.broadcast_to(latent[None], (blocks * feats, nodes, width))]
    unnamed x24 -> x26, local copies, waits for them, and re-layouts: 1.42 us -> 2.11 us
    pallas_call x11 -> x12, Pallas kernels: 6.25 us -> 6.46 us  [stage(): pl.pallas_call(kernel, out_shape=[jax.ShapeDtypeStruct(shape, kind) for s...]
  transfers between devices with their start and end apart: 17 -> 17, of which waited for: 8 -> 8; matrix products, arithmetic and copies ran while one was open for 3% -> 0% of each run, Pallas kernels for 6% -> 8%
where the time goes in v13:
time: 40.9 us; the launch traced here: 40.5 us
  starting transfers between devices  18.8 us (46%)
  waiting for transfers between devices  11.9 us (29%)
  Pallas kernels  6.46 us (16%)
  local copies, waits for them, and re-layouts  2.48 us (6%)
  between operations  0.79 us (2%)
    ppermute x15, waiting for transfers between devices, swapped(): return lax.ppermute(values, 'feat', [(i, i ^ bits) for i in range(feats)])  10.2 us
    ppermute x15, starting transfers between devices, swapped(): return lax.ppermute(values, 'feat', [(i, i ^ bits) for i in range(feats)])  9.71 us
    pallas_call x12, Pallas kernels, stage(): pl.pallas_call(kernel, out_shape=[jax.ShapeDtypeStruct(shape, kind) for s...  6.46 us
    all_to_all x1, starting transfers between devices, shards(): latents = lax.all_to_all(spread, everyone, 0, 0)  5.61 us
    all_to_all x1, starting transfers between devices, shards(): shares = lax.all_to_all(spread, everyone, 0, 0)  3.5 us
    unnamed x26, local copies, waits for them, and re-layouts  2.11 us
    all_to_all x1, waiting for transfers between devices, shards(): latents = lax.all_to_all(spread, everyone, 0, 0)  1.69 us
  transfers between devices with their start and end apart: 17, of which 8 were waited for; matrix products, arithmetic and copies ran while one was open for 0% of the time, Pallas kernels for 8%

profile of v13, /device:TPU:0, one launch (start us, length us, event | category | flops | bytes accessed | tf_op | source)
XLA Modules:
  0.0 40.5 jit_solution(14912505879701442825)
XLA Ops:
  0.7 0.5 %collective-permute-start.2 = (bf16[128,1536]{1,0:T(8,128)(2,1)}, bf16[128,1536]{1,0:T(8,128)(2,1)S(1)}, u32[]{:S(2)}, u32[]{:S(2)}) collective-permute-start(bf16[128,1536]{1,0:T(8,128)(2,1)} %e_mine.1), channel_id=1, source_target_pairs={{0,1},{1,0},{2,3},{3,2},{4,5},{5,4},{6,7},{7,6},{8,9},{9,8},{10,11... | collective-permute-start | bytes 1179656 | tf_op jit(solution)/shard_map/ppermute | solution.py:339
  1.7 3.0 %collective-permute-start.9 = (bf16[128,1024]{1,0:T(8,128)(2,1)S(1)}, bf16[128,1024]{1,0:T(8,128)(2,1)S(1)}, u32[]{:S(2)}, u32[]{:S(2)}) collective-permute-start(bf16[128,1024]{1,0:T(8,128)(2,1)S(1)} %pad_maximum_fusion), channel_id=1, source_target_pairs={{0,2},{1,3},{2,0},{3,1},{4,6},{5,7},{6,4},{7,5},{8,10},{9,11},{10,... | collective-permute-start | bytes 786440 | tf_op jit(solution)/shard_map/ppermute | solution.py:339
  4.7 0.8 %collective-permute-start = (bf16[256,128]{1,0:T(8,128)(2,1)S(1)}, bf16[256,128]{1,0:T(8,128)(2,1)S(1)}, u32[]{:S(2)}, u32[]{:S(2)}) collective-permute-start(bf16[256,128]{1,0:T(8,128)(2,1)S(1)} %copy-done.4), channel_id=1, source_target_pairs={{0,2},{1,3},{2,0},{3,1},{4,6},{5,7},{6,4},{7,5},{8,10},{9,11},{10,... | collective-permute-start | bytes 196616 | tf_op jit(solution)/shard_map/ppermute | solution.py:339
  5.7 0.7 %copy-done.8 = bf16[16,128]{1,0:T(8,128)(2,1)S(1)} copy-done((bf16[16,128]{1,0:T(8,128)(2,1)S(1)}, bf16[16,128]{1,0:T(8,128)(2,1)}, u32[]{:S(2)}) %copy-start.8) | copy-done | bytes 4120
  6.4 0.6 %shard_map.156 = bf16[16,16,128]{2,1,0:T(8,128)(2,1)} custom-call(bf16[16,128]{1,0:T(8,128)(2,1)S(1)} %copy-done.8), custom_call_target="tpu_custom_call" | custom-call | flops 16777216 | bytes 4096 | tf_op jit(solution)/shard_map/pallas_call | solution.py:73
  7.1 5.6 %all-to-all-start = ((bf16[16,16,128]{2,1,0:T(8,128)(2,1)}), bf16[16,16,128]{2,1,0:T(8,128)(2,1)S(1)}, u32[]{:S(2)}, u32[]{:S(2)}) async-start(bf16[16,16,128]{2,1,0:T(8,128)(2,1)} %shard_map.156), calls=%async_computation | async-start | bytes 131072 | tf_op jit(solution)/shard_map/all_to_all | solution.py:352
  12.7 0.5 %collective-permute-start.10 = (bf16[128,1024]{1,0:T(8,128)(2,1)S(1)}, bf16[128,1024]{1,0:T(8,128)(2,1)S(1)}, u32[]{:S(2)}, u32[]{:S(2)}) collective-permute-start(bf16[128,1024]{1,0:T(8,128)(2,1)S(1)} %collective-permute-done.9.refs_0_), channel_id=1, source_target_pairs={{0,1},{1,0},{2,3},{3,2},{4,5},{5,4},{6,7},{7,6},{8,9},{9,8},{10,11... | collective-permute-start | bytes 786440 | tf_op jit(solution)/shard_map/ppermute | solution.py:339
  13.4 0.5 %copy-done.6 = bf16[16,128]{1,0:T(8,128)(2,1)S(1)} copy-done((bf16[16,128]{1,0:T(8,128)(2,1)S(1)}, bf16[16,128]{1,0:T(8,128)(2,1)}, u32[]{:S(2)}) %copy-start.6) | copy-done | bytes 4120
  14.5 1.8 %collective-permute-start.6 = (bf16[288,128]{1,0:T(8,128)(2,1)S(1)}, bf16[288,128]{1,0:T(8,128)(2,1)S(1)}, u32[]{:S(2)}, u32[]{:S(2)}) collective-permute-start(bf16[288,128]{1,0:T(8,128)(2,1)S(1)} %shard_map.160.refs_0_.refs_3_), channel_id=1, source_target_pairs={{0,2},{1,3},{2,0},{3,1},{4,6},{5,7},{6,4},{7,5},{8,10},{9,11},{10,... | collective-permute-start | bytes 221192 | tf_op jit(solution)/shard_map/ppermute | solution.py:339
  16.3 0.7 %copy-done.9 = s32[256]{0:T(256)S(1)} copy-done((s32[256]{0:T(256)S(1)}, s32[256]{0:T(256)}, u32[]{:S(2)}) %copy-start.9) | copy-done | bytes 1048
  17.0 0.9 %shard_map.158 = (bf16[128,512]{1,0:T(8,128)(2,1)S(1)}, f32[128,256]{1,0:T(8,128)S(1)}, bf16[64,128]{1,0:T(8,128)(2,1)S(1)}, bf16[16,128]{1,0:T(8,128)(2,1)S(1)}) custom-call(bf16[256,128]{1,0:T(8,128)(2,1)S(1)} %copy-done.4, bf16[256,128]{1,0:T(8,128)(2,1)S(1)} %collective-permute-done.refs_1_, bf16[128,256]{1,0:T(8,128)(2,1)S(1)} %collective-permute-done.1.refs_2_, ...), custom_call_target="tpu_custom_call" | custom-call | flops 16777216 | bytes 985600 | tf_op jit(solution)/shard_map/pallas_call | solution.py:73
  17.9 1.7 %all-to-all-done.came = bf16[16,16,128]{2,1,0:T(8,128)(2,1)S(1)} async-done(((bf16[16,16,128]{2,1,0:T(8,128)(2,1)}), bf16[16,16,128]{2,1,0:T(8,128)(2,1)S(1)}, u32[]{:S(2)}, u32[]{:S(2)}) %all-to-all-start) | async-done | bytes 65568 | tf_op jit(solution)/shard_map/all_to_all | solution.py:352
  19.6 0.6 %shard_map.159 = (f32[128,256]{1,0:T(8,128)S(1)}, f32[128,512]{1,0:T(8,128)S(1)}, bf16[144,512]{1,0:T(8,128)(2,1)S(1)}, bf16[16,512]{1,0:T(8,128)(2,1)S(1)}, f32[16,256]{1,0:T(8,128)S(1)}) custom-call(bf16[16,16,128]{2,1,0:T(8,128)(2,1)S(1)} %all-to-all-done.came, f32[128,256]{1,0:T(8,128)S(1)} %get-tuple-element.30.pre, ...), custom_call_target="tpu_custom_call" | custom-call | flops 16777216 | bytes 1789952 | tf_op jit(solution)/shard_map/pallas_call | solution.py:73
  20.4 0.6 %collective-permute-start.7 = (bf16[160,256]{1,0:T(8,128)(2,1)S(1)}, bf16[160,256]{1,0:T(8,128)(2,1)S(1)}, u32[]{:S(2)}, u32[]{:S(2)}) collective-permute-start(bf16[160,256]{1,0:T(8,128)(2,1)S(1)} %shard_map.161), channel_id=1, source_target_pairs={{0,1},{1,0},{2,3},{3,2},{4,5},{5,4},{6,7},{7,6},{8,9},{9,8},{10,11... | collective-permute-start | bytes 245768 | tf_op jit(solution)/shard_map/ppermute | solution.py:339
  21.0 0.9 %collective-permute-done.7.refs_5_ = bf16[160,256]{1,0:T(8,128)(2,1)S(1)} collective-permute-done((bf16[160,256]{1,0:T(8,128)(2,1)S(1)}, bf16[160,256]{1,0:T(8,128)(2,1)S(1)}, u32[]{:S(2)}, u32[]{:S(2)}) %collective-permute-start.7) | collective-permute-done | bytes 81952 | tf_op jit(solution)/shard_map/ppermute | solution.py:339
  21.9 3.7 %collective-permute-done.5.refs_2_ = bf16[144,512]{1,0:T(8,128)(2,1)S(1)} collective-permute-done((bf16[144,512]{1,0:T(8,128)(2,1)S(1)}, bf16[144,512]{1,0:T(8,128)(2,1)S(1)}, u32[]{:S(2)}, u32[]{:S(2)}) %collective-permute-start.5) | collective-permute-done | bytes 147488 | tf_op jit(solution)/shard_map/ppermute | solution.py:339
  25.8 1.2 %collective-permute-done.11.refs_3_ = f32[16,512]{1,0:T(8,128)S(1)} collective-permute-done((f32[16,512]{1,0:T(8,128)S(1)}, f32[16,512]{1,0:T(8,128)S(1)}, u32[]{:S(2)}, u32[]{:S(2)}) %collective-permute-start.11) | collective-permute-done | bytes 32800 | tf_op jit(solution)/shard_map/ppermute | solution.py:339
  27.0 2.5 %shard_map.163 = (bf16[16,128]{1,0:T(8,128)(2,1)}, bf16[128,256]{1,0:T(8,128)(2,1)S(1)}, f32[128,512]{1,0:T(8,128)S(1)}, bf16[16,16,128]{2,1,0:T(8,128)(2,1)}) custom-call(bf16[128,1024]{1,0:T(8,128)(2,1)S(1)} %collective-permute-done.9.refs_0_, bf16[128,1024]{1,0:T(8,128)(2,1)S(1)} %collective-permute-done.10.refs_1_, ...), custom_call_target="tpu_custom_call" | custom-call | flops 16777216 | bytes 3052032 | tf_op jit(solution)/shard_map/pallas_call | solution.py:73
  29.5 3.5 %all-to-all-start.1 = ((bf16[16,16,128]{2,1,0:T(8,128)(2,1)}), bf16[16,16,128]{2,1,0:T(8,128)(2,1)S(1)}, u32[]{:S(2)}, u32[]{:S(2)}) async-start(bf16[16,16,128]{2,1,0:T(8,128)(2,1)} %get-tuple-element.55), calls=%async_computation.1 | async-start | bytes 131072 | tf_op jit(solution)/shard_map/all_to_all | solution.py:420
  33.2 1.9 %collective-permute-start.13 = (bf16[128,256]{1,0:T(8,128)(2,1)S(1)}, bf16[128,256]{1,0:T(8,128)(2,1)S(1)}, u32[]{:S(2)}, u32[]{:S(2)}) collective-permute-start(bf16[128,256]{1,0:T(8,128)(2,1)S(1)} %get-tuple-element.49), channel_id=1, source_target_pairs={{0,2},{1,3},{2,0},{3,1},{4,6},{5,7},{6,4},{7,5},{8,10},{9,11},{10,... | collective-permute-start | bytes 196616 | tf_op jit(solution)/shard_map/ppermute | solution.py:339
  35.1 2.7 %collective-permute-done.13.refs_1_ = bf16[128,256]{1,0:T(8,128)(2,1)S(1)} collective-permute-done((bf16[128,256]{1,0:T(8,128)(2,1)S(1)}, bf16[128,256]{1,0:T(8,128)(2,1)S(1)}, u32[]{:S(2)}, u32[]{:S(2)}) %collective-permute-start.13) | collective-permute-done | bytes 65568 | tf_op jit(solution)/shard_map/ppermute | solution.py:339
  38.0 1.2 %collective-permute-done.14.grad_came = bf16[128,128]{1,0:T(8,128)(2,1)S(1)} collective-permute-done((bf16[128,128]{1,0:T(8,128)(2,1)S(1)}, bf16[128,128]{1,0:T(8,128)(2,1)S(1)}, u32[]{:S(2)}, u32[]{:S(2)}) %collective-permute-start.14) | collective-permute-done | bytes 32800 | tf_op jit(solution)/shard_map/ppermute | solution.py:339
  39.2 0.7 %shard_map.166 = (bf16[256,128]{1,0:T(8,128)(2,1)}, bf16[256,128]{1,0:T(8,128)(2,1)}) custom-call(bf16[128,128]{1,0:T(8,128)(2,1)S(1)} %get-tuple-element.37.next_mine, bf16[128,128]{1,0:T(8,128)(2,1)S(1)} %collective-permute-done.8.next_came, bf16[128,128]{1,0:T(8,128)(2,1)S(1)} %get-tuple-element.50.grad_mine, ...), custom_call_target="tpu_custom_call" | custom-call | flops 16777216 | bytes 131072 | tf_op jit(solution)/shard_map/pallas_call | solution.py:73
  39.9 0.6 %shard_map.167 = bf16[16,128]{1,0:T(8,128)(2,1)} custom-call(bf16[16,16,128]{2,1,0:T(8,128)(2,1)S(1)} %all-to-all-done.1.shares, bf16[16,128]{1,0:T(8,128)(2,1)S(1)} %copy-done.6), custom_call_target="tpu_custom_call" | custom-call | flops 16777216 | bytes 69632 | tf_op jit(solution)/shard_map/pallas_call | solution.py:73
  (51 shorter events, 2.4 us)
Async XLA Ops:
  0.7 15.7 %collective-permute-start.2 = (bf16[128,1536]{1,0:T(8,128)(2,1)}, bf16[128,1536]{1,0:T(8,128)(2,1)S(1)}, u32[]{:S(2)}, u32[]{:S(2)}) collective-permute-start(bf16[128,1536]{1,0:T(8,128)(2,1)} %e_mine.1), channel_id=1, source_target_pairs={{0,1},{1,0},{2,3},{3,2},{4,5},{5,4},{6,7},{7,6},{8,9},{9,8},{10,11... | collective-permute-start | bytes 1179656 | tf_op jit(solution)/shard_map/ppermute | solution.py:339
  1.6 3.1 %copy-start.1 = (bf16[128,1024]{1,0:T(8,128)(2,1)S(1)}, bf16[128,1024]{1,0:T(8,128)(2,1)}, u32[]{:S(2)}) copy-start(bf16[128,1024]{1,0:T(8,128)(2,1)} %refs_16_.1) | copy-start | bytes 786436
  1.6 3.1 %copy-start.4 = (bf16[256,128]{1,0:T(8,128)(2,1)S(1)}, bf16[256,128]{1,0:T(8,128)(2,1)}, u32[]{:S(2)}) copy-start(bf16[256,128]{1,0:T(8,128)(2,1)} %refs_0_.3) | copy-start | bytes 196612
  1.6 3.9 %copy-start.2 = (bf16[128,512]{1,0:T(8,128)(2,1)S(1)}, bf16[128,512]{1,0:T(8,128)(2,1)}, u32[]{:S(2)}) copy-start(bf16[128,512]{1,0:T(8,128)(2,1)} %refs_14_.1) | copy-start | bytes 393220
  1.6 11.7 %copy-start.5 = (bf16[256,128]{1,0:T(8,128)(2,1)S(1)}, bf16[256,128]{1,0:T(8,128)(2,1)}, u32[]{:S(2)}) copy-start(bf16[256,128]{1,0:T(8,128)(2,1)} %edge_cot.1) | copy-start | bytes 196612
  1.6 14.7 %copy-start = (bf16[128,1536]{1,0:T(8,128)(2,1)S(1)}, bf16[128,1536]{1,0:T(8,128)(2,1)}, u32[]{:S(2)}) copy-start(bf16[128,1536]{1,0:T(8,128)(2,1)} %e_mine.1) | copy-start | bytes 1179652
  1.7 11.0 %collective-permute-start.9 = (bf16[128,1024]{1,0:T(8,128)(2,1)S(1)}, bf16[128,1024]{1,0:T(8,128)(2,1)S(1)}, u32[]{:S(2)}, u32[]{:S(2)}) collective-permute-start(bf16[128,1024]{1,0:T(8,128)(2,1)S(1)} %pad_maximum_fusion), channel_id=1, source_target_pairs={{0,2},{1,3},{2,0},{3,1},{4,6},{5,7},{6,4},{7,5},{8,10},{9,11},{10,... | collective-permute-start | bytes 786440 | tf_op jit(solution)/shard_map/ppermute | solution.py:339
  4.7 14.9 %collective-permute-start.4 = (bf16[128,1024]{1,0:T(8,128)(2,1)S(1)}, bf16[128,1024]{1,0:T(8,128)(2,1)S(1)}, u32[]{:S(2)}, u32[]{:S(2)}) collective-permute-start(bf16[128,1024]{1,0:T(8,128)(2,1)S(1)} %copy-done.1), channel_id=1, source_target_pairs={{0,1},{1,0},{2,3},{3,2},{4,5},{5,4},{6,7},{7,6},{8,9},{9,8},{10,11... | collective-permute-start | bytes 786440 | tf_op jit(solution)/shard_map/ppermute | solution.py:339
  4.7 8.5 %collective-permute-start = (bf16[256,128]{1,0:T(8,128)(2,1)S(1)}, bf16[256,128]{1,0:T(8,128)(2,1)S(1)}, u32[]{:S(2)}, u32[]{:S(2)}) collective-permute-start(bf16[256,128]{1,0:T(8,128)(2,1)S(1)} %copy-done.4), channel_id=1, source_target_pairs={{0,2},{1,3},{2,0},{3,1},{4,6},{5,7},{6,4},{7,5},{8,10},{9,11},{10,... | collective-permute-start | bytes 196616 | tf_op jit(solution)/shard_map/ppermute | solution.py:339
  5.5 14.1 %collective-permute-start.3 = (bf16[128,512]{1,0:T(8,128)(2,1)S(1)}, bf16[128,512]{1,0:T(8,128)(2,1)S(1)}, u32[]{:S(2)}, u32[]{:S(2)}) collective-permute-start(bf16[128,512]{1,0:T(8,128)(2,1)S(1)} %copy-done.2), channel_id=1, source_target_pairs={{0,1},{1,0},{2,3},{3,2},{4,5},{5,4},{6,7},{7,6},{8,9},{9,8},{10,11... | collective-permute-start | bytes 393224 | tf_op jit(solution)/shard_map/ppermute | solution.py:339
  7.1 12.5 %all-to-all-start = ((bf16[16,16,128]{2,1,0:T(8,128)(2,1)}), bf16[16,16,128]{2,1,0:T(8,128)(2,1)S(1)}, u32[]{:S(2)}, u32[]{:S(2)}) async-start(bf16[16,16,128]{2,1,0:T(8,128)(2,1)} %shard_map.156), calls=%async_computation | async-start | bytes 131072 | tf_op jit(solution)/shard_map/all_to_all | solution.py:352
  12.7 13.1 %collective-permute-start.10 = (bf16[128,1024]{1,0:T(8,128)(2,1)S(1)}, bf16[128,1024]{1,0:T(8,128)(2,1)S(1)}, u32[]{:S(2)}, u32[]{:S(2)}) collective-permute-start(bf16[128,1024]{1,0:T(8,128)(2,1)S(1)} %collective-permute-done.9.refs_0_), channel_id=1, source_target_pairs={{0,1},{1,0},{2,3},{3,2},{4,5},{5,4},{6,7},{7,6},{8,9},{9,8},{10,11... | collective-permute-start | bytes 786440 | tf_op jit(solution)/shard_map/ppermute | solution.py:339
  13.2 1.3 %collective-permute-start.1 = (bf16[128,256]{1,0:T(8,128)(2,1)S(1)}, bf16[128,256]{1,0:T(8,128)(2,1)S(1)}, u32[]{:S(2)}, u32[]{:S(2)}) collective-permute-start(bf16[128,256]{1,0:T(8,128)(2,1)S(1)} %shard_map.157), channel_id=1, source_target_pairs={{0,1},{1,0},{2,3},{3,2},{4,5},{5,4},{6,7},{7,6},{8,9},{9,8},{10,11... | collective-permute-start | bytes 196616 | tf_op jit(solution)/shard_map/ppermute | solution.py:339
  14.0 2.3 %copy-start.7 = (s32[4,4,8]{2,1,0:T(4,128)S(1)}, s32[4,4,8]{2,1,0:T(4,128)}, u32[]{:S(2)}) copy-start(s32[4,4,8]{2,1,0:T(4,128)} %refs_7_.1) | copy-start | bytes 1540
  14.0 2.3 %copy-start.10 = (s32[256]{0:T(256)S(1)}, s32[256]{0:T(256)}, u32[]{:S(2)}) copy-start(s32[256]{0:T(256)} %param.17) | copy-start | bytes 3076
  14.5 5.9 %collective-permute-start.6 = (bf16[288,128]{1,0:T(8,128)(2,1)S(1)}, bf16[288,128]{1,0:T(8,128)(2,1)S(1)}, u32[]{:S(2)}, u32[]{:S(2)}) collective-permute-start(bf16[288,128]{1,0:T(8,128)(2,1)S(1)} %shard_map.160.refs_0_.refs_3_), channel_id=1, source_target_pairs={{0,2},{1,3},{2,0},{3,1},{4,6},{5,7},{6,4},{7,5},{8,10},{9,11},{10,... | collective-permute-start | bytes 221192 | tf_op jit(solution)/shard_map/ppermute | solution.py:339
  20.2 5.3 %collective-permute-start.5 = (bf16[144,512]{1,0:T(8,128)(2,1)S(1)}, bf16[144,512]{1,0:T(8,128)(2,1)S(1)}, u32[]{:S(2)}, u32[]{:S(2)}) collective-permute-start(bf16[144,512]{1,0:T(8,128)(2,1)S(1)} %get-tuple-element.35), channel_id=1, source_target_pairs={{0,2},{1,3},{2,0},{3,1},{4,6},{5,7},{6,4},{7,5},{8,10},{9,11},{10,... | collective-permute-start | bytes 442376 | tf_op jit(solution)/shard_map/ppermute | solution.py:339
  20.4 5.5 %collective-permute-start.12 = (bf16[128,512]{1,0:T(8,128)(2,1)S(1)}, bf16[128,512]{1,0:T(8,128)(2,1)S(1)}, u32[]{:S(2)}, u32[]{:S(2)}) collective-permute-start(bf16[128,512]{1,0:T(8,128)(2,1)S(1)} %copy-done.3), channel_id=1, source_target_pairs={{0,1},{1,0},{2,3},{3,2},{4,5},{5,4},{6,7},{7,6},{8,9},{9,8},{10,11... | collective-permute-start | bytes 393224 | tf_op jit(solution)/shard_map/ppermute | solution.py:339
  20.4 1.5 %collective-permute-start.7 = (bf16[160,256]{1,0:T(8,128)(2,1)S(1)}, bf16[160,256]{1,0:T(8,128)(2,1)S(1)}, u32[]{:S(2)}, u32[]{:S(2)}) collective-permute-start(bf16[160,256]{1,0:T(8,128)(2,1)S(1)} %shard_map.161), channel_id=1, source_target_pairs={{0,1},{1,0},{2,3},{3,2},{4,5},{5,4},{6,7},{7,6},{8,9},{9,8},{10,11... | collective-permute-start | bytes 245768 | tf_op jit(solution)/shard_map/ppermute | solution.py:339
  25.8 1.2 %collective-permute-start.11 = (f32[16,512]{1,0:T(8,128)S(1)}, f32[16,512]{1,0:T(8,128)S(1)}, u32[]{:S(2)}, u32[]{:S(2)}) collective-permute-start(f32[16,512]{1,0:T(8,128)S(1)} %get-tuple-element.39.refs_2_), channel_id=1, source_target_pairs={{0,1},{1,0},{2,3},{3,2},{4,5},{5,4},{6,7},{7,6},{8,9},{9,8},{10,11... | collective-permute-start | bytes 98312 | tf_op jit(solution)/shard_map/ppermute | solution.py:339
  29.5 10.4 %all-to-all-start.1 = ((bf16[16,16,128]{2,1,0:T(8,128)(2,1)}), bf16[16,16,128]{2,1,0:T(8,128)(2,1)S(1)}, u32[]{:S(2)}, u32[]{:S(2)}) async-start(bf16[16,16,128]{2,1,0:T(8,128)(2,1)} %get-tuple-element.55), calls=%async_computation.1 | async-start | bytes 131072 | tf_op jit(solution)/shard_map/all_to_all | solution.py:420
  33.2 4.6 %collective-permute-start.13 = (bf16[128,256]{1,0:T(8,128)(2,1)S(1)}, bf16[128,256]{1,0:T(8,128)(2,1)S(1)}, u32[]{:S(2)}, u32[]{:S(2)}) collective-permute-start(bf16[128,256]{1,0:T(8,128)(2,1)S(1)} %get-tuple-element.49), channel_id=1, source_target_pairs={{0,2},{1,3},{2,0},{3,1},{4,6},{5,7},{6,4},{7,5},{8,10},{9,11},{10,... | collective-permute-start | bytes 196616 | tf_op jit(solution)/shard_map/ppermute | solution.py:339
  35.1 2.8 %collective-permute-start.8 = (bf16[128,128]{1,0:T(8,128)(2,1)S(1)}, bf16[128,128]{1,0:T(8,128)(2,1)S(1)}, u32[]{:S(2)}, u32[]{:S(2)}) collective-permute-start(bf16[128,128]{1,0:T(8,128)(2,1)S(1)} %get-tuple-element.38), channel_id=1, source_target_pairs={{0,1},{1,0},{2,3},{3,2},{4,5},{5,4},{6,7},{7,6},{8,9},{9,8},{10,11... | collective-permute-start | bytes 98312 | tf_op jit(solution)/shard_map/ppermute | solution.py:339
  37.9 1.3 %collective-permute-start.14 = (bf16[128,128]{1,0:T(8,128)(2,1)S(1)}, bf16[128,128]{1,0:T(8,128)(2,1)S(1)}, u32[]{:S(2)}, u32[]{:S(2)}) collective-permute-start(bf16[128,128]{1,0:T(8,128)(2,1)S(1)} %get-tuple-element.51), channel_id=1, source_target_pairs={{0,1},{1,0},{2,3},{3,2},{4,5},{5,4},{6,7},{7,6},{8,9},{9,8},{10,11... | collective-permute-start | bytes 98312 | tf_op jit(solution)/shard_map/ppermute | solution.py:339
  (7 other events, 5.2 us)

commit v14 on v13

--- a/solution.py
+++ b/solution.py
@@ -96,8 +96,9 @@
     return value
 
 
-def spread_latent(latent, spread):
-    spread[...] = jnp.broadcast_to(latent[...][None], spread.shape)
+def spread_latent(block, spread):
+    _, nodes, width = spread.shape
+    spread[...] = jnp.broadcast_to(block[:nodes, block.shape[1] - width :][None], spread.shape)
 
 
 def pack_extra(edge_cot, node_cot, gain_e, gain_n, pack):
@@ -229,7 +230,7 @@
     from_agg = jnp.concatenate(
         [in_mine[:, features:], in_other[:, features:]] + [f[:, :features] for f in far], axis=0
     )
-    to_out = jnp.concatenate([n_mine[...], n_other[...]] + [f[:, features:] for f in far], axis=0)
+    to_out = jnp.concatenate([n_mine[...], n_other[...]] + [f[:, features : 2 * features] for f in far], axis=0)
     together = (aggregate[...] + aggregate2[...]).astype(bf16)
     pre = lat_all[...] + dot_rows(together, from_agg)
     act = (pre * sigmoid(pre)).astype(bf16)
@@ -348,7 +349,11 @@
     slot_rows = sender_slot.reshape(cores, half)
     receiver_rows = receiver_row.reshape(cores, half)
 
-    (spread,) = stage(spread_latent, [((blocks * feats, nodes, width), bf16)], [latent])
+    hid = edge_in_weight.shape[0]
+    block = jnp.concatenate(
+        [node_in_weight[:, features:], node_out_weight, jnp.pad(latent, ((0, hid - nodes), (0, 0)))], axis=1
+    )
+    (spread,) = stage(spread_latent, [((blocks * feats, nodes, width), bf16)], [block])
     latents = lax.all_to_all(spread, everyone, 0, 0)
     states = [edge_state] + over_groups(edge_state)
     e_in = (edge_in_weight, over_cores(edge_in_weight))
@@ -356,7 +361,7 @@
     n_in = (node_in_weight, over_cores(node_in_weight))
     n_out = (node_out_weight, over_cores(node_out_weight))
     far = []
-    for weights in over_groups(jnp.concatenate([node_in_weight[:, features:], node_out_weight], axis=1)):
+    for weights in over_groups(block):
         far += [weights, over_cores(weights)]
     (sent,) = stage(functools.partial(send_half, groups), [((half, groups * width), bf16)], states)
     state, pre, pick, take = stage(

time: 40.9 us -> 41.9 us (1.024)
  other arithmetic: 0.02 us -> 0.97 us
    all_to_all x1, starting transfers between devices: 5.61 us -> 6.6 us  [shards(): latents = lax.all_to_all(spread, everyone, 0, 0)]
    concatenate x1, other arithmetic: 0.02 us -> 0.97 us  [shards(): jnp.concatenate([node_in_weight[:, features:], node_out_weight, jnp.pad(l...]
    ppermute x15, starting transfers between devices: 9.71 us -> 8.78 us  [swapped(): return lax.ppermute(values, 'feat', [(i, i ^ bits) for i in range(feats)])]
    unnamed x26, local copies, waits for them, and re-layouts: 2.11 us -> 1.5 us
    slice x2, local copies, waits for them, and re-layouts: 0.37 us -> 0.88 us  [shards(): node_in_weight[:, features:]]
where the time goes in v14:
time: 41.9 us; the launch traced here: 41.5 us
  starting transfers between devices  19 us (45%)
  waiting for transfers between devices  11.9 us (28%)
  Pallas kernels  6.45 us (15%)
  local copies, waits for them, and re-layouts  2.37 us (6%)
  other arithmetic  0.97 us (2%)
  between operations  0.79 us (2%)
    ppermute x15, waiting for transfers between devices, swapped(): return lax.ppermute(values, 'feat', [(i, i ^ bits) for i in range(feats)])  10.3 us
    ppermute x15, starting transfers between devices, swapped(): return lax.ppermute(values, 'feat', [(i, i ^ bits) for i in range(feats)])  8.78 us
    all_to_all x1, starting transfers between devices, shards(): latents = lax.all_to_all(spread, everyone, 0, 0)  6.6 us
    pallas_call x12, Pallas kernels, stage(): pl.pallas_call(kernel, out_shape=[jax.ShapeDtypeStruct(shape, kind) for s...  6.45 us
    all_to_all x1, starting transfers between devices, shards(): shares = lax.all_to_all(spread, everyone, 0, 0)  3.65 us
    all_to_all x1, waiting for transfers between devices, shards(): latents = lax.all_to_all(spread, everyone, 0, 0)  1.63 us
    unnamed x26, local copies, waits for them, and re-layouts  1.5 us
    concatenate x1, other arithmetic, shards(): jnp.concatenate([node_in_weight[:, features:], node_out_weight, jnp.pad(l...  0.97 us
  transfers between devices with their start and end apart: 17, of which 8 were waited for; matrix products, arithmetic and copies ran while one was open for 0% of the time, Pallas kernels for 8%

profile of v14, /device:TPU:0, one launch (start us, length us, event | category | flops | bytes accessed | tf_op | source)
XLA Modules:
  0.0 41.5 jit_solution(6775917243477003181)
XLA Ops:
  0.7 0.9 %slice-done = bf16[128,512]{1,0:T(8,128)(2,1)S(1)} async-done(((bf16[128,1024]{1,0:T(8,128)(2,1)}), bf16[128,512]{1,0:T(8,128)(2,1)S(1)}, s32[]{:S(2)}) %slice-start) | async-done | bytes 131096 | tf_op jit(solution)/shard_map/slice | solution.py:354
  1.5 1.0 %fusion.1.block = bf16[128,1152]{1,0:T(8,128)(2,1)S(1)} fusion(bf16[16,128]{1,0:T(8,128)(2,1)S(1)} %copy-done.12, bf16[128,512]{1,0:T(8,128)(2,1)} %refs_18_.1, bf16[128,512]{1,0:T(8,128)(2,1)S(1)} %slice-done), kind=kLoop, calls=%fused_computation.2 | loop fusion | flops 1179648 | bytes 561152 | tf_op jit(solution)/shard_map/concatenate | solution.py:353
  2.5 3.0 %collective-permute-start.9 = (bf16[128,1152]{1,0:T(8,128)(2,1)S(1)}, bf16[128,1152]{1,0:T(8,128)(2,1)S(1)}, u32[]{:S(2)}, u32[]{:S(2)}) collective-permute-start(bf16[128,1152]{1,0:T(8,128)(2,1)S(1)} %fusion.1.block), channel_id=1, source_target_pairs={{0,2},{1,3},{2,0},{3,1},{4,6},{5,7},{6,4},{7,5},{8,10},{9,11},{10,... | collective-permute-start | bytes 884744 | tf_op jit(solution)/shard_map/ppermute | solution.py:340
  5.5 0.5 %collective-permute-start.4 = (bf16[128,1024]{1,0:T(8,128)(2,1)S(1)}, bf16[128,1024]{1,0:T(8,128)(2,1)S(1)}, u32[]{:S(2)}, u32[]{:S(2)}) collective-permute-start(bf16[128,1024]{1,0:T(8,128)(2,1)S(1)} %copy-done.1), channel_id=1, source_target_pairs={{0,1},{1,0},{2,3},{3,2},{4,5},{5,4},{6,7},{7,6},{8,9},{9,8},{10,11... | collective-permute-start | bytes 786440 | tf_op jit(solution)/shard_map/ppermute | solution.py:340
  6.1 0.6 %shard_map.156 = bf16[16,16,128]{2,1,0:T(8,128)(2,1)} custom-call(bf16[128,1152]{1,0:T(8,128)(2,1)S(1)} %fusion.1.block), custom_call_target="tpu_custom_call" | custom-call | flops 16777216 | bytes 294912 | tf_op jit(solution)/shard_map/pallas_call | solution.py:73
  6.8 6.6 %all-to-all-start = ((bf16[16,16,128]{2,1,0:T(8,128)(2,1)}), bf16[16,16,128]{2,1,0:T(8,128)(2,1)S(1)}, u32[]{:S(2)}, u32[]{:S(2)}) async-start(bf16[16,16,128]{2,1,0:T(8,128)(2,1)} %shard_map.156), calls=%async_computation | async-start | bytes 131072 | tf_op jit(solution)/shard_map/all_to_all | solution.py:357
  13.4 0.5 %collective-permute-start.10 = (bf16[128,1152]{1,0:T(8,128)(2,1)S(1)}, bf16[128,1152]{1,0:T(8,128)(2,1)S(1)}, u32[]{:S(2)}, u32[]{:S(2)}) collective-permute-start(bf16[128,1152]{1,0:T(8,128)(2,1)S(1)} %collective-permute-done.9.refs_0_), channel_id=1, source_target_pairs={{0,1},{1,0},{2,3},{3,2},{4,5},{5,4},{6,7},{7,6},{8,9},{9,8},{10,11... | collective-permute-start | bytes 884744 | tf_op jit(solution)/shard_map/ppermute | solution.py:340
  14.8 0.5 %collective-permute-done.1.refs_2_ = bf16[128,256]{1,0:T(8,128)(2,1)S(1)} collective-permute-done((bf16[128,256]{1,0:T(8,128)(2,1)S(1)}, bf16[128,256]{1,0:T(8,128)(2,1)S(1)}, u32[]{:S(2)}, u32[]{:S(2)}) %collective-permute-start.1) | collective-permute-done | bytes 65568 | tf_op jit(solution)/shard_map/ppermute | solution.py:340
  15.3 1.8 %collective-permute-start.6 = (bf16[288,128]{1,0:T(8,128)(2,1)S(1)}, bf16[288,128]{1,0:T(8,128)(2,1)S(1)}, u32[]{:S(2)}, u32[]{:S(2)}) collective-permute-start(bf16[288,128]{1,0:T(8,128)(2,1)S(1)} %shard_map.160.refs_0_.refs_3_), channel_id=1, source_target_pairs={{0,2},{1,3},{2,0},{3,1},{4,6},{5,7},{6,4},{7,5},{8,10},{9,11},{10,... | collective-permute-start | bytes 221192 | tf_op jit(solution)/shard_map/ppermute | solution.py:340
  17.1 0.7 %copy-done.8 = s32[256]{0:T(256)S(1)} copy-done((s32[256]{0:T(256)S(1)}, s32[256]{0:T(256)}, u32[]{:S(2)}) %copy-start.8) | copy-done | bytes 1048
  17.7 0.9 %shard_map.158 = (bf16[128,512]{1,0:T(8,128)(2,1)S(1)}, f32[128,256]{1,0:T(8,128)S(1)}, bf16[64,128]{1,0:T(8,128)(2,1)S(1)}, bf16[16,128]{1,0:T(8,128)(2,1)S(1)}) custom-call(bf16[256,128]{1,0:T(8,128)(2,1)S(1)} %copy-done.4, bf16[256,128]{1,0:T(8,128)(2,1)S(1)} %collective-permute-done.refs_1_, bf16[128,256]{1,0:T(8,128)(2,1)S(1)} %collective-permute-done.1.refs_2_, ...), custom_call_target="tpu_custom_call" | custom-call | flops 16777216 | bytes 985600 | tf_op jit(solution)/shard_map/pallas_call | solution.py:73
  18.6 1.6 %all-to-all-done.came = bf16[16,16,128]{2,1,0:T(8,128)(2,1)S(1)} async-done(((bf16[16,16,128]{2,1,0:T(8,128)(2,1)}), bf16[16,16,128]{2,1,0:T(8,128)(2,1)S(1)}, u32[]{:S(2)}, u32[]{:S(2)}) %all-to-all-start) | async-done | bytes 65568 | tf_op jit(solution)/shard_map/all_to_all | solution.py:357
  20.3 0.6 %shard_map.159 = (f32[128,256]{1,0:T(8,128)S(1)}, f32[128,512]{1,0:T(8,128)S(1)}, bf16[144,512]{1,0:T(8,128)(2,1)S(1)}, bf16[16,512]{1,0:T(8,128)(2,1)S(1)}, f32[16,256]{1,0:T(8,128)S(1)}) custom-call(bf16[16,16,128]{2,1,0:T(8,128)(2,1)S(1)} %all-to-all-done.came, f32[128,256]{1,0:T(8,128)S(1)} %get-tuple-element.30.pre, ...), custom_call_target="tpu_custom_call" | custom-call | flops 16777216 | bytes 1789952 | tf_op jit(solution)/shard_map/pallas_call | solution.py:73
  21.2 0.6 %collective-permute-start.7 = (bf16[160,256]{1,0:T(8,128)(2,1)S(1)}, bf16[160,256]{1,0:T(8,128)(2,1)S(1)}, u32[]{:S(2)}, u32[]{:S(2)}) collective-permute-start(bf16[160,256]{1,0:T(8,128)(2,1)S(1)} %shard_map.161), channel_id=1, source_target_pairs={{0,1},{1,0},{2,3},{3,2},{4,5},{5,4},{6,7},{7,6},{8,9},{9,8},{10,11... | collective-permute-start | bytes 245768 | tf_op jit(solution)/shard_map/ppermute | solution.py:340
  21.8 0.9 %collective-permute-done.7.refs_5_ = bf16[160,256]{1,0:T(8,128)(2,1)S(1)} collective-permute-done((bf16[160,256]{1,0:T(8,128)(2,1)S(1)}, bf16[160,256]{1,0:T(8,128)(2,1)S(1)}, u32[]{:S(2)}, u32[]{:S(2)}) %collective-permute-start.7) | collective-permute-done | bytes 81952 | tf_op jit(solution)/shard_map/ppermute | solution.py:340
  22.7 3.6 %collective-permute-done.5.refs_2_ = bf16[144,512]{1,0:T(8,128)(2,1)S(1)} collective-permute-done((bf16[144,512]{1,0:T(8,128)(2,1)S(1)}, bf16[144,512]{1,0:T(8,128)(2,1)S(1)}, u32[]{:S(2)}, u32[]{:S(2)}) %collective-permute-start.5) | collective-permute-done | bytes 147488 | tf_op jit(solution)/shard_map/ppermute | solution.py:340
  26.5 1.2 %collective-permute-done.11.refs_3_ = f32[16,512]{1,0:T(8,128)S(1)} collective-permute-done((f32[16,512]{1,0:T(8,128)S(1)}, f32[16,512]{1,0:T(8,128)S(1)}, u32[]{:S(2)}, u32[]{:S(2)}) %collective-permute-start.11) | collective-permute-done | bytes 32800 | tf_op jit(solution)/shard_map/ppermute | solution.py:340
  27.8 2.5 %shard_map.163 = (bf16[16,128]{1,0:T(8,128)(2,1)}, bf16[128,256]{1,0:T(8,128)(2,1)S(1)}, f32[128,512]{1,0:T(8,128)S(1)}, bf16[16,16,128]{2,1,0:T(8,128)(2,1)}) custom-call(bf16[128,1152]{1,0:T(8,128)(2,1)S(1)} %collective-permute-done.9.refs_0_, bf16[128,1152]{1,0:T(8,128)(2,1)S(1)} %collective-permute-done.10.refs_1_, ...), custom_call_target="tpu_custom_call" | custom-call | flops 16777216 | bytes 3117568 | tf_op jit(solution)/shard_map/pallas_call | solution.py:73
  30.2 3.7 %all-to-all-start.1 = ((bf16[16,16,128]{2,1,0:T(8,128)(2,1)}), bf16[16,16,128]{2,1,0:T(8,128)(2,1)S(1)}, u32[]{:S(2)}, u32[]{:S(2)}) async-start(bf16[16,16,128]{2,1,0:T(8,128)(2,1)} %get-tuple-element.55), calls=%async_computation.1 | async-start | bytes 131072 | tf_op jit(solution)/shard_map/all_to_all | solution.py:425
  34.1 2.0 %collective-permute-start.13 = (bf16[128,256]{1,0:T(8,128)(2,1)S(1)}, bf16[128,256]{1,0:T(8,128)(2,1)S(1)}, u32[]{:S(2)}, u32[]{:S(2)}) collective-permute-start(bf16[128,256]{1,0:T(8,128)(2,1)S(1)} %get-tuple-element.49), channel_id=1, source_target_pairs={{0,2},{1,3},{2,0},{3,1},{4,6},{5,7},{6,4},{7,5},{8,10},{9,11},{10,... | collective-permute-start | bytes 196616 | tf_op jit(solution)/shard_map/ppermute | solution.py:340
  36.1 2.8 %collective-permute-done.13.refs_1_ = bf16[128,256]{1,0:T(8,128)(2,1)S(1)} collective-permute-done((bf16[128,256]{1,0:T(8,128)(2,1)S(1)}, bf16[128,256]{1,0:T(8,128)(2,1)S(1)}, u32[]{:S(2)}, u32[]{:S(2)}) %collective-permute-start.13) | collective-permute-done | bytes 65568 | tf_op jit(solution)/shard_map/ppermute | solution.py:340
  39.0 1.2 %collective-permute-done.14.grad_came = bf16[128,128]{1,0:T(8,128)(2,1)S(1)} collective-permute-done((bf16[128,128]{1,0:T(8,128)(2,1)S(1)}, bf16[128,128]{1,0:T(8,128)(2,1)S(1)}, u32[]{:S(2)}, u32[]{:S(2)}) %collective-permute-start.14) | collective-permute-done | bytes 32800 | tf_op jit(solution)/shard_map/ppermute | solution.py:340
  40.2 0.7 %shard_map.166 = (bf16[256,128]{1,0:T(8,128)(2,1)}, bf16[256,128]{1,0:T(8,128)(2,1)}) custom-call(bf16[128,128]{1,0:T(8,128)(2,1)S(1)} %get-tuple-element.37.next_mine, bf16[128,128]{1,0:T(8,128)(2,1)S(1)} %collective-permute-done.8.next_came, bf16[128,128]{1,0:T(8,128)(2,1)S(1)} %get-tuple-element.50.grad_mine, ...), custom_call_target="tpu_custom_call" | custom-call | flops 16777216 | bytes 131072 | tf_op jit(solution)/shard_map/pallas_call | solution.py:73
  40.9 0.6 %shard_map.167 = bf16[16,128]{1,0:T(8,128)(2,1)} custom-call(bf16[16,16,128]{2,1,0:T(8,128)(2,1)S(1)} %all-to-all-done.1.shares, bf16[16,128]{1,0:T(8,128)(2,1)S(1)} %copy-done.6), custom_call_target="tpu_custom_call" | custom-call | flops 16777216 | bytes 69632 | tf_op jit(solution)/shard_map/pallas_call | solution.py:73
  (51 shorter events, 1.9 us)
Async XLA Ops:
  0.7 4.9 %copy-start = (bf16[128,1536]{1,0:T(8,128)(2,1)S(1)}, bf16[128,1536]{1,0:T(8,128)(2,1)}, u32[]{:S(2)}) copy-start(bf16[128,1536]{1,0:T(8,128)(2,1)} %e_mine.1) | copy-start | bytes 1179652
  1.5 4.0 %copy-start.1 = (bf16[128,1024]{1,0:T(8,128)(2,1)S(1)}, bf16[128,1024]{1,0:T(8,128)(2,1)}, u32[]{:S(2)}) copy-start(bf16[128,1024]{1,0:T(8,128)(2,1)} %refs_16_.1) | copy-start | bytes 786436
  2.5 10.9 %collective-permute-start.9 = (bf16[128,1152]{1,0:T(8,128)(2,1)S(1)}, bf16[128,1152]{1,0:T(8,128)(2,1)S(1)}, u32[]{:S(2)}, u32[]{:S(2)}) collective-permute-start(bf16[128,1152]{1,0:T(8,128)(2,1)S(1)} %fusion.1.block), channel_id=1, source_target_pairs={{0,2},{1,3},{2,0},{3,1},{4,6},{5,7},{6,4},{7,5},{8,10},{9,11},{10,... | collective-permute-start | bytes 884744 | tf_op jit(solution)/shard_map/ppermute | solution.py:340
  5.5 11.5 %collective-permute-start.2 = (bf16[128,1536]{1,0:T(8,128)(2,1)S(1)}, bf16[128,1536]{1,0:T(8,128)(2,1)S(1)}, u32[]{:S(2)}, u32[]{:S(2)}) collective-permute-start(bf16[128,1536]{1,0:T(8,128)(2,1)S(1)} %copy-done), channel_id=1, source_target_pairs={{0,1},{1,0},{2,3},{3,2},{4,5},{5,4},{6,7},{7,6},{8,9},{9,8},{10,11... | collective-permute-start | bytes 1179656 | tf_op jit(solution)/shard_map/ppermute | solution.py:340
  5.5 14.7 %collective-permute-start.4 = (bf16[128,1024]{1,0:T(8,128)(2,1)S(1)}, bf16[128,1024]{1,0:T(8,128)(2,1)S(1)}, u32[]{:S(2)}, u32[]{:S(2)}) collective-permute-start(bf16[128,1024]{1,0:T(8,128)(2,1)S(1)} %copy-done.1), channel_id=1, source_target_pairs={{0,1},{1,0},{2,3},{3,2},{4,5},{5,4},{6,7},{7,6},{8,9},{9,8},{10,11... | collective-permute-start | bytes 786440 | tf_op jit(solution)/shard_map/ppermute | solution.py:340
  6.0 7.9 %collective-permute-start = (bf16[256,128]{1,0:T(8,128)(2,1)}, bf16[256,128]{1,0:T(8,128)(2,1)S(1)}, u32[]{:S(2)}, u32[]{:S(2)}) collective-permute-start(bf16[256,128]{1,0:T(8,128)(2,1)} %refs_0_.3), channel_id=1, source_target_pairs={{0,2},{1,3},{2,0},{3,1},{4,6},{5,7},{6,4},{7,5},{8,10},{9,11},{10,... | collective-permute-start | bytes 196616 | tf_op jit(solution)/shard_map/ppermute | solution.py:340
  6.1 14.2 %collective-permute-start.3 = (bf16[128,512]{1,0:T(8,128)(2,1)}, bf16[128,512]{1,0:T(8,128)(2,1)S(1)}, u32[]{:S(2)}, u32[]{:S(2)}) collective-permute-start(bf16[128,512]{1,0:T(8,128)(2,1)} %refs_14_.1), channel_id=1, source_target_pairs={{0,1},{1,0},{2,3},{3,2},{4,5},{5,4},{6,7},{7,6},{8,9},{9,8},{10,11... | collective-permute-start | bytes 393224 | tf_op jit(solution)/shard_map/ppermute | solution.py:340
  6.8 7.2 %copy-start.4 = (bf16[256,128]{1,0:T(8,128)(2,1)S(1)}, bf16[256,128]{1,0:T(8,128)(2,1)}, u32[]{:S(2)}) copy-start(bf16[256,128]{1,0:T(8,128)(2,1)} %refs_0_.3) | copy-start | bytes 196612
  6.8 13.5 %all-to-all-start = ((bf16[16,16,128]{2,1,0:T(8,128)(2,1)}), bf16[16,16,128]{2,1,0:T(8,128)(2,1)S(1)}, u32[]{:S(2)}, u32[]{:S(2)}) async-start(bf16[16,16,128]{2,1,0:T(8,128)(2,1)} %shard_map.156), calls=%async_computation | async-start | bytes 131072 | tf_op jit(solution)/shard_map/all_to_all | solution.py:357
  13.4 14.4 %collective-permute-start.10 = (bf16[128,1152]{1,0:T(8,128)(2,1)S(1)}, bf16[128,1152]{1,0:T(8,128)(2,1)S(1)}, u32[]{:S(2)}, u32[]{:S(2)}) collective-permute-start(bf16[128,1152]{1,0:T(8,128)(2,1)S(1)} %collective-permute-done.9.refs_0_), channel_id=1, source_target_pairs={{0,1},{1,0},{2,3},{3,2},{4,5},{5,4},{6,7},{7,6},{8,9},{9,8},{10,11... | collective-permute-start | bytes 884744 | tf_op jit(solution)/shard_map/ppermute | solution.py:340
  14.0 1.3 %collective-permute-start.1 = (bf16[128,256]{1,0:T(8,128)(2,1)S(1)}, bf16[128,256]{1,0:T(8,128)(2,1)S(1)}, u32[]{:S(2)}, u32[]{:S(2)}) collective-permute-start(bf16[128,256]{1,0:T(8,128)(2,1)S(1)} %shard_map.157), channel_id=1, source_target_pairs={{0,1},{1,0},{2,3},{3,2},{4,5},{5,4},{6,7},{7,6},{8,9},{9,8},{10,11... | collective-permute-start | bytes 196616 | tf_op jit(solution)/shard_map/ppermute | solution.py:340
  14.8 2.3 %copy-start.7 = (s32[4,4,8]{2,1,0:T(4,128)S(1)}, s32[4,4,8]{2,1,0:T(4,128)}, u32[]{:S(2)}) copy-start(s32[4,4,8]{2,1,0:T(4,128)} %refs_7_.1) | copy-start | bytes 1540
  14.8 2.3 %copy-start.9 = (s32[256]{0:T(256)S(1)}, s32[256]{0:T(256)}, u32[]{:S(2)}) copy-start(s32[256]{0:T(256)} %param.17) | copy-start | bytes 3076
  15.3 5.9 %collective-permute-start.6 = (bf16[288,128]{1,0:T(8,128)(2,1)S(1)}, bf16[288,128]{1,0:T(8,128)(2,1)S(1)}, u32[]{:S(2)}, u32[]{:S(2)}) collective-permute-start(bf16[288,128]{1,0:T(8,128)(2,1)S(1)} %shard_map.160.refs_0_.refs_3_), channel_id=1, source_target_pairs={{0,2},{1,3},{2,0},{3,1},{4,6},{5,7},{6,4},{7,5},{8,10},{9,11},{10,... | collective-permute-start | bytes 221192 | tf_op jit(solution)/shard_map/ppermute | solution.py:340
  17.7 2.5 %copy-start.3 = (bf16[128,512]{1,0:T(8,128)(2,1)S(1)}, bf16[128,512]{1,0:T(8,128)(2,1)}, u32[]{:S(2)}) copy-start(bf16[128,512]{1,0:T(8,128)(2,1)} %refs_14_.1) | copy-start | bytes 393220
  20.3 0.9 %copy-start.2 = (bf16[128,512]{1,0:T(8,128)(2,1)S(1)}, bf16[128,512]{1,0:T(8,128)(2,1)}, u32[]{:S(2)}) copy-start(bf16[128,512]{1,0:T(8,128)(2,1)} %refs_18_.1) | copy-start | bytes 393220
  20.9 5.3 %collective-permute-start.5 = (bf16[144,512]{1,0:T(8,128)(2,1)S(1)}, bf16[144,512]{1,0:T(8,128)(2,1)S(1)}, u32[]{:S(2)}, u32[]{:S(2)}) collective-permute-start(bf16[144,512]{1,0:T(8,128)(2,1)S(1)} %get-tuple-element.35), channel_id=1, source_target_pairs={{0,2},{1,3},{2,0},{3,1},{4,6},{5,7},{6,4},{7,5},{8,10},{9,11},{10,... | collective-permute-start | bytes 442376 | tf_op jit(solution)/shard_map/ppermute | solution.py:340
  21.2 5.4 %collective-permute-start.12 = (bf16[128,512]{1,0:T(8,128)(2,1)S(1)}, bf16[128,512]{1,0:T(8,128)(2,1)S(1)}, u32[]{:S(2)}, u32[]{:S(2)}) collective-permute-start(bf16[128,512]{1,0:T(8,128)(2,1)S(1)} %copy-done.2), channel_id=1, source_target_pairs={{0,1},{1,0},{2,3},{3,2},{4,5},{5,4},{6,7},{7,6},{8,9},{9,8},{10,11... | collective-permute-start | bytes 393224 | tf_op jit(solution)/shard_map/ppermute | solution.py:340
  21.2 1.5 %collective-permute-start.7 = (bf16[160,256]{1,0:T(8,128)(2,1)S(1)}, bf16[160,256]{1,0:T(8,128)(2,1)S(1)}, u32[]{:S(2)}, u32[]{:S(2)}) collective-permute-start(bf16[160,256]{1,0:T(8,128)(2,1)S(1)} %shard_map.161), channel_id=1, source_target_pairs={{0,1},{1,0},{2,3},{3,2},{4,5},{5,4},{6,7},{7,6},{8,9},{9,8},{10,11... | collective-permute-start | bytes 245768 | tf_op jit(solution)/shard_map/ppermute | solution.py:340
  26.5 1.2 %collective-permute-start.11 = (f32[16,512]{1,0:T(8,128)S(1)}, f32[16,512]{1,0:T(8,128)S(1)}, u32[]{:S(2)}, u32[]{:S(2)}) collective-permute-start(f32[16,512]{1,0:T(8,128)S(1)} %get-tuple-element.39.refs_2_), channel_id=1, source_target_pairs={{0,1},{1,0},{2,3},{3,2},{4,5},{5,4},{6,7},{7,6},{8,9},{9,8},{10,11... | collective-permute-start | bytes 98312 | tf_op jit(solution)/shard_map/ppermute | solution.py:340
  30.2 10.6 %all-to-all-start.1 = ((bf16[16,16,128]{2,1,0:T(8,128)(2,1)}), bf16[16,16,128]{2,1,0:T(8,128)(2,1)S(1)}, u32[]{:S(2)}, u32[]{:S(2)}) async-start(bf16[16,16,128]{2,1,0:T(8,128)(2,1)} %get-tuple-element.55), calls=%async_computation.1 | async-start | bytes 131072 | tf_op jit(solution)/shard_map/all_to_all | solution.py:425
  34.1 4.8 %collective-permute-start.13 = (bf16[128,256]{1,0:T(8,128)(2,1)S(1)}, bf16[128,256]{1,0:T(8,128)(2,1)S(1)}, u32[]{:S(2)}, u32[]{:S(2)}) collective-permute-start(bf16[128,256]{1,0:T(8,128)(2,1)S(1)} %get-tuple-element.49), channel_id=1, source_target_pairs={{0,2},{1,3},{2,0},{3,1},{4,6},{5,7},{6,4},{7,5},{8,10},{9,11},{10,... | collective-permute-start | bytes 196616 | tf_op jit(solution)/shard_map/ppermute | solution.py:340
  36.1 2.9 %collective-permute-start.8 = (bf16[128,128]{1,0:T(8,128)(2,1)S(1)}, bf16[128,128]{1,0:T(8,128)(2,1)S(1)}, u32[]{:S(2)}, u32[]{:S(2)}) collective-permute-start(bf16[128,128]{1,0:T(8,128)(2,1)S(1)} %get-tuple-element.38), channel_id=1, source_target_pairs={{0,1},{1,0},{2,3},{3,2},{4,5},{5,4},{6,7},{7,6},{8,9},{9,8},{10,11... | collective-permute-start | bytes 98312 | tf_op jit(solution)/shard_map/ppermute | solution.py:340
  38.9 1.3 %collective-permute-start.14 = (bf16[128,128]{1,0:T(8,128)(2,1)S(1)}, bf16[128,128]{1,0:T(8,128)(2,1)S(1)}, u32[]{:S(2)}, u32[]{:S(2)}) collective-permute-start(bf16[128,128]{1,0:T(8,128)(2,1)S(1)} %get-tuple-element.51), channel_id=1, source_target_pairs={{0,1},{1,0},{2,3},{3,2},{4,5},{5,4},{6,7},{7,6},{8,9},{9,8},{10,11... | collective-permute-start | bytes 98312 | tf_op jit(solution)/shard_map/ppermute | solution.py:340
  (7 other events, 5.4 us)

commit v15 on v13

--- a/solution.py
+++ b/solution.py
@@ -356,7 +356,8 @@
     n_in = (node_in_weight, over_cores(node_in_weight))
     n_out = (node_out_weight, over_cores(node_out_weight))
     far = []
-    for weights in over_groups(jnp.concatenate([node_in_weight[:, features:], node_out_weight], axis=1)):
+    far_in, far_out, _ = lax.optimization_barrier((node_in_weight, node_out_weight, e_in[1]))
+    for weights in over_groups(jnp.concatenate([far_in[:, features:], far_out], axis=1)):
         far += [weights, over_cores(weights)]
     (sent,) = stage(functools.partial(send_half, groups), [((half, groups * width), bf16)], states)
     state, pre, pick, take = stage(

time: 40.9 us -> 42 us (1.027)
  waiting for transfers between devices: 11.9 us -> 13.3 us
  local copies, waits for them, and re-layouts: 2.48 us -> 2.05 us
    ppermute x15, waiting for transfers between devices: 10.2 us -> 11.3 us  [swapped(): return lax.ppermute(values, 'feat', [(i, i ^ bits) for i in range(feats)])]
where the time goes in v15:
time: 42 us; the launch traced here: 41.6 us
  starting transfers between devices  18.9 us (45%)
  waiting for transfers between devices  13.3 us (32%)
  Pallas kernels  6.46 us (15%)
  local copies, waits for them, and re-layouts  2.05 us (5%)
  between operations  0.8 us (2%)
    ppermute x15, waiting for transfers between devices, swapped(): return lax.ppermute(values, 'feat', [(i, i ^ bits) for i in range(feats)])  11.3 us
    ppermute x15, starting transfers between devices, swapped(): return lax.ppermute(values, 'feat', [(i, i ^ bits) for i in range(feats)])  9.8 us
    pallas_call x12, Pallas kernels, stage(): pl.pallas_call(kernel, out_shape=[jax.ShapeDtypeStruct(shape, kind) for s...  6.46 us
    all_to_all x1, starting transfers between devices, shards(): latents = lax.all_to_all(spread, everyone, 0, 0)  5.63 us
    all_to_all x1, starting transfers between devices, shards(): shares = lax.all_to_all(spread, everyone, 0, 0)  3.5 us
    unnamed x26, local copies, waits for them, and re-layouts  2.05 us
    all_to_all x1, waiting for transfers between devices, shards(): latents = lax.all_to_all(spread, everyone, 0, 0)  1.97 us
  transfers between devices with their start and end apart: 17, of which 8 were waited for; matrix products, arithmetic and copies ran while one was open for 0% of the time, Pallas kernels for 8%

profile of v15, /device:TPU:0, one launch (start us, length us, event | category | flops | bytes accessed | tf_op | source)
XLA Modules:
  0.0 41.6 jit_solution(8932527493057205295)
XLA Ops:
  0.7 0.5 %collective-permute-start.2 = (bf16[128,1536]{1,0:T(8,128)(2,1)}, bf16[128,1536]{1,0:T(8,128)(2,1)S(1)}, u32[]{:S(2)}, u32[]{:S(2)}) collective-permute-start(bf16[128,1536]{1,0:T(8,128)(2,1)} %e_mine.1), channel_id=1, source_target_pairs={{0,1},{1,0},{2,3},{3,2},{4,5},{5,4},{6,7},{7,6},{8,9},{9,8},{10,11... | collective-permute-start | bytes 1179656 | tf_op jit(solution)/shard_map/ppermute | solution.py:339
  1.2 1.6 %collective-permute-done.2.refs_4_.other.refs_13_.e_other = bf16[128,1536]{1,0:T(8,128)(2,1)S(1)} collective-permute-done((bf16[128,1536]{1,0:T(8,128)(2,1)}, bf16[128,1536]{1,0:T(8,128)(2,1)S(1)}, u32[]{:S(2)}, u32[]{:S(2)}) %collective-permute-start.2) | collective-permute-done | bytes 393248 | tf_op jit(solution)/shard_map/ppermute | solution.py:339
  2.8 2.9 %collective-permute-start.9 = (bf16[128,1024]{1,0:T(8,128)(2,1)S(1)}, bf16[128,1024]{1,0:T(8,128)(2,1)S(1)}, u32[]{:S(2)}, u32[]{:S(2)}) collective-permute-start(bf16[128,1024]{1,0:T(8,128)(2,1)S(1)} %pad_maximum_fusion), channel_id=1, source_target_pairs={{0,2},{1,3},{2,0},{3,1},{4,6},{5,7},{6,4},{7,5},{8,10},{9,11},{10,... | collective-permute-start | bytes 786440 | tf_op jit(solution)/shard_map/ppermute | solution.py:339
  5.7 1.0 %collective-permute-start = (bf16[256,128]{1,0:T(8,128)(2,1)S(1)}, bf16[256,128]{1,0:T(8,128)(2,1)S(1)}, u32[]{:S(2)}, u32[]{:S(2)}) collective-permute-start(bf16[256,128]{1,0:T(8,128)(2,1)S(1)} %copy-done.4), channel_id=1, source_target_pairs={{0,2},{1,3},{2,0},{3,1},{4,6},{5,7},{6,4},{7,5},{8,10},{9,11},{10,... | collective-permute-start | bytes 196616 | tf_op jit(solution)/shard_map/ppermute | solution.py:339
  6.8 0.7 %copy-done.8 = bf16[16,128]{1,0:T(8,128)(2,1)S(1)} copy-done((bf16[16,128]{1,0:T(8,128)(2,1)S(1)}, bf16[16,128]{1,0:T(8,128)(2,1)}, u32[]{:S(2)}) %copy-start.8) | copy-done | bytes 4120
  7.5 0.6 %shard_map.156 = bf16[16,16,128]{2,1,0:T(8,128)(2,1)} custom-call(bf16[16,128]{1,0:T(8,128)(2,1)S(1)} %copy-done.8), custom_call_target="tpu_custom_call" | custom-call | flops 16777216 | bytes 4096 | tf_op jit(solution)/shard_map/pallas_call | solution.py:73
  8.1 5.6 %all-to-all-start = ((bf16[16,16,128]{2,1,0:T(8,128)(2,1)}), bf16[16,16,128]{2,1,0:T(8,128)(2,1)S(1)}, u32[]{:S(2)}, u32[]{:S(2)}) async-start(bf16[16,16,128]{2,1,0:T(8,128)(2,1)} %shard_map.156), calls=%async_computation | async-start | bytes 131072 | tf_op jit(solution)/shard_map/all_to_all | solution.py:352
  14.4 0.5 %copy-done.6 = bf16[16,128]{1,0:T(8,128)(2,1)S(1)} copy-done((bf16[16,128]{1,0:T(8,128)(2,1)S(1)}, bf16[16,128]{1,0:T(8,128)(2,1)}, u32[]{:S(2)}) %copy-start.6) | copy-done | bytes 4120
  15.1 2.0 %collective-permute-start.6 = (bf16[288,128]{1,0:T(8,128)(2,1)S(1)}, bf16[288,128]{1,0:T(8,128)(2,1)S(1)}, u32[]{:S(2)}, u32[]{:S(2)}) collective-permute-start(bf16[288,128]{1,0:T(8,128)(2,1)S(1)} %shard_map.160.refs_0_.refs_3_), channel_id=1, source_target_pairs={{0,2},{1,3},{2,0},{3,1},{4,6},{5,7},{6,4},{7,5},{8,10},{9,11},{10,... | collective-permute-start | bytes 221192 | tf_op jit(solution)/shard_map/ppermute | solution.py:339
  17.1 0.7 %copy-done.9 = s32[256]{0:T(256)S(1)} copy-done((s32[256]{0:T(256)S(1)}, s32[256]{0:T(256)}, u32[]{:S(2)}) %copy-start.9) | copy-done | bytes 1048
  17.8 0.9 %shard_map.158 = (bf16[128,512]{1,0:T(8,128)(2,1)S(1)}, f32[128,256]{1,0:T(8,128)S(1)}, bf16[64,128]{1,0:T(8,128)(2,1)S(1)}, bf16[16,128]{1,0:T(8,128)(2,1)S(1)}) custom-call(bf16[256,128]{1,0:T(8,128)(2,1)S(1)} %copy-done.4, bf16[256,128]{1,0:T(8,128)(2,1)S(1)} %collective-permute-done.refs_1_, bf16[128,256]{1,0:T(8,128)(2,1)S(1)} %collective-permute-done.1.refs_2_, ...), custom_call_target="tpu_custom_call" | custom-call | flops 16777216 | bytes 985600 | tf_op jit(solution)/shard_map/pallas_call | solution.py:73
  18.7 2.0 %all-to-all-done.came = bf16[16,16,128]{2,1,0:T(8,128)(2,1)S(1)} async-done(((bf16[16,16,128]{2,1,0:T(8,128)(2,1)}), bf16[16,16,128]{2,1,0:T(8,128)(2,1)S(1)}, u32[]{:S(2)}, u32[]{:S(2)}) %all-to-all-start) | async-done | bytes 65568 | tf_op jit(solution)/shard_map/all_to_all | solution.py:352
  20.6 0.6 %shard_map.159 = (f32[128,256]{1,0:T(8,128)S(1)}, f32[128,512]{1,0:T(8,128)S(1)}, bf16[144,512]{1,0:T(8,128)(2,1)S(1)}, bf16[16,512]{1,0:T(8,128)(2,1)S(1)}, f32[16,256]{1,0:T(8,128)S(1)}) custom-call(bf16[16,16,128]{2,1,0:T(8,128)(2,1)S(1)} %all-to-all-done.came, f32[128,256]{1,0:T(8,128)S(1)} %get-tuple-element.32.pre, ...), custom_call_target="tpu_custom_call" | custom-call | flops 16777216 | bytes 1789952 | tf_op jit(solution)/shard_map/pallas_call | solution.py:73
  21.5 0.6 %collective-permute-start.7 = (bf16[160,256]{1,0:T(8,128)(2,1)S(1)}, bf16[160,256]{1,0:T(8,128)(2,1)S(1)}, u32[]{:S(2)}, u32[]{:S(2)}) collective-permute-start(bf16[160,256]{1,0:T(8,128)(2,1)S(1)} %shard_map.161), channel_id=1, source_target_pairs={{0,1},{1,0},{2,3},{3,2},{4,5},{5,4},{6,7},{7,6},{8,9},{9,8},{10,11... | collective-permute-start | bytes 245768 | tf_op jit(solution)/shard_map/ppermute | solution.py:339
  22.0 0.9 %collective-permute-done.7.refs_5_ = bf16[160,256]{1,0:T(8,128)(2,1)S(1)} collective-permute-done((bf16[160,256]{1,0:T(8,128)(2,1)S(1)}, bf16[160,256]{1,0:T(8,128)(2,1)S(1)}, u32[]{:S(2)}, u32[]{:S(2)}) %collective-permute-start.7) | collective-permute-done | bytes 81952 | tf_op jit(solution)/shard_map/ppermute | solution.py:339
  23.0 3.7 %collective-permute-done.5.refs_2_ = bf16[144,512]{1,0:T(8,128)(2,1)S(1)} collective-permute-done((bf16[144,512]{1,0:T(8,128)(2,1)S(1)}, bf16[144,512]{1,0:T(8,128)(2,1)S(1)}, u32[]{:S(2)}, u32[]{:S(2)}) %collective-permute-start.5) | collective-permute-done | bytes 147488 | tf_op jit(solution)/shard_map/ppermute | solution.py:339
  26.9 1.2 %collective-permute-done.11.refs_3_ = f32[16,512]{1,0:T(8,128)S(1)} collective-permute-done((f32[16,512]{1,0:T(8,128)S(1)}, f32[16,512]{1,0:T(8,128)S(1)}, u32[]{:S(2)}, u32[]{:S(2)}) %collective-permute-start.11) | collective-permute-done | bytes 32800 | tf_op jit(solution)/shard_map/ppermute | solution.py:339
  28.1 2.5 %shard_map.163 = (bf16[16,128]{1,0:T(8,128)(2,1)}, bf16[128,256]{1,0:T(8,128)(2,1)S(1)}, f32[128,512]{1,0:T(8,128)S(1)}, bf16[16,16,128]{2,1,0:T(8,128)(2,1)}) custom-call(bf16[128,1024]{1,0:T(8,128)(2,1)S(1)} %collective-permute-done.9.refs_0_, bf16[128,1024]{1,0:T(8,128)(2,1)S(1)} %collective-permute-done.10.refs_1_, ...), custom_call_target="tpu_custom_call" | custom-call | flops 16777216 | bytes 3052032 | tf_op jit(solution)/shard_map/pallas_call | solution.py:73
  30.6 3.5 %all-to-all-start.1 = ((bf16[16,16,128]{2,1,0:T(8,128)(2,1)}), bf16[16,16,128]{2,1,0:T(8,128)(2,1)S(1)}, u32[]{:S(2)}, u32[]{:S(2)}) async-start(bf16[16,16,128]{2,1,0:T(8,128)(2,1)} %get-tuple-element.59), calls=%async_computation.1 | async-start | bytes 131072 | tf_op jit(solution)/shard_map/all_to_all | solution.py:421
  34.3 1.9 %collective-permute-start.13 = (bf16[128,256]{1,0:T(8,128)(2,1)S(1)}, bf16[128,256]{1,0:T(8,128)(2,1)S(1)}, u32[]{:S(2)}, u32[]{:S(2)}) collective-permute-start(bf16[128,256]{1,0:T(8,128)(2,1)S(1)} %get-tuple-element.53), channel_id=1, source_target_pairs={{0,2},{1,3},{2,0},{3,1},{4,6},{5,7},{6,4},{7,5},{8,10},{9,11},{10,... | collective-permute-start | bytes 196616 | tf_op jit(solution)/shard_map/ppermute | solution.py:339
  36.2 2.7 %collective-permute-done.13.refs_1_ = bf16[128,256]{1,0:T(8,128)(2,1)S(1)} collective-permute-done((bf16[128,256]{1,0:T(8,128)(2,1)S(1)}, bf16[128,256]{1,0:T(8,128)(2,1)S(1)}, u32[]{:S(2)}, u32[]{:S(2)}) %collective-permute-start.13) | collective-permute-done | bytes 65568 | tf_op jit(solution)/shard_map/ppermute | solution.py:339
  39.1 1.2 %collective-permute-done.14.grad_came = bf16[128,128]{1,0:T(8,128)(2,1)S(1)} collective-permute-done((bf16[128,128]{1,0:T(8,128)(2,1)S(1)}, bf16[128,128]{1,0:T(8,128)(2,1)S(1)}, u32[]{:S(2)}, u32[]{:S(2)}) %collective-permute-start.14) | collective-permute-done | bytes 32800 | tf_op jit(solution)/shard_map/ppermute | solution.py:339
  40.2 0.7 %shard_map.166 = (bf16[256,128]{1,0:T(8,128)(2,1)}, bf16[256,128]{1,0:T(8,128)(2,1)}) custom-call(bf16[128,128]{1,0:T(8,128)(2,1)S(1)} %get-tuple-element.39.next_mine, bf16[128,128]{1,0:T(8,128)(2,1)S(1)} %collective-permute-done.8.next_came, bf16[128,128]{1,0:T(8,128)(2,1)S(1)} %get-tuple-element.54.grad_mine, ...), custom_call_target="tpu_custom_call" | custom-call | flops 16777216 | bytes 131072 | tf_op jit(solution)/shard_map/pallas_call | solution.py:73
  41.0 0.6 %shard_map.167 = bf16[16,128]{1,0:T(8,128)(2,1)} custom-call(bf16[16,16,128]{2,1,0:T(8,128)(2,1)S(1)} %all-to-all-done.1.shares, bf16[16,128]{1,0:T(8,128)(2,1)S(1)} %copy-done.6), custom_call_target="tpu_custom_call" | custom-call | flops 16777216 | bytes 69632 | tf_op jit(solution)/shard_map/pallas_call | solution.py:73
  (51 shorter events, 1.8 us)
Async XLA Ops:
  0.6 2.1 %slice-start = ((bf16[128,1024]{1,0:T(8,128)(2,1)}), bf16[128,512]{1,0:T(8,128)(2,1)S(1)}, s32[]{:S(2)}) async-start(bf16[128,1024]{1,0:T(8,128)(2,1)} %refs_16_.1), calls=%async_computation.2 | async-start | bytes 262144 | tf_op jit(solution)/shard_map/slice | solution.py:360
  0.6 2.1 %copy-start.3 = (bf16[128,512]{1,0:T(8,128)(2,1)S(1)}, bf16[128,512]{1,0:T(8,128)(2,1)}, u32[]{:S(2)}) copy-start(bf16[128,512]{1,0:T(8,128)(2,1)} %refs_18_.1) | copy-start | bytes 393220
  0.7 2.1 %collective-permute-start.2 = (bf16[128,1536]{1,0:T(8,128)(2,1)}, bf16[128,1536]{1,0:T(8,128)(2,1)S(1)}, u32[]{:S(2)}, u32[]{:S(2)}) collective-permute-start(bf16[128,1536]{1,0:T(8,128)(2,1)} %e_mine.1), channel_id=1, source_target_pairs={{0,1},{1,0},{2,3},{3,2},{4,5},{5,4},{6,7},{7,6},{8,9},{9,8},{10,11... | collective-permute-start | bytes 1179656 | tf_op jit(solution)/shard_map/ppermute | solution.py:339
  2.7 3.0 %copy-start.1 = (bf16[128,1024]{1,0:T(8,128)(2,1)S(1)}, bf16[128,1024]{1,0:T(8,128)(2,1)}, u32[]{:S(2)}) copy-start(bf16[128,1024]{1,0:T(8,128)(2,1)} %refs_16_.1) | copy-start | bytes 786436
  2.7 3.0 %copy-start.4 = (bf16[256,128]{1,0:T(8,128)(2,1)S(1)}, bf16[256,128]{1,0:T(8,128)(2,1)}, u32[]{:S(2)}) copy-start(bf16[256,128]{1,0:T(8,128)(2,1)} %refs_0_.3) | copy-start | bytes 196612
  2.7 4.0 %copy-start.2 = (bf16[128,512]{1,0:T(8,128)(2,1)S(1)}, bf16[128,512]{1,0:T(8,128)(2,1)}, u32[]{:S(2)}) copy-start(bf16[128,512]{1,0:T(8,128)(2,1)} %refs_14_.1) | copy-start | bytes 393220
  2.8 11.7 %copy-start.5 = (bf16[256,128]{1,0:T(8,128)(2,1)S(1)}, bf16[256,128]{1,0:T(8,128)(2,1)}, u32[]{:S(2)}) copy-start(bf16[256,128]{1,0:T(8,128)(2,1)} %edge_cot.1) | copy-start | bytes 196612
  2.8 14.3 %copy-start = (bf16[128,1536]{1,0:T(8,128)(2,1)S(1)}, bf16[128,1536]{1,0:T(8,128)(2,1)}, u32[]{:S(2)}) copy-start(bf16[128,1536]{1,0:T(8,128)(2,1)} %e_mine.1) | copy-start | bytes 1179652
  2.8 10.9 %collective-permute-start.9 = (bf16[128,1024]{1,0:T(8,128)(2,1)S(1)}, bf16[128,1024]{1,0:T(8,128)(2,1)S(1)}, u32[]{:S(2)}, u32[]{:S(2)}) collective-permute-start(bf16[128,1024]{1,0:T(8,128)(2,1)S(1)} %pad_maximum_fusion), channel_id=1, source_target_pairs={{0,2},{1,3},{2,0},{3,1},{4,6},{5,7},{6,4},{7,5},{8,10},{9,11},{10,... | collective-permute-start | bytes 786440 | tf_op jit(solution)/shard_map/ppermute | solution.py:339
  5.7 14.9 %collective-permute-start.4 = (bf16[128,1024]{1,0:T(8,128)(2,1)S(1)}, bf16[128,1024]{1,0:T(8,128)(2,1)S(1)}, u32[]{:S(2)}, u32[]{:S(2)}) collective-permute-start(bf16[128,1024]{1,0:T(8,128)(2,1)S(1)} %copy-done.1), channel_id=1, source_target_pairs={{0,1},{1,0},{2,3},{3,2},{4,5},{5,4},{6,7},{7,6},{8,9},{9,8},{10,11... | collective-permute-start | bytes 786440 | tf_op jit(solution)/shard_map/ppermute | solution.py:339
  5.7 8.5 %collective-permute-start = (bf16[256,128]{1,0:T(8,128)(2,1)S(1)}, bf16[256,128]{1,0:T(8,128)(2,1)S(1)}, u32[]{:S(2)}, u32[]{:S(2)}) collective-permute-start(bf16[256,128]{1,0:T(8,128)(2,1)S(1)} %copy-done.4), channel_id=1, source_target_pairs={{0,2},{1,3},{2,0},{3,1},{4,6},{5,7},{6,4},{7,5},{8,10},{9,11},{10,... | collective-permute-start | bytes 196616 | tf_op jit(solution)/shard_map/ppermute | solution.py:339
  6.7 13.9 %collective-permute-start.3 = (bf16[128,512]{1,0:T(8,128)(2,1)S(1)}, bf16[128,512]{1,0:T(8,128)(2,1)S(1)}, u32[]{:S(2)}, u32[]{:S(2)}) collective-permute-start(bf16[128,512]{1,0:T(8,128)(2,1)S(1)} %copy-done.2), channel_id=1, source_target_pairs={{0,1},{1,0},{2,3},{3,2},{4,5},{5,4},{6,7},{7,6},{8,9},{9,8},{10,11... | collective-permute-start | bytes 393224 | tf_op jit(solution)/shard_map/ppermute | solution.py:339
  8.1 12.5 %all-to-all-start = ((bf16[16,16,128]{2,1,0:T(8,128)(2,1)}), bf16[16,16,128]{2,1,0:T(8,128)(2,1)S(1)}, u32[]{:S(2)}, u32[]{:S(2)}) async-start(bf16[16,16,128]{2,1,0:T(8,128)(2,1)} %shard_map.156), calls=%async_computation | async-start | bytes 131072 | tf_op jit(solution)/shard_map/all_to_all | solution.py:352
  13.8 14.3 %collective-permute-start.10 = (bf16[128,1024]{1,0:T(8,128)(2,1)S(1)}, bf16[128,1024]{1,0:T(8,128)(2,1)S(1)}, u32[]{:S(2)}, u32[]{:S(2)}) collective-permute-start(bf16[128,1024]{1,0:T(8,128)(2,1)S(1)} %collective-permute-done.9.refs_0_), channel_id=1, source_target_pairs={{0,1},{1,0},{2,3},{3,2},{4,5},{5,4},{6,7},{7,6},{8,9},{9,8},{10,11... | collective-permute-start | bytes 786440 | tf_op jit(solution)/shard_map/ppermute | solution.py:339
  14.2 2.8 %collective-permute-start.1 = (bf16[128,256]{1,0:T(8,128)(2,1)S(1)}, bf16[128,256]{1,0:T(8,128)(2,1)S(1)}, u32[]{:S(2)}, u32[]{:S(2)}) collective-permute-start(bf16[128,256]{1,0:T(8,128)(2,1)S(1)} %shard_map.157), channel_id=1, source_target_pairs={{0,1},{1,0},{2,3},{3,2},{4,5},{5,4},{6,7},{7,6},{8,9},{9,8},{10,11... | collective-permute-start | bytes 196616 | tf_op jit(solution)/shard_map/ppermute | solution.py:339
  15.1 6.3 %collective-permute-start.6 = (bf16[288,128]{1,0:T(8,128)(2,1)S(1)}, bf16[288,128]{1,0:T(8,128)(2,1)S(1)}, u32[]{:S(2)}, u32[]{:S(2)}) collective-permute-start(bf16[288,128]{1,0:T(8,128)(2,1)S(1)} %shard_map.160.refs_0_.refs_3_), channel_id=1, source_target_pairs={{0,2},{1,3},{2,0},{3,1},{4,6},{5,7},{6,4},{7,5},{8,10},{9,11},{10,... | collective-permute-start | bytes 221192 | tf_op jit(solution)/shard_map/ppermute | solution.py:339
  21.3 5.3 %collective-permute-start.5 = (bf16[144,512]{1,0:T(8,128)(2,1)S(1)}, bf16[144,512]{1,0:T(8,128)(2,1)S(1)}, u32[]{:S(2)}, u32[]{:S(2)}) collective-permute-start(bf16[144,512]{1,0:T(8,128)(2,1)S(1)} %get-tuple-element.37), channel_id=1, source_target_pairs={{0,2},{1,3},{2,0},{3,1},{4,6},{5,7},{6,4},{7,5},{8,10},{9,11},{10,... | collective-permute-start | bytes 442376 | tf_op jit(solution)/shard_map/ppermute | solution.py:339
  21.4 5.5 %collective-permute-start.12 = (bf16[128,512]{1,0:T(8,128)(2,1)S(1)}, bf16[128,512]{1,0:T(8,128)(2,1)S(1)}, u32[]{:S(2)}, u32[]{:S(2)}) collective-permute-start(bf16[128,512]{1,0:T(8,128)(2,1)S(1)} %copy-done.3), channel_id=1, source_target_pairs={{0,1},{1,0},{2,3},{3,2},{4,5},{5,4},{6,7},{7,6},{8,9},{9,8},{10,11... | collective-permute-start | bytes 393224 | tf_op jit(solution)/shard_map/ppermute | solution.py:339
  21.5 1.5 %collective-permute-start.7 = (bf16[160,256]{1,0:T(8,128)(2,1)S(1)}, bf16[160,256]{1,0:T(8,128)(2,1)S(1)}, u32[]{:S(2)}, u32[]{:S(2)}) collective-permute-start(bf16[160,256]{1,0:T(8,128)(2,1)S(1)} %shard_map.161), channel_id=1, source_target_pairs={{0,1},{1,0},{2,3},{3,2},{4,5},{5,4},{6,7},{7,6},{8,9},{9,8},{10,11... | collective-permute-start | bytes 245768 | tf_op jit(solution)/shard_map/ppermute | solution.py:339
  26.9 1.2 %collective-permute-start.11 = (f32[16,512]{1,0:T(8,128)S(1)}, f32[16,512]{1,0:T(8,128)S(1)}, u32[]{:S(2)}, u32[]{:S(2)}) collective-permute-start(f32[16,512]{1,0:T(8,128)S(1)} %get-tuple-element.43.refs_2_), channel_id=1, source_target_pairs={{0,1},{1,0},{2,3},{3,2},{4,5},{5,4},{6,7},{7,6},{8,9},{9,8},{10,11... | collective-permute-start | bytes 98312 | tf_op jit(solution)/shard_map/ppermute | solution.py:339
  30.6 10.4 %all-to-all-start.1 = ((bf16[16,16,128]{2,1,0:T(8,128)(2,1)}), bf16[16,16,128]{2,1,0:T(8,128)(2,1)S(1)}, u32[]{:S(2)}, u32[]{:S(2)}) async-start(bf16[16,16,128]{2,1,0:T(8,128)(2,1)} %get-tuple-element.59), calls=%async_computation.1 | async-start | bytes 131072 | tf_op jit(solution)/shard_map/all_to_all | solution.py:421
  34.3 4.6 %collective-permute-start.13 = (bf16[128,256]{1,0:T(8,128)(2,1)S(1)}, bf16[128,256]{1,0:T(8,128)(2,1)S(1)}, u32[]{:S(2)}, u32[]{:S(2)}) collective-permute-start(bf16[128,256]{1,0:T(8,128)(2,1)S(1)} %get-tuple-element.53), channel_id=1, source_target_pairs={{0,2},{1,3},{2,0},{3,1},{4,6},{5,7},{6,4},{7,5},{8,10},{9,11},{10,... | collective-permute-start | bytes 196616 | tf_op jit(solution)/shard_map/ppermute | solution.py:339
  36.2 2.8 %collective-permute-start.8 = (bf16[128,128]{1,0:T(8,128)(2,1)S(1)}, bf16[128,128]{1,0:T(8,128)(2,1)S(1)}, u32[]{:S(2)}, u32[]{:S(2)}) collective-permute-start(bf16[128,128]{1,0:T(8,128)(2,1)S(1)} %get-tuple-element.40), channel_id=1, source_target_pairs={{0,1},{1,0},{2,3},{3,2},{4,5},{5,4},{6,7},{7,6},{8,9},{9,8},{10,11... | collective-permute-start | bytes 98312 | tf_op jit(solution)/shard_map/ppermute | solution.py:339
  39.0 1.3 %collective-permute-start.14 = (bf16[128,128]{1,0:T(8,128)(2,1)S(1)}, bf16[128,128]{1,0:T(8,128)(2,1)S(1)}, u32[]{:S(2)}, u32[]{:S(2)}) collective-permute-start(bf16[128,128]{1,0:T(8,128)(2,1)S(1)} %get-tuple-element.55), channel_id=1, source_target_pairs={{0,1},{1,0},{2,3},{3,2},{4,5},{5,4},{6,7},{7,6},{8,9},{9,8},{10,11... | collective-permute-start | bytes 98312 | tf_op jit(solution)/shard_map/ppermute | solution.py:339
  (7 other events, 7.4 us)

commit v16 on v13

--- a/solution.py
+++ b/solution.py
@@ -100,19 +100,24 @@
     spread[...] = jnp.broadcast_to(latent[...][None], spread.shape)
 
 
-def pack_extra(edge_cot, node_cot, gain_e, gain_n, pack):
+def pack_extra(edge_cot, node_cot, gain_e, gain_n, out_weight, pack):
     edge_dev = edge_cot.shape[0]
     nodes = node_cot.shape[0]
     pack[:edge_dev] = edge_cot[...]
     pack[edge_dev : edge_dev + nodes] = node_cot[...]
-    pack[edge_dev + nodes :] = gains(gain_e, gain_n, nodes)
-
-
-def half_rows(pack, core, half):
+    first = edge_dev + 2 * nodes
+    pack[edge_dev + nodes : first] = gains(gain_e, gain_n, nodes)
+    hid, width = out_weight.shape[0], pack.shape[1]
+    for index in range(out_weight.shape[1] // width):
+        columns = slice(index * width, (index + 1) * width)
+        pack[first + index * hid : first + (index + 1) * hid] = out_weight[:, columns]
+
+
+def half_rows(pack, core, half, shared=0):
     rows = pack[pl.ds(pl.multiple_of(core * half, half), half)]
-    if pack.shape[0] == cores * half:
+    if shared == 0:
         return rows
-    return jnp.concatenate([rows, pack[cores * half :]], axis=0)
+    return jnp.concatenate([rows, pack[cores * half : cores * half + shared]], axis=0)
 
 
 def send_half(groups, *refs):
@@ -150,11 +155,11 @@
     pre[...] = dot_rows(state[...], weight)
 
 
-def finish_edges(came, pre, pick, take, mine, other, out_mine, out_other, n_mine, n_other, edge_pre, part, sent, own, lat, table):
+def finish_edges(came, pre, pick, take, mine, other, n_mine, n_other, edge_pre, sent, own, lat, table):
     block = lax.axis_index("nodes")
     count, nodes, width = came.shape
     rows, features = table.shape
-    half, hidden = pre.shape
+    half = pre.shape[0]
     feats = features // width
     for source in range(count):
         first, column = source // feats * nodes, source % feats * width
@@ -171,34 +176,35 @@
     chosen = jnp.concatenate([pick[...], pick[...], take[...], take[...]], axis=0)
     value = pre[...] + dot_cols(chosen, jnp.concatenate([high, low, here_high, here_low], axis=0))
     edge_pre[...] = value
-    act = (value * sigmoid(value)).astype(bf16)
-    out = dot(act, jnp.concatenate([out_mine[...], out_other[...]], axis=0))
-    part[...] = out
-    sent[:half] = out.astype(bf16)
+    sent[:half] = (value * sigmoid(value)).astype(bf16)
     nodes_pre = dot_rows(latent, jnp.concatenate([n_mine[:, :features], n_other[:, :features]], axis=0))
     lat[...] = nodes_pre
-    high, low = split(nodes_pre)
-    sent[half:] = jnp.zeros((nodes, features), bf16)
-    sent[half:, :hidden] = high
-    sent[half:, hidden : 2 * hidden] = low
+    sent[half:] = jnp.concatenate(split(nodes_pre), axis=0)
 
 
 def update_edges(groups, *refs):
-    part, lat, came, packs = refs[0], refs[1], refs[2 : groups + 1], refs[groups + 1 : 2 * groups + 1]
-    theirs, state, take, normed, inverse, kept, lent, aggregate, lat_all, extra, next_all = refs[2 * groups + 1 :]
+    feats = groups * cores
+    lat, acts, packs, refs = refs[0], refs[1 : groups + 1], refs[groups + 1 : groups + 1 + feats], refs[groups + 1 + feats :]
+    state, take, normed, inverse, kept, lent, aggregate, lat_all, extra, next_all = refs
     group, core = place()
     nodes, half = take.shape
     width = kept.shape[1]
     hidden = lat.shape[1]
-    for step, pack in enumerate(packs):
-        both = pair(half_rows(pack, core, half), theirs[:, step * width : (step + 1) * width], core)
+    hid = hidden // cores
+    weights = []
+    for step in range(groups):
+        ours, theirs = packs[cores * step], packs[cores * step + 1]
+        both = pair(half_rows(ours, core, half, 2 * nodes), half_rows(theirs, core, half, 2 * nodes), core)
         extra[:, lanes(group ^ step, width * cores)] = both
-    value = part[...]
+        for pack in (ours, theirs):
+            first = cores * half + 2 * nodes
+            parts = [pack[first + index * hid : first + (index + 1) * hid] for index in range(feats)]
+            weights.append(jnp.concatenate(parts, axis=1))
     lat_all[:, :hidden] = lat[...]
-    for step, ref in enumerate(came, 1):
-        value = value + ref[:half].astype(f32)
-        high, low = ref[half:, :hidden], ref[half:, hidden : 2 * hidden]
+    for step, act in enumerate(acts[1:], 1):
+        high, low = act[half : half + nodes], act[half + nodes :]
         lat_all[:, step * hidden : (step + 1) * hidden] = high.astype(f32) + low.astype(f32)
+    value = dot(jnp.concatenate([act[:half] for act in acts], axis=1), jnp.concatenate(weights, axis=0))
     normed_rows, inverse_rows = normalize(value)
     normed[...] = normed_rows
     inverse[...] = inverse_rows
@@ -365,21 +371,20 @@
         [*states, over_cores(sent), *e_in, slot_rows, receiver_rows, send_rows],
         scalars=1,
     )
-    rows = edge_dev + 2 * nodes
-    (pack,) = stage(pack_extra, [((rows, width), bf16)], [edge_cot, node_cot, gain_e, gain_n])
-    packs = [pack] + over_groups(pack)
-    (sent,) = stage(functools.partial(send_half, groups), [((rows - half, groups * width), bf16)], packs)
-    extra_came = over_cores(sent)
-    edge_pre, part, sent, own, lat = stage(
+    rows = edge_dev + 2 * nodes + feats * edge_out_weight.shape[0]
+    (pack,) = stage(
+        pack_extra, [((rows, width), bf16)], [edge_cot, node_cot, gain_e, gain_n, edge_out_weight]
+    )
+    packs = [part for came in [pack] + over_groups(pack) for part in (came, over_cores(came))]
+    edge_pre, sent, own, lat = stage(
         finish_edges,
         [
             ((half, hidden), f32),
-            ((half, features), f32),
-            ((half + nodes, features), bf16),
+            ((half + 2 * nodes, hidden), bf16),
             ((nodes, features), bf16),
             ((nodes, hidden), f32),
         ],
-        [latents, pre, pick, take, *e_in, *e_out, *n_in],
+        [latents, pre, pick, take, *e_in, *n_in],
         scratch=[((table, features), bf16)],
     )
     normed, inverse, next_mine, next_sent, aggregate, lat_all, extra = stage(
@@ -393,7 +398,7 @@
             ((nodes, features), f32),
             ((half + 2 * nodes, features), bf16),
         ],
-        [part, lat, *over_groups(sent), *packs, extra_came, state, take],
+        [lat, sent, *over_groups(sent), *packs, state, take],
         scratch=[((half, features), bf16)],
     )
     aggregate2 = over_cores(aggregate)

time: 40.9 us -> 52.6 us (1.29)
  waiting for transfers between devices: 11.9 us -> 19.9 us
  local copies, waits for them, and re-layouts: 2.48 us -> 5.41 us
  starting transfers between devices: 18.8 us -> 19.4 us
    ppermute x15 -> x16, waiting for transfers between devices: 10.2 us -> 17 us  [swapped(): return lax.ppermute(values, 'feat', [(i, i ^ bits) for i in range(feats)])]
    unnamed x26 -> x42, local copies, waits for them, and re-layouts: 2.11 us -> 5.04 us
    all_to_all x1, waiting for transfers between devices: 1.69 us -> 2.83 us  [shards(): latents = lax.all_to_all(spread, everyone, 0, 0)]
    all_to_all x1, starting transfers between devices: 5.61 us -> 6.61 us  [shards(): latents = lax.all_to_all(spread, everyone, 0, 0)]
    ppermute x15 -> x16, starting transfers between devices: 9.71 us -> 9.32 us  [swapped(): return lax.ppermute(values, 'feat', [(i, i ^ bits) for i in range(feats)])]
    pallas_call x12 -> x11, Pallas kernels: 6.46 us -> 6.52 us  [stage(): pl.pallas_call(kernel, out_shape=[jax.ShapeDtypeStruct(shape, kind) for s...]
  transfers between devices with their start and end apart: 17 -> 18, of which waited for: 8 -> 7; matrix products, arithmetic and copies ran while one was open for 0% -> 0% of each run, Pallas kernels for 8% -> 7%
where the time goes in v16:
time: 52.6 us; the launch traced here: 52.1 us
  waiting for transfers between devices  19.9 us (38%)
  starting transfers between devices  19.4 us (37%)
  Pallas kernels  6.52 us (12%)
  local copies, waits for them, and re-layouts  5.41 us (10%)
  between operations  0.85 us (2%)
    ppermute x16, waiting for transfers between devices, swapped(): return lax.ppermute(values, 'feat', [(i, i ^ bits) for i in range(feats)])  17 us
    ppermute x16, starting transfers between devices, swapped(): return lax.ppermute(values, 'feat', [(i, i ^ bits) for i in range(feats)])  9.32 us
    all_to_all x1, starting transfers between devices, shards(): latents = lax.all_to_all(spread, everyone, 0, 0)  6.61 us
    pallas_call x11, Pallas kernels, stage(): pl.pallas_call(kernel, out_shape=[jax.ShapeDtypeStruct(shape, kind) for s...  6.52 us
    unnamed x42, local copies, waits for them, and re-layouts  5.04 us
    all_to_all x1, starting transfers between devices, shards(): shares = lax.all_to_all(spread, everyone, 0, 0)  3.49 us
    all_to_all x1, waiting for transfers between devices, shards(): latents = lax.all_to_all(spread, everyone, 0, 0)  2.83 us
  transfers between devices with their start and end apart: 18, of which 7 were waited for; matrix products, arithmetic and copies ran while one was open for 0% of the time, Pallas kernels for 7%

profile of v16, /device:TPU:0, one launch (start us, length us, event | category | flops | bytes accessed | tf_op | source)
XLA Modules:
  0.0 52.1 jit_solution(9129212589515833998)
XLA Ops:
  1.7 3.0 %collective-permute-start.9 = (bf16[128,1024]{1,0:T(8,128)(2,1)S(1)}, bf16[128,1024]{1,0:T(8,128)(2,1)S(1)}, u32[]{:S(2)}, u32[]{:S(2)}) collective-permute-start(bf16[128,1024]{1,0:T(8,128)(2,1)S(1)} %pad_maximum_fusion), channel_id=1, source_target_pairs={{0,2},{1,3},{2,0},{3,1},{4,6},{5,7},{6,4},{7,5},{8,10},{9,11},{10,... | collective-permute-start | bytes 786440 | tf_op jit(solution)/shard_map/ppermute | solution.py:345
  4.7 0.7 %collective-permute-start = (bf16[256,128]{1,0:T(8,128)(2,1)S(1)}, bf16[256,128]{1,0:T(8,128)(2,1)S(1)}, u32[]{:S(2)}, u32[]{:S(2)}) collective-permute-start(bf16[256,128]{1,0:T(8,128)(2,1)S(1)} %copy-done.4), channel_id=1, source_target_pairs={{0,2},{1,3},{2,0},{3,1},{4,6},{5,7},{6,4},{7,5},{8,10},{9,11},{10,... | collective-permute-start | bytes 196616 | tf_op jit(solution)/shard_map/ppermute | solution.py:345
  5.5 1.4 %collective-permute-start.6 = (bf16[800,128]{1,0:T(8,128)(2,1)S(1)}, bf16[800,128]{1,0:T(8,128)(2,1)S(1)}, u32[]{:S(2)}, u32[]{:S(2)}) collective-permute-start(bf16[800,128]{1,0:T(8,128)(2,1)S(1)} %shard_map.160.refs_3_), channel_id=1, source_target_pairs={{0,2},{1,3},{2,0},{3,1},{4,6},{5,7},{6,4},{7,5},{8,10},{9,11},{10,... | collective-permute-start | bytes 614408 | tf_op jit(solution)/shard_map/ppermute | solution.py:345
  6.9 6.4 %collective-permute-done.refs_1_ = bf16[256,128]{1,0:T(8,128)(2,1)S(1)} collective-permute-done((bf16[256,128]{1,0:T(8,128)(2,1)S(1)}, bf16[256,128]{1,0:T(8,128)(2,1)S(1)}, u32[]{:S(2)}, u32[]{:S(2)}) %collective-permute-start) | collective-permute-done | bytes 65568 | tf_op jit(solution)/shard_map/ppermute | solution.py:345
  13.3 1.2 %collective-permute-done.1.refs_2_ = bf16[128,256]{1,0:T(8,128)(2,1)S(1)} collective-permute-done((bf16[128,256]{1,0:T(8,128)(2,1)S(1)}, bf16[128,256]{1,0:T(8,128)(2,1)S(1)}, u32[]{:S(2)}, u32[]{:S(2)}) %collective-permute-start.1) | collective-permute-done | bytes 65568 | tf_op jit(solution)/shard_map/ppermute | solution.py:345
  14.6 0.6 %copy-done.8 = bf16[128,256]{1,0:T(8,128)(2,1)} copy-done((bf16[128,256]{1,0:T(8,128)(2,1)}, bf16[128,256]{1,0:T(8,128)(2,1)S(1)}, u32[]{:S(2)}) %copy-start.8) | copy-done | bytes 65560
  15.7 0.6 %shard_map.156 = bf16[16,16,128]{2,1,0:T(8,128)(2,1)} custom-call(bf16[16,128]{1,0:T(8,128)(2,1)S(1)} %copy-done.14), custom_call_target="tpu_custom_call" | custom-call | flops 16777216 | bytes 4096 | tf_op jit(solution)/shard_map/pallas_call | solution.py:73
  16.3 6.6 %all-to-all-start = ((bf16[16,16,128]{2,1,0:T(8,128)(2,1)}), bf16[16,16,128]{2,1,0:T(8,128)(2,1)S(1)}, u32[]{:S(2)}, u32[]{:S(2)}) async-start(bf16[16,16,128]{2,1,0:T(8,128)(2,1)} %shard_map.156), calls=%async_computation | async-start | bytes 131072 | tf_op jit(solution)/shard_map/all_to_all | solution.py:358
  24.0 0.7 %copy-done.15 = s32[256]{0:T(256)S(1)} copy-done((s32[256]{0:T(256)S(1)}, s32[256]{0:T(256)}, u32[]{:S(2)}) %copy-start.15) | copy-done | bytes 1048
  24.6 0.8 %copy-done.9 = bf16[128,256]{1,0:T(8,128)(2,1)S(1)} copy-done((bf16[128,256]{1,0:T(8,128)(2,1)S(1)}, bf16[128,256]{1,0:T(8,128)(2,1)}, u32[]{:S(2)}) %copy-start.9) | copy-done | bytes 65560
  25.5 0.9 %shard_map.158 = (bf16[128,512]{1,0:T(8,128)(2,1)S(1)}, f32[128,256]{1,0:T(8,128)S(1)}, bf16[64,128]{1,0:T(8,128)(2,1)S(1)}, bf16[16,128]{1,0:T(8,128)(2,1)S(1)}) custom-call(bf16[256,128]{1,0:T(8,128)(2,1)S(1)} %copy-done.4, bf16[256,128]{1,0:T(8,128)(2,1)S(1)} %collective-permute-done.refs_1_, bf16[128,256]{1,0:T(8,128)(2,1)S(1)} %copy-done.9, ...), custom_call_target="tpu_custom_call" | custom-call | flops 16777216 | bytes 985600 | tf_op jit(solution)/shard_map/pallas_call | solution.py:73
  26.4 0.6 %copy-done.5 = f32[128,256]{1,0:T(8,128)} copy-done((f32[128,256]{1,0:T(8,128)}, f32[128,256]{1,0:T(8,128)S(1)}, u32[]{:S(2)}) %copy-start.5) | copy-done | bytes 131096
  27.0 2.8 %all-to-all-done.came = bf16[16,16,128]{2,1,0:T(8,128)(2,1)S(1)} async-done(((bf16[16,16,128]{2,1,0:T(8,128)(2,1)}), bf16[16,16,128]{2,1,0:T(8,128)(2,1)S(1)}, u32[]{:S(2)}, u32[]{:S(2)}) %all-to-all-start) | async-done | bytes 65568 | tf_op jit(solution)/shard_map/all_to_all | solution.py:358
  29.9 0.9 %copy-done.6 = f32[128,256]{1,0:T(8,128)S(1)} copy-done((f32[128,256]{1,0:T(8,128)S(1)}, f32[128,256]{1,0:T(8,128)}, u32[]{:S(2)}) %copy-start.6) | copy-done | bytes 131096
  31.4 4.3 %collective-permute-done.4.refs_2_ = bf16[160,256]{1,0:T(8,128)(2,1)S(1)} collective-permute-done((bf16[160,256]{1,0:T(8,128)(2,1)S(1)}, bf16[160,256]{1,0:T(8,128)(2,1)S(1)}, u32[]{:S(2)}, u32[]{:S(2)}) %collective-permute-start.4) | collective-permute-done | bytes 81952 | tf_op jit(solution)/shard_map/ppermute | solution.py:345
  36.2 0.6 %copy-done.10 = bf16[128,128]{1,0:T(8,128)(2,1)} copy-done((bf16[128,128]{1,0:T(8,128)(2,1)}, bf16[128,128]{1,0:T(8,128)(2,1)S(1)}, u32[]{:S(2)}) %copy-start.10) | copy-done | bytes 32792
  37.5 1.2 %collective-permute-done.11.refs_3_ = f32[16,512]{1,0:T(8,128)S(1)} collective-permute-done((f32[16,512]{1,0:T(8,128)S(1)}, f32[16,512]{1,0:T(8,128)S(1)}, u32[]{:S(2)}, u32[]{:S(2)}) %collective-permute-start.11) | collective-permute-done | bytes 32800 | tf_op jit(solution)/shard_map/ppermute | solution.py:345
  38.7 2.5 %shard_map.162 = (bf16[16,128]{1,0:T(8,128)(2,1)}, bf16[128,256]{1,0:T(8,128)(2,1)S(1)}, f32[128,512]{1,0:T(8,128)S(1)}, bf16[16,16,128]{2,1,0:T(8,128)(2,1)}) custom-call(bf16[128,1024]{1,0:T(8,128)(2,1)S(1)} %collective-permute-done.9.refs_0_, bf16[128,1024]{1,0:T(8,128)(2,1)S(1)} %collective-permute-done.10.refs_1_, ...), custom_call_target="tpu_custom_call" | custom-call | flops 16777216 | bytes 3052032 | tf_op jit(solution)/shard_map/pallas_call | solution.py:73
  41.2 3.5 %all-to-all-start.1 = ((bf16[16,16,128]{2,1,0:T(8,128)(2,1)}), bf16[16,16,128]{2,1,0:T(8,128)(2,1)S(1)}, u32[]{:S(2)}, u32[]{:S(2)}) async-start(bf16[16,16,128]{2,1,0:T(8,128)(2,1)} %get-tuple-element.53), calls=%async_computation.1 | async-start | bytes 131072 | tf_op jit(solution)/shard_map/all_to_all | solution.py:425
  44.9 1.9 %collective-permute-start.14 = (bf16[128,256]{1,0:T(8,128)(2,1)S(1)}, bf16[128,256]{1,0:T(8,128)(2,1)S(1)}, u32[]{:S(2)}, u32[]{:S(2)}) collective-permute-start(bf16[128,256]{1,0:T(8,128)(2,1)S(1)} %get-tuple-element.47), channel_id=1, source_target_pairs={{0,2},{1,3},{2,0},{3,1},{4,6},{5,7},{6,4},{7,5},{8,10},{9,11},{10,... | collective-permute-start | bytes 196616 | tf_op jit(solution)/shard_map/ppermute | solution.py:345
  46.8 2.7 %collective-permute-done.14.refs_1_ = bf16[128,256]{1,0:T(8,128)(2,1)S(1)} collective-permute-done((bf16[128,256]{1,0:T(8,128)(2,1)S(1)}, bf16[128,256]{1,0:T(8,128)(2,1)S(1)}, u32[]{:S(2)}, u32[]{:S(2)}) %collective-permute-start.14) | collective-permute-done | bytes 65568 | tf_op jit(solution)/shard_map/ppermute | solution.py:345
  49.6 1.2 %collective-permute-done.15.grad_came = bf16[128,128]{1,0:T(8,128)(2,1)S(1)} collective-permute-done((bf16[128,128]{1,0:T(8,128)(2,1)S(1)}, bf16[128,128]{1,0:T(8,128)(2,1)S(1)}, u32[]{:S(2)}, u32[]{:S(2)}) %collective-permute-start.15) | collective-permute-done | bytes 32800 | tf_op jit(solution)/shard_map/ppermute | solution.py:345
  50.8 0.7 %shard_map.165 = (bf16[256,128]{1,0:T(8,128)(2,1)}, bf16[256,128]{1,0:T(8,128)(2,1)}) custom-call(bf16[128,128]{1,0:T(8,128)(2,1)S(1)} %copy-done.11, bf16[128,128]{1,0:T(8,128)(2,1)S(1)} %collective-permute-done.8.next_came, bf16[128,128]{1,0:T(8,128)(2,1)S(1)} %get-tuple-element.48.grad_mine, bf16[128,128]{1,0:T(8,128)(2,1)S(1)} %collective-permute-done.15.grad_came), custom_call_target="tpu_custom_call" | custom-call | flops 16777216 | bytes 131072 | tf_op jit(solution)/shard_map/pallas_call | solution.py:73
  51.5 0.6 %shard_map.166 = bf16[16,128]{1,0:T(8,128)(2,1)} custom-call(bf16[16,16,128]{2,1,0:T(8,128)(2,1)S(1)} %all-to-all-done.1.shares, bf16[16,128]{1,0:T(8,128)(2,1)S(1)} %copy-done.12), custom_call_target="tpu_custom_call" | custom-call | flops 16777216 | bytes 69632 | tf_op jit(solution)/shard_map/pallas_call | solution.py:73
  (68 shorter events, 4.8 us)
Async XLA Ops:
  0.7 22.9 %collective-permute-start.2 = (bf16[128,1536]{1,0:T(8,128)(2,1)}, bf16[128,1536]{1,0:T(8,128)(2,1)S(1)}, u32[]{:S(2)}, u32[]{:S(2)}) collective-permute-start(bf16[128,1536]{1,0:T(8,128)(2,1)} %e_mine.1), channel_id=1, source_target_pairs={{0,1},{1,0},{2,3},{3,2},{4,5},{5,4},{6,7},{7,6},{8,9},{9,8},{10,11... | collective-permute-start | bytes 1179656 | tf_op jit(solution)/shard_map/ppermute | solution.py:345
  1.6 3.8 %copy-start.17 = (bf16[128]{0:T(256)(128)(2,1)S(1)}, bf16[128]{0:T(256)(128)(2,1)}, u32[]{:S(2)}) copy-start(bf16[128]{0:T(256)(128)(2,1)} %param.20) | copy-start | bytes 772
  1.7 5.2 %copy-start.1 = (bf16[128,1024]{1,0:T(8,128)(2,1)S(1)}, bf16[128,1024]{1,0:T(8,128)(2,1)}, u32[]{:S(2)}) copy-start(bf16[128,1024]{1,0:T(8,128)(2,1)} %refs_16_.1) | copy-start | bytes 786436
  1.7 13.7 %collective-permute-start.9 = (bf16[128,1024]{1,0:T(8,128)(2,1)S(1)}, bf16[128,1024]{1,0:T(8,128)(2,1)S(1)}, u32[]{:S(2)}, u32[]{:S(2)}) collective-permute-start(bf16[128,1024]{1,0:T(8,128)(2,1)S(1)} %pad_maximum_fusion), channel_id=1, source_target_pairs={{0,2},{1,3},{2,0},{3,1},{4,6},{5,7},{6,4},{7,5},{8,10},{9,11},{10,... | collective-permute-start | bytes 786440 | tf_op jit(solution)/shard_map/ppermute | solution.py:345
  4.7 8.5 %collective-permute-start = (bf16[256,128]{1,0:T(8,128)(2,1)S(1)}, bf16[256,128]{1,0:T(8,128)(2,1)S(1)}, u32[]{:S(2)}, u32[]{:S(2)}) collective-permute-start(bf16[256,128]{1,0:T(8,128)(2,1)S(1)} %copy-done.4), channel_id=1, source_target_pairs={{0,2},{1,3},{2,0},{3,1},{4,6},{5,7},{6,4},{7,5},{8,10},{9,11},{10,... | collective-permute-start | bytes 196616 | tf_op jit(solution)/shard_map/ppermute | solution.py:345
  5.4 10.3 %copy-start.14 = (bf16[16,128]{1,0:T(8,128)(2,1)S(1)}, bf16[16,128]{1,0:T(8,128)(2,1)}, u32[]{:S(2)}) copy-start(bf16[16,128]{1,0:T(8,128)(2,1)} %latent.1) | copy-start | bytes 12292
  5.4 18.5 %copy-start = (bf16[128,1536]{1,0:T(8,128)(2,1)S(1)}, bf16[128,1536]{1,0:T(8,128)(2,1)}, u32[]{:S(2)}) copy-start(bf16[128,1536]{1,0:T(8,128)(2,1)} %e_mine.1) | copy-start | bytes 1179652
  5.5 17.5 %collective-permute-start.6 = (bf16[800,128]{1,0:T(8,128)(2,1)S(1)}, bf16[800,128]{1,0:T(8,128)(2,1)S(1)}, u32[]{:S(2)}, u32[]{:S(2)}) collective-permute-start(bf16[800,128]{1,0:T(8,128)(2,1)S(1)} %shard_map.160.refs_3_), channel_id=1, source_target_pairs={{0,2},{1,3},{2,0},{3,1},{4,6},{5,7},{6,4},{7,5},{8,10},{9,11},{10,... | collective-permute-start | bytes 614408 | tf_op jit(solution)/shard_map/ppermute | solution.py:345
  6.9 16.6 %collective-permute-start.3 = (bf16[128,1024]{1,0:T(8,128)(2,1)S(1)}, bf16[128,1024]{1,0:T(8,128)(2,1)S(1)}, u32[]{:S(2)}, u32[]{:S(2)}) collective-permute-start(bf16[128,1024]{1,0:T(8,128)(2,1)S(1)} %copy-done.1), channel_id=1, source_target_pairs={{0,1},{1,0},{2,3},{3,2},{4,5},{5,4},{6,7},{7,6},{8,9},{9,8},{10,11... | collective-permute-start | bytes 786440 | tf_op jit(solution)/shard_map/ppermute | solution.py:345
  13.2 1.3 %collective-permute-start.1 = (bf16[128,256]{1,0:T(8,128)(2,1)S(1)}, bf16[128,256]{1,0:T(8,128)(2,1)S(1)}, u32[]{:S(2)}, u32[]{:S(2)}) collective-permute-start(bf16[128,256]{1,0:T(8,128)(2,1)S(1)} %shard_map.157), channel_id=1, source_target_pairs={{0,1},{1,0},{2,3},{3,2},{4,5},{5,4},{6,7},{7,6},{8,9},{9,8},{10,11... | collective-permute-start | bytes 196616 | tf_op jit(solution)/shard_map/ppermute | solution.py:345
  15.2 16.1 %collective-permute-start.5 = (bf16[800,128]{1,0:T(8,128)(2,1)S(1)}, bf16[800,128]{1,0:T(8,128)(2,1)S(1)}, u32[]{:S(2)}, u32[]{:S(2)}) collective-permute-start(bf16[800,128]{1,0:T(8,128)(2,1)S(1)} %shard_map.160.refs_3_), channel_id=1, source_target_pairs={{0,1},{1,0},{2,3},{3,2},{4,5},{5,4},{6,7},{7,6},{8,9},{9,8},{10,11... | collective-permute-start | bytes 614408 | tf_op jit(solution)/shard_map/ppermute | solution.py:345
  15.3 23.3 %collective-permute-start.10 = (bf16[128,1024]{1,0:T(8,128)(2,1)S(1)}, bf16[128,1024]{1,0:T(8,128)(2,1)S(1)}, u32[]{:S(2)}, u32[]{:S(2)}) collective-permute-start(bf16[128,1024]{1,0:T(8,128)(2,1)S(1)} %collective-permute-done.9.refs_0_), channel_id=1, source_target_pairs={{0,1},{1,0},{2,3},{3,2},{4,5},{5,4},{6,7},{7,6},{8,9},{9,8},{10,11... | collective-permute-start | bytes 786440 | tf_op jit(solution)/shard_map/ppermute | solution.py:345
  16.3 7.6 %copy-start.13 = (s32[4,4,8]{2,1,0:T(4,128)S(1)}, s32[4,4,8]{2,1,0:T(4,128)}, u32[]{:S(2)}) copy-start(s32[4,4,8]{2,1,0:T(4,128)} %refs_7_.1) | copy-start | bytes 1540
  16.3 7.6 %copy-start.16 = (s32[256]{0:T(256)S(1)}, s32[256]{0:T(256)}, u32[]{:S(2)}) copy-start(s32[256]{0:T(256)} %param.17) | copy-start | bytes 3076
  16.3 13.5 %all-to-all-start = ((bf16[16,16,128]{2,1,0:T(8,128)(2,1)}), bf16[16,16,128]{2,1,0:T(8,128)(2,1)S(1)}, u32[]{:S(2)}, u32[]{:S(2)}) async-start(bf16[16,16,128]{2,1,0:T(8,128)(2,1)} %shard_map.156), calls=%async_computation | async-start | bytes 131072 | tf_op jit(solution)/shard_map/all_to_all | solution.py:358
  23.0 8.5 %collective-permute-start.7 = (bf16[800,128]{1,0:T(8,128)(2,1)S(1)}, bf16[800,128]{1,0:T(8,128)(2,1)S(1)}, u32[]{:S(2)}, u32[]{:S(2)}) collective-permute-start(bf16[800,128]{1,0:T(8,128)(2,1)S(1)} %collective-permute-done.6.refs_5_), channel_id=1, source_target_pairs={{0,1},{1,0},{2,3},{3,2},{4,5},{5,4},{6,7},{7,6},{8,9},{9,8},{10,11... | collective-permute-start | bytes 614408 | tf_op jit(solution)/shard_map/ppermute | solution.py:345
  23.4 14.0 %collective-permute-start.12 = (bf16[128,512]{1,0:T(8,128)(2,1)S(1)}, bf16[128,512]{1,0:T(8,128)(2,1)S(1)}, u32[]{:S(2)}, u32[]{:S(2)}) collective-permute-start(bf16[128,512]{1,0:T(8,128)(2,1)S(1)} %copy-done.2), channel_id=1, source_target_pairs={{0,1},{1,0},{2,3},{3,2},{4,5},{5,4},{6,7},{7,6},{8,9},{9,8},{10,11... | collective-permute-start | bytes 393224 | tf_op jit(solution)/shard_map/ppermute | solution.py:345
  23.6 13.9 %collective-permute-start.13 = (bf16[128,512]{1,0:T(8,128)(2,1)S(1)}, bf16[128,512]{1,0:T(8,128)(2,1)S(1)}, u32[]{:S(2)}, u32[]{:S(2)}) collective-permute-start(bf16[128,512]{1,0:T(8,128)(2,1)S(1)} %copy-done.3), channel_id=1, source_target_pairs={{0,1},{1,0},{2,3},{3,2},{4,5},{5,4},{6,7},{7,6},{8,9},{9,8},{10,11... | collective-permute-start | bytes 393224 | tf_op jit(solution)/shard_map/ppermute | solution.py:345
  31.2 4.5 %collective-permute-start.4 = (bf16[160,256]{1,0:T(8,128)(2,1)S(1)}, bf16[160,256]{1,0:T(8,128)(2,1)S(1)}, u32[]{:S(2)}, u32[]{:S(2)}) collective-permute-start(bf16[160,256]{1,0:T(8,128)(2,1)S(1)} %get-tuple-element.33.refs_1_), channel_id=1, source_target_pairs={{0,2},{1,3},{2,0},{3,1},{4,6},{5,7},{6,4},{7,5},{8,10},{9,11},{10,... | collective-permute-start | bytes 245768 | tf_op jit(solution)/shard_map/ppermute | solution.py:345
  37.5 1.2 %collective-permute-start.11 = (f32[16,512]{1,0:T(8,128)S(1)}, f32[16,512]{1,0:T(8,128)S(1)}, u32[]{:S(2)}, u32[]{:S(2)}) collective-permute-start(f32[16,512]{1,0:T(8,128)S(1)} %get-tuple-element.37.refs_2_), channel_id=1, source_target_pairs={{0,1},{1,0},{2,3},{3,2},{4,5},{5,4},{6,7},{7,6},{8,9},{9,8},{10,11... | collective-permute-start | bytes 98312 | tf_op jit(solution)/shard_map/ppermute | solution.py:345
  41.2 10.4 %all-to-all-start.1 = ((bf16[16,16,128]{2,1,0:T(8,128)(2,1)}), bf16[16,16,128]{2,1,0:T(8,128)(2,1)S(1)}, u32[]{:S(2)}, u32[]{:S(2)}) async-start(bf16[16,16,128]{2,1,0:T(8,128)(2,1)} %get-tuple-element.53), calls=%async_computation.1 | async-start | bytes 131072 | tf_op jit(solution)/shard_map/all_to_all | solution.py:425
  44.9 4.6 %collective-permute-start.14 = (bf16[128,256]{1,0:T(8,128)(2,1)S(1)}, bf16[128,256]{1,0:T(8,128)(2,1)S(1)}, u32[]{:S(2)}, u32[]{:S(2)}) collective-permute-start(bf16[128,256]{1,0:T(8,128)(2,1)S(1)} %get-tuple-element.47), channel_id=1, source_target_pairs={{0,2},{1,3},{2,0},{3,1},{4,6},{5,7},{6,4},{7,5},{8,10},{9,11},{10,... | collective-permute-start | bytes 196616 | tf_op jit(solution)/shard_map/ppermute | solution.py:345
  46.8 2.8 %collective-permute-start.8 = (bf16[128,128]{1,0:T(8,128)(2,1)S(1)}, bf16[128,128]{1,0:T(8,128)(2,1)S(1)}, u32[]{:S(2)}, u32[]{:S(2)}) collective-permute-start(bf16[128,128]{1,0:T(8,128)(2,1)S(1)} %copy-done.20), channel_id=1, source_target_pairs={{0,1},{1,0},{2,3},{3,2},{4,5},{5,4},{6,7},{7,6},{8,9},{9,8},{10,11... | collective-permute-start | bytes 98312 | tf_op jit(solution)/shard_map/ppermute | solution.py:345
  49.5 1.3 %collective-permute-start.15 = (bf16[128,128]{1,0:T(8,128)(2,1)S(1)}, bf16[128,128]{1,0:T(8,128)(2,1)S(1)}, u32[]{:S(2)}, u32[]{:S(2)}) collective-permute-start(bf16[128,128]{1,0:T(8,128)(2,1)S(1)} %get-tuple-element.49), channel_id=1, source_target_pairs={{0,1},{1,0},{2,3},{3,2},{4,5},{5,4},{6,7},{7,6},{8,9},{9,8},{10,11... | collective-permute-start | bytes 98312 | tf_op jit(solution)/shard_map/ppermute | solution.py:345
  (16 other events, 28.4 us)

commit v17 on v13

--- a/solution.py
+++ b/solution.py
@@ -212,7 +212,8 @@
 
 
 def turn(groups, *refs):
-    far, refs = refs[: 2 * (groups - 1)], refs[2 * (groups - 1) :]
+    count = cores * (groups - 1)
+    far_in, far_out, refs = refs[:count], refs[count : 2 * count], refs[2 * count :]
     aggregate, aggregate2, own, lat_all, extra, take, pick, normed, inverse, edge_pre = refs[:10]
     e_mine, e_other, out_mine, out_other, in_mine, in_other, n_mine, n_other = refs[10:18]
     node_next, dpre_ref, total_ref, spread, next_all, grads = refs[18:]
@@ -227,9 +228,9 @@
     edge_gain, node_gain = gain_rows[0:1], gain_rows[1:2]
 
     from_agg = jnp.concatenate(
-        [in_mine[:, features:], in_other[:, features:]] + [f[:, :features] for f in far], axis=0
-    )
-    to_out = jnp.concatenate([n_mine[...], n_other[...]] + [f[:, features:] for f in far], axis=0)
+        [in_mine[:, features:], in_other[:, features:]] + [f[...] for f in far_in], axis=0
+    )
+    to_out = jnp.concatenate([n_mine[...], n_other[...]] + [f[...] for f in far_out], axis=0)
     together = (aggregate[...] + aggregate2[...]).astype(bf16)
     pre = lat_all[...] + dot_rows(together, from_agg)
     act = (pre * sigmoid(pre)).astype(bf16)
@@ -355,9 +356,9 @@
     e_out = (edge_out_weight, over_cores(edge_out_weight))
     n_in = (node_in_weight, over_cores(node_in_weight))
     n_out = (node_out_weight, over_cores(node_out_weight))
-    far = []
-    for weights in over_groups(jnp.concatenate([node_in_weight[:, features:], node_out_weight], axis=1)):
-        far += [weights, over_cores(weights)]
+    far_out = [part for came in over_groups(node_out_weight) for part in (came, over_cores(came))]
+    far_in = [part for came in over_groups(node_in_weight[:, features:]) for part in (came, over_cores(came))]
+    far = far_in + far_out
     (sent,) = stage(functools.partial(send_half, groups), [((half, groups * width), bf16)], states)
     state, pre, pick, take = stage(
         functools.partial(prepare_edges, groups),

time: 40.9 us -> 48 us (1.17)
  starting transfers between devices: 18.8 us -> 22.6 us
  waiting for transfers between devices: 11.9 us -> 13.8 us
  local copies, waits for them, and re-layouts: 2.48 us -> 3.9 us
    ppermute x15 -> x17, waiting for transfers between devices: 10.2 us -> 13.8 us  [swapped(): return lax.ppermute(values, 'feat', [(i, i ^ bits) for i in range(feats)])]
    all_to_all x1, starting transfers between devices: 3.5 us -> 5.24 us  [shards(): shares = lax.all_to_all(spread, everyone, 0, 0)]
    all_to_all x1, waiting for transfers between devices: 1.69 us -> 0.01 us  [shards(): latents = lax.all_to_all(spread, everyone, 0, 0)]
    ppermute x15 -> x17, starting transfers between devices: 9.71 us -> 11 us  [swapped(): return lax.ppermute(values, 'feat', [(i, i ^ bits) for i in range(feats)])]
    unnamed x26 -> x28, local copies, waits for them, and re-layouts: 2.11 us -> 2.94 us
    all_to_all x1, starting transfers between devices: 5.61 us -> 6.35 us  [shards(): latents = lax.all_to_all(spread, everyone, 0, 0)]
    slice x2 -> x1, local copies, waits for them, and re-layouts: 0.37 us -> 0.97 us  [shards(): node_in_weight[:, features:]]
  transfers between devices with their start and end apart: 17 -> 19, of which waited for: 8 -> 8; matrix products, arithmetic and copies ran while one was open for 0% -> 2% of each run, Pallas kernels for 8% -> 7%
where the time goes in v17:
time: 48 us; the launch traced here: 47.6 us
  starting transfers between devices  22.6 us (47%)
  waiting for transfers between devices  13.8 us (29%)
  Pallas kernels  6.44 us (13%)
  local copies, waits for them, and re-layouts  3.9 us (8%)
  between operations  0.83 us (2%)
    ppermute x17, waiting for transfers between devices, swapped(): return lax.ppermute(values, 'feat', [(i, i ^ bits) for i in range(feats)])  13.8 us
    ppermute x17, starting transfers between devices, swapped(): return lax.ppermute(values, 'feat', [(i, i ^ bits) for i in range(feats)])  11 us
    pallas_call x12, Pallas kernels, stage(): pl.pallas_call(kernel, out_shape=[jax.ShapeDtypeStruct(shape, kind) for s...  6.44 us
    all_to_all x1, starting transfers between devices, shards(): latents = lax.all_to_all(spread, everyone, 0, 0)  6.35 us
    all_to_all x1, starting transfers between devices, shards(): shares = lax.all_to_all(spread, everyone, 0, 0)  5.24 us
    unnamed x28, local copies, waits for them, and re-layouts  2.94 us
    slice x1, local copies, waits for them, and re-layouts, shards(): node_in_weight[:, features:]  0.97 us
  transfers between devices with their start and end apart: 19, of which 8 were waited for; matrix products, arithmetic and copies ran while one was open for 2% of the time, Pallas kernels for 7%

profile of v17, /device:TPU:0, one launch (start us, length us, event | category | flops | bytes accessed | tf_op | source)
XLA Modules:
  0.0 47.6 jit_solution(10462451536633100957)
XLA Ops:
  1.2 2.9 %collective-permute-start = (bf16[256,128]{1,0:T(8,128)(2,1)}, bf16[256,128]{1,0:T(8,128)(2,1)S(1)}, u32[]{:S(2)}, u32[]{:S(2)}) collective-permute-start(bf16[256,128]{1,0:T(8,128)(2,1)} %refs_0_.3), channel_id=1, source_target_pairs={{0,2},{1,3},{2,0},{3,1},{4,6},{5,7},{6,4},{7,5},{8,10},{9,11},{10,... | collective-permute-start | bytes 196616 | tf_op jit(solution)/shard_map/ppermute | solution.py:340
  4.2 2.5 %collective-permute-done.refs_1_ = bf16[256,128]{1,0:T(8,128)(2,1)S(1)} collective-permute-done((bf16[256,128]{1,0:T(8,128)(2,1)}, bf16[256,128]{1,0:T(8,128)(2,1)S(1)}, u32[]{:S(2)}, u32[]{:S(2)}) %collective-permute-start) | collective-permute-done | bytes 65568 | tf_op jit(solution)/shard_map/ppermute | solution.py:340
  6.7 0.8 %copy-done.3 = bf16[256,128]{1,0:T(8,128)(2,1)S(1)} copy-done((bf16[256,128]{1,0:T(8,128)(2,1)S(1)}, bf16[256,128]{1,0:T(8,128)(2,1)}, u32[]{:S(2)}) %copy-start.3) | copy-done | bytes 65560
  8.1 0.7 %copy-done.9 = bf16[16,128]{1,0:T(8,128)(2,1)S(1)} copy-done((bf16[16,128]{1,0:T(8,128)(2,1)S(1)}, bf16[16,128]{1,0:T(8,128)(2,1)}, u32[]{:S(2)}) %copy-start.9) | copy-done | bytes 4120
  8.8 0.6 %shard_map.156 = bf16[16,16,128]{2,1,0:T(8,128)(2,1)} custom-call(bf16[16,128]{1,0:T(8,128)(2,1)S(1)} %copy-done.9), custom_call_target="tpu_custom_call" | custom-call | flops 16777216 | bytes 4096 | tf_op jit(solution)/shard_map/pallas_call | solution.py:73
  9.5 6.4 %all-to-all-start = ((bf16[16,16,128]{2,1,0:T(8,128)(2,1)}), bf16[16,16,128]{2,1,0:T(8,128)(2,1)S(1)}, u32[]{:S(2)}, u32[]{:S(2)}) async-start(bf16[16,16,128]{2,1,0:T(8,128)(2,1)} %shard_map.156), calls=%async_computation | async-start | bytes 131072 | tf_op jit(solution)/shard_map/all_to_all | solution.py:353
  15.9 1.0 %slice.3 = bf16[128,512]{1,0:T(8,128)(2,1)S(1)} slice(bf16[128,1024]{1,0:T(8,128)(2,1)} %refs_18_.1), slice={[0:128], [512:1024]} | slice | bytes 262144 | tf_op jit(solution)/shard_map/slice | solution.py:360
  16.8 2.0 %collective-permute-start.9 = (bf16[128,512]{1,0:T(8,128)(2,1)S(1)}, bf16[128,512]{1,0:T(8,128)(2,1)S(1)}, u32[]{:S(2)}, u32[]{:S(2)}) collective-permute-start(bf16[128,512]{1,0:T(8,128)(2,1)S(1)} %slice.3), channel_id=1, source_target_pairs={{0,2},{1,3},{2,0},{3,1},{4,6},{5,7},{6,4},{7,5},{8,10},{9,11},{10,... | collective-permute-start | bytes 393224 | tf_op jit(solution)/shard_map/ppermute | solution.py:340
  18.9 0.6 %copy-done.12 = bf16[128]{0:T(256)(128)(2,1)S(1)} copy-done((bf16[128]{0:T(256)(128)(2,1)S(1)}, bf16[128]{0:T(256)(128)(2,1)}, u32[]{:S(2)}) %copy-start.12) | copy-done | bytes 280
  19.6 2.0 %collective-permute-start.6 = (bf16[288,128]{1,0:T(8,128)(2,1)S(1)}, bf16[288,128]{1,0:T(8,128)(2,1)S(1)}, u32[]{:S(2)}, u32[]{:S(2)}) collective-permute-start(bf16[288,128]{1,0:T(8,128)(2,1)S(1)} %shard_map.160.refs_0_.refs_3_), channel_id=1, source_target_pairs={{0,2},{1,3},{2,0},{3,1},{4,6},{5,7},{6,4},{7,5},{8,10},{9,11},{10,... | collective-permute-start | bytes 221192 | tf_op jit(solution)/shard_map/ppermute | solution.py:340
  21.6 0.7 %copy-done.10 = s32[256]{0:T(256)S(1)} copy-done((s32[256]{0:T(256)S(1)}, s32[256]{0:T(256)}, u32[]{:S(2)}) %copy-start.10) | copy-done | bytes 1048
  22.3 0.9 %shard_map.158 = (bf16[128,512]{1,0:T(8,128)(2,1)S(1)}, f32[128,256]{1,0:T(8,128)S(1)}, bf16[64,128]{1,0:T(8,128)(2,1)S(1)}, bf16[16,128]{1,0:T(8,128)(2,1)S(1)}) custom-call(bf16[256,128]{1,0:T(8,128)(2,1)S(1)} %copy-done.4, bf16[256,128]{1,0:T(8,128)(2,1)S(1)} %collective-permute-done.refs_1_, bf16[128,256]{1,0:T(8,128)(2,1)S(1)} %collective-permute-done.1.refs_2_, ...), custom_call_target="tpu_custom_call" | custom-call | flops 16777216 | bytes 985600 | tf_op jit(solution)/shard_map/pallas_call | solution.py:73
  23.3 0.6 %shard_map.159 = (f32[128,256]{1,0:T(8,128)S(1)}, f32[128,512]{1,0:T(8,128)S(1)}, bf16[144,512]{1,0:T(8,128)(2,1)S(1)}, bf16[16,512]{1,0:T(8,128)(2,1)S(1)}, f32[16,256]{1,0:T(8,128)S(1)}) custom-call(bf16[16,16,128]{2,1,0:T(8,128)(2,1)S(1)} %all-to-all-done.came, f32[128,256]{1,0:T(8,128)S(1)} %get-tuple-element.30.pre, ...), custom_call_target="tpu_custom_call" | custom-call | flops 16777216 | bytes 1789952 | tf_op jit(solution)/shard_map/pallas_call | solution.py:73
  24.6 1.8 %collective-permute-done.11.refs_2_ = bf16[128,512]{1,0:T(8,128)(2,1)S(1)} collective-permute-done((bf16[128,512]{1,0:T(8,128)(2,1)S(1)}, bf16[128,512]{1,0:T(8,128)(2,1)S(1)}, u32[]{:S(2)}, u32[]{:S(2)}) %collective-permute-start.11) | collective-permute-done | bytes 131104 | tf_op jit(solution)/shard_map/ppermute | solution.py:340
  26.4 1.6 %collective-permute-done.6.refs_1_.refs_4_ = bf16[288,128]{1,0:T(8,128)(2,1)S(1)} collective-permute-done((bf16[288,128]{1,0:T(8,128)(2,1)S(1)}, bf16[288,128]{1,0:T(8,128)(2,1)S(1)}, u32[]{:S(2)}, u32[]{:S(2)}) %collective-permute-start.6) | collective-permute-done | bytes 73760 | tf_op jit(solution)/shard_map/ppermute | solution.py:340
  28.1 1.3 %collective-permute-done.7.refs_5_ = bf16[160,256]{1,0:T(8,128)(2,1)S(1)} collective-permute-done((bf16[160,256]{1,0:T(8,128)(2,1)S(1)}, bf16[160,256]{1,0:T(8,128)(2,1)S(1)}, u32[]{:S(2)}, u32[]{:S(2)}) %collective-permute-start.7) | collective-permute-done | bytes 81952 | tf_op jit(solution)/shard_map/ppermute | solution.py:340
  29.3 1.4 %collective-permute-done.5.refs_2_ = bf16[144,512]{1,0:T(8,128)(2,1)S(1)} collective-permute-done((bf16[144,512]{1,0:T(8,128)(2,1)S(1)}, bf16[144,512]{1,0:T(8,128)(2,1)S(1)}, u32[]{:S(2)}, u32[]{:S(2)}) %collective-permute-start.5) | collective-permute-done | bytes 147488 | tf_op jit(solution)/shard_map/ppermute | solution.py:340
  31.1 1.2 %collective-permute-done.13.refs_5_ = f32[16,512]{1,0:T(8,128)S(1)} collective-permute-done((f32[16,512]{1,0:T(8,128)S(1)}, f32[16,512]{1,0:T(8,128)S(1)}, u32[]{:S(2)}, u32[]{:S(2)}) %collective-permute-start.13) | collective-permute-done | bytes 32800 | tf_op jit(solution)/shard_map/ppermute | solution.py:340
  32.2 2.5 %shard_map.163 = (bf16[16,128]{1,0:T(8,128)(2,1)}, bf16[128,256]{1,0:T(8,128)(2,1)S(1)}, f32[128,512]{1,0:T(8,128)S(1)}, bf16[16,16,128]{2,1,0:T(8,128)(2,1)}) custom-call(bf16[128,512]{1,0:T(8,128)(2,1)S(1)} %collective-permute-done.9.refs_0_, bf16[128,512]{1,0:T(8,128)(2,1)S(1)} %collective-permute-done.10.refs_1_, ...), custom_call_target="tpu_custom_call" | custom-call | flops 16777216 | bytes 3052032 | tf_op jit(solution)/shard_map/pallas_call | solution.py:73
  34.7 5.2 %all-to-all-start.1 = ((bf16[16,16,128]{2,1,0:T(8,128)(2,1)}), bf16[16,16,128]{2,1,0:T(8,128)(2,1)S(1)}, u32[]{:S(2)}, u32[]{:S(2)}) async-start(bf16[16,16,128]{2,1,0:T(8,128)(2,1)} %get-tuple-element.55), calls=%async_computation.1 | async-start | bytes 131072 | tf_op jit(solution)/shard_map/all_to_all | solution.py:421
  40.2 2.0 %collective-permute-start.15 = (bf16[128,256]{1,0:T(8,128)(2,1)S(1)}, bf16[128,256]{1,0:T(8,128)(2,1)S(1)}, u32[]{:S(2)}, u32[]{:S(2)}) collective-permute-start(bf16[128,256]{1,0:T(8,128)(2,1)S(1)} %get-tuple-element.49), channel_id=1, source_target_pairs={{0,2},{1,3},{2,0},{3,1},{4,6},{5,7},{6,4},{7,5},{8,10},{9,11},{10,... | collective-permute-start | bytes 196616 | tf_op jit(solution)/shard_map/ppermute | solution.py:340
  42.2 2.8 %collective-permute-done.15.refs_1_ = bf16[128,256]{1,0:T(8,128)(2,1)S(1)} collective-permute-done((bf16[128,256]{1,0:T(8,128)(2,1)S(1)}, bf16[128,256]{1,0:T(8,128)(2,1)S(1)}, u32[]{:S(2)}, u32[]{:S(2)}) %collective-permute-start.15) | collective-permute-done | bytes 65568 | tf_op jit(solution)/shard_map/ppermute | solution.py:340
  45.1 1.2 %collective-permute-done.16.grad_came = bf16[128,128]{1,0:T(8,128)(2,1)S(1)} collective-permute-done((bf16[128,128]{1,0:T(8,128)(2,1)S(1)}, bf16[128,128]{1,0:T(8,128)(2,1)S(1)}, u32[]{:S(2)}, u32[]{:S(2)}) %collective-permute-start.16) | collective-permute-done | bytes 32800 | tf_op jit(solution)/shard_map/ppermute | solution.py:340
  46.3 0.7 %shard_map.166 = (bf16[256,128]{1,0:T(8,128)(2,1)}, bf16[256,128]{1,0:T(8,128)(2,1)}) custom-call(bf16[128,128]{1,0:T(8,128)(2,1)S(1)} %get-tuple-element.37.next_mine, bf16[128,128]{1,0:T(8,128)(2,1)S(1)} %collective-permute-done.8.next_came, bf16[128,128]{1,0:T(8,128)(2,1)S(1)} %get-tuple-element.50.grad_mine, ...), custom_call_target="tpu_custom_call" | custom-call | flops 16777216 | bytes 131072 | tf_op jit(solution)/shard_map/pallas_call | solution.py:73
  (55 shorter events, 3.4 us)
Async XLA Ops:
  0.6 21.0 %copy-start = (bf16[128,1536]{1,0:T(8,128)(2,1)S(1)}, bf16[128,1536]{1,0:T(8,128)(2,1)}, u32[]{:S(2)}) copy-start(bf16[128,1536]{1,0:T(8,128)(2,1)} %e_mine.1) | copy-start | bytes 1179652
  0.6 19.0 %collective-permute-start.2 = (bf16[128,1536]{1,0:T(8,128)(2,1)}, bf16[128,1536]{1,0:T(8,128)(2,1)S(1)}, u32[]{:S(2)}, u32[]{:S(2)}) collective-permute-start(bf16[128,1536]{1,0:T(8,128)(2,1)} %e_mine.1), channel_id=1, source_target_pairs={{0,1},{1,0},{2,3},{3,2},{4,5},{5,4},{6,7},{7,6},{8,9},{9,8},{10,11... | collective-permute-start | bytes 1179656 | tf_op jit(solution)/shard_map/ppermute | solution.py:340
  1.2 22.1 %collective-permute-start.4 = (bf16[128,1024]{1,0:T(8,128)(2,1)}, bf16[128,1024]{1,0:T(8,128)(2,1)S(1)}, u32[]{:S(2)}, u32[]{:S(2)}) collective-permute-start(bf16[128,1024]{1,0:T(8,128)(2,1)} %refs_18_.1), channel_id=1, source_target_pairs={{0,1},{1,0},{2,3},{3,2},{4,5},{5,4},{6,7},{7,6},{8,9},{9,8},{10,11... | collective-permute-start | bytes 786440 | tf_op jit(solution)/shard_map/ppermute | solution.py:340
  1.2 5.5 %collective-permute-start = (bf16[256,128]{1,0:T(8,128)(2,1)}, bf16[256,128]{1,0:T(8,128)(2,1)S(1)}, u32[]{:S(2)}, u32[]{:S(2)}) collective-permute-start(bf16[256,128]{1,0:T(8,128)(2,1)} %refs_0_.3), channel_id=1, source_target_pairs={{0,2},{1,3},{2,0},{3,1},{4,6},{5,7},{6,4},{7,5},{8,10},{9,11},{10,... | collective-permute-start | bytes 196616 | tf_op jit(solution)/shard_map/ppermute | solution.py:340
  7.6 11.3 %collective-permute-start.1 = (bf16[128,256]{1,0:T(8,128)(2,1)S(1)}, bf16[128,256]{1,0:T(8,128)(2,1)S(1)}, u32[]{:S(2)}, u32[]{:S(2)}) collective-permute-start(bf16[128,256]{1,0:T(8,128)(2,1)S(1)} %shard_map.157), channel_id=1, source_target_pairs={{0,1},{1,0},{2,3},{3,2},{4,5},{5,4},{6,7},{7,6},{8,9},{9,8},{10,11... | collective-permute-start | bytes 196616 | tf_op jit(solution)/shard_map/ppermute | solution.py:340
  7.6 15.6 %collective-permute-start.3 = (bf16[128,512]{1,0:T(8,128)(2,1)}, bf16[128,512]{1,0:T(8,128)(2,1)S(1)}, u32[]{:S(2)}, u32[]{:S(2)}) collective-permute-start(bf16[128,512]{1,0:T(8,128)(2,1)} %refs_16_.1), channel_id=1, source_target_pairs={{0,1},{1,0},{2,3},{3,2},{4,5},{5,4},{6,7},{7,6},{8,9},{9,8},{10,11... | collective-permute-start | bytes 393224 | tf_op jit(solution)/shard_map/ppermute | solution.py:340
  9.5 13.7 %all-to-all-start = ((bf16[16,16,128]{2,1,0:T(8,128)(2,1)}), bf16[16,16,128]{2,1,0:T(8,128)(2,1)S(1)}, u32[]{:S(2)}, u32[]{:S(2)}) async-start(bf16[16,16,128]{2,1,0:T(8,128)(2,1)} %shard_map.156), calls=%async_computation | async-start | bytes 131072 | tf_op jit(solution)/shard_map/all_to_all | solution.py:353
  15.8 3.0 %copy-start.5 = (bf16[128,512]{1,0:T(8,128)(2,1)S(1)}, bf16[128,512]{1,0:T(8,128)(2,1)}, u32[]{:S(2)}) copy-start(bf16[128,512]{1,0:T(8,128)(2,1)} %refs_20_.1) | copy-start | bytes 393220
  15.8 3.1 %copy-start.6 = (bf16[256,128]{1,0:T(8,128)(2,1)S(1)}, bf16[256,128]{1,0:T(8,128)(2,1)}, u32[]{:S(2)}) copy-start(bf16[256,128]{1,0:T(8,128)(2,1)} %edge_cot.1) | copy-start | bytes 196612
  15.8 3.1 %copy-start.7 = (bf16[16,128]{1,0:T(8,128)(2,1)S(1)}, bf16[16,128]{1,0:T(8,128)(2,1)}, u32[]{:S(2)}) copy-start(bf16[16,128]{1,0:T(8,128)(2,1)} %node_cot.3) | copy-start | bytes 12292
  16.8 7.2 %collective-permute-start.9 = (bf16[128,512]{1,0:T(8,128)(2,1)S(1)}, bf16[128,512]{1,0:T(8,128)(2,1)S(1)}, u32[]{:S(2)}, u32[]{:S(2)}) collective-permute-start(bf16[128,512]{1,0:T(8,128)(2,1)S(1)} %slice.3), channel_id=1, source_target_pairs={{0,2},{1,3},{2,0},{3,1},{4,6},{5,7},{6,4},{7,5},{8,10},{9,11},{10,... | collective-permute-start | bytes 393224 | tf_op jit(solution)/shard_map/ppermute | solution.py:340
  18.8 7.6 %collective-permute-start.11 = (bf16[128,512]{1,0:T(8,128)(2,1)S(1)}, bf16[128,512]{1,0:T(8,128)(2,1)S(1)}, u32[]{:S(2)}, u32[]{:S(2)}) collective-permute-start(bf16[128,512]{1,0:T(8,128)(2,1)S(1)} %copy-done.5), channel_id=1, source_target_pairs={{0,2},{1,3},{2,0},{3,1},{4,6},{5,7},{6,4},{7,5},{8,10},{9,11},{10,... | collective-permute-start | bytes 393224 | tf_op jit(solution)/shard_map/ppermute | solution.py:340
  19.6 2.0 %copy-start.11 = (s32[256]{0:T(256)S(1)}, s32[256]{0:T(256)}, u32[]{:S(2)}) copy-start(s32[256]{0:T(256)} %param.17) | copy-start | bytes 3076
  19.6 8.4 %collective-permute-start.6 = (bf16[288,128]{1,0:T(8,128)(2,1)S(1)}, bf16[288,128]{1,0:T(8,128)(2,1)S(1)}, u32[]{:S(2)}, u32[]{:S(2)}) collective-permute-start(bf16[288,128]{1,0:T(8,128)(2,1)S(1)} %shard_map.160.refs_0_.refs_3_), channel_id=1, source_target_pairs={{0,2},{1,3},{2,0},{3,1},{4,6},{5,7},{6,4},{7,5},{8,10},{9,11},{10,... | collective-permute-start | bytes 221192 | tf_op jit(solution)/shard_map/ppermute | solution.py:340
  23.9 6.9 %collective-permute-start.5 = (bf16[144,512]{1,0:T(8,128)(2,1)S(1)}, bf16[144,512]{1,0:T(8,128)(2,1)S(1)}, u32[]{:S(2)}, u32[]{:S(2)}) collective-permute-start(bf16[144,512]{1,0:T(8,128)(2,1)S(1)} %get-tuple-element.35), channel_id=1, source_target_pairs={{0,2},{1,3},{2,0},{3,1},{4,6},{5,7},{6,4},{7,5},{8,10},{9,11},{10,... | collective-permute-start | bytes 442376 | tf_op jit(solution)/shard_map/ppermute | solution.py:340
  24.0 7.0 %collective-permute-start.14 = (bf16[128,512]{1,0:T(8,128)(2,1)S(1)}, bf16[128,512]{1,0:T(8,128)(2,1)S(1)}, u32[]{:S(2)}, u32[]{:S(2)}) collective-permute-start(bf16[128,512]{1,0:T(8,128)(2,1)S(1)} %copy-done.5), channel_id=1, source_target_pairs={{0,1},{1,0},{2,3},{3,2},{4,5},{5,4},{6,7},{7,6},{8,9},{9,8},{10,11... | collective-permute-start | bytes 393224 | tf_op jit(solution)/shard_map/ppermute | solution.py:340
  24.0 7.0 %collective-permute-start.10 = (bf16[128,512]{1,0:T(8,128)(2,1)S(1)}, bf16[128,512]{1,0:T(8,128)(2,1)S(1)}, u32[]{:S(2)}, u32[]{:S(2)}) collective-permute-start(bf16[128,512]{1,0:T(8,128)(2,1)S(1)} %collective-permute-done.9.refs_0_), channel_id=1, source_target_pairs={{0,1},{1,0},{2,3},{3,2},{4,5},{5,4},{6,7},{7,6},{8,9},{9,8},{10,11... | collective-permute-start | bytes 393224 | tf_op jit(solution)/shard_map/ppermute | solution.py:340
  26.4 4.6 %collective-permute-start.12 = (bf16[128,512]{1,0:T(8,128)(2,1)S(1)}, bf16[128,512]{1,0:T(8,128)(2,1)S(1)}, u32[]{:S(2)}, u32[]{:S(2)}) collective-permute-start(bf16[128,512]{1,0:T(8,128)(2,1)S(1)} %collective-permute-done.11.refs_2_), channel_id=1, source_target_pairs={{0,1},{1,0},{2,3},{3,2},{4,5},{5,4},{6,7},{7,6},{8,9},{9,8},{10,11... | collective-permute-start | bytes 393224 | tf_op jit(solution)/shard_map/ppermute | solution.py:340
  28.0 1.3 %collective-permute-start.7 = (bf16[160,256]{1,0:T(8,128)(2,1)S(1)}, bf16[160,256]{1,0:T(8,128)(2,1)S(1)}, u32[]{:S(2)}, u32[]{:S(2)}) collective-permute-start(bf16[160,256]{1,0:T(8,128)(2,1)S(1)} %shard_map.161), channel_id=1, source_target_pairs={{0,1},{1,0},{2,3},{3,2},{4,5},{5,4},{6,7},{7,6},{8,9},{9,8},{10,11... | collective-permute-start | bytes 245768 | tf_op jit(solution)/shard_map/ppermute | solution.py:340
  31.0 1.2 %collective-permute-start.13 = (f32[16,512]{1,0:T(8,128)S(1)}, f32[16,512]{1,0:T(8,128)S(1)}, u32[]{:S(2)}, u32[]{:S(2)}) collective-permute-start(f32[16,512]{1,0:T(8,128)S(1)} %get-tuple-element.39.refs_4_), channel_id=1, source_target_pairs={{0,1},{1,0},{2,3},{3,2},{4,5},{5,4},{6,7},{7,6},{8,9},{9,8},{10,11... | collective-permute-start | bytes 98312 | tf_op jit(solution)/shard_map/ppermute | solution.py:340
  34.7 12.2 %all-to-all-start.1 = ((bf16[16,16,128]{2,1,0:T(8,128)(2,1)}), bf16[16,16,128]{2,1,0:T(8,128)(2,1)S(1)}, u32[]{:S(2)}, u32[]{:S(2)}) async-start(bf16[16,16,128]{2,1,0:T(8,128)(2,1)} %get-tuple-element.55), calls=%async_computation.1 | async-start | bytes 131072 | tf_op jit(solution)/shard_map/all_to_all | solution.py:421
  40.2 4.8 %collective-permute-start.15 = (bf16[128,256]{1,0:T(8,128)(2,1)S(1)}, bf16[128,256]{1,0:T(8,128)(2,1)S(1)}, u32[]{:S(2)}, u32[]{:S(2)}) collective-permute-start(bf16[128,256]{1,0:T(8,128)(2,1)S(1)} %get-tuple-element.49), channel_id=1, source_target_pairs={{0,2},{1,3},{2,0},{3,1},{4,6},{5,7},{6,4},{7,5},{8,10},{9,11},{10,... | collective-permute-start | bytes 196616 | tf_op jit(solution)/shard_map/ppermute | solution.py:340
  42.2 2.9 %collective-permute-start.8 = (bf16[128,128]{1,0:T(8,128)(2,1)S(1)}, bf16[128,128]{1,0:T(8,128)(2,1)S(1)}, u32[]{:S(2)}, u32[]{:S(2)}) collective-permute-start(bf16[128,128]{1,0:T(8,128)(2,1)S(1)} %get-tuple-element.38), channel_id=1, source_target_pairs={{0,1},{1,0},{2,3},{3,2},{4,5},{5,4},{6,7},{7,6},{8,9},{9,8},{10,11... | collective-permute-start | bytes 98312 | tf_op jit(solution)/shard_map/ppermute | solution.py:340
  45.0 1.3 %collective-permute-start.16 = (bf16[128,128]{1,0:T(8,128)(2,1)S(1)}, bf16[128,128]{1,0:T(8,128)(2,1)S(1)}, u32[]{:S(2)}, u32[]{:S(2)}) collective-permute-start(bf16[128,128]{1,0:T(8,128)(2,1)S(1)} %get-tuple-element.51), channel_id=1, source_target_pairs={{0,1},{1,0},{2,3},{3,2},{4,5},{5,4},{6,7},{7,6},{8,9},{9,8},{10,11... | collective-permute-start | bytes 98312 | tf_op jit(solution)/shard_map/ppermute | solution.py:340
  (9 other events, 9.5 us)

commit v18 on v13

--- a/solution.py
+++ b/solution.py
@@ -256,8 +256,7 @@
     def weighted(values, index):
         columns = slice(index * features, (index + 1) * features)
         weight = jnp.concatenate([e_mine[:, columns], e_other[:, columns]], axis=0)
-        both = dot(jnp.concatenate(split(values), axis=0), weight)
-        return both[: values.shape[0]] + both[values.shape[0] :]
+        return dot(values.astype(bf16), weight)
 
     grads[...] = weighted(dot(pick[...], dpre), 1)
     home = weighted(dot(taken, dpre), 2)

time: 40.9 us -> 40.8 us (level)
  no operation moved by 1% of the time
where the time goes in v18:
time: 40.8 us; the launch traced here: 40.4 us
  starting transfers between devices  18.8 us (46%)
  waiting for transfers between devices  11.9 us (29%)
  Pallas kernels  6.4 us (16%)
  local copies, waits for them, and re-layouts  2.48 us (6%)
  between operations  0.79 us (2%)
    ppermute x15, waiting for transfers between devices, swapped(): return lax.ppermute(values, 'feat', [(i, i ^ bits) for i in range(feats)])  10.2 us
    ppermute x15, starting transfers between devices, swapped(): return lax.ppermute(values, 'feat', [(i, i ^ bits) for i in range(feats)])  9.7 us
    pallas_call x12, Pallas kernels, stage(): pl.pallas_call(kernel, out_shape=[jax.ShapeDtypeStruct(shape, kind) for s...  6.4 us
    all_to_all x1, starting transfers between devices, shards(): latents = lax.all_to_all(spread, everyone, 0, 0)  5.61 us
    all_to_all x1, starting transfers between devices, shards(): shares = lax.all_to_all(spread, everyone, 0, 0)  3.5 us
    unnamed x26, local copies, waits for them, and re-layouts  2.11 us
    all_to_all x1, waiting for transfers between devices, shards(): latents = lax.all_to_all(spread, everyone, 0, 0)  1.69 us
  transfers between devices with their start and end apart: 17, of which 8 were waited for; matrix products, arithmetic and copies ran while one was open for 0% of the time, Pallas kernels for 8%

profile of v18, /device:TPU:0, one launch (start us, length us, event | category | flops | bytes accessed | tf_op | source)
XLA Modules:
  0.0 40.4 jit_solution(13979051938859874161)
XLA Ops:
  0.7 0.5 %collective-permute-start.2 = (bf16[128,1536]{1,0:T(8,128)(2,1)}, bf16[128,1536]{1,0:T(8,128)(2,1)S(1)}, u32[]{:S(2)}, u32[]{:S(2)}) collective-permute-start(bf16[128,1536]{1,0:T(8,128)(2,1)} %e_mine.1), channel_id=1, source_target_pairs={{0,1},{1,0},{2,3},{3,2},{4,5},{5,4},{6,7},{7,6},{8,9},{9,8},{10,11... | collective-permute-start | bytes 1179656 | tf_op jit(solution)/shard_map/ppermute | solution.py:338
  1.7 3.0 %collective-permute-start.9 = (bf16[128,1024]{1,0:T(8,128)(2,1)S(1)}, bf16[128,1024]{1,0:T(8,128)(2,1)S(1)}, u32[]{:S(2)}, u32[]{:S(2)}) collective-permute-start(bf16[128,1024]{1,0:T(8,128)(2,1)S(1)} %pad_maximum_fusion), channel_id=1, source_target_pairs={{0,2},{1,3},{2,0},{3,1},{4,6},{5,7},{6,4},{7,5},{8,10},{9,11},{10,... | collective-permute-start | bytes 786440 | tf_op jit(solution)/shard_map/ppermute | solution.py:338
  4.7 0.8 %collective-permute-start = (bf16[256,128]{1,0:T(8,128)(2,1)S(1)}, bf16[256,128]{1,0:T(8,128)(2,1)S(1)}, u32[]{:S(2)}, u32[]{:S(2)}) collective-permute-start(bf16[256,128]{1,0:T(8,128)(2,1)S(1)} %copy-done.4), channel_id=1, source_target_pairs={{0,2},{1,3},{2,0},{3,1},{4,6},{5,7},{6,4},{7,5},{8,10},{9,11},{10,... | collective-permute-start | bytes 196616 | tf_op jit(solution)/shard_map/ppermute | solution.py:338
  5.7 0.7 %copy-done.8 = bf16[16,128]{1,0:T(8,128)(2,1)S(1)} copy-done((bf16[16,128]{1,0:T(8,128)(2,1)S(1)}, bf16[16,128]{1,0:T(8,128)(2,1)}, u32[]{:S(2)}) %copy-start.8) | copy-done | bytes 4120
  6.4 0.6 %shard_map.156 = bf16[16,16,128]{2,1,0:T(8,128)(2,1)} custom-call(bf16[16,128]{1,0:T(8,128)(2,1)S(1)} %copy-done.8), custom_call_target="tpu_custom_call" | custom-call | flops 16777216 | bytes 4096 | tf_op jit(solution)/shard_map/pallas_call | solution.py:73
  7.1 5.6 %all-to-all-start = ((bf16[16,16,128]{2,1,0:T(8,128)(2,1)}), bf16[16,16,128]{2,1,0:T(8,128)(2,1)S(1)}, u32[]{:S(2)}, u32[]{:S(2)}) async-start(bf16[16,16,128]{2,1,0:T(8,128)(2,1)} %shard_map.156), calls=%async_computation | async-start | bytes 131072 | tf_op jit(solution)/shard_map/all_to_all | solution.py:351
  12.7 0.5 %collective-permute-start.10 = (bf16[128,1024]{1,0:T(8,128)(2,1)S(1)}, bf16[128,1024]{1,0:T(8,128)(2,1)S(1)}, u32[]{:S(2)}, u32[]{:S(2)}) collective-permute-start(bf16[128,1024]{1,0:T(8,128)(2,1)S(1)} %collective-permute-done.9.refs_0_), channel_id=1, source_target_pairs={{0,1},{1,0},{2,3},{3,2},{4,5},{5,4},{6,7},{7,6},{8,9},{9,8},{10,11... | collective-permute-start | bytes 786440 | tf_op jit(solution)/shard_map/ppermute | solution.py:338
  13.4 0.5 %copy-done.6 = bf16[16,128]{1,0:T(8,128)(2,1)S(1)} copy-done((bf16[16,128]{1,0:T(8,128)(2,1)S(1)}, bf16[16,128]{1,0:T(8,128)(2,1)}, u32[]{:S(2)}) %copy-start.6) | copy-done | bytes 4120
  14.5 1.8 %collective-permute-start.6 = (bf16[288,128]{1,0:T(8,128)(2,1)S(1)}, bf16[288,128]{1,0:T(8,128)(2,1)S(1)}, u32[]{:S(2)}, u32[]{:S(2)}) collective-permute-start(bf16[288,128]{1,0:T(8,128)(2,1)S(1)} %shard_map.160.refs_0_.refs_3_), channel_id=1, source_target_pairs={{0,2},{1,3},{2,0},{3,1},{4,6},{5,7},{6,4},{7,5},{8,10},{9,11},{10,... | collective-permute-start | bytes 221192 | tf_op jit(solution)/shard_map/ppermute | solution.py:338
  16.3 0.7 %copy-done.9 = s32[256]{0:T(256)S(1)} copy-done((s32[256]{0:T(256)S(1)}, s32[256]{0:T(256)}, u32[]{:S(2)}) %copy-start.9) | copy-done | bytes 1048
  17.0 0.9 %shard_map.158 = (bf16[128,512]{1,0:T(8,128)(2,1)S(1)}, f32[128,256]{1,0:T(8,128)S(1)}, bf16[64,128]{1,0:T(8,128)(2,1)S(1)}, bf16[16,128]{1,0:T(8,128)(2,1)S(1)}) custom-call(bf16[256,128]{1,0:T(8,128)(2,1)S(1)} %copy-done.4, bf16[256,128]{1,0:T(8,128)(2,1)S(1)} %collective-permute-done.refs_1_, bf16[128,256]{1,0:T(8,128)(2,1)S(1)} %collective-permute-done.1.refs_2_, ...), custom_call_target="tpu_custom_call" | custom-call | flops 16777216 | bytes 985600 | tf_op jit(solution)/shard_map/pallas_call | solution.py:73
  17.9 1.7 %all-to-all-done.came = bf16[16,16,128]{2,1,0:T(8,128)(2,1)S(1)} async-done(((bf16[16,16,128]{2,1,0:T(8,128)(2,1)}), bf16[16,16,128]{2,1,0:T(8,128)(2,1)S(1)}, u32[]{:S(2)}, u32[]{:S(2)}) %all-to-all-start) | async-done | bytes 65568 | tf_op jit(solution)/shard_map/all_to_all | solution.py:351
  19.6 0.6 %shard_map.159 = (f32[128,256]{1,0:T(8,128)S(1)}, f32[128,512]{1,0:T(8,128)S(1)}, bf16[144,512]{1,0:T(8,128)(2,1)S(1)}, bf16[16,512]{1,0:T(8,128)(2,1)S(1)}, f32[16,256]{1,0:T(8,128)S(1)}) custom-call(bf16[16,16,128]{2,1,0:T(8,128)(2,1)S(1)} %all-to-all-done.came, f32[128,256]{1,0:T(8,128)S(1)} %get-tuple-element.30.pre, ...), custom_call_target="tpu_custom_call" | custom-call | flops 16777216 | bytes 1789952 | tf_op jit(solution)/shard_map/pallas_call | solution.py:73
  20.4 0.6 %collective-permute-start.7 = (bf16[160,256]{1,0:T(8,128)(2,1)S(1)}, bf16[160,256]{1,0:T(8,128)(2,1)S(1)}, u32[]{:S(2)}, u32[]{:S(2)}) collective-permute-start(bf16[160,256]{1,0:T(8,128)(2,1)S(1)} %shard_map.161), channel_id=1, source_target_pairs={{0,1},{1,0},{2,3},{3,2},{4,5},{5,4},{6,7},{7,6},{8,9},{9,8},{10,11... | collective-permute-start | bytes 245768 | tf_op jit(solution)/shard_map/ppermute | solution.py:338
  21.0 0.9 %collective-permute-done.7.refs_5_ = bf16[160,256]{1,0:T(8,128)(2,1)S(1)} collective-permute-done((bf16[160,256]{1,0:T(8,128)(2,1)S(1)}, bf16[160,256]{1,0:T(8,128)(2,1)S(1)}, u32[]{:S(2)}, u32[]{:S(2)}) %collective-permute-start.7) | collective-permute-done | bytes 81952 | tf_op jit(solution)/shard_map/ppermute | solution.py:338
  21.9 3.7 %collective-permute-done.5.refs_2_ = bf16[144,512]{1,0:T(8,128)(2,1)S(1)} collective-permute-done((bf16[144,512]{1,0:T(8,128)(2,1)S(1)}, bf16[144,512]{1,0:T(8,128)(2,1)S(1)}, u32[]{:S(2)}, u32[]{:S(2)}) %collective-permute-start.5) | collective-permute-done | bytes 147488 | tf_op jit(solution)/shard_map/ppermute | solution.py:338
  25.8 1.2 %collective-permute-done.11.refs_3_ = f32[16,512]{1,0:T(8,128)S(1)} collective-permute-done((f32[16,512]{1,0:T(8,128)S(1)}, f32[16,512]{1,0:T(8,128)S(1)}, u32[]{:S(2)}, u32[]{:S(2)}) %collective-permute-start.11) | collective-permute-done | bytes 32800 | tf_op jit(solution)/shard_map/ppermute | solution.py:338
  27.0 2.4 %shard_map.163 = (bf16[16,128]{1,0:T(8,128)(2,1)}, bf16[128,256]{1,0:T(8,128)(2,1)S(1)}, f32[128,512]{1,0:T(8,128)S(1)}, bf16[16,16,128]{2,1,0:T(8,128)(2,1)}) custom-call(bf16[128,1024]{1,0:T(8,128)(2,1)S(1)} %collective-permute-done.9.refs_0_, bf16[128,1024]{1,0:T(8,128)(2,1)S(1)} %collective-permute-done.10.refs_1_, ...), custom_call_target="tpu_custom_call" | custom-call | flops 16777216 | bytes 3052032 | tf_op jit(solution)/shard_map/pallas_call | solution.py:73
  29.5 3.5 %all-to-all-start.1 = ((bf16[16,16,128]{2,1,0:T(8,128)(2,1)}), bf16[16,16,128]{2,1,0:T(8,128)(2,1)S(1)}, u32[]{:S(2)}, u32[]{:S(2)}) async-start(bf16[16,16,128]{2,1,0:T(8,128)(2,1)} %get-tuple-element.55), calls=%async_computation.1 | async-start | bytes 131072 | tf_op jit(solution)/shard_map/all_to_all | solution.py:419
  33.2 1.9 %collective-permute-start.13 = (bf16[128,256]{1,0:T(8,128)(2,1)S(1)}, bf16[128,256]{1,0:T(8,128)(2,1)S(1)}, u32[]{:S(2)}, u32[]{:S(2)}) collective-permute-start(bf16[128,256]{1,0:T(8,128)(2,1)S(1)} %get-tuple-element.49), channel_id=1, source_target_pairs={{0,2},{1,3},{2,0},{3,1},{4,6},{5,7},{6,4},{7,5},{8,10},{9,11},{10,... | collective-permute-start | bytes 196616 | tf_op jit(solution)/shard_map/ppermute | solution.py:338
  35.1 2.7 %collective-permute-done.13.refs_1_ = bf16[128,256]{1,0:T(8,128)(2,1)S(1)} collective-permute-done((bf16[128,256]{1,0:T(8,128)(2,1)S(1)}, bf16[128,256]{1,0:T(8,128)(2,1)S(1)}, u32[]{:S(2)}, u32[]{:S(2)}) %collective-permute-start.13) | collective-permute-done | bytes 65568 | tf_op jit(solution)/shard_map/ppermute | solution.py:338
  37.9 1.2 %collective-permute-done.14.grad_came = bf16[128,128]{1,0:T(8,128)(2,1)S(1)} collective-permute-done((bf16[128,128]{1,0:T(8,128)(2,1)S(1)}, bf16[128,128]{1,0:T(8,128)(2,1)S(1)}, u32[]{:S(2)}, u32[]{:S(2)}) %collective-permute-start.14) | collective-permute-done | bytes 32800 | tf_op jit(solution)/shard_map/ppermute | solution.py:338
  39.1 0.7 %shard_map.166 = (bf16[256,128]{1,0:T(8,128)(2,1)}, bf16[256,128]{1,0:T(8,128)(2,1)}) custom-call(bf16[128,128]{1,0:T(8,128)(2,1)S(1)} %get-tuple-element.37.next_mine, bf16[128,128]{1,0:T(8,128)(2,1)S(1)} %collective-permute-done.8.next_came, bf16[128,128]{1,0:T(8,128)(2,1)S(1)} %get-tuple-element.50.grad_mine, ...), custom_call_target="tpu_custom_call" | custom-call | flops 16777216 | bytes 131072 | tf_op jit(solution)/shard_map/pallas_call | solution.py:73
  39.8 0.6 %shard_map.167 = bf16[16,128]{1,0:T(8,128)(2,1)} custom-call(bf16[16,16,128]{2,1,0:T(8,128)(2,1)S(1)} %all-to-all-done.1.shares, bf16[16,128]{1,0:T(8,128)(2,1)S(1)} %copy-done.6), custom_call_target="tpu_custom_call" | custom-call | flops 16777216 | bytes 69632 | tf_op jit(solution)/shard_map/pallas_call | solution.py:73
  (51 shorter events, 2.4 us)
Async XLA Ops:
  0.7 15.7 %collective-permute-start.2 = (bf16[128,1536]{1,0:T(8,128)(2,1)}, bf16[128,1536]{1,0:T(8,128)(2,1)S(1)}, u32[]{:S(2)}, u32[]{:S(2)}) collective-permute-start(bf16[128,1536]{1,0:T(8,128)(2,1)} %e_mine.1), channel_id=1, source_target_pairs={{0,1},{1,0},{2,3},{3,2},{4,5},{5,4},{6,7},{7,6},{8,9},{9,8},{10,11... | collective-permute-start | bytes 1179656 | tf_op jit(solution)/shard_map/ppermute | solution.py:338
  1.6 3.1 %copy-start.1 = (bf16[128,1024]{1,0:T(8,128)(2,1)S(1)}, bf16[128,1024]{1,0:T(8,128)(2,1)}, u32[]{:S(2)}) copy-start(bf16[128,1024]{1,0:T(8,128)(2,1)} %refs_16_.1) | copy-start | bytes 786436
  1.6 3.1 %copy-start.4 = (bf16[256,128]{1,0:T(8,128)(2,1)S(1)}, bf16[256,128]{1,0:T(8,128)(2,1)}, u32[]{:S(2)}) copy-start(bf16[256,128]{1,0:T(8,128)(2,1)} %refs_0_.3) | copy-start | bytes 196612
  1.6 3.9 %copy-start.2 = (bf16[128,512]{1,0:T(8,128)(2,1)S(1)}, bf16[128,512]{1,0:T(8,128)(2,1)}, u32[]{:S(2)}) copy-start(bf16[128,512]{1,0:T(8,128)(2,1)} %refs_14_.1) | copy-start | bytes 393220
  1.6 11.7 %copy-start.5 = (bf16[256,128]{1,0:T(8,128)(2,1)S(1)}, bf16[256,128]{1,0:T(8,128)(2,1)}, u32[]{:S(2)}) copy-start(bf16[256,128]{1,0:T(8,128)(2,1)} %edge_cot.1) | copy-start | bytes 196612
  1.6 14.7 %copy-start = (bf16[128,1536]{1,0:T(8,128)(2,1)S(1)}, bf16[128,1536]{1,0:T(8,128)(2,1)}, u32[]{:S(2)}) copy-start(bf16[128,1536]{1,0:T(8,128)(2,1)} %e_mine.1) | copy-start | bytes 1179652
  1.7 11.0 %collective-permute-start.9 = (bf16[128,1024]{1,0:T(8,128)(2,1)S(1)}, bf16[128,1024]{1,0:T(8,128)(2,1)S(1)}, u32[]{:S(2)}, u32[]{:S(2)}) collective-permute-start(bf16[128,1024]{1,0:T(8,128)(2,1)S(1)} %pad_maximum_fusion), channel_id=1, source_target_pairs={{0,2},{1,3},{2,0},{3,1},{4,6},{5,7},{6,4},{7,5},{8,10},{9,11},{10,... | collective-permute-start | bytes 786440 | tf_op jit(solution)/shard_map/ppermute | solution.py:338
  4.7 14.9 %collective-permute-start.4 = (bf16[128,1024]{1,0:T(8,128)(2,1)S(1)}, bf16[128,1024]{1,0:T(8,128)(2,1)S(1)}, u32[]{:S(2)}, u32[]{:S(2)}) collective-permute-start(bf16[128,1024]{1,0:T(8,128)(2,1)S(1)} %copy-done.1), channel_id=1, source_target_pairs={{0,1},{1,0},{2,3},{3,2},{4,5},{5,4},{6,7},{7,6},{8,9},{9,8},{10,11... | collective-permute-start | bytes 786440 | tf_op jit(solution)/shard_map/ppermute | solution.py:338
  4.7 8.5 %collective-permute-start = (bf16[256,128]{1,0:T(8,128)(2,1)S(1)}, bf16[256,128]{1,0:T(8,128)(2,1)S(1)}, u32[]{:S(2)}, u32[]{:S(2)}) collective-permute-start(bf16[256,128]{1,0:T(8,128)(2,1)S(1)} %copy-done.4), channel_id=1, source_target_pairs={{0,2},{1,3},{2,0},{3,1},{4,6},{5,7},{6,4},{7,5},{8,10},{9,11},{10,... | collective-permute-start | bytes 196616 | tf_op jit(solution)/shard_map/ppermute | solution.py:338
  5.5 14.1 %collective-permute-start.3 = (bf16[128,512]{1,0:T(8,128)(2,1)S(1)}, bf16[128,512]{1,0:T(8,128)(2,1)S(1)}, u32[]{:S(2)}, u32[]{:S(2)}) collective-permute-start(bf16[128,512]{1,0:T(8,128)(2,1)S(1)} %copy-done.2), channel_id=1, source_target_pairs={{0,1},{1,0},{2,3},{3,2},{4,5},{5,4},{6,7},{7,6},{8,9},{9,8},{10,11... | collective-permute-start | bytes 393224 | tf_op jit(solution)/shard_map/ppermute | solution.py:338
  7.1 12.5 %all-to-all-start = ((bf16[16,16,128]{2,1,0:T(8,128)(2,1)}), bf16[16,16,128]{2,1,0:T(8,128)(2,1)S(1)}, u32[]{:S(2)}, u32[]{:S(2)}) async-start(bf16[16,16,128]{2,1,0:T(8,128)(2,1)} %shard_map.156), calls=%async_computation | async-start | bytes 131072 | tf_op jit(solution)/shard_map/all_to_all | solution.py:351
  12.7 13.1 %collective-permute-start.10 = (bf16[128,1024]{1,0:T(8,128)(2,1)S(1)}, bf16[128,1024]{1,0:T(8,128)(2,1)S(1)}, u32[]{:S(2)}, u32[]{:S(2)}) collective-permute-start(bf16[128,1024]{1,0:T(8,128)(2,1)S(1)} %collective-permute-done.9.refs_0_), channel_id=1, source_target_pairs={{0,1},{1,0},{2,3},{3,2},{4,5},{5,4},{6,7},{7,6},{8,9},{9,8},{10,11... | collective-permute-start | bytes 786440 | tf_op jit(solution)/shard_map/ppermute | solution.py:338
  13.2 1.3 %collective-permute-start.1 = (bf16[128,256]{1,0:T(8,128)(2,1)S(1)}, bf16[128,256]{1,0:T(8,128)(2,1)S(1)}, u32[]{:S(2)}, u32[]{:S(2)}) collective-permute-start(bf16[128,256]{1,0:T(8,128)(2,1)S(1)} %shard_map.157), channel_id=1, source_target_pairs={{0,1},{1,0},{2,3},{3,2},{4,5},{5,4},{6,7},{7,6},{8,9},{9,8},{10,11... | collective-permute-start | bytes 196616 | tf_op jit(solution)/shard_map/ppermute | solution.py:338
  14.0 2.3 %copy-start.7 = (s32[4,4,8]{2,1,0:T(4,128)S(1)}, s32[4,4,8]{2,1,0:T(4,128)}, u32[]{:S(2)}) copy-start(s32[4,4,8]{2,1,0:T(4,128)} %refs_7_.1) | copy-start | bytes 1540
  14.0 2.3 %copy-start.10 = (s32[256]{0:T(256)S(1)}, s32[256]{0:T(256)}, u32[]{:S(2)}) copy-start(s32[256]{0:T(256)} %param.17) | copy-start | bytes 3076
  14.5 5.9 %collective-permute-start.6 = (bf16[288,128]{1,0:T(8,128)(2,1)S(1)}, bf16[288,128]{1,0:T(8,128)(2,1)S(1)}, u32[]{:S(2)}, u32[]{:S(2)}) collective-permute-start(bf16[288,128]{1,0:T(8,128)(2,1)S(1)} %shard_map.160.refs_0_.refs_3_), channel_id=1, source_target_pairs={{0,2},{1,3},{2,0},{3,1},{4,6},{5,7},{6,4},{7,5},{8,10},{9,11},{10,... | collective-permute-start | bytes 221192 | tf_op jit(solution)/shard_map/ppermute | solution.py:338
  20.2 5.3 %collective-permute-start.5 = (bf16[144,512]{1,0:T(8,128)(2,1)S(1)}, bf16[144,512]{1,0:T(8,128)(2,1)S(1)}, u32[]{:S(2)}, u32[]{:S(2)}) collective-permute-start(bf16[144,512]{1,0:T(8,128)(2,1)S(1)} %get-tuple-element.35), channel_id=1, source_target_pairs={{0,2},{1,3},{2,0},{3,1},{4,6},{5,7},{6,4},{7,5},{8,10},{9,11},{10,... | collective-permute-start | bytes 442376 | tf_op jit(solution)/shard_map/ppermute | solution.py:338
  20.4 5.5 %collective-permute-start.12 = (bf16[128,512]{1,0:T(8,128)(2,1)S(1)}, bf16[128,512]{1,0:T(8,128)(2,1)S(1)}, u32[]{:S(2)}, u32[]{:S(2)}) collective-permute-start(bf16[128,512]{1,0:T(8,128)(2,1)S(1)} %copy-done.3), channel_id=1, source_target_pairs={{0,1},{1,0},{2,3},{3,2},{4,5},{5,4},{6,7},{7,6},{8,9},{9,8},{10,11... | collective-permute-start | bytes 393224 | tf_op jit(solution)/shard_map/ppermute | solution.py:338
  20.4 1.5 %collective-permute-start.7 = (bf16[160,256]{1,0:T(8,128)(2,1)S(1)}, bf16[160,256]{1,0:T(8,128)(2,1)S(1)}, u32[]{:S(2)}, u32[]{:S(2)}) collective-permute-start(bf16[160,256]{1,0:T(8,128)(2,1)S(1)} %shard_map.161), channel_id=1, source_target_pairs={{0,1},{1,0},{2,3},{3,2},{4,5},{5,4},{6,7},{7,6},{8,9},{9,8},{10,11... | collective-permute-start | bytes 245768 | tf_op jit(solution)/shard_map/ppermute | solution.py:338
  25.8 1.2 %collective-permute-start.11 = (f32[16,512]{1,0:T(8,128)S(1)}, f32[16,512]{1,0:T(8,128)S(1)}, u32[]{:S(2)}, u32[]{:S(2)}) collective-permute-start(f32[16,512]{1,0:T(8,128)S(1)} %get-tuple-element.39.refs_2_), channel_id=1, source_target_pairs={{0,1},{1,0},{2,3},{3,2},{4,5},{5,4},{6,7},{7,6},{8,9},{9,8},{10,11... | collective-permute-start | bytes 98312 | tf_op jit(solution)/shard_map/ppermute | solution.py:338
  29.5 10.4 %all-to-all-start.1 = ((bf16[16,16,128]{2,1,0:T(8,128)(2,1)}), bf16[16,16,128]{2,1,0:T(8,128)(2,1)S(1)}, u32[]{:S(2)}, u32[]{:S(2)}) async-start(bf16[16,16,128]{2,1,0:T(8,128)(2,1)} %get-tuple-element.55), calls=%async_computation.1 | async-start | bytes 131072 | tf_op jit(solution)/shard_map/all_to_all | solution.py:419
  33.2 4.6 %collective-permute-start.13 = (bf16[128,256]{1,0:T(8,128)(2,1)S(1)}, bf16[128,256]{1,0:T(8,128)(2,1)S(1)}, u32[]{:S(2)}, u32[]{:S(2)}) collective-permute-start(bf16[128,256]{1,0:T(8,128)(2,1)S(1)} %get-tuple-element.49), channel_id=1, source_target_pairs={{0,2},{1,3},{2,0},{3,1},{4,6},{5,7},{6,4},{7,5},{8,10},{9,11},{10,... | collective-permute-start | bytes 196616 | tf_op jit(solution)/shard_map/ppermute | solution.py:338
  35.1 2.8 %collective-permute-start.8 = (bf16[128,128]{1,0:T(8,128)(2,1)S(1)}, bf16[128,128]{1,0:T(8,128)(2,1)S(1)}, u32[]{:S(2)}, u32[]{:S(2)}) collective-permute-start(bf16[128,128]{1,0:T(8,128)(2,1)S(1)} %get-tuple-element.38), channel_id=1, source_target_pairs={{0,1},{1,0},{2,3},{3,2},{4,5},{5,4},{6,7},{7,6},{8,9},{9,8},{10,11... | collective-permute-start | bytes 98312 | tf_op jit(solution)/shard_map/ppermute | solution.py:338
  37.8 1.3 %collective-permute-start.14 = (bf16[128,128]{1,0:T(8,128)(2,1)S(1)}, bf16[128,128]{1,0:T(8,128)(2,1)S(1)}, u32[]{:S(2)}, u32[]{:S(2)}) collective-permute-start(bf16[128,128]{1,0:T(8,128)(2,1)S(1)} %get-tuple-element.51), channel_id=1, source_target_pairs={{0,1},{1,0},{2,3},{3,2},{4,5},{5,4},{6,7},{7,6},{8,9},{9,8},{10,11... | collective-permute-start | bytes 98312 | tf_op jit(solution)/shard_map/ppermute | solution.py:338
  (7 other events, 5.2 us)
